TPU v7x, 32 devices: a whole 2x2x4 slice. The times are simulated.
32 devices in a mesh: section: 2 (over core), seq: 16 (over z, y, x).
Axes of the slice: x: 2, y: 2, z: 4, core: 2. Of those that a mesh axis runs over, the one named last changes fastest.
Arguments:
- byte_values: int32 [3, 4096], P(None, 'seq'), may hold values from 0 to 255
- item_lengths: int32 [3, 4], replicated, may hold values from 0 to 4096, as said below
- embed_tables: bfloat16 [2, 256, 768], P('section'), may hold values from -6 to 6
- patch_weight: bfloat16 [6144, 768], P(('section', 'seq')), may hold values from -0.078125 to 0.078125
- norm_gains: float32 [2, 2, 768], P('section'), may hold values from 0.25 to 1.75
- norm_biases: float32 [2, 2, 768], P('section'), may hold values from -3 to 3
- heads_in: bfloat16 [2, 768, 2304], P('section'), may hold values from -0.21875 to 0.21875
- heads_out: bfloat16 [2, 768, 768], P('section'), may hold values from -0.875 to 0.875
- expand_weight: bfloat16 [2, 768, 3072], P('section'), may hold values from -0.21875 to 0.21875
- contract_weight: bfloat16 [2, 3072, 768], P('section'), may hold values from -0.109375 to 0.109375
- out_grad: bfloat16 [3, 4096, 768], P(None, 'seq'), may hold values from -6 to 6
Outputs:
- activations: bfloat16 [2, 3, 4096, 768], P('section', None, 'seq')
- table_grads: float32 [2, 256, 768], P('section', 'seq')
- patch_grads: float32 [6144, 768], P(('section', 'seq'))
- gain_grads: float32 [2, 2, 768], P('section', None, 'seq')
- bias_grads: float32 [2, 2, 768], P('section', None, 'seq')
- heads_in_grads: float32 [2, 768, 2304], P('section', 'seq')
- heads_out_grads: float32 [2, 768, 768], P('section', 'seq')
- expand_grads: float32 [2, 768, 3072], P('section', 'seq')
- contract_grads: float32 [2, 3072, 768], P('section', 'seq')
Inputs may be any that keep to these rules, and one draw needn't show every extreme that they name: `item_lengths`: row m lists the byte lengths of the items of micro-batch m in order; a 0 is an empty slot; the items, each padded to whole patches, fit in 4096 bytes. In one micro-batch a single item fills all 4096 bytes and the other slots are empty; in the others every item has 1 to 1024 bytes.
All inputs are finite; a program needn't handle non-finite values.
Results may differ from a plain program's by a relative error of at most 0.02.
Values may be sent and summed in bfloat16 or wider, within the bound.
No kernel may reach another device: no remote copies, remote signals or barrier semaphores. Data moves between devices by JAX's collectives and lax.ppermute only.
A program may use at most 384 MiB of HBM per device.

v0:
```python
from functools import partial

import jax
import jax.numpy as jnp
from jax import lax
from jax.sharding import PartitionSpec as P

HEADS = 12
HEAD_SIZE = 64
VOCAB = 256
PATCH = 8
ITEMS = 4


EPSILON = 1e-05
MASKED = -1e30
LAYER_NAMES = (
    "gain_grads",
    "bias_grads",
    "mix_in_grads",
    "mix_out_grads",
    "expand_grads",
    "contract_grads",
)


def from_behind(x, axis, by):
    peers = lax.axis_size(axis)
    pairs = [(i, i + by) for i in range(peers) if 0 <= i + by < peers]
    return lax.ppermute(x, axis, pairs)


def for_sending(x):
    return jax.tree.map(lambda a: a.astype(jnp.bfloat16) if a.dtype == jnp.float32 else a, x)


def partner(x, axis, stride):
    return lax.ppermute(x, axis, [(i, i ^ 1 << stride) for i in range(lax.axis_size(axis))])


def layer_norm(values, norm_gain, norm_bias):
    average = jnp.mean(values, axis=-1, keepdims=True)
    centered = values - average
    inverse_root = lax.rsqrt(jnp.mean(centered * centered, axis=-1, keepdims=True) + EPSILON)
    return centered * inverse_root * norm_gain + norm_bias


def locate(positions, lengths_row):
    padded = (lengths_row + PATCH - 1) // PATCH * PATCH
    item_ends = jnp.cumsum(padded)
    starts = item_ends - padded
    inside = (positions[:, None] >= starts[None, :]) & (positions[:, None] < item_ends[None, :])
    offsets = jnp.arange(ITEMS, dtype=jnp.int32)[None, :] - ITEMS
    owners = jnp.sum(jnp.where(inside, offsets, 0), axis=1) + ITEMS
    live_mask = jnp.any(inside & (positions[:, None] < (starts + lengths_row)[None, :]), axis=1)
    return (owners, live_mask)


def global_mask(query_places, key_places, lengths_row):
    query_owners = locate(query_places * PATCH, lengths_row)[0]
    key_owners = locate(key_places * PATCH, lengths_row)[0]
    return (key_places[None, :] <= query_places[:, None]) & (
        key_owners[None, :] == query_owners[:, None]
    )


def product(former, latter):
    return jnp.dot(former, latter, preferred_element_type=jnp.float32)


def transposed_product(former, latter):
    return lax.dot_general(
        former, latter, (((0,), (0,)), ((), ())), preferred_element_type=jnp.float32
    )


def product_transposed(former, latter):
    return lax.dot_general(
        former, latter, (((1,), (1,)), ((), ())), preferred_element_type=jnp.float32
    )


def block_forward(stream, layer_weights, attend):
    gain_rows, bias_rows, mix_in, mix_out, expand, contract = layer_weights
    normed = layer_norm(stream, gain_rows[0], bias_rows[0]).astype(jnp.bfloat16)
    mixed_heads = product(normed, mix_in).astype(jnp.bfloat16)
    attended, softmax_logs = attend(mixed_heads)
    middle = stream + product(attended, mix_out)
    normed_two = layer_norm(middle, gain_rows[1], bias_rows[1]).astype(jnp.bfloat16)
    upward = product(normed_two, expand)
    hidden = jax.nn.gelu(upward).astype(jnp.bfloat16)
    result = middle + product(hidden, contract)
    return (
        result,
        (stream, normed, mixed_heads, attended, softmax_logs, middle, normed_two, upward, hidden),
    )


def block_backward(grad_result, kept_values, layer_weights, attend_back):
    stream, normed, mixed_heads, attended, softmax_logs, middle, normed_two, upward, hidden = (
        kept_values
    )
    gain_rows, bias_rows, mix_in, mix_out, expand, contract = layer_weights
    grad_branch = grad_result.astype(jnp.bfloat16)
    grad_contract = transposed_product(hidden, grad_branch)
    grad_hidden = product_transposed(grad_branch, contract)
    grad_upward = jax.vjp(jax.nn.gelu, upward)[1](grad_hidden)[0].astype(jnp.bfloat16)
    grad_expand = transposed_product(normed_two, grad_upward)
    grad_normed_two = product_transposed(grad_upward, expand)
    grad_middle, gain_two, bias_two = jax.vjp(layer_norm, middle, gain_rows[1], bias_rows[1])[1](
        grad_normed_two
    )
    grad_middle = grad_middle + grad_result
    attend_branch = grad_middle.astype(jnp.bfloat16)
    grad_mix_out = transposed_product(attended, attend_branch)
    grad_attended = product_transposed(attend_branch, mix_out).astype(jnp.bfloat16)
    grad_mixed = attend_back(grad_attended, mixed_heads, attended, softmax_logs)
    grad_mix_in = transposed_product(normed, grad_mixed)
    grad_normed = product_transposed(grad_mixed, mix_in)
    grad_stream, gain_one, bias_one = jax.vjp(layer_norm, stream, gain_rows[0], bias_rows[0])[1](
        grad_normed
    )
    grad_stream = grad_stream + grad_middle
    layer_grads = (
        jnp.stack([gain_one, gain_two]),
        jnp.stack([bias_one, bias_two]),
        grad_mix_in,
        grad_mix_out,
        grad_expand,
        grad_contract,
    )
    return (grad_stream, layer_grads)


def local_scores(mixed_heads, live_mask):
    row_count = mixed_heads.shape[0]
    shaped = mixed_heads.reshape(row_count // PATCH, PATCH, 3, HEADS, HEAD_SIZE)
    queries, key_rows, value_rows = (shaped[:, :, 0], shaped[:, :, 1], shaped[:, :, 2])
    scores = jnp.einsum(
        "pqhd,pkhd->phqk", queries, key_rows, preferred_element_type=jnp.float32
    ) * HEAD_SIZE ** (-0.5)
    places = jnp.arange(PATCH, dtype=jnp.int32)
    causal = places[None, :] <= places[:, None]
    itself = places[None, :] == places[:, None]
    alive_keys = live_mask.reshape(row_count // PATCH, 1, 1, PATCH)
    allowed = causal[None, None] & (alive_keys | itself[None, None])
    probabilities = jax.nn.softmax(jnp.where(allowed, scores, MASKED), axis=-1)
    return (queries, key_rows, value_rows, probabilities)


def local_forward(mixed_heads, live_mask):
    queries, key_rows, value_rows, probabilities = local_scores(mixed_heads, live_mask)
    attended = jnp.einsum(
        "phqk,pkhd->pqhd",
        probabilities.astype(jnp.bfloat16),
        value_rows,
        preferred_element_type=jnp.float32,
    )
    return (
        attended.reshape(mixed_heads.shape[0], HEADS * HEAD_SIZE).astype(jnp.bfloat16),
        jnp.zeros((1,), jnp.float32),
    )


def local_backward(grad_attended, mixed_heads, attended, softmax_logs, live_mask):
    row_count = mixed_heads.shape[0]
    queries, key_rows, value_rows, probabilities = local_scores(mixed_heads, live_mask)
    grad_heads = grad_attended.reshape(row_count // PATCH, PATCH, HEADS, HEAD_SIZE)
    prob_grads = jnp.einsum(
        "pqhd,pkhd->phqk", grad_heads, value_rows, preferred_element_type=jnp.float32
    )
    row_delta = jnp.sum(probabilities * prob_grads, axis=-1, keepdims=True)
    score_grads = (probabilities * (prob_grads - row_delta)).astype(jnp.bfloat16)
    score_scale = HEAD_SIZE ** (-0.5)
    grad_queries = (
        jnp.einsum("phqk,pkhd->pqhd", score_grads, key_rows, preferred_element_type=jnp.float32)
        * score_scale
    )
    grad_keys = (
        jnp.einsum("phqk,pqhd->pkhd", score_grads, queries, preferred_element_type=jnp.float32)
        * score_scale
    )
    grad_values = jnp.einsum(
        "phqk,pqhd->pkhd",
        probabilities.astype(jnp.bfloat16),
        grad_heads,
        preferred_element_type=jnp.float32,
    )
    stacked = jnp.stack([grad_queries, grad_keys, grad_values], axis=2)
    return stacked.reshape(row_count, 3 * HEADS * HEAD_SIZE).astype(jnp.bfloat16)


def on_device(
    byte_values,
    item_lengths,
    embed_tables,
    patch_weight,
    norm_gains,
    norm_biases,
    heads_in,
    heads_out,
    expand_weight,
    contract_weight,
    out_grad,
):
    seq_index = lax.axis_index("seq")
    seq_count = lax.axis_size("seq")
    is_global = lax.axis_index("section") == 0
    batches, byte_rows = byte_values.shape
    patch_rows = byte_rows // PATCH
    model_width = heads_out.shape[2]
    hidden_width = expand_weight.shape[2]
    key_count = patch_rows * seq_count
    score_scale = HEAD_SIZE ** (-0.5)
    layer_weights = (
        norm_gains[0],
        norm_biases[0],
        heads_in[0],
        heads_out[0],
        expand_weight[0],
        contract_weight[0],
    )
    byte_table = embed_tables[0]
    patch_full = lax.all_gather(patch_weight, ("section", "seq"), axis=0, tiled=True)
    byte_places = seq_index * byte_rows + jnp.arange(byte_rows, dtype=jnp.int32)
    patch_places = seq_index * patch_rows + jnp.arange(patch_rows, dtype=jnp.int32)
    vocabulary = jnp.arange(VOCAB, dtype=jnp.int32)

    def embed_bytes(micro_batch):
        onehot = (byte_values[micro_batch][:, None] == vocabulary[None, :]).astype(jnp.bfloat16)
        return (onehot, product(onehot, byte_table))

    def same_item(micro_batch):
        lengths_row = item_lengths[micro_batch]
        current = locate(patch_places * PATCH, lengths_row)[0]
        earlier = locate(patch_places * PATCH - PATCH, lengths_row)[0]
        return (current == earlier)[:, None]

    def spread_rows(patch_values):
        return jnp.broadcast_to(patch_values[:, None, :], (patch_rows, PATCH, model_width)).reshape(
            byte_rows, model_width
        )

    def add_layer(carry_state, layer_grads):
        for entry_name, update in zip(LAYER_NAMES, layer_grads):
            carry_state[entry_name] = carry_state[entry_name] + update
        return carry_state

    def global_forward(carry_state, micro_batch):
        lengths_row = item_lengths[micro_batch]
        onehot, embedded = embed_bytes(micro_batch)
        patches = embedded.astype(jnp.bfloat16).reshape(patch_rows, PATCH * model_width)
        stream = product(patches, patch_full)

        def attend(mixed_heads):
            queries = mixed_heads[:, :model_width].reshape(patch_rows, HEADS, HEAD_SIZE)
            key_rows, value_rows = (
                lax.all_gather(
                    mixed_heads[:, model_width : 2 * model_width], "seq", axis=0, tiled=True
                ),
                lax.all_gather(mixed_heads[:, 2 * model_width :], "seq", axis=0, tiled=True),
            )
            scores = (
                jnp.einsum(
                    "phd,nhd->hpn",
                    queries,
                    key_rows.reshape(key_count, HEADS, HEAD_SIZE),
                    preferred_element_type=jnp.float32,
                )
                * score_scale
            )
            allowed = global_mask(patch_places, jnp.arange(key_count, dtype=jnp.int32), lengths_row)
            scores = jnp.where(allowed[None], scores, MASKED)
            row_peak = jnp.max(scores, axis=-1, keepdims=True)
            exponents = jnp.exp(scores - row_peak)
            row_total = jnp.sum(exponents, axis=-1, keepdims=True)
            probabilities = (exponents / row_total).astype(jnp.bfloat16)
            attended = jnp.einsum(
                "hpn,nhd->phd",
                probabilities,
                value_rows.reshape(key_count, HEADS, HEAD_SIZE),
                preferred_element_type=jnp.float32,
            )
            return (
                attended.reshape(patch_rows, model_width).astype(jnp.bfloat16),
                (row_peak + jnp.log(row_total))[:, :, 0],
            )

        result, kept_values = block_forward(stream, layer_weights, attend)
        sent_rows = result.astype(jnp.bfloat16)
        live_mask = locate(byte_places, lengths_row)[1]
        carry_state["outputs"] = (
            carry_state["outputs"]
            .at[micro_batch]
            .set(jnp.where(live_mask[:, None], spread_rows(sent_rows), jnp.zeros((), jnp.bfloat16)))
        )
        before = from_behind(sent_rows[-1:], "seq", 1)
        shifted = jnp.concatenate([before, sent_rows[:-1]], axis=0)
        carry_state["outgoing"] = jnp.where(
            same_item(micro_batch), shifted, jnp.zeros_like(shifted)
        )
        carry_state["global_kept"] = jax.tree.map(
            lambda stacked, member: stacked.at[micro_batch].set(member),
            carry_state["global_kept"],
            (patches,) + kept_values,
        )
        return carry_state

    def global_backward(carry_state, micro_batch):
        lengths_row = item_lengths[micro_batch]
        stored = tuple((member[micro_batch] for member in carry_state["global_kept"]))
        patches = stored[0]
        grad_shifted = jnp.where(
            same_item(micro_batch), carry_state["received"], jnp.zeros_like(carry_state["received"])
        )
        after = from_behind(for_sending(grad_shifted[:1]), "seq", -1)
        grad_result = jnp.concatenate([grad_shifted[1:], after], axis=0).astype(jnp.float32)

        def fetch_keys(mixed_heads):
            return (
                lax.all_gather(
                    for_sending(mixed_heads[:, model_width : 2 * model_width]),
                    "seq",
                    axis=0,
                    tiled=True,
                ),
                lax.all_gather(
                    for_sending(mixed_heads[:, 2 * model_width :]), "seq", axis=0, tiled=True
                ),
            )

        def attend_back(grad_attended, mixed_heads, attended, softmax_logs):
            grad_heads = grad_attended.reshape(patch_rows, HEADS, HEAD_SIZE)
            queries = mixed_heads[:, :model_width].reshape(patch_rows, HEADS, HEAD_SIZE)
            key_rows, value_rows = fetch_keys(mixed_heads)
            key_heads = key_rows.reshape(key_count, HEADS, HEAD_SIZE)
            value_heads = value_rows.reshape(key_count, HEADS, HEAD_SIZE)
            scores = (
                jnp.einsum("phd,nhd->hpn", queries, key_heads, preferred_element_type=jnp.float32)
                * score_scale
            )
            allowed = global_mask(patch_places, jnp.arange(key_count, dtype=jnp.int32), lengths_row)
            probabilities = jnp.where(
                allowed[None], jnp.exp(scores - softmax_logs[:, :, None]), 0.0
            )
            prob_grads = jnp.einsum(
                "phd,nhd->hpn", grad_heads, value_heads, preferred_element_type=jnp.float32
            )
            row_delta = jnp.sum(probabilities * prob_grads, axis=-1, keepdims=True)
            score_grads = (probabilities * (prob_grads - row_delta)).astype(jnp.bfloat16)
            probs_low = probabilities.astype(jnp.bfloat16)
            grad_queries = (
                jnp.einsum(
                    "hpn,nhd->phd", score_grads, key_heads, preferred_element_type=jnp.float32
                ).reshape(patch_rows, model_width)
                * score_scale
            )
            row_count = patch_rows * lax.axis_size("seq")
            part_grads = lax.slice_in_dim(score_grads, 0, row_count, axis=2)
            part_probs = lax.slice_in_dim(probs_low, 0, row_count, axis=2)
            grad_keys = (
                jnp.einsum(
                    "hpn,phd->nhd", part_grads, queries, preferred_element_type=jnp.float32
                ).reshape(row_count, model_width)
                * score_scale
            )
            grad_values = jnp.einsum(
                "hpn,phd->nhd", part_probs, grad_heads, preferred_element_type=jnp.float32
            ).reshape(row_count, model_width)
            own_terms = lax.psum_scatter(
                jnp.concatenate([grad_keys, grad_values], axis=1),
                "seq",
                scatter_dimension=0,
                tiled=True,
            )
            return jnp.concatenate([grad_queries, own_terms], axis=1).astype(jnp.bfloat16)

        grad_stream, layer_grads = block_backward(
            grad_result, stored[1:], layer_weights, attend_back
        )
        carry_state = add_layer(carry_state, layer_grads)
        stream_low = grad_stream.astype(jnp.bfloat16)
        carry_state["patch_grads"] = carry_state["patch_grads"] + transposed_product(
            patches, stream_low
        )
        grad_embedded = (
            product_transposed(stream_low, patch_full)
            .reshape(byte_rows, model_width)
            .astype(jnp.bfloat16)
        )
        onehot = embed_bytes(micro_batch)[0]
        carry_state["table_grads"] = carry_state["table_grads"] + transposed_product(
            onehot, grad_embedded
        )
        return carry_state

    carry_state = {
        "received": jnp.zeros((patch_rows, model_width), jnp.bfloat16),
        "outgoing": jnp.zeros((patch_rows, model_width), jnp.bfloat16),
        "outputs": jnp.zeros((batches, byte_rows, model_width), jnp.bfloat16),
        "gain_grads": jnp.zeros((2, model_width), jnp.float32),
        "bias_grads": jnp.zeros((2, model_width), jnp.float32),
        "mix_in_grads": jnp.zeros(heads_in.shape[1:], jnp.float32),
        "mix_out_grads": jnp.zeros(heads_out.shape[1:], jnp.float32),
        "expand_grads": jnp.zeros(expand_weight.shape[1:], jnp.float32),
        "contract_grads": jnp.zeros(contract_weight.shape[1:], jnp.float32),
        "table_grads": jnp.zeros((VOCAB, model_width), jnp.float32),
        "patch_grads": jnp.zeros((PATCH * model_width, model_width), jnp.float32),
        "global_kept": (
            jnp.zeros((batches, patch_rows, PATCH * model_width), jnp.bfloat16),
            jnp.zeros((batches, patch_rows, model_width), jnp.float32),
            jnp.zeros((batches, patch_rows, model_width), jnp.bfloat16),
            jnp.zeros((batches, patch_rows, 3 * model_width), jnp.bfloat16),
            jnp.zeros((batches, patch_rows, model_width), jnp.bfloat16),
            jnp.zeros((batches, HEADS, patch_rows), jnp.float32),
            jnp.zeros((batches, patch_rows, model_width), jnp.float32),
            jnp.zeros((batches, patch_rows, model_width), jnp.bfloat16),
            jnp.zeros((batches, patch_rows, hidden_width), jnp.float32),
            jnp.zeros((batches, patch_rows, hidden_width), jnp.bfloat16),
        ),
    }
    for tick_number in range(batches + 2):
        backward_batch = tick_number - 2
        local_batch = tick_number - 1
        global_state = dict(carry_state)
        if backward_batch >= 0:
            global_state = global_backward(global_state, backward_batch)
        if tick_number < batches:
            global_state = global_forward(global_state, tick_number)
        local_state = dict(carry_state)
        if 0 <= local_batch < batches:
            local_carry_state = local_state
            local_lengths_row = item_lengths[local_batch]
            local_live_mask = locate(byte_places, local_lengths_row)[1]
            local_onehot, local_embedded = embed_bytes(local_batch)
            local_stream = local_embedded + spread_rows(
                local_carry_state["received"].astype(jnp.float32)
            )
            local_result, local_kept_values = block_forward(
                local_stream, layer_weights, partial(local_forward, live_mask=local_live_mask)
            )
            local_carry_state["outputs"] = (
                local_carry_state["outputs"]
                .at[local_batch]
                .set(jnp.where(local_live_mask[:, None], local_result, 0.0).astype(jnp.bfloat16))
            )
            local_grad_result = jnp.where(
                local_live_mask[:, None], out_grad[local_batch].astype(jnp.float32), 0.0
            )
            local_grad_stream, local_layer_grads = block_backward(
                local_grad_result,
                local_kept_values,
                layer_weights,
                partial(local_backward, live_mask=local_live_mask),
            )
            local_carry_state = add_layer(local_carry_state, local_layer_grads)
            local_carry_state["table_grads"] = local_carry_state[
                "table_grads"
            ] + transposed_product(local_onehot, local_grad_stream.astype(jnp.bfloat16))
            local_carry_state["outgoing"] = jnp.sum(
                local_grad_stream.reshape(patch_rows, PATCH, model_width), axis=1
            ).astype(jnp.bfloat16)
            local_state = local_carry_state
        carry_state = jax.tree.map(
            lambda upper, lower: jnp.where(is_global, upper, lower), global_state, local_state
        )
        if tick_number <= batches:
            carry_state = dict(carry_state)
            carry_state["received"] = partner(for_sending(carry_state["outgoing"]), "section", 0)
    stacked_grads = tuple((carry_state[entry_name][None] for entry_name in LAYER_NAMES)) + (
        carry_state["table_grads"][None],
    )
    reduced = (
        lax.psum_scatter(stacked_grads[0], "seq", scatter_dimension=2, tiled=True),
        lax.psum_scatter(stacked_grads[1], "seq", scatter_dimension=2, tiled=True),
        lax.psum_scatter(stacked_grads[2], "seq", scatter_dimension=1, tiled=True),
        lax.psum_scatter(stacked_grads[3], "seq", scatter_dimension=1, tiled=True),
        lax.psum_scatter(stacked_grads[4], "seq", scatter_dimension=1, tiled=True),
        lax.psum_scatter(stacked_grads[5], "seq", scatter_dimension=1, tiled=True),
        lax.psum_scatter(stacked_grads[6], "seq", scatter_dimension=1, tiled=True),
    )
    patch_total = lax.psum_scatter(
        carry_state["patch_grads"], ("section", "seq"), scatter_dimension=0, tiled=True
    )
    return (
        carry_state["outputs"][None],
        reduced[6],
        patch_total,
        reduced[0],
        reduced[1],
        reduced[2],
        reduced[3],
        reduced[4],
        reduced[5],
    )


def solution(mesh):
    placed = (
        P(None, "seq"),
        P(),
        P("section", None, None),
        P(("section", "seq"), None),
        P("section", None, None),
        P("section", None, None),
        P("section", None, None),
        P("section", None, None),
        P("section", None, None),
        P("section", None, None),
        P(None, "seq", None),
    )
    return jax.shard_map(
        on_device,
        mesh=mesh,
        in_specs=placed,
        out_specs=(
            P("section", None, "seq", None),
            P("section", "seq", None),
            P(("section", "seq"), None),
            P("section", None, "seq"),
            P("section", None, "seq"),
            P("section", "seq", None),
            P("section", "seq", None),
            P("section", "seq", None),
            P("section", "seq", None),
        ),
        check_vma=False,
    )
```

profile of v0, /device:TPU:0, one launch (start us, length us, event | category | flops | bytes accessed | tf_op | source)
XLA Modules:
  0.0 2443.8 jit_solution(6994944041724504658)
XLA Ops:
  35.8 59.8 %all-gather.2.cloned.1.call-done = bf16[6144,768]{1,0:T(8,128)(2,1)} async-done(((bf16[192,768]{1,0:T(8,128)(2,1)}), bf16[6144,768]{1,0:T(8,128)(2,1)}) %all-gather.2.cloned.1.call-update) | async-done | bytes 9437200 | tf_op jit(solution)/shard_map/all_gather | solution.py:224
  104.1 45.3 %all_gather.40 = bf16[512,768]{1,0:T(8,128)(2,1)} all-gather(bf16[32,768]{1,0:T(8,128)(2,1)S(1)} %get-tuple-element.585), channel_id=1, replica_groups=mesh['section'=2,'seq'=16] {'seq'}, dimensions={0}, use_global_device_ids=true | all-gather | bytes 835584 | tf_op jit(solution)/shard_map/all_gather | solution.py:261
  151.7 42.5 %all_gather.41 = bf16[512,768]{1,0:T(8,128)(2,1)} all-gather(bf16[32,768]{1,0:T(8,128)(2,1)} %get-tuple-element.584), channel_id=1, replica_groups=mesh['section'=2,'seq'=16] {'seq'}, dimensions={0}, use_global_device_ids=true | all-gather | bytes 835584 | tf_op jit(solution)/shard_map/all_gather | solution.py:258
  216.1 45.2 %all_gather.42 = bf16[512,768]{1,0:T(8,128)(2,1)} all-gather(bf16[32,768]{1,0:T(8,128)(2,1)S(1)} %get-tuple-element.582), channel_id=1, replica_groups=mesh['section'=2,'seq'=16] {'seq'}, dimensions={0}, use_global_device_ids=true | all-gather | bytes 835584 | tf_op jit(solution)/shard_map/all_gather | solution.py:261
  263.6 42.8 %all_gather.43 = bf16[512,768]{1,0:T(8,128)(2,1)} all-gather(bf16[32,768]{1,0:T(8,128)(2,1)} %get-tuple-element.581), channel_id=1, replica_groups=mesh['section'=2,'seq'=16] {'seq'}, dimensions={0}, use_global_device_ids=true | all-gather | bytes 835584 | tf_op jit(solution)/shard_map/all_gather | solution.py:258
  343.2 42.3 %all_gather.44 = bf16[512,768]{1,0:T(8,128)(2,1)} all-gather(bf16[32,768]{1,0:T(8,128)(2,1)S(1)} %get-tuple-element.579), channel_id=1, replica_groups=mesh['section'=2,'seq'=16] {'seq'}, dimensions={0}, use_global_device_ids=true | all-gather | bytes 835584 | tf_op jit(solution)/shard_map/all_gather | solution.py:261
  387.9 45.2 %all_gather.45 = bf16[512,768]{1,0:T(8,128)(2,1)} all-gather(bf16[32,768]{1,0:T(8,128)(2,1)} %get-tuple-element.578), channel_id=1, replica_groups=mesh['section'=2,'seq'=16] {'seq'}, dimensions={0}, use_global_device_ids=true | all-gather | bytes 835584 | tf_op jit(solution)/shard_map/all_gather | solution.py:258
  460.7 42.5 %all_gather.51 = bf16[512,768]{1,0:T(8,128)(2,1)} all-gather(bf16[32,768]{1,0:T(8,128)(2,1)S(1)} %get-tuple-element.568), channel_id=1, replica_groups=mesh['section'=2,'seq'=16] {'seq'}, dimensions={0}, use_global_device_ids=true | all-gather | bytes 835584 | tf_op jit(solution)/shard_map/all_gather | solution.py:327
  503.2 44.3 %all_gather.50 = bf16[512,768]{1,0:T(8,128)(2,1)} all-gather(bf16[32,768]{1,0:T(8,128)(2,1)S(1)} %get-tuple-element.570), channel_id=1, replica_groups=mesh['section'=2,'seq'=16] {'seq'}, dimensions={0}, use_global_device_ids=true | all-gather | bytes 835584 | tf_op jit(solution)/shard_map/all_gather | solution.py:321
  799.8 48.4 %all_gather.49 = bf16[512,768]{1,0:T(8,128)(2,1)} all-gather(bf16[32,768]{1,0:T(8,128)(2,1)S(1)} %get-tuple-element.571), channel_id=1, replica_groups=mesh['section'=2,'seq'=16] {'seq'}, dimensions={0}, use_global_device_ids=true | all-gather | bytes 835584 | tf_op jit(solution)/shard_map/all_gather | solution.py:327
  850.5 42.7 %all_gather.48 = bf16[512,768]{1,0:T(8,128)(2,1)} all-gather(bf16[32,768]{1,0:T(8,128)(2,1)} %get-tuple-element.573), channel_id=1, replica_groups=mesh['section'=2,'seq'=16] {'seq'}, dimensions={0}, use_global_device_ids=true | all-gather | bytes 835584 | tf_op jit(solution)/shard_map/all_gather | solution.py:321
  919.9 47.1 %all_gather.47 = bf16[512,768]{1,0:T(8,128)(2,1)} all-gather(bf16[32,768]{1,0:T(8,128)(2,1)S(1)} %get-tuple-element.574), channel_id=1, replica_groups=mesh['section'=2,'seq'=16] {'seq'}, dimensions={0}, use_global_device_ids=true | all-gather | bytes 835584 | tf_op jit(solution)/shard_map/all_gather | solution.py:327
  969.3 43.5 %all_gather.46 = bf16[512,768]{1,0:T(8,128)(2,1)} all-gather(bf16[32,768]{1,0:T(8,128)(2,1)} %get-tuple-element.576), channel_id=1, replica_groups=mesh['section'=2,'seq'=16] {'seq'}, dimensions={0}, use_global_device_ids=true | all-gather | bytes 835584 | tf_op jit(solution)/shard_map/all_gather | solution.py:321
  1127.5 74.1 %reduce-scatter.34.cloned.1.call-done = f32[32,1536]{1,0:T(8,128)} async-done(((f32[512,1536]{1,0:T(8,128)}), f32[32,1536]{1,0:T(8,128)}) %reduce-scatter.34.cloned.1.call-update) | async-done | bytes 196624 | tf_op jit(solution)/shard_map/reduce_scatter | solution.py:370
  1212.6 6.4 fusion.111
  1219.7 6.6 convolution_convert_fusion.2
  1226.7 6.6 convolution_convert_fusion.1
  1233.8 6.6 convolution_convert_fusion
  1244.6 17.7 fusion.3
  1263.5 8.0 fusion.334
  1293.2 17.3 fusion.4
  1333.0 15.8 fusion.5
  1349.8 7.9 fusion.347
  1357.7 8.0 fusion.349
  1365.7 20.8 add_select_fusion
  1406.4 49.1 %reduce-scatter.42.cloned.1.call-done = f32[48,2]{1,0:T(8,128)} async-done(((f32[768,2]{1,0:T(8,128)}), f32[48,2]{1,0:T(8,128)}) %reduce-scatter.42.cloned.1.call-update) | async-done | bytes 400
  1456.9 130.7 %reduce-scatter.28.cloned.1.call-done = f32[1,48,768]{2,1,0:T(8,128)} async-done(((f32[1,768,768]{2,1,0:T(8,128)}), f32[1,48,768]{2,1,0:T(8,128)}) %reduce-scatter.28.cloned.1.call-update) | async-done | bytes 147472 | tf_op jit(solution)/shard_map/reduce_scatter | solution.py:477
  1587.6 127.4 %reduce-scatter.22.cloned.1.call-done = f32[1,16,768]{2,1,0:T(8,128)} async-done(((f32[1,256,768]{2,1,0:T(8,128)}), f32[1,16,768]{2,1,0:T(8,128)}) %reduce-scatter.22.cloned.1.call-update) | async-done | bytes 49168 | tf_op jit(solution)/shard_map/reduce_scatter | solution.py:480
  1715.0 177.4 %reduce-scatter.30.cloned.1.call-done = f32[1,48,3072]{2,1,0:T(8,128)} async-done(((f32[1,768,3072]{2,1,0:T(8,128)}), f32[1,48,3072]{2,1,0:T(8,128)}) %reduce-scatter.30.cloned.1.call-update) | async-done | bytes 589840 | tf_op jit(solution)/shard_map/reduce_scatter | solution.py:478
  1892.4 176.2 %reduce-scatter.32.cloned.1.call-done = f32[1,192,768]{2,1,0:T(8,128)} async-done(((f32[1,3072,768]{2,1,0:T(8,128)}), f32[1,192,768]{2,1,0:T(8,128)}) %reduce-scatter.32.cloned.1.call-update) | async-done | bytes 589840 | tf_op jit(solution)/shard_map/reduce_scatter | solution.py:479
  2068.6 156.1 %reduce-scatter.26.cloned.1.call-done = f32[1,48,2304]{2,1,0:T(8,128)} async-done(((f32[1,768,2304]{2,1,0:T(8,128)}), f32[1,48,2304]{2,1,0:T(8,128)}) %reduce-scatter.26.cloned.1.call-update) | async-done | bytes 442384 | tf_op jit(solution)/shard_map/reduce_scatter | solution.py:476
  2224.7 211.9 %reduce-scatter.24.cloned.1.call-done = f32[192,768]{1,0:T(8,128)} async-done(((f32[6144,768]{1,0:T(8,128)}), f32[192,768]{1,0:T(8,128)}) %reduce-scatter.24.cloned.1.call-update) | async-done | bytes 589840 | tf_op jit(solution)/shard_map/reduce_scatter | solution.py:482
  (1170 shorter events, 608.2 us)
Async XLA Ops:
  7.2 94.8 %copy-start = (bf16[1,768,2304]{2,1,0:T(8,128)(2,1)S(1)}, bf16[1,768,2304]{2,1,0:T(8,128)(2,1)}, u32[]{:S(2)}) copy-start(bf16[1,768,2304]{2,1,0:T(8,128)(2,1)} %param.89) | copy-start | bytes 10616836
  7.2 88.5 %all-gather.2.cloned.1.call-start = ((), (), s32[]{:S(2)}) async-start(), calls=%async_computation.11 | async-start | bytes 9732096 | tf_op jit(solution)/shard_map/all_gather | solution.py:224
  7.9 1110.5 %reduce-scatter.38.cloned.1.call-start = ((), (), s32[]{:S(2)}) async-start(), calls=%async_computation.20 | async-start | bytes 3342336 | tf_op jit(solution)/shard_map/reduce_scatter | solution.py:370
  29.3 669.8 %copy-start.99 = (f32[768]{0:T(1024)}, f32[768]{0:T(1024)S(1)}, u32[]{:S(2)}) copy-start(f32[768]{0:T(1024)S(1)} %get-tuple-element.504) | copy-start | bytes 9220
  334.1 213.9 %collective-permute-start = (bf16[1,768]{1,0:T(2,128)(2,1)}, bf16[1,768]{1,0:T(2,128)(2,1)}, u32[]{:S(2)}, u32[]{:S(2)}) collective-permute-start(bf16[1,768]{1,0:T(2,128)(2,1)} %slice.1016), channel_id=1, source_target_pairs={{0,1},{1,2},{2,3},{3,4},{4,5},{5,6},{6,7},{7,8},{8,9},{9,10},{10,1... | collective-permute-start | bytes 4616 | tf_op jit(solution)/shard_map/ppermute | solution.py:30
  445.9 101.6 %copy-start.335 = (f32[32]{0:T(128)}, f32[32]{0:T(128)S(1)}, u32[]{:S(2)}) copy-start(f32[32]{0:T(128)S(1)} %get-tuple-element.481) | copy-start | bytes 388
  450.2 97.9 %copy-start.154 = (bf16[32,768]{1,0:T(8,128)(2,1)S(1)}, bf16[32,768]{1,0:T(8,128)(2,1)}, u32[]{:S(2)}) copy-start(bf16[32,768]{1,0:T(8,128)(2,1)} %copy-done.153) | copy-start | bytes 147460
  450.2 97.9 %copy-start.319 = (pred[32]{0:T(512)(128)(4,1)S(1)}, pred[32]{0:T(512)(128)(4,1)}, u32[]{:S(2)}) copy-start(pred[32]{0:T(512)(128)(4,1)} %add_compare_fusion.2) | copy-start | bytes 100
  450.2 98.7 %copy-start.333 = (f32[32]{0:T(128)S(1)}, f32[32]{0:T(128)}, u32[]{:S(2)}) copy-start(f32[32]{0:T(128)} %get-tuple-element.497) | copy-start | bytes 388
  450.2 99.9 %copy-start.11 = (f32[256,768]{1,0:T(8,128)S(1)}, f32[256,768]{1,0:T(8,128)}, u32[]{:S(2)}) copy-start(f32[256,768]{1,0:T(8,128)} %get-tuple-element.623) | copy-start | bytes 2359300
  453.7 95.8 %copy-start.158 = (bf16[32,768]{1,0:T(8,128)(2,1)}, bf16[32,768]{1,0:T(8,128)(2,1)S(1)}, u32[]{:S(2)}) copy-start(bf16[32,768]{1,0:T(8,128)(2,1)S(1)} %fusion.230) | copy-start | bytes 147460
  455.0 158.0 %collective-permute-start.2 = (bf16[1,768]{1,0:T(2,128)(2,1)}, bf16[1,768]{1,0:T(2,128)(2,1)}, u32[]{:S(2)}, u32[]{:S(2)}) collective-permute-start(bf16[1,768]{1,0:T(2,128)(2,1)} %slice.1024), channel_id=1, source_target_pairs={{0,1},{1,2},{2,3},{3,4},{4,5},{5,6},{6,7},{7,8},{8,9},{9,10},{10,1... | collective-permute-start | bytes 4616 | tf_op jit(solution)/shard_map/ppermute | solution.py:30
  457.4 233.4 %collective-permute-start.4 = (bf16[1,768]{1,0:T(2,128)(2,1)}, bf16[1,768]{1,0:T(2,128)(2,1)}, u32[]{:S(2)}, u32[]{:S(2)}) collective-permute-start(bf16[1,768]{1,0:T(2,128)(2,1)} %slice.1029), channel_id=1, source_target_pairs={{0,1},{1,2},{2,3},{3,4},{4,5},{5,6},{6,7},{7,8},{8,9},{9,10},{10,1... | collective-permute-start | bytes 4616 | tf_op jit(solution)/shard_map/ppermute | solution.py:30
  548.8 1.3 collective-permute-start.1
  614.4 6.9 collective-permute-start.3
  687.3 5.5 collective-permute-start.6
  691.8 5.6 collective-permute-start.5
  761.3 5.5 collective-permute-start.7
  764.9 5.8 collective-permute-start.8
  766.8 135.5 %copy-start.192 = (bf16[1,768]{1,0:T(2,128)(2,1)}, bf16[1,768]{1,0:T(2,128)(2,1)S(1)}, u32[]{:S(2)}) copy-start(bf16[1,768]{1,0:T(2,128)(2,1)S(1)} %collective-permute-done.7) | copy-start | bytes 4612
  770.8 6.2 collective-permute-start.9
  798.3 321.8 %reduce-scatter.36.cloned.1.call-start = ((), (), s32[]{:S(2)}) async-start(), calls=%async_computation.19 | async-start | bytes 3342336 | tf_op jit(solution)/shard_map/reduce_scatter | solution.py:370
  918.4 283.2 %reduce-scatter.34.cloned.1.call-start = ((), (), s32[]{:S(2)}) async-start(), calls=%async_computation.18 | async-start | bytes 3342336 | tf_op jit(solution)/shard_map/reduce_scatter | solution.py:370
  1046.2 358.9 %reduce-scatter.40.cloned.1.call-start = ((), (), s32[]{:S(2)}) async-start(), calls=%async_computation.21 | async-start | bytes 417792
  1208.5 247.0 %reduce-scatter.42.cloned.1.call-start = ((), (), s32[]{:S(2)}) async-start(), calls=%async_computation.22 | async-start | bytes 417792
  1212.6 375.0 %reduce-scatter.28.cloned.1.call-start = ((), (), s32[]{:S(2)}) async-start(), calls=%async_computation.15 | async-start | bytes 2506752 | tf_op jit(solution)/shard_map/reduce_scatter | solution.py:477
  1219.1 495.9 %reduce-scatter.22.cloned.1.call-start = ((), (), s32[]{:S(2)}) async-start(), calls=%async_computation.12 | async-start | bytes 835584 | tf_op jit(solution)/shard_map/reduce_scatter | solution.py:480
  1244.5 647.9 %reduce-scatter.30.cloned.1.call-start = ((), (), s32[]{:S(2)}) async-start(), calls=%async_computation.16 | async-start | bytes 10027008 | tf_op jit(solution)/shard_map/reduce_scatter | solution.py:478
  1262.3 806.3 %reduce-scatter.32.cloned.1.call-start = ((), (), s32[]{:S(2)}) async-start(), calls=%async_computation.17 | async-start | bytes 10027008 | tf_op jit(solution)/shard_map/reduce_scatter | solution.py:479
  1310.6 914.1 %reduce-scatter.26.cloned.1.call-start = ((), (), s32[]{:S(2)}) async-start(), calls=%async_computation.14 | async-start | bytes 7520256 | tf_op jit(solution)/shard_map/reduce_scatter | solution.py:476
  1348.8 1087.7 %reduce-scatter.24.cloned.1.call-start = ((), (), s32[]{:S(2)}) async-start(), calls=%async_computation.13 | async-start | bytes 19464192 | tf_op jit(solution)/shard_map/reduce_scatter | solution.py:482
  1402.3 1034.2 %copy-start.1 = (bf16[1,768,2304]{2,1,0:T(8,128)(2,1)S(1)}, bf16[1,768,2304]{2,1,0:T(8,128)(2,1)}, u32[]{:S(2)}) copy-start(bf16[1,768,2304]{2,1,0:T(8,128)(2,1)} %param.89) | copy-start | bytes 10616836
  (349 other events, 1730.0 us)
Sparse Core Ops, SparseCore 0:
  10.9 84.7 all-gather.1
  798.4 132.1 reduce-scatter.37
  935.6 131.5 reduce-scatter.35
  1072.0 129.4 reduce-scatter.33
  1208.6 120.8 reduce-scatter.39
  1334.8 120.7 reduce-scatter.41
  1461.0 126.5 reduce-scatter.27
  1593.6 121.3 reduce-scatter.21
  1722.2 170.1 reduce-scatter.29
  1898.5 170.0 reduce-scatter.31
  2075.4 149.2 reduce-scatter.25
  2232.6 203.8 reduce-scatter.23
where the time goes:
time: 2450 us; the launch traced here: 2440 us
  waiting for transfers between devices  1170 us (48%)
  blocking collectives  532 us (22%)
  matrix products  422 us (17%)
  local copies, waits for them, and re-layouts  218 us (9%)
  other arithmetic  67.7 us (3%)
    reduce_scatter x1, waiting for transfers between devices, on_device(): lax.psum_scatter(carry_state['patch_grads'], ('section', 'seq'), scatter_...  212 us
    dot_general x33, matrix products, transposed_product(): lax.dot_general(former, latter, (((0,), (0,)), ((), ())), preferred_eleme...  188 us
    reduce_scatter x1, waiting for transfers between devices, on_device(): lax.psum_scatter(stacked_grads[4], 'seq', scatter_dimension=1, tiled=True)  177 us
    reduce_scatter x1, waiting for transfers between devices, on_device(): lax.psum_scatter(stacked_grads[5], 'seq', scatter_dimension=1, tiled=True)  176 us
    reduce_scatter x1, waiting for transfers between devices, on_device(): lax.psum_scatter(stacked_grads[2], 'seq', scatter_dimension=1, tiled=True)  156 us
    all_gather x3, blocking collectives, fetch_keys(): lax.all_gather(for_sending(mixed_heads[:, 2 * model_width:]), 'seq', axis...  138 us
    all_gather x3, blocking collectives, attend(): lax.all_gather(mixed_heads[:, 2 * model_width:], 'seq', axis=0, tiled=True)  133 us
    reduce_scatter x1, waiting for transfers between devices, on_device(): lax.psum_scatter(stacked_grads[3], 'seq', scatter_dimension=1, tiled=True)  131 us
  transfers between devices with their start and end apart: 22, of which 13 were waited for; matrix products, arithmetic and copies ran while one was open for 22% of the time, Pallas kernels for 0%

commit v1 on v0

v1 whole, which is shorter than its diff:
```python
from functools import partial

import jax
import jax.numpy as jnp
from jax import lax
from jax.experimental import pallas as pl
from jax.experimental.pallas import tpu as pltpu
from jax.sharding import PartitionSpec as P

HEADS = 12
HEAD_SIZE = 64
VOCAB = 256
PATCH = 8
ITEMS = 4
PAIRS = HEADS // 2
PAIR = 2 * HEAD_SIZE
SCALE = HEAD_SIZE ** (-0.5)
EPSILON = 1e-05
MASKED = -1e30
BLOCK = 128
VMEM = 48 * 1024 * 1024

bf16 = jnp.bfloat16
f32 = jnp.float32


def product(former, latter):
    return jnp.dot(former, latter, preferred_element_type=f32)


def transposed_product(former, latter):
    return lax.dot_general(former, latter, (((0,), (0,)), ((), ())), preferred_element_type=f32)


def product_transposed(former, latter):
    return lax.dot_general(former, latter, (((1,), (1,)), ((), ())), preferred_element_type=f32)


def normalise(values):
    average = jnp.mean(values, axis=-1, keepdims=True)
    centered = values - average
    inverse_root = lax.rsqrt(jnp.mean(centered * centered, axis=-1, keepdims=True) + EPSILON)
    return centered * inverse_root, inverse_root


def layer_norm(values, gain, bias):
    return normalise(values)[0] * gain + bias


def layer_norm_back(values, gain, grad):
    unit, inverse_root = normalise(values)
    scaled = grad * gain
    grad_values = inverse_root * (
        scaled
        - jnp.mean(scaled, axis=-1, keepdims=True)
        - unit * jnp.mean(scaled * unit, axis=-1, keepdims=True)
    )
    return grad_values, jnp.sum(grad * unit, axis=0), jnp.sum(grad, axis=0)


def locate(positions, lengths_row):
    padded = (lengths_row + PATCH - 1) // PATCH * PATCH
    item_ends = jnp.cumsum(padded)
    starts = item_ends - padded
    inside = (positions[:, None] >= starts[None, :]) & (positions[:, None] < item_ends[None, :])
    offsets = jnp.arange(ITEMS, dtype=jnp.int32)[None, :] - ITEMS
    owners = jnp.sum(jnp.where(inside, offsets, 0), axis=1) + ITEMS
    live_mask = jnp.any(inside & (positions[:, None] < (starts + lengths_row)[None, :]), axis=1)
    return (owners, live_mask)


def patch_mask(live_row):
    rows = lax.broadcasted_iota(jnp.int32, (BLOCK, BLOCK), 0)
    columns = lax.broadcasted_iota(jnp.int32, (BLOCK, BLOCK), 1)
    same = (rows // PATCH) == (columns // PATCH)
    return same & (columns <= rows) & ((live_row > 0) | (columns == rows))


def softmax_rows(scores):
    peak = jnp.max(scores, axis=-1, keepdims=True)
    exponents = jnp.exp(scores - peak)
    return exponents / jnp.sum(exponents, axis=-1, keepdims=True)


def local_forward_kernel(live_ref, mixed_ref, out_ref):
    width = HEADS * HEAD_SIZE
    allowed = patch_mask(live_ref[0])
    for pair in range(PAIRS):
        parts = []
        for head in (2 * pair, 2 * pair + 1):
            at = head * HEAD_SIZE
            queries = mixed_ref[:, at : at + HEAD_SIZE]
            keys = mixed_ref[:, width + at : width + at + HEAD_SIZE]
            values = mixed_ref[:, 2 * width + at : 2 * width + at + HEAD_SIZE]
            scores = jnp.where(allowed, product_transposed(queries, keys) * SCALE, MASKED)
            parts.append(product(softmax_rows(scores).astype(bf16), values))
        out_ref[:, pair * PAIR : (pair + 1) * PAIR] = jnp.concatenate(parts, axis=1).astype(bf16)


def local_backward_kernel(live_ref, mixed_ref, grad_ref, out_ref):
    width = HEADS * HEAD_SIZE
    allowed = patch_mask(live_ref[0])
    for pair in range(PAIRS):
        parts = ([], [], [])
        for head in (2 * pair, 2 * pair + 1):
            at = head * HEAD_SIZE
            queries = mixed_ref[:, at : at + HEAD_SIZE]
            keys = mixed_ref[:, width + at : width + at + HEAD_SIZE]
            values = mixed_ref[:, 2 * width + at : 2 * width + at + HEAD_SIZE]
            grads = grad_ref[:, at : at + HEAD_SIZE]
            scores = jnp.where(allowed, product_transposed(queries, keys) * SCALE, MASKED)
            probabilities = softmax_rows(scores)
            prob_grads = product_transposed(grads, values)
            delta = jnp.sum(probabilities * prob_grads, axis=-1, keepdims=True)
            score_grads = (probabilities * (prob_grads - delta)).astype(bf16)
            parts[0].append(product(score_grads, keys) * SCALE)
            parts[1].append(transposed_product(score_grads, queries) * SCALE)
            parts[2].append(transposed_product(probabilities.astype(bf16), grads))
        for which in range(3):
            at = which * width + pair * PAIR
            out_ref[:, at : at + PAIR] = jnp.concatenate(parts[which], axis=1).astype(bf16)


def local_attention(mixed, live_rows, grads=None):
    row_count, wide = mixed.shape
    width = wide // 3
    steps = row_count // BLOCK
    live_rows = live_rows.astype(jnp.int32).reshape(steps, 1, BLOCK)
    specs = [
        pl.BlockSpec((1, 1, BLOCK), lambda i: (i, 0, 0)),
        pl.BlockSpec((BLOCK, wide), lambda i: (i, 0)),
    ]
    if grads is None:
        return pl.pallas_call(
            local_forward_kernel,
            grid=(steps,),
            in_specs=specs,
            out_specs=pl.BlockSpec((BLOCK, width), lambda i: (i, 0)),
            out_shape=jax.ShapeDtypeStruct((row_count, width), bf16),
            compiler_params=pltpu.CompilerParams(vmem_limit_bytes=VMEM),
        )(live_rows, mixed)
    return pl.pallas_call(
        local_backward_kernel,
        grid=(steps,),
        in_specs=specs + [pl.BlockSpec((BLOCK, width), lambda i: (i, 0))],
        out_specs=pl.BlockSpec((BLOCK, wide), lambda i: (i, 0)),
        out_shape=jax.ShapeDtypeStruct((row_count, wide), bf16),
        compiler_params=pltpu.CompilerParams(vmem_limit_bytes=VMEM),
    )(live_rows, mixed, grads)


def causal_mask(start, owner_column, owner_row):
    shape = (BLOCK, owner_row.shape[1])
    rows = lax.broadcasted_iota(jnp.int32, shape, 0) + start
    columns = lax.broadcasted_iota(jnp.int32, shape, 1)
    return (columns <= rows) & (owner_column == owner_row)


def global_forward_kernel(column_ref, row_ref, qkv_ref, out_ref):
    start = pl.multiple_of(pl.program_id(0) * BLOCK, BLOCK)
    allowed = causal_mask(start, column_ref[...], row_ref[...])
    parts = []
    for head in range(2):
        at = head * HEAD_SIZE
        queries = qkv_ref[pl.ds(start, BLOCK), at : at + HEAD_SIZE]
        keys = qkv_ref[:, PAIR + at : PAIR + at + HEAD_SIZE]
        values = qkv_ref[:, 2 * PAIR + at : 2 * PAIR + at + HEAD_SIZE]
        scores = jnp.where(allowed, product_transposed(queries, keys) * SCALE, MASKED)
        parts.append(product(softmax_rows(scores).astype(bf16), values))
    out_ref[...] = jnp.concatenate(parts, axis=1).astype(bf16)


def global_backward_kernel(column_ref, row_ref, qkv_ref, grad_ref, out_ref, key_sum, value_sum):
    step = pl.program_id(0)
    start = pl.multiple_of(step * BLOCK, BLOCK)
    allowed = causal_mask(start, column_ref[...], row_ref[...])

    @pl.when(step == 0)
    def _():
        key_sum[...] = jnp.zeros_like(key_sum)
        value_sum[...] = jnp.zeros_like(value_sum)

    parts = ([], [], [])
    for head in range(2):
        at = head * HEAD_SIZE
        queries = qkv_ref[pl.ds(start, BLOCK), at : at + HEAD_SIZE]
        keys = qkv_ref[:, PAIR + at : PAIR + at + HEAD_SIZE]
        values = qkv_ref[:, 2 * PAIR + at : 2 * PAIR + at + HEAD_SIZE]
        grads = grad_ref[:, at : at + HEAD_SIZE]
        scores = jnp.where(allowed, product_transposed(queries, keys) * SCALE, MASKED)
        probabilities = softmax_rows(scores)
        prob_grads = product_transposed(grads, values)
        delta = jnp.sum(probabilities * prob_grads, axis=-1, keepdims=True)
        score_grads = (probabilities * (prob_grads - delta)).astype(bf16)
        parts[0].append(product(score_grads, keys) * SCALE)
        parts[1].append(transposed_product(score_grads, queries) * SCALE)
        parts[2].append(transposed_product(probabilities.astype(bf16), grads))
    out_ref[pl.ds(start, BLOCK), 0:PAIR] = jnp.concatenate(parts[0], axis=1).astype(bf16)
    key_sum[...] += jnp.concatenate(parts[1], axis=1)
    value_sum[...] += jnp.concatenate(parts[2], axis=1)

    @pl.when(step == pl.num_programs(0) - 1)
    def _():
        out_ref[:, PAIR : 2 * PAIR] = key_sum[...].astype(bf16)
        out_ref[:, 2 * PAIR : 3 * PAIR] = value_sum[...].astype(bf16)


def global_attention(qkv, owners, grads=None):
    count = qkv.shape[0]
    column, row = owners[:, None], owners[None, :]
    specs = [
        pl.BlockSpec((BLOCK, 1), lambda i: (i, 0)),
        pl.BlockSpec((1, count), lambda i: (0, 0)),
        pl.BlockSpec((count, 3 * PAIR), lambda i: (0, 0)),
    ]
    blocks = pl.BlockSpec((BLOCK, PAIR), lambda i: (i, 0))
    if grads is None:
        return pl.pallas_call(
            global_forward_kernel,
            grid=(count // BLOCK,),
            in_specs=specs,
            out_specs=blocks,
            out_shape=jax.ShapeDtypeStruct((count, PAIR), bf16),
            compiler_params=pltpu.CompilerParams(vmem_limit_bytes=VMEM),
        )(column, row, qkv)
    return pl.pallas_call(
        global_backward_kernel,
        grid=(count // BLOCK,),
        in_specs=specs + [blocks],
        out_specs=pl.BlockSpec((count, 3 * PAIR), lambda i: (0, 0)),
        out_shape=jax.ShapeDtypeStruct((count, 3 * PAIR), bf16),
        scratch_shapes=[pltpu.VMEM((count, PAIR), f32), pltpu.VMEM((count, PAIR), f32)],
        compiler_params=pltpu.CompilerParams(vmem_limit_bytes=VMEM),
    )(column, row, qkv, grads)


def section_send(x, origin, target, pairs):
    count = lax.axis_size("seq")
    joint = [(origin * count + i, target * count + j) for i, j in pairs]
    return lax.ppermute(x, ("section", "seq"), joint)


def scatter_sum(parts, section, order):
    count = lax.axis_size("seq")
    place = lax.axis_index("seq")
    bits = list(range(count.bit_length() - 1))[::-1]
    running = parts.reshape((2,) * len(bits) + parts.shape[1:])
    for step, bit in enumerate(order):
        axis = bits.index(bit)
        bits.pop(axis)
        mine = (place >> bit) & 1
        kept = lax.dynamic_index_in_dim(running, mine, axis, keepdims=False)
        leaving = lax.dynamic_index_in_dim(running, 1 - mine, axis, keepdims=False)
        pairs = [(i, i ^ (1 << bit)) for i in range(count)]
        arrived = section_send(leaving.astype(bf16), section, section, pairs)
        running = kept.astype(f32) + arrived.astype(f32)
        if step + 1 < len(order):
            running = running.astype(bf16)
    return running


def feed_forward(stream, attended, gains, biases, heads_out, expand, contract):
    middle = stream + product(attended, heads_out)
    normed_two = layer_norm(middle, gains[1], biases[1]).astype(bf16)
    upward = product(normed_two, expand)
    hidden = jax.nn.gelu(upward).astype(bf16)
    result = middle + product(hidden, contract)
    return result, (middle, normed_two, upward, hidden)


def feed_backward(grad_result, kept, attended, gains, heads_out, expand, contract):
    middle, normed_two, upward, hidden = kept
    branch = grad_result.astype(bf16)
    grad_contract = transposed_product(hidden, branch).astype(bf16)
    grad_hidden = product_transposed(branch, contract)
    grad_upward = jax.vjp(jax.nn.gelu, upward)[1](grad_hidden)[0].astype(bf16)
    grad_expand = transposed_product(normed_two, grad_upward).astype(bf16)
    grad_normed_two = product_transposed(grad_upward, expand)
    grad_middle, gain_two, bias_two = layer_norm_back(middle, gains[1], grad_normed_two)
    grad_middle = grad_middle + grad_result
    attend_branch = grad_middle.astype(bf16)
    grad_heads_out = transposed_product(attended, attend_branch).astype(bf16)
    grad_attended = product_transposed(attend_branch, heads_out).astype(bf16)
    return grad_middle, grad_attended, (gain_two, bias_two, grad_heads_out, grad_expand, grad_contract)


def heads_backward(grad_mixed, grad_middle, stream, normed, gains, heads_in):
    grad_heads_in = transposed_product(normed, grad_mixed).astype(bf16)
    grad_normed = product_transposed(grad_mixed, heads_in)
    grad_stream, gain_one, bias_one = layer_norm_back(stream, gains[0], grad_normed)
    return grad_stream + grad_middle, (gain_one, bias_one, grad_heads_in)


def on_device(
    byte_values,
    item_lengths,
    embed_tables,
    patch_weight,
    norm_gains,
    norm_biases,
    heads_in,
    heads_out,
    expand_weight,
    contract_weight,
    out_grad,
):
    place = lax.axis_index("seq")
    count = lax.axis_size("seq")
    section = lax.axis_index("section")
    is_global = section == 0
    batches, byte_rows = byte_values.shape
    patch_rows = byte_rows // PATCH
    width = heads_out.shape[2]
    rows = batches * patch_rows
    total_patches = patch_rows * count
    gains, biases = norm_gains[0], norm_biases[0]
    heads_in, heads_out = heads_in[0], heads_out[0]
    expand, contract = expand_weight[0], contract_weight[0]
    own_table = embed_tables[0]
    straight = [(i, i) for i in range(count)]
    vocabulary = jnp.arange(VOCAB, dtype=jnp.int32)

    def onehot_of(ids):
        return (ids[:, None] == vocabulary[None, :]).astype(bf16)

    quarters = PATCH // 2
    span = count // quarters
    group, member = place // span, place % span
    shard_rows = patch_weight.shape[0]
    byte_weight = jnp.zeros((span * shard_rows, width), bf16)
    byte_weight = lax.dynamic_update_slice(byte_weight, patch_weight, (member * shard_rows, 0))
    for k in range(1, span):
        piece = lax.ppermute(patch_weight, "seq", [(i, i ^ k) for i in range(count)])
        byte_weight = lax.dynamic_update_slice(byte_weight, piece, ((member ^ k) * shard_rows, 0))
    global_table = jnp.where(
        is_global, own_table, section_send(own_table, 0, 1, straight)
    )
    which_byte = section * quarters + group
    byte_ids = []
    for k in range(quarters):
        theirs = byte_values
        if k:
            theirs = lax.ppermute(byte_values, "seq", [(i, i ^ (k * span)) for i in range(count)])
        theirs = theirs.reshape(rows, PATCH)
        byte_ids.append(lax.dynamic_index_in_dim(theirs, which_byte, 1, keepdims=False))
    patch_onehot = onehot_of(jnp.concatenate(byte_ids))
    embedded = product(patch_onehot, global_table).astype(bf16)
    shares = product(embedded, byte_weight)
    shares = shares + section_send(shares.astype(bf16), 1, 0, straight).astype(f32)
    shares = shares.reshape(quarters, rows, width)
    stream = shares[0]
    for k in range(1, quarters):
        pairs = [(i, i ^ (k * span)) for i in range(count)]
        stream = stream + section_send(shares[k].astype(bf16), 0, 0, pairs).astype(f32)

    tasks = batches * PAIRS
    first_tasks = min(tasks, count)
    spare_tasks = tasks - first_tasks

    def to_tasks(blocks):
        columns = blocks.shape[2]
        slots = jnp.pad(blocks[:first_tasks], ((0, count - first_tasks), (0, 0), (0, 0)))
        if spare_tasks:
            spare = section_send(blocks[first_tasks:], 0, 1, straight)
            spare = jnp.pad(spare, ((0, count - spare_tasks), (0, 0), (0, 0)))
            slots = jnp.where(is_global, slots, spare)
        landed = lax.all_to_all(slots, "seq", 0, 0)
        return landed.reshape(total_patches, columns)

    def from_tasks(results):
        columns = results.shape[1]
        slots = lax.all_to_all(results.reshape(count, patch_rows, columns), "seq", 0, 0)
        blocks = slots[:first_tasks]
        if spare_tasks:
            spare = section_send(slots[:spare_tasks], 1, 0, straight)
            blocks = jnp.concatenate([blocks, spare])
        return blocks

    def by_pair(values, parts):
        split = values.reshape(batches, patch_rows, parts, PAIRS, PAIR)
        return jnp.transpose(split, (0, 3, 1, 2, 4)).reshape(tasks, patch_rows, parts * PAIR)

    def from_pairs(blocks, parts):
        split = blocks.reshape(batches, PAIRS, patch_rows, parts, PAIR)
        return jnp.transpose(split, (0, 2, 3, 1, 4)).reshape(rows, parts * width)

    task = jnp.minimum(jnp.where(is_global, place, first_tasks + place), tasks - 1)
    task_lengths = lax.dynamic_index_in_dim(item_lengths, task // PAIRS, 0, keepdims=False)
    task_owners = locate(jnp.arange(total_patches, dtype=jnp.int32) * PATCH, task_lengths)[0]

    normed = layer_norm(stream, gains[0], biases[0]).astype(bf16)
    mixed = product(normed, heads_in).astype(bf16)
    qkv = to_tasks(by_pair(mixed, 3))
    attended = from_pairs(from_tasks(global_attention(qkv, task_owners)), 1)
    global_out, global_kept = feed_forward(
        stream, attended, gains, biases, heads_out, expand, contract
    )
    sent = global_out.astype(bf16).reshape(batches, patch_rows, width)

    byte_places = place * byte_rows + jnp.arange(byte_rows, dtype=jnp.int32)
    patch_places = byte_places[::PATCH]
    live_rows = jnp.stack([locate(byte_places, item_lengths[m])[1] for m in range(batches)])
    same_item = jnp.stack(
        [
            locate(patch_places, item_lengths[m])[0]
            == locate(patch_places - PATCH, item_lengths[m])[0]
            for m in range(batches)
        ]
    )[:, :, None]
    onward = [(i, i + 1) for i in range(count - 1)]
    backward = [(i + 1, i) for i in range(count - 1)]
    near = section_send(sent, 0, 1, straight)
    edge = section_send(sent[:, -1:], 0, 1, onward)
    shifted = jnp.concatenate([edge, near[:, :-1]], axis=1)
    shifted = jnp.where(same_item, shifted, jnp.zeros((), bf16))

    byte_count = batches * byte_rows
    live_column = live_rows.reshape(byte_count, 1)
    local_onehot = onehot_of(byte_values.reshape(byte_count))
    spread = jnp.broadcast_to(
        shifted.astype(f32).reshape(rows, 1, width), (rows, PATCH, width)
    ).reshape(byte_count, width)
    local_stream = product(local_onehot, own_table) + spread
    local_normed = layer_norm(local_stream, gains[0], biases[0]).astype(bf16)
    local_mixed = product(local_normed, heads_in).astype(bf16)
    local_attended = local_attention(local_mixed, live_rows)
    local_out, local_kept = feed_forward(
        local_stream, local_attended, gains, biases, heads_out, expand, contract
    )
    own_sent = jnp.broadcast_to(
        sent.reshape(rows, 1, width), (rows, PATCH, width)
    ).reshape(byte_count, width)
    activations = jnp.where(
        live_column,
        jnp.where(is_global, own_sent, local_out.astype(bf16)),
        jnp.zeros((), bf16),
    ).reshape(batches, byte_rows, width)

    local_grad_out = jnp.where(
        live_column, out_grad.reshape(byte_count, width).astype(f32), 0.0
    )
    local_grad_middle, local_grad_attended, local_tops = feed_backward(
        local_grad_out, local_kept, local_attended, gains, heads_out, expand, contract
    )
    local_grad_mixed = local_attention(local_mixed, live_rows, local_grad_attended)
    local_grad_stream, local_bottoms = heads_backward(
        local_grad_mixed, local_grad_middle, local_stream, local_normed, gains, heads_in
    )
    local_table_grad = transposed_product(local_onehot, local_grad_stream.astype(bf16))
    grad_shifted = jnp.sum(local_grad_stream.reshape(batches, patch_rows, PATCH, width), axis=2)
    grad_shifted = jnp.where(same_item, grad_shifted.astype(bf16), jnp.zeros((), bf16))

    near_back = section_send(grad_shifted, 1, 0, straight)
    edge_back = section_send(grad_shifted[:, :1], 1, 0, backward)
    grad_sent = jnp.concatenate([near_back[:, 1:], edge_back], axis=1)
    grad_sent = grad_sent.reshape(rows, width).astype(f32)
    grad_middle, grad_attended, tops = feed_backward(
        grad_sent, global_kept, attended, gains, heads_out, expand, contract
    )
    task_grads = to_tasks(by_pair(grad_attended, 1))
    grad_mixed = from_pairs(
        from_tasks(global_attention(qkv, task_owners, task_grads)), 3
    )
    grad_stream, bottoms = heads_backward(grad_mixed, grad_middle, stream, normed, gains, heads_in)

    own_rows = grad_stream.astype(bf16)
    gathered = [own_rows]
    for k in range(1, quarters):
        pairs = [(i, i ^ (k * span)) for i in range(count)]
        gathered.append(section_send(own_rows, 0, 0, pairs))
    gathered = jnp.concatenate(gathered)
    gathered = jnp.where(is_global, gathered, section_send(gathered, 0, 1, straight))
    patch_share = transposed_product(embedded, gathered).astype(bf16)
    patch_share = patch_share.reshape(span, shard_rows, width)
    patch_grads = lax.dynamic_index_in_dim(patch_share, member, 0, keepdims=False).astype(f32)
    for k in range(1, span):
        leaving = lax.dynamic_index_in_dim(patch_share, member ^ k, 0, keepdims=False)
        patch_grads = patch_grads + lax.ppermute(
            leaving, "seq", [(i, i ^ k) for i in range(count)]
        ).astype(f32)
    grad_embedded = product_transposed(gathered, byte_weight).astype(bf16)
    table_share = transposed_product(patch_onehot, grad_embedded)
    table_share = table_share + section_send(
        table_share.astype(bf16), 1, 0, straight
    ).astype(f32)

    depth = count.bit_length() - 1
    up = list(range(depth))
    swapped = [1, 0] + up[2:]

    def reduced(from_section, grads):
        gain_two, bias_two, grad_heads_out, grad_expand, grad_contract = grads[0]
        gain_one, bias_one, grad_heads_in = grads[1]
        small = jnp.stack([gain_one, gain_two, bias_one, bias_two])
        small = jnp.transpose(small.reshape(4, count, width // count), (1, 0, 2))

        def split(x):
            return x.reshape(count, x.shape[0] // count, x.shape[1])

        contract_sum = scatter_sum(split(grad_contract), from_section, up)
        expand_sum = scatter_sum(split(grad_expand), from_section, swapped)
        out_sum = scatter_sum(split(grad_heads_out), from_section, up)
        in_sum = scatter_sum(split(grad_heads_in), from_section, swapped)
        table_sum = scatter_sum(split(grads[2].astype(bf16)), from_section, up)
        small_sum = scatter_sum(small.astype(bf16), from_section, up)
        return table_sum, small_sum, in_sum, out_sum, expand_sum, contract_sum

    local_sums = reduced(1, (local_tops, local_bottoms, local_table_grad))
    global_sums = reduced(0, (tops, bottoms, table_share))
    table_sum, small_sum, in_sum, out_sum, expand_sum, contract_sum = (
        jnp.where(is_global, upper, lower) for upper, lower in zip(global_sums, local_sums)
    )
    return (
        activations[None],
        table_sum[None],
        patch_grads,
        small_sum[None, 0:2],
        small_sum[None, 2:4],
        in_sum[None],
        out_sum[None],
        expand_sum[None],
        contract_sum[None],
    )


def solution(mesh):
    placed = (
        P(None, "seq"),
        P(),
        P("section", None, None),
        P(("section", "seq"), None),
        P("section", None, None),
        P("section", None, None),
        P("section", None, None),
        P("section", None, None),
        P("section", None, None),
        P("section", None, None),
        P(None, "seq", None),
    )
    return jax.shard_map(
        on_device,
        mesh=mesh,
        in_specs=placed,
        out_specs=(
            P("section", None, "seq", None),
            P("section", "seq", None),
            P(("section", "seq"), None),
            P("section", None, "seq"),
            P("section", None, "seq"),
            P("section", "seq", None),
            P("section", "seq", None),
            P("section", "seq", None),
            P("section", "seq", None),
        ),
        check_vma=False,
    )
```

time: 2450 us -> 683 us (0.28)
  waiting for transfers between devices: 1170 us -> 117 us
  blocking collectives: 532 us -> 0 us
  matrix products: 422 us -> 117 us
  starting transfers between devices: 15.1 us -> 183 us
  local copies, waits for them, and re-layouts: 218 us -> 112 us
  Pallas kernels: 0 us -> 73.7 us
    reduce_scatter x9 -> x0, waiting for transfers between devices: 1050 us -> none  [the longest x1 212 us: on_device(): lax.psum_scatter(carry_state['patch_grads'], ('section', 'seq'), scatter_...]
    all_gather x12 -> x0, blocking collectives: 532 us -> none  [the longest x3 138 us: fetch_keys(): lax.all_gather(for_sending(mixed_heads[:, 2 * model_width:]), 'seq', axis...]
    ppermute x10 -> x75, starting transfers between devices: 13.8 us -> 165 us  [the longest x66 152 us: section_send(): return lax.ppermute(x, ('section', 'seq'), joint)]
    dot_general x33 -> x11, matrix products: 188 us -> 41.4 us  [transposed_product(): lax.dot_general(former, latter, (((0,), (0,)), ((), ())), preferred_eleme...]
    ppermute x10 -> x75, waiting for transfers between devices: 6.13 us -> 107 us  [the longest x66 97.2 us: section_send(): return lax.ppermute(x, ('section', 'seq'), joint)]
    dot_general x66 -> x11, matrix products: 134 us -> 38.9 us  [product(): return jnp.dot(former, latter, preferred_element_type=f32)]
    pallas_call x0 -> x4, Pallas kernels: none -> 73.7 us  [the longest x1 36 us: local_attention(): pl.pallas_call(local_backward_kernel, grid=(steps,), in_specs=specs + [pl...]
    all_gather x1 -> x0, waiting for transfers between devices: 59.8 us -> none  [on_device(): lax.all_gather(patch_weight, ('section', 'seq'), axis=0, tiled=True)]
  transfers between devices with their start and end apart: 22 -> 79, of which waited for: 13 -> 27; matrix products, arithmetic and copies ran while one was open for 22% -> 25% of each run, Pallas kernels for 0% -> 1%
where the time goes in v1:
time: 683 us; the launch traced here: 672 us
  starting transfers between devices  183 us (27%)
  waiting for transfers between devices  117 us (17%)
  matrix products  117 us (17%)
  local copies, waits for them, and re-layouts  112 us (16%)
  Pallas kernels  73.7 us (11%)
  other arithmetic  65.8 us (10%)
    ppermute x66, starting transfers between devices, section_send(): return lax.ppermute(x, ('section', 'seq'), joint)  152 us
    ppermute x66, waiting for transfers between devices, section_send(): return lax.ppermute(x, ('section', 'seq'), joint)  97.2 us
    dot_general x11, matrix products, transposed_product(): lax.dot_general(former, latter, (((0,), (0,)), ((), ())), preferred_eleme...  41.4 us
    dot_general x11, matrix products, product(): return jnp.dot(former, latter, preferred_element_type=f32)  38.9 us
    dot_general x8, matrix products, product_transposed(): lax.dot_general(former, latter, (((1,), (1,)), ((), ())), preferred_eleme...  36.7 us
    pallas_call x1, Pallas kernels, local_attention(): pl.pallas_call(local_backward_kernel, grid=(steps,), in_specs=specs + [pl...  36 us
    pallas_call x1, Pallas kernels, local_attention(): pl.pallas_call(local_forward_kernel, grid=(steps,), in_specs=specs, out_s...  25.6 us
    dynamic_slice x11, local copies, waits for them, and re-layouts, scatter_sum(): kept = lax.dynamic_index_in_dim(running, mine, axis, keepdims=False)  23 us
  transfers between devices with their start and end apart: 79, of which 27 were waited for; matrix products, arithmetic and copies ran while one was open for 25% of the time, Pallas kernels for 1%

profile of v1, /device:TPU:0, one launch (start us, length us, event | category | flops | bytes accessed | tf_op | source)
XLA Modules:
  0.0 672.5 jit_solution(3240080153361155580)
XLA Ops:
  44.4 4.8 collective-permute-start.10
  53.3 5.4 collective-permute-done.9
  72.6 5.1 all-to-all-start
  91.9 4.9 shard_map.178
  97.4 4.9 all-to-all-start.1
  104.9 5.3 all-to-all-done.1
  121.0 4.5 fusion.90
  143.1 25.6 %shard_map.179 = bf16[768,768]{1,0:T(8,128)(2,1)S(1)} custom-call(s32[6,1,128]{2,1,0:T(1,128)S(1)} %reshape.753.live_ref, bf16[768,2304]{1,0:T(8,128)(2,1)S(1)} %convolution_convert_fusion.1.mixed_ref), custom_call_target="tpu_custom_call" | custom-call | tf_op jit(solution)/shard_map/pallas_call | solution.py:134
  171.8 6.4 fusion.23
  178.2 12.0 %fusion.6 = bf16[768,3072]{1,0:T(8,128)(2,1)} fusion(f32[768,3072]{1,0:T(8,128)} %fusion.23, bf16[768,768]{1,0:T(8,128)(2,1)S(1)} %bitcast.583, bf16[1,3072,768]{2,1,0:T(8,128)(2,1)S(1)} %bitcast.615), kind=kOutput, calls=%fused_computation.8 | convolution fusion | flops 3671064576 | bytes 20054016 | tf_op jit(solution)/shard_map/dot_general | solution.py:36
  190.3 6.9 %multiply_reduce_fusion = (bf16[768]{0:T(1024)(128)(2,1)}, f32[768]{0:T(1024)S(1)}, f32[768]{0:T(1024)S(1)}, bf16[768]{0:T(1024)(128)(2,1)}, f32[768,768]{1,0:T(8,128)S(1)}) fusion(f32[768,768]{1,0:T(8,128)S(1)} %get-tuple-element.112, f32[768]{0:T(1024)S(1)} %add_rsqrt_fusion, f32[768]{0:T(1024)S(1)} %broadcast_multiply_fusion.4, ...), kind=kOutput, calls=%fused_computation.71 | convolution fusion | flops 3629184000 | bytes 14174208 | tf_op jit(solution)/shard_map/dot_general | solution.py:36
  197.2 8.4 %convolution_convert_fusion.4 = bf16[768,3072]{1,0:T(8,128)(2,1)} fusion(bf16[768,3072]{1,0:T(8,128)(2,1)} %fusion.6, f32[768,768]{1,0:T(8,128)S(1)} %get-tuple-element.112, f32[768]{0:T(1024)S(1)} %get-tuple-element.27, f32[768]{0:T(1024)S(1)} %get-tuple-element.120, f32[768]{0:T(1024)S(1)} %add_rsqrt_fusion, f32[768]{0:T(1024)S(1)} %broadcast_multiply_fusion.4), kind=kOutput, calls=%fused_computation.14 | convolution fusion | flops 3629187072 | bytes 11808768 | tf_op jit(solution)/shard_map/dot_general | solution.py:32
  205.6 9.1 %fusion.55 = bf16[768,768]{1,0:T(8,128)(2,1)} fusion(f32[768,768]{1,0:T(8,128)S(1)} %get-tuple-element.112, bf16[1,3072,768]{2,1,0:T(8,128)(2,1)S(1)} %bitcast.615, pred[768]{0:T(1024)(128)(4,1)S(1)} %copy-done.89, pred[]{:T(512)S(6)} %eq.72, bf16[96,768]{1,0:T(8,128)(2,1)} %fusion.90, f32[768,3072]{1,0:T(8,128)} %fusion.23), kind=kOutput, calls=%fused_computation.107 | convolution fusion | flops 3647471616 | bytes 17842944 | tf_op jit(solution)/shard_map/dot_general | solution.py:28
  220.0 36.0 %shard_map.180 = bf16[768,2304]{1,0:T(8,128)(2,1)S(1)} custom-call(s32[6,1,128]{2,1,0:T(1,128)S(1)} %reshape.753.live_ref, bf16[768,2304]{1,0:T(8,128)(2,1)} %copy-done.1, bf16[768,768]{1,0:T(8,128)(2,1)S(1)} %convolution_convert_fusion.10.grad_ref), custom_call_target="tpu_custom_call" | custom-call | tf_op jit(solution)/shard_map/pallas_call | solution.py:142
  256.0 5.4 multiply_reduce_fusion.1
  261.4 4.7 convolution_convert_fusion
  266.8 8.4 %convolution_convert_fusion.2 = bf16[3072,768]{1,0:T(8,128)(2,1)S(1)} fusion(bf16[768,768]{1,0:T(8,128)(2,1)} %get-tuple-element.68, f32[768,3072]{1,0:T(8,128)} %fusion.23), kind=kOutput, calls=%fused_computation.12 | convolution fusion | flops 3647471616 | bytes 15335424 | tf_op jit(solution)/shard_map/dot_general | solution.py:32
  364.5 13.3 %collective-permute-start.17 = (bf16[2,32,128]{2,1,0:T(8,128)(2,1)S(1)}, bf16[2,32,128]{2,1,0:T(8,128)(2,1)S(1)}, u32[]{:S(2)}, u32[]{:S(2)}) collective-permute-start(bf16[2,32,128]{2,1,0:T(8,128)(2,1)S(1)} %slice.133), channel_id=1, source_target_pairs={{0,16},{1,17},{2,18},{3,19},{4,20},{5,21},{6,22},{7,23},{8,24},{9,... | collective-permute-start | bytes 49160 | tf_op jit(solution)/shard_map/ppermute | solution.py:240
  381.1 4.4 all-to-all-start.2
  394.6 7.2 %shard_map.181 = bf16[512,384]{1,0:T(8,128)(2,1)S(1)} custom-call(s32[512,1]{1,0:T(8,128)S(1)} %copy-done.3, s32[1,512]{1,0:T(1,128)S(1)} %bitcast.554, bf16[512,384]{1,0:T(8,128)(2,1)} %bitcast.24.qkv_ref, bf16[512,128]{1,0:T(8,128)(2,1)} %bitcast.45.grad_ref), custom_call_target="tpu_custom_call" | custom-call | tf_op jit(solution)/shard_map/pallas_call | solution.py:226
  414.8 6.6 collective-permute-done.52
  470.6 4.5 collective-permute-start.38
  478.9 4.8 collective-permute-start.21
  513.4 6.4 collective-permute-done.34
  541.5 20.1 %collective-permute-done.67 = bf16[2,2,2,192,768]{4,3,0,1,2:T(8,128)(2,1)S(1)} collective-permute-done((bf16[2,2,2,192,768]{4,3,0,1,2:T(8,128)(2,1)}, bf16[2,2,2,192,768]{4,3,0,1,2:T(8,128)(2,1)S(1)}, u32[]{:S(2)}, u32[]{:S(2)}) %collective-permute-start.67) | collective-permute-done | bytes 2359328 | tf_op jit(solution)/shard_map/ppermute | solution.py:240
  574.4 15.4 %collective-permute-done.25 = bf16[2,2,16,768]{3,2,0,1:T(8,128)(2,1)S(1)} collective-permute-done((bf16[2,2,16,768]{3,2,0,1:T(8,128)(2,1)S(1)}, bf16[2,2,16,768]{3,2,0,1:T(8,128)(2,1)S(1)}, u32[]{:S(2)}, u32[]{:S(2)}) %collective-permute-start.25) | collective-permute-done | bytes 98336 | tf_op jit(solution)/shard_map/ppermute | solution.py:240
  592.8 4.4 collective-permute-done.26
  606.0 6.5 collective-permute-start.60
  619.7 6.9 %collective-permute-done.60 = bf16[2,2,48,3072]{3,2,0,1:T(8,128)(2,1)S(1)} collective-permute-done((bf16[2,2,48,3072]{3,2,0,1:T(8,128)(2,1)S(1)}, bf16[2,2,48,3072]{3,2,0,1:T(8,128)(2,1)S(1)}, u32[]{:S(2)}, u32[]{:S(2)}) %collective-permute-start.60) | collective-permute-done | bytes 1179680 | tf_op jit(solution)/shard_map/ppermute | solution.py:240
  629.0 7.1 %collective-permute-done.44 = bf16[2,2,48,2304]{3,2,0,1:T(8,128)(2,1)S(1)} collective-permute-done((bf16[2,2,48,2304]{3,2,0,1:T(8,128)(2,1)S(1)}, bf16[2,2,48,2304]{3,2,0,1:T(8,128)(2,1)S(1)}, u32[]{:S(2)}, u32[]{:S(2)}) %collective-permute-start.44) | collective-permute-done | bytes 884768 | tf_op jit(solution)/shard_map/ppermute | solution.py:240
  655.0 4.6 collective-permute-start.62
  659.6 8.3 %collective-permute-done.46 = bf16[48,2304]{1,0:T(8,128)(2,1)S(1)} collective-permute-done((bf16[48,2304]{1,0:T(8,128)(2,1)S(1)}, bf16[48,2304]{1,0:T(8,128)(2,1)S(1)}, u32[]{:S(2)}, u32[]{:S(2)}) %collective-permute-start.46) | collective-permute-done | bytes 221216 | tf_op jit(solution)/shard_map/ppermute | solution.py:240
  (599 shorter events, 390.2 us)
Async XLA Ops:
  0.7 21.7 %collective-permute-start.4 = (bf16[192,768]{1,0:T(8,128)(2,1)}, bf16[192,768]{1,0:T(8,128)(2,1)}, u32[]{:S(2)}, u32[]{:S(2)}) collective-permute-start(bf16[192,768]{1,0:T(8,128)(2,1)} %param.14), channel_id=1, source_target_pairs={{0,1},{1,0},{2,3},{3,2},{4,5},{5,4},{6,7},{7,6},{8,9},{9,8},{10,11... | collective-permute-start | bytes 884744 | tf_op jit(solution)/shard_map/ppermute | solution.py:333
  8.0 16.0 %collective-permute-start.5 = (bf16[192,768]{1,0:T(8,128)(2,1)}, bf16[192,768]{1,0:T(8,128)(2,1)}, u32[]{:S(2)}, u32[]{:S(2)}) collective-permute-start(bf16[192,768]{1,0:T(8,128)(2,1)} %param.14), channel_id=1, source_target_pairs={{0,2},{1,3},{2,0},{3,1},{4,6},{5,7},{6,4},{7,5},{8,10},{9,11},{10,... | collective-permute-start | bytes 884744 | tf_op jit(solution)/shard_map/ppermute | solution.py:333
  72.6 18.3 %all-to-all-start = ((bf16[16,32,384]{2,1,0:T(8,128)(2,1)}), bf16[16,32,384]{2,1,0:T(8,128)(2,1)}, u32[]{:S(2)}, u32[]{:S(2)}) async-start(bf16[16,32,384]{2,1,0:T(8,128)(2,1)} %slice_select_fusion), calls=%async_computation | async-start | bytes 786432 | tf_op jit(solution)/shard_map/all_to_all | solution.py:367
  281.4 125.4 %collective-permute-start.55 = (bf16[2,2,2,48,768]{4,3,0,1,2:T(8,128)(2,1)}, bf16[2,2,2,48,768]{4,3,0,1,2:T(8,128)(2,1)}, u32[]{:S(2)}, u32[]{:S(2)}) collective-permute-start(bf16[2,2,2,48,768]{4,3,0,1,2:T(8,128)(2,1)} %bitcast.540), channel_id=1, source_target_pairs={{16,17},{17,16},{18,19},{19,18},{20,21},{21,20},{22,23},{23,22},{2... | collective-permute-start | bytes 1769480 | tf_op jit(solution)/shard_map/ppermute | solution.py:240
  291.8 245.5 %collective-permute-start.63 = (bf16[2,2,2,48,3072]{4,3,0,1,2:T(8,128)(2,1)}, bf16[2,2,2,48,3072]{4,3,0,1,2:T(8,128)(2,1)}, u32[]{:S(2)}, u32[]{:S(2)}) collective-permute-start(bf16[2,2,2,48,3072]{4,3,0,1,2:T(8,128)(2,1)} %bitcast.536), channel_id=1, source_target_pairs={{16,18},{17,19},{18,16},{19,17},{20,22},{21,23},{22,20},{23,21},{2... | collective-permute-start | bytes 7077896 | tf_op jit(solution)/shard_map/ppermute | solution.py:240
  325.2 32.6 %collective-permute-start.28 = (bf16[2,2,2,16,768]{4,3,0,1,2:T(8,128)(2,1)}, bf16[2,2,2,16,768]{4,3,0,1,2:T(8,128)(2,1)}, u32[]{:S(2)}, u32[]{:S(2)}) collective-permute-start(bf16[2,2,2,16,768]{4,3,0,1,2:T(8,128)(2,1)} %bitcast.542), channel_id=1, source_target_pairs={{16,17},{17,16},{18,19},{19,18},{20,21},{21,20},{22,23},{23,22},{2... | collective-permute-start | bytes 589832 | tf_op jit(solution)/shard_map/ppermute | solution.py:240
  327.1 169.8 %collective-permute-start.47 = (bf16[2,2,2,48,2304]{4,3,0,1,2:T(8,128)(2,1)}, bf16[2,2,2,48,2304]{4,3,0,1,2:T(8,128)(2,1)}, u32[]{:S(2)}, u32[]{:S(2)}) collective-permute-start(bf16[2,2,2,48,2304]{4,3,0,1,2:T(8,128)(2,1)} %bitcast.538), channel_id=1, source_target_pairs={{16,18},{17,19},{18,16},{19,17},{20,22},{21,23},{22,20},{23,21},{2... | collective-permute-start | bytes 5308424 | tf_op jit(solution)/shard_map/ppermute | solution.py:240
  329.2 147.4 %collective-permute-start.42 = (bf16[4,48]{1,0:T(4,128)(2,1)}, bf16[4,48]{1,0:T(4,128)(2,1)}, u32[]{:S(2)}, u32[]{:S(2)}) collective-permute-start(bf16[4,48]{1,0:T(4,128)(2,1)} %fusion.151), channel_id=1, source_target_pairs={{16,24},{17,25},{18,26},{19,27},{20,28},{21,29},{22,30},{23,31},{2... | collective-permute-start | bytes 1160 | tf_op jit(solution)/shard_map/ppermute | solution.py:240
  385.5 23.5 %collective-permute-start.51 = (bf16[2,2,2,48,768]{4,3,0,1,2:T(8,128)(2,1)}, bf16[2,2,2,48,768]{4,3,0,1,2:T(8,128)(2,1)}, u32[]{:S(2)}, u32[]{:S(2)}) collective-permute-start(bf16[2,2,2,48,768]{4,3,0,1,2:T(8,128)(2,1)} %bitcast.586), channel_id=1, source_target_pairs={{0,1},{1,0},{2,3},{3,2},{4,5},{5,4},{6,7},{7,6},{8,9},{9,8},{10,11... | collective-permute-start | bytes 1769480 | tf_op jit(solution)/shard_map/ppermute | solution.py:240
  402.6 26.6 %all-to-all-start.3 = ((bf16[16,32,384]{2,1,0:T(8,128)(2,1)}), bf16[16,32,384]{2,1,0:T(8,128)(2,1)}, u32[]{:S(2)}, u32[]{:S(2)}) async-start(bf16[16,32,384]{2,1,0:T(8,128)(2,1)} %bitcast.550), calls=%async_computation.3 | async-start | bytes 786432 | tf_op jit(solution)/shard_map/all_to_all | solution.py:372
  427.9 57.0 %collective-permute-start.58 = (bf16[48,768]{1,0:T(8,128)(2,1)}, bf16[48,768]{1,0:T(8,128)(2,1)}, u32[]{:S(2)}, u32[]{:S(2)}) collective-permute-start(bf16[48,768]{1,0:T(8,128)(2,1)} %dynamic-slice_bitcast_fusion.27), channel_id=1, source_target_pairs={{16,24},{17,25},{18,26},{19,27},{20,28},{21,29},{22,30},{23,31},{2... | collective-permute-start | bytes 221192 | tf_op jit(solution)/shard_map/ppermute | solution.py:240
  491.8 40.2 %collective-permute-start.71 = (bf16[2,2,2,192,768]{4,3,0,1,2:T(8,128)(2,1)}, bf16[2,2,2,192,768]{4,3,0,1,2:T(8,128)(2,1)}, u32[]{:S(2)}, u32[]{:S(2)}) collective-permute-start(bf16[2,2,2,192,768]{4,3,0,1,2:T(8,128)(2,1)} %bitcast.534), channel_id=1, source_target_pairs={{16,17},{17,16},{18,19},{19,18},{20,21},{21,20},{22,23},{23,22},{2... | collective-permute-start | bytes 7077896 | tf_op jit(solution)/shard_map/ppermute | solution.py:240
  507.4 23.9 %collective-permute-start.23 = (bf16[256,768]{1,0:T(8,128)(2,1)}, bf16[256,768]{1,0:T(8,128)(2,1)S(1)}, u32[]{:S(2)}, u32[]{:S(2)}) collective-permute-start(bf16[256,768]{1,0:T(8,128)(2,1)} %get-tuple-element.117), channel_id=1, source_target_pairs={{16,0},{17,1},{18,2},{19,3},{20,4},{21,5},{22,6},{23,7},{24,8},{25... | collective-permute-start | bytes 1179656 | tf_op jit(solution)/shard_map/ppermute | solution.py:240
  519.8 41.8 %collective-permute-start.67 = (bf16[2,2,2,192,768]{4,3,0,1,2:T(8,128)(2,1)}, bf16[2,2,2,192,768]{4,3,0,1,2:T(8,128)(2,1)S(1)}, u32[]{:S(2)}, u32[]{:S(2)}) collective-permute-start(bf16[2,2,2,192,768]{4,3,0,1,2:T(8,128)(2,1)} %bitcast.570), channel_id=1, source_target_pairs={{0,1},{1,0},{2,3},{3,2},{4,5},{5,4},{6,7},{7,6},{8,9},{9,8},{10,11... | collective-permute-start | bytes 7077896 | tf_op jit(solution)/shard_map/ppermute | solution.py:240
  526.2 39.0 %collective-permute-start.59 = (bf16[2,2,2,48,3072]{4,3,0,1,2:T(8,128)(2,1)}, bf16[2,2,2,48,3072]{4,3,0,1,2:T(8,128)(2,1)S(1)}, u32[]{:S(2)}, u32[]{:S(2)}) collective-permute-start(bf16[2,2,2,48,3072]{4,3,0,1,2:T(8,128)(2,1)} %bitcast.569), channel_id=1, source_target_pairs={{0,2},{1,3},{2,0},{3,1},{4,6},{5,7},{6,4},{7,5},{8,10},{9,11},{10,... | collective-permute-start | bytes 7077896 | tf_op jit(solution)/shard_map/ppermute | solution.py:240
  531.3 68.5 %collective-permute-start.31 = (bf16[16,768]{1,0:T(8,128)(2,1)S(1)}, bf16[16,768]{1,0:T(8,128)(2,1)S(1)}, u32[]{:S(2)}, u32[]{:S(2)}) collective-permute-start(bf16[16,768]{1,0:T(8,128)(2,1)S(1)} %copy-done.65), channel_id=1, source_target_pairs={{16,24},{17,25},{18,26},{19,27},{20,28},{21,29},{22,30},{23,31},{2... | collective-permute-start | bytes 73736 | tf_op jit(solution)/shard_map/ppermute | solution.py:240
  532.1 81.0 %collective-permute-start.43 = (bf16[2,2,2,48,2304]{4,3,0,1,2:T(8,128)(2,1)S(1)}, bf16[2,2,2,48,2304]{4,3,0,1,2:T(8,128)(2,1)S(1)}, u32[]{:S(2)}, u32[]{:S(2)}) collective-permute-start(bf16[2,2,2,48,2304]{4,3,0,1,2:T(8,128)(2,1)S(1)} %bitcast.573), channel_id=1, source_target_pairs={{0,2},{1,3},{2,0},{3,1},{4,6},{5,7},{6,4},{7,5},{8,10},{9,11},{10,... | collective-permute-start | bytes 5308424 | tf_op jit(solution)/shard_map/ppermute | solution.py:240
  537.2 53.3 %collective-permute-start.48 = (bf16[2,2,48,2304]{3,2,0,1:T(8,128)(2,1)S(1)}, bf16[2,2,48,2304]{3,2,0,1:T(8,128)(2,1)S(1)}, u32[]{:S(2)}, u32[]{:S(2)}) collective-permute-start(bf16[2,2,48,2304]{3,2,0,1:T(8,128)(2,1)S(1)} %dynamic-slice_bitcast_fusion.4), channel_id=1, source_target_pairs={{16,17},{17,16},{18,19},{19,18},{20,21},{21,20},{22,23},{23,22},{2... | collective-permute-start | bytes 2654216 | tf_op jit(solution)/shard_map/ppermute | solution.py:240
  565.2 51.2 %collective-permute-start.64 = (bf16[2,2,48,3072]{3,2,0,1:T(8,128)(2,1)S(1)}, bf16[2,2,48,3072]{3,2,0,1:T(8,128)(2,1)S(1)}, u32[]{:S(2)}, u32[]{:S(2)}) collective-permute-start(bf16[2,2,48,3072]{3,2,0,1:T(8,128)(2,1)S(1)} %dynamic-slice_bitcast_fusion.2), channel_id=1, source_target_pairs={{16,17},{17,16},{18,19},{19,18},{20,21},{21,20},{22,23},{23,22},{2... | collective-permute-start | bytes 3538952 | tf_op jit(solution)/shard_map/ppermute | solution.py:240
  571.4 18.4 %collective-permute-start.25 = (bf16[2,2,16,768]{3,2,0,1:T(8,128)(2,1)S(1)}, bf16[2,2,16,768]{3,2,0,1:T(8,128)(2,1)S(1)}, u32[]{:S(2)}, u32[]{:S(2)}) collective-permute-start(bf16[2,2,16,768]{3,2,0,1:T(8,128)(2,1)S(1)} %dynamic-slice_bitcast_fusion.26), channel_id=1, source_target_pairs={{0,2},{1,3},{2,0},{3,1},{4,6},{5,7},{6,4},{7,5},{8,10},{9,11},{10,... | collective-permute-start | bytes 294920 | tf_op jit(solution)/shard_map/ppermute | solution.py:240
  589.8 27.8 %collective-permute-start.72 = (bf16[2,2,192,768]{3,2,0,1:T(8,128)(2,1)S(1)}, bf16[2,2,192,768]{3,2,0,1:T(8,128)(2,1)S(1)}, u32[]{:S(2)}, u32[]{:S(2)}) collective-permute-start(bf16[2,2,192,768]{3,2,0,1:T(8,128)(2,1)S(1)} %dynamic-slice_bitcast_fusion), channel_id=1, source_target_pairs={{16,18},{17,19},{18,16},{19,17},{20,22},{21,23},{22,20},{23,21},{2... | collective-permute-start | bytes 3538952 | tf_op jit(solution)/shard_map/ppermute | solution.py:240
  599.8 18.9 %collective-permute-start.68 = (bf16[2,2,192,768]{3,2,0,1:T(8,128)(2,1)S(1)}, bf16[2,2,192,768]{3,2,0,1:T(8,128)(2,1)S(1)}, u32[]{:S(2)}, u32[]{:S(2)}) collective-permute-start(bf16[2,2,192,768]{3,2,0,1:T(8,128)(2,1)S(1)} %dynamic-slice_bitcast_fusion.1), channel_id=1, source_target_pairs={{0,2},{1,3},{2,0},{3,1},{4,6},{5,7},{6,4},{7,5},{8,10},{9,11},{10,... | collective-permute-start | bytes 3538952 | tf_op jit(solution)/shard_map/ppermute | solution.py:240
  606.0 20.7 %collective-permute-start.60 = (bf16[2,2,48,3072]{3,2,0,1:T(8,128)(2,1)S(1)}, bf16[2,2,48,3072]{3,2,0,1:T(8,128)(2,1)S(1)}, u32[]{:S(2)}, u32[]{:S(2)}) collective-permute-start(bf16[2,2,48,3072]{3,2,0,1:T(8,128)(2,1)S(1)} %dynamic-slice_bitcast_fusion.3), channel_id=1, source_target_pairs={{0,1},{1,0},{2,3},{3,2},{4,5},{5,4},{6,7},{7,6},{8,9},{9,8},{10,11... | collective-permute-start | bytes 3538952 | tf_op jit(solution)/shard_map/ppermute | solution.py:240
  614.3 21.8 %collective-permute-start.44 = (bf16[2,2,48,2304]{3,2,0,1:T(8,128)(2,1)S(1)}, bf16[2,2,48,2304]{3,2,0,1:T(8,128)(2,1)S(1)}, u32[]{:S(2)}, u32[]{:S(2)}) collective-permute-start(bf16[2,2,48,2304]{3,2,0,1:T(8,128)(2,1)S(1)} %dynamic-slice_bitcast_fusion.5), channel_id=1, source_target_pairs={{0,1},{1,0},{2,3},{3,2},{4,5},{5,4},{6,7},{7,6},{8,9},{9,8},{10,11... | collective-permute-start | bytes 2654216 | tf_op jit(solution)/shard_map/ppermute | solution.py:240
  616.4 38.6 %collective-permute-start.50 = (bf16[48,2304]{1,0:T(8,128)(2,1)S(1)}, bf16[48,2304]{1,0:T(8,128)(2,1)S(1)}, u32[]{:S(2)}, u32[]{:S(2)}) collective-permute-start(bf16[48,2304]{1,0:T(8,128)(2,1)S(1)} %dynamic-slice_bitcast_fusion.21), channel_id=1, source_target_pairs={{16,24},{17,25},{18,26},{19,27},{20,28},{21,29},{22,30},{23,31},{2... | collective-permute-start | bytes 663560 | tf_op jit(solution)/shard_map/ppermute | solution.py:240
  617.6 20.7 %collective-permute-start.65 = (bf16[2,48,3072]{2,1,0:T(8,128)(2,1)S(1)}, bf16[2,48,3072]{2,1,0:T(8,128)(2,1)S(1)}, u32[]{:S(2)}, u32[]{:S(2)}) collective-permute-start(bf16[2,48,3072]{2,1,0:T(8,128)(2,1)S(1)} %dynamic-slice_bitcast_fusion.8), channel_id=1, source_target_pairs={{16,20},{17,21},{18,22},{19,23},{20,16},{21,17},{22,18},{23,19},{2... | collective-permute-start | bytes 1769480 | tf_op jit(solution)/shard_map/ppermute | solution.py:240
  618.7 23.8 %collective-permute-start.73 = (bf16[2,192,768]{2,1,0:T(8,128)(2,1)S(1)}, bf16[2,192,768]{2,1,0:T(8,128)(2,1)S(1)}, u32[]{:S(2)}, u32[]{:S(2)}) collective-permute-start(bf16[2,192,768]{2,1,0:T(8,128)(2,1)S(1)} %dynamic-slice_bitcast_fusion.6), channel_id=1, source_target_pairs={{16,20},{17,21},{18,22},{19,23},{20,16},{21,17},{22,18},{23,19},{2... | collective-permute-start | bytes 1769480 | tf_op jit(solution)/shard_map/ppermute | solution.py:240
  626.6 16.7 %collective-permute-start.69 = (bf16[2,192,768]{2,1,0:T(8,128)(2,1)S(1)}, bf16[2,192,768]{2,1,0:T(8,128)(2,1)S(1)}, u32[]{:S(2)}, u32[]{:S(2)}) collective-permute-start(bf16[2,192,768]{2,1,0:T(8,128)(2,1)S(1)} %dynamic-slice_bitcast_fusion.7), channel_id=1, source_target_pairs={{0,4},{1,5},{2,6},{3,7},{4,0},{5,1},{6,2},{7,3},{8,12},{9,13},{10,... | collective-permute-start | bytes 1769480 | tf_op jit(solution)/shard_map/ppermute | solution.py:240
  642.5 27.3 %collective-permute-start.66 = (bf16[48,3072]{1,0:T(8,128)(2,1)S(1)}, bf16[48,3072]{1,0:T(8,128)(2,1)S(1)}, u32[]{:S(2)}, u32[]{:S(2)}) collective-permute-start(bf16[48,3072]{1,0:T(8,128)(2,1)S(1)} %dynamic-slice_bitcast_fusion.14), channel_id=1, source_target_pairs={{16,24},{17,25},{18,26},{19,27},{20,28},{21,29},{22,30},{23,31},{2... | collective-permute-start | bytes 884744 | tf_op jit(solution)/shard_map/ppermute | solution.py:240
  643.4 25.4 %collective-permute-start.74 = (bf16[192,768]{1,0:T(8,128)(2,1)S(1)}, bf16[192,768]{1,0:T(8,128)(2,1)S(1)}, u32[]{:S(2)}, u32[]{:S(2)}) collective-permute-start(bf16[192,768]{1,0:T(8,128)(2,1)S(1)} %dynamic-slice_bitcast_fusion.12), channel_id=1, source_target_pairs={{16,24},{17,25},{18,26},{19,27},{20,28},{21,29},{22,30},{23,31},{2... | collective-permute-start | bytes 884744 | tf_op jit(solution)/shard_map/ppermute | solution.py:240
  647.9 20.9 %collective-permute-start.70 = (bf16[192,768]{1,0:T(8,128)(2,1)S(1)}, bf16[192,768]{1,0:T(8,128)(2,1)S(1)}, u32[]{:S(2)}, u32[]{:S(2)}) collective-permute-start(bf16[192,768]{1,0:T(8,128)(2,1)S(1)} %dynamic-slice_bitcast_fusion.13), channel_id=1, source_target_pairs={{0,8},{1,9},{2,10},{3,11},{4,12},{5,13},{6,14},{7,15},{8,0},{9,1},... | collective-permute-start | bytes 884744 | tf_op jit(solution)/shard_map/ppermute | solution.py:240
  655.0 16.1 %collective-permute-start.62 = (bf16[48,3072]{1,0:T(8,128)(2,1)S(1)}, bf16[48,3072]{1,0:T(8,128)(2,1)S(1)}, u32[]{:S(2)}, u32[]{:S(2)}) collective-permute-start(bf16[48,3072]{1,0:T(8,128)(2,1)S(1)} %dynamic-slice_bitcast_fusion.15), channel_id=1, source_target_pairs={{0,8},{1,9},{2,10},{3,11},{4,12},{5,13},{6,14},{7,15},{8,0},{9,1},... | collective-permute-start | bytes 884744 | tf_op jit(solution)/shard_map/ppermute | solution.py:240
  (155 other events, 1967.4 us)

commit v2 on v1

v2 whole, which is shorter than its diff:
```python
from functools import partial

import jax
import jax.numpy as jnp
from jax import lax
from jax.experimental import pallas as pl
from jax.experimental.pallas import tpu as pltpu
from jax.sharding import PartitionSpec as P

HEADS = 12
HEAD_SIZE = 64
VOCAB = 256
PATCH = 8
ITEMS = 4
PAIRS = HEADS // 2
PAIR = 2 * HEAD_SIZE
SCALE = HEAD_SIZE ** (-0.5)
EPSILON = 1e-05
MASKED = -1e30
BLOCK = 128
TILE = 384
GROUPS = 16
VMEM = 60 * 1024 * 1024

bf16 = jnp.bfloat16
f32 = jnp.float32


def product(former, latter):
    return jnp.dot(former, latter, preferred_element_type=f32)


def transposed_product(former, latter):
    return lax.dot_general(former, latter, (((0,), (0,)), ((), ())), preferred_element_type=f32)


def product_transposed(former, latter):
    return lax.dot_general(former, latter, (((1,), (1,)), ((), ())), preferred_element_type=f32)


def normalise(values):
    average = jnp.mean(values, axis=-1, keepdims=True)
    centered = values - average
    inverse_root = lax.rsqrt(jnp.mean(centered * centered, axis=-1, keepdims=True) + EPSILON)
    return centered * inverse_root, inverse_root


def layer_norm(values, gain, bias):
    return normalise(values)[0] * gain + bias


def layer_norm_back(values, gain, grad):
    unit, inverse_root = normalise(values)
    scaled = grad * gain
    grad_values = inverse_root * (
        scaled
        - jnp.mean(scaled, axis=-1, keepdims=True)
        - unit * jnp.mean(scaled * unit, axis=-1, keepdims=True)
    )
    return (
        grad_values,
        jnp.sum(grad * unit, axis=0, keepdims=True),
        jnp.sum(grad, axis=0, keepdims=True),
    )


def locate(positions, lengths_row):
    padded = (lengths_row + PATCH - 1) // PATCH * PATCH
    item_ends = jnp.cumsum(padded)
    starts = item_ends - padded
    inside = (positions[:, None] >= starts[None, :]) & (positions[:, None] < item_ends[None, :])
    offsets = jnp.arange(ITEMS, dtype=jnp.int32)[None, :] - ITEMS
    owners = jnp.sum(jnp.where(inside, offsets, 0), axis=1) + ITEMS
    live_mask = jnp.any(inside & (positions[:, None] < (starts + lengths_row)[None, :]), axis=1)
    return (owners, live_mask)


def slot_of(q, count, swap):
    if count != GROUPS:
        return q
    bits = [(q >> b) & 1 for b in range(GROUPS.bit_length() - 1)]
    if swap:
        bits[0], bits[1] = bits[1], bits[0]
    slot = 0
    for bit in bits:
        slot = 2 * slot + bit
    return slot


def store_rows(buffer, value, count, swap, start, columns=slice(None)):
    rows = value.shape[0] // GROUPS
    for q in range(GROUPS):
        buffer[slot_of(q, count, swap), pl.ds(start, rows), columns] = value[
            q * rows : (q + 1) * rows
        ].astype(bf16)


def patch_bias(live_row):
    rows = lax.broadcasted_iota(jnp.int32, (BLOCK, BLOCK), 0)
    columns = lax.broadcasted_iota(jnp.int32, (BLOCK, BLOCK), 1)
    same = (rows // PATCH) == (columns // PATCH)
    allowed = same & (columns <= rows) & ((live_row > 0) | (columns == rows))
    bias = jnp.where(allowed, 0.0, MASKED)
    return jnp.concatenate([bias, bias], axis=0)


def softmax_rows(scores):
    peak = jnp.max(scores, axis=-1, keepdims=True)
    exponents = jnp.exp(scores - peak)
    return exponents * (1.0 / jnp.sum(exponents, axis=-1, keepdims=True))


def lane_masks():
    lanes = lax.broadcasted_iota(jnp.int32, (1, PAIR), 1)
    low = jnp.where(lanes < HEAD_SIZE, 1.0, 0.0)
    return lanes < HEAD_SIZE, low.astype(bf16), (1.0 - low).astype(bf16)


def stacked(values, low, high, scale=1.0):
    return jnp.concatenate([values * (low * scale), values * (high * scale)], axis=0)


def unstacked(values, is_low):
    half = values.shape[0] // 2
    return jnp.where(is_low, values[:half], values[half:])


def pair_forward(queries, keys, values, bias, masks):
    is_low, low, high = masks
    scores = product_transposed(stacked(queries, low, high, SCALE), keys) + bias
    return unstacked(product(softmax_rows(scores).astype(bf16), values), is_low)


def pair_backward(queries, keys, values, grads, bias, masks):
    is_low, low, high = masks
    both = stacked(queries, low, high, SCALE)
    both_grads = stacked(grads, low, high)
    probabilities = softmax_rows(product_transposed(both, keys) + bias)
    prob_grads = product_transposed(both_grads, values)
    delta = jnp.sum(probabilities * prob_grads, axis=-1, keepdims=True)
    score_grads = (probabilities * (prob_grads - delta)).astype(bf16)
    return (
        unstacked(product(score_grads, keys), is_low) * SCALE,
        transposed_product(score_grads, both),
        transposed_product(probabilities.astype(bf16), both_grads),
    )


def gelu_and_slope(x):
    root = 0.7978845608028654
    cubic = 0.044715
    square = x * x
    bent = jnp.tanh(x * (root + (root * cubic) * square))
    half = 0.5 * (1.0 + bent)
    slope = half + (0.5 * x) * (1.0 - bent * bent) * (root + (3.0 * root * cubic) * square)
    return x * half, slope


def fetch(section, own, arrived, target, sem):
    @pl.when(section == 0)
    def _():
        pltpu.make_async_copy(arrived, target, sem).start()

    @pl.when(section != 0)
    def _():
        pltpu.make_async_copy(own, target, sem).start()


def leave(section, first, second, keep, send, sems):
    @pl.when(section == 0)
    def _():
        pltpu.make_async_copy(first, keep, sems.at[0]).start()
        pltpu.make_async_copy(second, send, sems.at[1]).start()

    @pl.when(section != 0)
    def _():
        pltpu.make_async_copy(second, keep, sems.at[0]).start()
        pltpu.make_async_copy(first, send, sems.at[1]).start()

    pltpu.make_async_copy(first, keep, sems.at[0]).wait()
    pltpu.make_async_copy(second, send, sems.at[1]).wait()


def local_first_kernel(
    count,
    section_ref,
    ids_ref,
    table_ref,
    shifted_ref,
    gains_ref,
    biases_ref,
    live_row_ref,
    live_column_ref,
    out_grad_ref,
    own_in,
    own_out,
    own_expand,
    own_contract,
    new_in,
    new_out,
    new_expand,
    new_contract,
    act_ref,
    stream_ref,
    normed_ref,
    mixed_ref,
    attended_ref,
    grad_middle_ref,
    small_ref,
    keep_ref,
    send_ref,
    w_in,
    w_out,
    w_expand,
    w_contract,
    middle_ref,
    normed_two_ref,
    branch_ref,
    hidden_ref,
    slope_ref,
    upward_ref,
    contract_sum,
    expand_sum,
    sems,
    out_sems,
):
    section = section_ref[0]
    fetch(section, own_in, new_in, w_in, sems.at[0])
    fetch(section, own_out, new_out, w_out, sems.at[1])
    fetch(section, own_expand, new_expand, w_expand, sems.at[2])
    fetch(section, own_contract, new_contract, w_contract, sems.at[3])
    rows, width = act_ref.shape
    steps = rows // BLOCK
    hidden_width = hidden_ref.shape[1]
    patches = shifted_ref.shape[0]

    def row_block(i):
        return pl.ds(pl.multiple_of(i * BLOCK, BLOCK), BLOCK)

    def column_block(i, size):
        return pl.ds(pl.multiple_of(i * size, 128), size)

    @pl.loop(0, steps)
    def _(i):
        at = row_block(i)
        vocabulary = lax.broadcasted_iota(jnp.int32, (BLOCK, VOCAB), 1)
        onehot = jnp.where(ids_ref[at, :] == vocabulary, 1.0, 0.0).astype(bf16)
        places = lax.broadcasted_iota(jnp.int32, (BLOCK, patches), 0) // PATCH
        columns = lax.broadcasted_iota(jnp.int32, (BLOCK, patches), 1)
        spread = jnp.where(places + i * (BLOCK // PATCH) == columns, 1.0, 0.0).astype(bf16)
        stream = product(onehot, table_ref[...]) + product(spread, shifted_ref[...])
        stream_ref[at, :] = stream
        normed_ref[at, :] = layer_norm(stream, gains_ref[0:1], biases_ref[0:1]).astype(bf16)
        branch_ref[at, :] = jnp.where(
            live_column_ref[at, :] > 0, out_grad_ref[at, :].astype(f32), 0.0
        ).astype(bf16)

    pltpu.make_async_copy(own_in, w_in, sems.at[0]).wait()

    @pl.loop(0, 3 * width // TILE)
    def _(i):
        at = column_block(i, TILE)
        mixed_ref[:, at] = product(normed_ref[...], w_in[:, at]).astype(bf16)

    masks = lane_masks()

    @pl.loop(0, steps)
    def _(i):
        at = row_block(i)
        bias = patch_bias(live_row_ref[i])
        for pair in range(PAIRS):
            first = slice(pair * PAIR, (pair + 1) * PAIR)
            second = slice(width + pair * PAIR, width + (pair + 1) * PAIR)
            third = slice(2 * width + pair * PAIR, 2 * width + (pair + 1) * PAIR)
            attended_ref[at, first] = pair_forward(
                mixed_ref[at, first], mixed_ref[at, second], mixed_ref[at, third], bias, masks
            ).astype(bf16)

    pltpu.make_async_copy(own_out, w_out, sems.at[1]).wait()

    @pl.loop(0, steps)
    def _(i):
        at = row_block(i)
        middle = stream_ref[at, :] + product(attended_ref[at, :], w_out[...])
        middle_ref[at, :] = middle
        normed_two_ref[at, :] = layer_norm(middle, gains_ref[1:2], biases_ref[1:2]).astype(bf16)

    pltpu.make_async_copy(own_expand, w_expand, sems.at[2]).wait()

    @pl.loop(0, hidden_width // TILE)
    def _(i):
        at = column_block(i, TILE)
        hidden, slope = gelu_and_slope(product(normed_two_ref[...], w_expand[:, at]))
        hidden_ref[:, at] = hidden.astype(bf16)
        slope_ref[:, at] = slope.astype(bf16)

    pltpu.make_async_copy(own_contract, w_contract, sems.at[3]).wait()

    @pl.loop(0, width // 256)
    def _(i):
        at = column_block(i, 256)
        result = middle_ref[:, at] + product(hidden_ref[...], w_contract[:, at])
        act_ref[:, at] = jnp.where(live_column_ref[...] > 0, result, 0.0).astype(bf16)

    tile_rows = TILE // (hidden_width // GROUPS)
    halves = width // TILE

    @pl.loop(0, hidden_width // width)
    def _(chunk):
        for half in range(halves):
            i = chunk * halves + half
            at = column_block(i, TILE)
            grad_hidden = product_transposed(branch_ref[...], w_contract[at, :])
            grad_upward = (grad_hidden * slope_ref[:, at].astype(f32)).astype(bf16)
            upward_ref[:, at] = grad_upward
            part = transposed_product(normed_two_ref[...], grad_upward)
            store_rows(
                expand_sum,
                part,
                count,
                True,
                pl.multiple_of(chunk * (width // GROUPS), 16),
                slice(half * TILE, (half + 1) * TILE),
            )

    for i in range(hidden_width // TILE):
        part = transposed_product(hidden_ref[:, i * TILE : (i + 1) * TILE], branch_ref[...])
        size = TILE // tile_rows
        for k in range(tile_rows):
            slot = slot_of(i * tile_rows + k, count, False)
            contract_sum[slot] = part[k * size : (k + 1) * size].astype(bf16)

    @pl.loop(0, width // 256)
    def _(i):
        at = column_block(i, 256)
        grad_middle_ref[:, at] = product_transposed(upward_ref[...], w_expand[at, :])

    def norm_back(i, sums):
        at = row_block(i)
        grad = grad_middle_ref[at, :]
        back, gain, bias = layer_norm_back(middle_ref[at, :], gains_ref[1:2], grad)
        grad_middle_ref[at, :] = back + branch_ref[at, :].astype(f32)
        return sums[0] + gain, sums[1] + bias

    zero = jnp.zeros((1, width), f32)
    gain, bias = lax.fori_loop(0, steps, norm_back, (zero, zero))
    small_ref[...] = jnp.concatenate([gain, bias], axis=0)
    leave(section, contract_sum, expand_sum, keep_ref, send_ref, out_sems)


def local_second_kernel(
    count,
    section_ref,
    ids_ref,
    same_ref,
    gains_ref,
    live_row_ref,
    stream_ref,
    normed_ref,
    mixed_ref,
    attended_ref,
    grad_middle_ref,
    small_ref,
    own_in,
    own_out,
    new_in,
    new_out,
    shifted_ref,
    keep_ref,
    send_ref,
    w_in,
    w_out,
    branch_ref,
    grad_attended_ref,
    grad_mixed_ref,
    grad_stream_ref,
    first_sum,
    second_sum,
    sems,
    out_sems,
):
    section = section_ref[0]
    fetch(section, own_out, new_out, w_out, sems.at[1])
    fetch(section, own_in, new_in, w_in, sems.at[0])
    rows, width = normed_ref.shape
    steps = rows // BLOCK
    shard = width // GROUPS

    def row_block(i):
        return pl.ds(pl.multiple_of(i * BLOCK, BLOCK), BLOCK)

    def column_block(i, size):
        return pl.ds(pl.multiple_of(i * size, 128), size)

    branch_ref[...] = grad_middle_ref[...].astype(bf16)
    store_rows(first_sum, transposed_product(attended_ref[...], branch_ref[...]), count, False, shard)
    pltpu.make_async_copy(own_out, w_out, sems.at[1]).wait()
    grad_attended_ref[...] = product_transposed(branch_ref[...], w_out[...]).astype(bf16)
    masks = lane_masks()

    @pl.loop(0, steps)
    def _(i):
        at = row_block(i)
        bias = patch_bias(live_row_ref[i])
        for pair in range(PAIRS):
            first = slice(pair * PAIR, (pair + 1) * PAIR)
            second = slice(width + pair * PAIR, width + (pair + 1) * PAIR)
            third = slice(2 * width + pair * PAIR, 2 * width + (pair + 1) * PAIR)
            parts = pair_backward(
                mixed_ref[at, first],
                mixed_ref[at, second],
                mixed_ref[at, third],
                grad_attended_ref[at, first],
                bias,
                masks,
            )
            for where, part in zip((first, second, third), parts):
                grad_mixed_ref[at, where] = part.astype(bf16)

    pltpu.make_async_copy(own_in, w_in, sems.at[0]).wait()

    @pl.loop(0, width // 256)
    def _(i):
        at = column_block(i, 256)
        grad_stream_ref[:, at] = product_transposed(grad_mixed_ref[...], w_in[at, :])

    def norm_back(i, sums):
        at = row_block(i)
        back, gain, bias = layer_norm_back(
            stream_ref[at, :], gains_ref[0:1], grad_stream_ref[at, :]
        )
        grad_stream_ref[at, :] = back + grad_middle_ref[at, :]
        return sums[0] + gain, sums[1] + bias

    zero = jnp.zeros((1, width), f32)
    gain, bias = lax.fori_loop(0, steps, norm_back, (zero, zero))
    summed = jnp.sum(grad_stream_ref[...].reshape(rows // PATCH, PATCH, width), axis=1)
    shifted_ref[...] = jnp.where(same_ref[...] > 0, summed, 0.0).astype(bf16)

    for chunk in range(3):
        part = transposed_product(
            normed_ref[...], grad_mixed_ref[:, chunk * width : (chunk + 1) * width]
        )
        if chunk == 0:
            store_rows(first_sum, part, count, False, 0)
        else:
            store_rows(second_sum, part, count, True, (chunk - 1) * shard)
    vocabulary = lax.broadcasted_iota(jnp.int32, (rows, VOCAB), 1)
    onehot = jnp.where(ids_ref[...] == vocabulary, 1.0, 0.0).astype(bf16)
    part = transposed_product(onehot, grad_stream_ref[...].astype(bf16))
    store_rows(first_sum, part, count, False, 2 * shard)
    store_small(first_sum, second_sum, gain, small_ref[0:1], bias, small_ref[1:2], shard)
    leave(section, first_sum, second_sum, keep_ref, send_ref, out_sems)


def store_small(first_sum, second_sum, gain_one, gain_two, bias_one, bias_two, shard):
    room = VOCAB // GROUPS
    width = gain_one.shape[1]
    small = jnp.concatenate(
        [gain_one, gain_two, bias_one, bias_two, jnp.zeros((room - 4, width), f32)], axis=0
    ).astype(bf16)
    for q in range(GROUPS):
        first_sum[q, 2 * shard + room : 2 * shard + 2 * room, :] = small
        second_sum[q, 2 * shard : 2 * shard + 2 * room, :] = jnp.zeros((2 * room, width), bf16)


ANY = pl.BlockSpec(memory_space=pl.ANY)
WHOLE = pl.BlockSpec(memory_space=pltpu.VMEM)
SCALARS = pl.BlockSpec(memory_space=pltpu.SMEM)


def local_first(count, section, ids, table, shifted, gains, biases, live, out_grad, own, new):
    rows, width = out_grad.shape
    hidden_width = own[3].shape[0]
    steps = rows // BLOCK
    shard = hidden_width // GROUPS
    flops = 2 * rows * width * (4 * width + 2 * hidden_width) + 8 * rows * width * hidden_width
    live = live.astype(jnp.int32)
    sums = jax.ShapeDtypeStruct((GROUPS, shard, width), bf16)

    def vmem(*shape, kind=bf16):
        return pltpu.VMEM(shape, kind)

    return pl.pallas_call(
        partial(local_first_kernel, count),
        in_specs=[SCALARS] + [WHOLE] * 8 + [ANY] * 8,
        out_specs=[WHOLE] * 7 + [ANY] * 2,
        out_shape=[
            jax.ShapeDtypeStruct((rows, width), bf16),
            jax.ShapeDtypeStruct((rows, width), f32),
            jax.ShapeDtypeStruct((rows, width), bf16),
            jax.ShapeDtypeStruct((rows, 3 * width), bf16),
            jax.ShapeDtypeStruct((rows, width), bf16),
            jax.ShapeDtypeStruct((rows, width), f32),
            jax.ShapeDtypeStruct((2, width), f32),
            sums,
            sums,
        ],
        scratch_shapes=[
            vmem(*own[0].shape),
            vmem(*own[1].shape),
            vmem(*own[2].shape),
            vmem(*own[3].shape),
            vmem(rows, width, kind=f32),
            vmem(rows, width),
            vmem(rows, width),
            vmem(rows, hidden_width),
            vmem(rows, hidden_width),
            vmem(rows, hidden_width),
            vmem(*sums.shape),
            vmem(*sums.shape),
            pltpu.SemaphoreType.DMA((4,)),
            pltpu.SemaphoreType.DMA((2,)),
        ],
        compiler_params=pltpu.CompilerParams(vmem_limit_bytes=VMEM),
        cost_estimate=pl.CostEstimate(
            flops=flops, bytes_accessed=40_000_000, transcendentals=rows * hidden_width
        ),
    )(
        section,
        ids.reshape(rows, 1),
        table,
        shifted,
        gains,
        biases,
        live.reshape(steps, 1, BLOCK),
        live.reshape(rows, 1),
        out_grad,
        *own,
        *new,
    )


def local_second(count, section, ids, same, gains, live, saved, small, own, new):
    stream, normed, mixed, attended, grad_middle = saved
    rows, width = normed.shape
    steps = rows // BLOCK
    sums = jax.ShapeDtypeStruct((GROUPS, 2 * (width + VOCAB) // GROUPS, width), bf16)
    flops = 2 * rows * width * 10 * width

    def vmem(*shape, kind=bf16):
        return pltpu.VMEM(shape, kind)

    return pl.pallas_call(
        partial(local_second_kernel, count),
        in_specs=[SCALARS] + [WHOLE] * 10 + [ANY] * 4,
        out_specs=[WHOLE] + [ANY] * 2,
        out_shape=[jax.ShapeDtypeStruct((rows // PATCH, width), bf16), sums, sums],
        scratch_shapes=[
            vmem(*own[0].shape),
            vmem(*own[1].shape),
            vmem(rows, width),
            vmem(rows, width),
            vmem(rows, 3 * width),
            vmem(rows, width, kind=f32),
            vmem(*sums.shape),
            vmem(*sums.shape),
            pltpu.SemaphoreType.DMA((2,)),
            pltpu.SemaphoreType.DMA((2,)),
        ],
        compiler_params=pltpu.CompilerParams(vmem_limit_bytes=VMEM),
        cost_estimate=pl.CostEstimate(
            flops=flops, bytes_accessed=20_000_000, transcendentals=rows * HEADS * BLOCK
        ),
    )(
        section,
        ids.reshape(rows, 1),
        same,
        gains,
        live.astype(jnp.int32).reshape(steps, 1, BLOCK),
        stream,
        normed,
        mixed,
        attended,
        grad_middle,
        small,
        own[0],
        own[1],
        new[0],
        new[1],
    )


def global_feed_kernel(count, hidden_ref, branch_ref, normed_two_ref, upward_ref, first, second):
    hidden_width, width = hidden_ref.shape[1], branch_ref.shape[1]
    halves = width // TILE
    tile_rows = TILE // (hidden_width // GROUPS)
    for i in range(hidden_width // TILE):
        part = transposed_product(hidden_ref[:, i * TILE : (i + 1) * TILE], branch_ref[...])
        size = TILE // tile_rows
        for k in range(tile_rows):
            slot = slot_of(i * tile_rows + k, count, False)
            first[slot] = part[k * size : (k + 1) * size].astype(bf16)

    @pl.loop(0, hidden_width // width)
    def _(chunk):
        for half in range(halves):
            i = chunk * halves + half
            at = pl.ds(pl.multiple_of(i * TILE, 128), TILE)
            part = transposed_product(normed_two_ref[...], upward_ref[:, at])
            store_rows(
                second,
                part,
                count,
                True,
                pl.multiple_of(chunk * (width // GROUPS), 16),
                slice(half * TILE, (half + 1) * TILE),
            )


def global_feed(count, hidden, branch, normed_two, upward):
    hidden_width, width = hidden.shape[1], branch.shape[1]
    sums = jax.ShapeDtypeStruct((GROUPS, hidden_width // GROUPS, width), bf16)
    return pl.pallas_call(
        partial(global_feed_kernel, count),
        out_shape=[sums, sums],
        compiler_params=pltpu.CompilerParams(vmem_limit_bytes=VMEM),
        cost_estimate=pl.CostEstimate(
            flops=4 * hidden.shape[0] * hidden_width * width,
            bytes_accessed=10_000_000,
            transcendentals=0,
        ),
    )(hidden, branch, normed_two, upward)


def global_heads_kernel(
    count, normed_ref, grad_mixed_ref, attended_ref, branch_ref, small_ref, first, second
):
    width = normed_ref.shape[1]
    shard = width // GROUPS
    room = VOCAB // GROUPS
    store_rows(first, transposed_product(attended_ref[...], branch_ref[...]), count, False, shard)
    for chunk in range(3):
        part = transposed_product(
            normed_ref[...], grad_mixed_ref[:, chunk * width : (chunk + 1) * width]
        )
        if chunk == 0:
            store_rows(first, part, count, False, 0)
        else:
            store_rows(second, part, count, True, (chunk - 1) * shard)
    for q in range(GROUPS):
        first[q, 2 * shard : 2 * shard + room, :] = jnp.zeros((room, width), bf16)
    small = [small_ref[k : k + 1] for k in range(4)]
    store_small(first, second, *small, shard)


def global_heads(count, normed, grad_mixed, attended, branch, small):
    rows, width = normed.shape
    sums = jax.ShapeDtypeStruct((GROUPS, 2 * (width + VOCAB) // GROUPS, width), bf16)
    return pl.pallas_call(
        partial(global_heads_kernel, count),
        out_shape=[sums, sums],
        compiler_params=pltpu.CompilerParams(vmem_limit_bytes=VMEM),
        cost_estimate=pl.CostEstimate(
            flops=8 * rows * width * width, bytes_accessed=7_000_000, transcendentals=0
        ),
    )(normed, grad_mixed, attended, branch, small)


def causal_bias(start, owner_column, owner_row):
    shape = (BLOCK, owner_row.shape[1])
    rows = lax.broadcasted_iota(jnp.int32, shape, 0) + start
    columns = lax.broadcasted_iota(jnp.int32, shape, 1)
    bias = jnp.where((columns <= rows) & (owner_column == owner_row), 0.0, MASKED)
    return jnp.concatenate([bias, bias], axis=0)


def global_forward_kernel(column_ref, row_ref, qkv_ref, out_ref):
    start = pl.multiple_of(pl.program_id(0) * BLOCK, BLOCK)
    bias = causal_bias(start, column_ref[...], row_ref[...])
    out_ref[...] = pair_forward(
        qkv_ref[pl.ds(start, BLOCK), 0:PAIR],
        qkv_ref[:, PAIR : 2 * PAIR],
        qkv_ref[:, 2 * PAIR : 3 * PAIR],
        bias,
        lane_masks(),
    ).astype(bf16)


def global_backward_kernel(column_ref, row_ref, qkv_ref, grad_ref, out_ref, key_sum, value_sum):
    step = pl.program_id(0)
    start = pl.multiple_of(step * BLOCK, BLOCK)
    bias = causal_bias(start, column_ref[...], row_ref[...])

    @pl.when(step == 0)
    def _():
        key_sum[...] = jnp.zeros_like(key_sum)
        value_sum[...] = jnp.zeros_like(value_sum)

    grad_queries, grad_keys, grad_values = pair_backward(
        qkv_ref[pl.ds(start, BLOCK), 0:PAIR],
        qkv_ref[:, PAIR : 2 * PAIR],
        qkv_ref[:, 2 * PAIR : 3 * PAIR],
        grad_ref[...],
        bias,
        lane_masks(),
    )
    out_ref[pl.ds(start, BLOCK), 0:PAIR] = grad_queries.astype(bf16)
    key_sum[...] += grad_keys
    value_sum[...] += grad_values

    @pl.when(step == pl.num_programs(0) - 1)
    def _():
        out_ref[:, PAIR : 2 * PAIR] = key_sum[...].astype(bf16)
        out_ref[:, 2 * PAIR : 3 * PAIR] = value_sum[...].astype(bf16)


def global_attention(qkv, owners, grads=None):
    count = qkv.shape[0]
    column, row = owners[:, None], owners[None, :]
    specs = [
        pl.BlockSpec((BLOCK, 1), lambda i: (i, 0)),
        pl.BlockSpec((1, count), lambda i: (0, 0)),
        pl.BlockSpec((count, 3 * PAIR), lambda i: (0, 0)),
    ]
    blocks = pl.BlockSpec((BLOCK, PAIR), lambda i: (i, 0))
    if grads is None:
        return pl.pallas_call(
            global_forward_kernel,
            grid=(count // BLOCK,),
            in_specs=specs,
            out_specs=blocks,
            out_shape=jax.ShapeDtypeStruct((count, PAIR), bf16),
            compiler_params=pltpu.CompilerParams(vmem_limit_bytes=VMEM),
        )(column, row, qkv)
    return pl.pallas_call(
        global_backward_kernel,
        grid=(count // BLOCK,),
        in_specs=specs + [blocks],
        out_specs=pl.BlockSpec((count, 3 * PAIR), lambda i: (0, 0)),
        out_shape=jax.ShapeDtypeStruct((count, 3 * PAIR), bf16),
        scratch_shapes=[pltpu.VMEM((count, PAIR), f32), pltpu.VMEM((count, PAIR), f32)],
        compiler_params=pltpu.CompilerParams(vmem_limit_bytes=VMEM),
    )(column, row, qkv, grads)


def section_send(x, origin, target, pairs):
    count = lax.axis_size("seq")
    joint = [(origin * count + i, target * count + j) for i, j in pairs]
    return lax.ppermute(x, ("section", "seq"), joint)


def section_swap(x):
    return lax.ppermute(x, "section", [(0, 1), (1, 0)])


def by_slot(buffer, count, swap, pieces):
    if count == GROUPS:
        return buffer
    depth = count.bit_length() - 1
    split = count // GROUPS
    parts, start = [], 0
    for size, shared in pieces:
        part = buffer[:, start : start + size]
        start += size
        kept = shared or size // split
        if shared:
            part = jnp.broadcast_to(part[:, None, :shared], (GROUPS, split, shared, part.shape[2]))
        parts.append(part.reshape(count, kept, part.shape[-1]))
    whole = jnp.concatenate(parts, axis=1)
    order = list(range(depth))
    if swap:
        order[0], order[1] = order[1], order[0]
    bits = whole.reshape((2,) * depth + whole.shape[1:])
    bits = jnp.transpose(bits, [depth - 1 - b for b in order] + [depth, depth + 1])
    return bits.reshape(whole.shape)


def halving_sum(parts):
    count = lax.axis_size("seq")
    place = lax.axis_index("seq")
    section = lax.axis_index("section")
    depth = count.bit_length() - 1
    shape = parts[0].shape[1:]
    held = [(part, 0) for part in parts]
    half = count
    for step in range(depth):
        bits = [step, step]
        if step < 2:
            bits[1] = 1 - step
        mine = jnp.where(section == 0, (place >> bits[0]) & 1, (place >> bits[1]) & 1)
        half //= 2

        def piece(entry, which):
            array, start = entry
            return lax.dynamic_slice(array, (start + which * half, 0, 0), (half,) + shape)

        leaving = sum(piece(entry, 1 - mine).astype(f32) for entry in held).astype(bf16)
        joint = []
        for origin in range(2):
            joint += [
                (origin * count + i, origin * count + (i ^ (1 << bits[origin])))
                for i in range(count)
            ]
        arrived = lax.ppermute(leaving, ("section", "seq"), joint)
        held = [(array, start + mine * half) for array, start in held] + [(arrived, 0)]
    total = sum(
        lax.dynamic_slice(array, (start, 0, 0), (1,) + shape).astype(f32) for array, start in held
    )
    return total[0]


def feed_forward(stream, attended, gains, biases, heads_out, expand, contract):
    middle = stream + product(attended, heads_out)
    normed_two = layer_norm(middle, gains[1], biases[1]).astype(bf16)
    hidden, slope = gelu_and_slope(product(normed_two, expand))
    hidden = hidden.astype(bf16)
    result = middle + product(hidden, contract)
    return result, (middle, normed_two, slope, hidden)


def feed_backward(grad_result, kept, gains, heads_out, expand, contract):
    middle, normed_two, slope, hidden = kept
    branch = grad_result.astype(bf16)
    grad_upward = (slope * product_transposed(branch, contract)).astype(bf16)
    grad_normed_two = product_transposed(grad_upward, expand)
    grad_middle, gain_two, bias_two = layer_norm_back(middle, gains[1:2], grad_normed_two)
    grad_middle = grad_middle + grad_result
    attend_branch = grad_middle.astype(bf16)
    grad_attended = product_transposed(attend_branch, heads_out).astype(bf16)
    return grad_middle, attend_branch, grad_attended, branch, grad_upward, (gain_two, bias_two)


def on_device(
    byte_values,
    item_lengths,
    embed_tables,
    patch_weight,
    norm_gains,
    norm_biases,
    heads_in,
    heads_out,
    expand_weight,
    contract_weight,
    out_grad,
):
    place = lax.axis_index("seq")
    count = lax.axis_size("seq")
    section = lax.axis_index("section")
    is_global = section == 0
    batches, byte_rows = byte_values.shape
    patch_rows = byte_rows // PATCH
    width = heads_out.shape[2]
    rows = batches * patch_rows
    total_patches = patch_rows * count
    gains, biases = norm_gains[0], norm_biases[0]
    heads_in, heads_out = heads_in[0], heads_out[0]
    expand, contract = expand_weight[0], contract_weight[0]
    own_table = embed_tables[0]
    straight = [(i, i) for i in range(count)]
    vocabulary = jnp.arange(VOCAB, dtype=jnp.int32)

    def onehot_of(ids):
        return (ids[:, None] == vocabulary[None, :]).astype(bf16)

    quarters = PATCH // 2
    span = count // quarters
    group, member = place // span, place % span
    shard_rows = patch_weight.shape[0]
    byte_weight = jnp.zeros((span * shard_rows, width), bf16)
    byte_weight = lax.dynamic_update_slice(byte_weight, patch_weight, (member * shard_rows, 0))
    for k in range(1, span):
        piece = lax.ppermute(patch_weight, "seq", [(i, i ^ k) for i in range(count)])
        byte_weight = lax.dynamic_update_slice(byte_weight, piece, ((member ^ k) * shard_rows, 0))
    other_table = section_swap(own_table)
    global_table = jnp.where(is_global, own_table, other_table)
    local_table = jnp.where(is_global, other_table, own_table)
    which_byte = section * quarters + group
    byte_ids = []
    for k in range(quarters):
        theirs = byte_values
        if k:
            theirs = lax.ppermute(byte_values, "seq", [(i, i ^ (k * span)) for i in range(count)])
        theirs = theirs.reshape(rows, PATCH)
        byte_ids.append(lax.dynamic_index_in_dim(theirs, which_byte, 1, keepdims=False))
    patch_onehot = onehot_of(jnp.concatenate(byte_ids))
    embedded = product(patch_onehot, global_table).astype(bf16)
    shares = product(embedded, byte_weight)
    shares = shares + section_send(shares.astype(bf16), 1, 0, straight).astype(f32)
    shares = shares.reshape(quarters, rows, width)
    stream = shares[0]
    for k in range(1, quarters):
        pairs = [(i, i ^ (k * span)) for i in range(count)]
        stream = stream + section_send(shares[k].astype(bf16), 0, 0, pairs).astype(f32)

    arrived = [section_send(w, 1, 0, straight) for w in (heads_in, heads_out, expand, contract)]
    other_norms = section_swap(jnp.concatenate([gains, biases]))
    local_gains = jnp.where(is_global, other_norms[:2], gains)
    local_biases = jnp.where(is_global, other_norms[2:], biases)

    tasks = batches * PAIRS
    first_tasks = min(tasks, count)
    spare_tasks = tasks - first_tasks

    def to_tasks(blocks):
        columns = blocks.shape[2]
        slots = jnp.pad(blocks[:first_tasks], ((0, count - first_tasks), (0, 0), (0, 0)))
        if spare_tasks:
            spare = section_send(blocks[first_tasks:], 0, 1, straight)
            spare = jnp.pad(spare, ((0, count - spare_tasks), (0, 0), (0, 0)))
            slots = jnp.where(is_global, slots, spare)
        landed = lax.all_to_all(slots, "seq", 0, 0)
        return landed.reshape(total_patches, columns)

    def from_tasks(results):
        columns = results.shape[1]
        slots = lax.all_to_all(results.reshape(count, patch_rows, columns), "seq", 0, 0)
        blocks = slots[:first_tasks]
        if spare_tasks:
            spare = section_send(slots[:spare_tasks], 1, 0, straight)
            blocks = jnp.concatenate([blocks, spare])
        return blocks

    def by_pair(values, parts):
        split = values.reshape(batches, patch_rows, parts, PAIRS, PAIR)
        return jnp.transpose(split, (0, 3, 1, 2, 4)).reshape(tasks, patch_rows, parts * PAIR)

    def from_pairs(blocks, parts):
        split = blocks.reshape(batches, PAIRS, patch_rows, parts, PAIR)
        return jnp.transpose(split, (0, 2, 3, 1, 4)).reshape(rows, parts * width)

    task = jnp.minimum(jnp.where(is_global, place, first_tasks + place), tasks - 1)
    task_lengths = lax.dynamic_index_in_dim(item_lengths, task // PAIRS, 0, keepdims=False)
    task_owners = locate(jnp.arange(total_patches, dtype=jnp.int32) * PATCH, task_lengths)[0]

    normed = layer_norm(stream, gains[0], biases[0]).astype(bf16)
    mixed = product(normed, heads_in).astype(bf16)
    qkv = to_tasks(by_pair(mixed, 3))
    attended = from_pairs(from_tasks(global_attention(qkv, task_owners)), 1)
    global_out, global_kept = feed_forward(
        stream, attended, gains, biases, heads_out, expand, contract
    )
    sent = global_out.astype(bf16).reshape(batches, patch_rows, width)

    half = patch_rows // 2
    half_bytes = half * PATCH
    chunks = half_bytes // BLOCK
    onward = [(i, i + 1) for i in range(count - 1)]
    backward = [(i + 1, i) for i in range(count - 1)]
    near = section_send(sent[:, half - 1 : patch_rows - 1], 0, 1, straight)
    edge = section_send(sent[:, patch_rows - 1 :], 0, 0, onward)
    shifted = jnp.where(is_global, jnp.concatenate([edge, sent[:, : half - 1]], axis=1), near)

    byte_places = place * byte_rows + jnp.arange(byte_rows, dtype=jnp.int32)
    live_bytes = jnp.stack([locate(byte_places, item_lengths[m])[1] for m in range(batches)])
    patch_places = place * byte_rows + section * half_bytes + PATCH * jnp.arange(half, dtype=jnp.int32)
    same_item = jnp.stack(
        [
            locate(patch_places, item_lengths[m])[0]
            == locate(patch_places - PATCH, item_lengths[m])[0]
            for m in range(batches)
        ]
    )[:, :, None]
    shifted = jnp.where(same_item, shifted, jnp.zeros((), bf16))
    half_start = section * half_bytes
    own_ids = lax.dynamic_slice_in_dim(byte_values, half_start, half_bytes, 1)
    own_live = lax.dynamic_slice_in_dim(live_bytes, half_start, half_bytes, 1)
    own_grad = lax.dynamic_slice_in_dim(out_grad, half_start, half_bytes, 1)
    weights = (heads_in, heads_out, expand, contract)
    flag = section.reshape(1).astype(jnp.int32)
    block_patches = BLOCK // PATCH

    local_outs, feed_sums, heads_sums, grads_shifted = [], [], [], []
    for c in range(chunks):
        here = slice(c * BLOCK, (c + 1) * BLOCK)
        there = slice(c * block_patches, (c + 1) * block_patches)
        ids = own_ids[:, here].reshape(batches * BLOCK)
        live = own_live[:, here].reshape(batches * BLOCK)
        same = same_item[:, there].astype(jnp.int32).reshape(batches * block_patches, 1)
        act, *saved, small, keep, send = local_first(
            count,
            flag,
            ids,
            local_table,
            shifted[:, there].reshape(batches * block_patches, width),
            local_gains,
            local_biases,
            live,
            own_grad[:, here].reshape(batches * BLOCK, width),
            weights,
            arrived,
        )
        local_outs.append(act.reshape(batches, BLOCK, width))
        feed_sums.append((keep, send))
        grad_shifted, keep, send = local_second(
            count, flag, ids, same, local_gains, live, saved, small, weights, arrived
        )
        heads_sums.append((keep, send))
        grads_shifted.append(grad_shifted.reshape(batches, block_patches, width))
    local_out = jnp.concatenate(local_outs, axis=1)
    grad_shifted = jnp.concatenate(grads_shifted, axis=1)

    other_out = section_send(local_out, 0, 1, straight)
    own_sent = jnp.broadcast_to(
        sent[:, :, None, :], (batches, patch_rows, PATCH, width)
    ).reshape(batches, byte_rows, width)
    own_sent = jnp.where(live_bytes[:, :, None], own_sent, jnp.zeros((), bf16))
    activations = jnp.where(
        is_global, own_sent, jnp.concatenate([other_out, local_out], axis=1)
    )

    near_back = section_send(grad_shifted, 1, 0, straight)
    edge_back = section_send(grad_shifted[:, :1], 0, 0, backward)
    grad_sent = jnp.concatenate([grad_shifted[:, 1:], near_back, edge_back], axis=1)
    grad_sent = grad_sent.reshape(rows, width).astype(f32)
    grad_middle, attend_branch, grad_attended, branch, grad_upward, twos = feed_backward(
        grad_sent, global_kept, gains, heads_out, expand, contract
    )
    task_grads = to_tasks(by_pair(grad_attended, 1))
    grad_mixed = from_pairs(from_tasks(global_attention(qkv, task_owners, task_grads)), 3)
    grad_normed = product_transposed(grad_mixed, heads_in)
    back, gain_one, bias_one = layer_norm_back(stream, gains[0:1], grad_normed)
    grad_stream = back + grad_middle

    own_rows = grad_stream.astype(bf16)
    gathered = [own_rows]
    for k in range(1, quarters):
        pairs = [(i, i ^ (k * span)) for i in range(count)]
        gathered.append(section_send(own_rows, 0, 0, pairs))
    gathered = jnp.concatenate(gathered)
    gathered = jnp.where(is_global, gathered, section_send(gathered, 0, 1, straight))
    patch_share = transposed_product(embedded, gathered).astype(bf16)
    patch_share = patch_share.reshape(span, shard_rows, width)
    patch_grads = lax.dynamic_index_in_dim(patch_share, member, 0, keepdims=False).astype(f32)
    for k in range(1, span):
        leaving = lax.dynamic_index_in_dim(patch_share, member ^ k, 0, keepdims=False)
        patch_grads = patch_grads + lax.ppermute(
            leaving, "seq", [(i, i ^ k) for i in range(count)]
        ).astype(f32)
    grad_embedded = product_transposed(gathered, byte_weight).astype(bf16)
    table_share = transposed_product(patch_onehot, grad_embedded).astype(bf16)
    table_share = table_share + section_send(table_share, 1, 0, straight)
    table_parts = lax.all_to_all(table_share.reshape(count, VOCAB // count, width), "seq", 0, 0)
    global_table_grad = jnp.sum(table_parts.astype(f32), axis=0)

    shard = width // count
    room = VOCAB // count
    group_shard, group_room = width // GROUPS, VOCAB // GROUPS
    small_rows = max(4, room)
    feed_pieces = {
        False: [(contract.shape[0] // GROUPS, 0)],
        True: [(group_shard, 0)] * (expand.shape[1] // width),
    }
    heads_pieces = {
        False: [(group_shard, 0), (group_shard, 0), (group_room, 0), (group_room, small_rows)],
        True: [(group_shard, 0), (group_shard, 0), (2 * group_room, room + small_rows)],
    }

    def ordered(buffer, pieces):
        if count == GROUPS:
            return buffer
        return jnp.where(
            is_global,
            by_slot(buffer, count, False, pieces[False]),
            by_slot(buffer, count, True, pieces[True]),
        )

    def local_sum(entries, pieces):
        parts = []
        for keep, send in entries:
            parts += [ordered(keep, pieces), ordered(section_swap(send), pieces)]
        return halving_sum(parts)

    def global_sum(first, second, pieces):
        crossed = section_send(second, 0, 1, straight)
        return halving_sum([ordered(jnp.where(is_global, first, crossed), pieces)])

    local_feed = local_sum(feed_sums, feed_pieces)
    local_heads = local_sum(heads_sums, heads_pieces)
    global_feed_sum = global_sum(
        *global_feed(count, global_kept[3], branch, global_kept[1], grad_upward), feed_pieces
    )
    small = jnp.concatenate([gain_one, twos[0], bias_one, twos[1]])
    global_heads_sum = global_sum(
        *global_heads(count, normed, grad_mixed, attended, attend_branch, small), heads_pieces
    )
    own_local = jnp.concatenate([local_feed, local_heads])
    own_global = jnp.concatenate([global_feed_sum, global_heads_sum])
    crossed = section_swap(jnp.where(is_global, own_local, own_global).astype(bf16)).astype(f32)
    first = jnp.where(is_global, own_global, crossed)
    second = jnp.where(is_global, crossed, own_local)

    feed_rows = contract.shape[0] // count
    contract_grad = first[:feed_rows]
    expand_grad = jnp.concatenate(
        [second[k * shard : (k + 1) * shard] for k in range(feed_rows // shard)], axis=1
    )
    first, second = first[feed_rows:], second[feed_rows:]
    in_grad = jnp.concatenate([first[:shard], second[:shard], second[shard : 2 * shard]], axis=1)
    out_grads = first[shard : 2 * shard]
    table_grad = jnp.where(is_global, global_table_grad, first[2 * shard : 2 * shard + room])
    small = lax.dynamic_slice_in_dim(first[2 * shard + room :][:4], place * shard, shard, 1)
    return (
        activations[None],
        table_grad[None],
        patch_grads,
        small[None, 0:2],
        small[None, 2:4],
        in_grad[None],
        out_grads[None],
        expand_grad[None],
        contract_grad[None],
    )


def solution(mesh):
    placed = (
        P(None, "seq"),
        P(),
        P("section", None, None),
        P(("section", "seq"), None),
        P("section", None, None),
        P("section", None, None),
        P("section", None, None),
        P("section", None, None),
        P("section", None, None),
        P("section", None, None),
        P(None, "seq", None),
    )
    return jax.shard_map(
        on_device,
        mesh=mesh,
        in_specs=placed,
        out_specs=(
            P("section", None, "seq", None),
            P("section", "seq", None),
            P(("section", "seq"), None),
            P("section", None, "seq"),
            P("section", None, "seq"),
            P("section", "seq", None),
            P("section", "seq", None),
            P("section", "seq", None),
            P("section", "seq", None),
        ),
        check_vma=False,
    )
```

time: 683 us -> 503 us (0.74)
  matrix products: 117 us -> 30.2 us
  starting transfers between devices: 183 us -> 98.7 us
  local copies, waits for them, and re-layouts: 112 us -> 31 us
  waiting for transfers between devices: 117 us -> 150 us
  blocking collectives: 0 us -> 28.9 us
  Pallas kernels: 73.7 us -> 84.1 us
    ppermute x0 -> x21, waiting for transfers between devices: none -> 108 us  [the longest x16 108 us: halving_sum(): arrived = lax.ppermute(leaving, ('section', 'seq'), joint)]
    ppermute x66 -> x24, starting transfers between devices: 152 us -> 53.2 us  [section_send(): return lax.ppermute(x, ('section', 'seq'), joint)]
    ppermute x66 -> x24, waiting for transfers between devices: 97.2 us -> 22.8 us  [section_send(): return lax.ppermute(x, ('section', 'seq'), joint)]
    dot_general x11 -> x2, matrix products: 41.4 us -> 2.7 us  [transposed_product(): lax.dot_general(former, latter, (((0,), (0,)), ((), ())), preferred_eleme...]
    dynamic_slice x25 -> x4, local copies, waits for them, and re-layouts: 39.2 us -> 4 us  [the longest x2 3.06 us: piece(): lax.dynamic_slice(array, (start + which * half, 0, 0), (half,) + shape)]
    all_to_all x0 -> x2, blocking collectives: none -> 28.9 us  [the longest x1 15.6 us: from_tasks(): lax.all_to_all(results.reshape(count, patch_rows, columns), 'seq', 0, 0)]
    dot_general x11 -> x6, matrix products: 38.9 us -> 14.3 us  [product(): return jnp.dot(former, latter, preferred_element_type=f32)]
    dot_general x8 -> x4, matrix products: 36.7 us -> 13.3 us  [product_transposed(): lax.dot_general(former, latter, (((1,), (1,)), ((), ())), preferred_eleme...]
  transfers between devices with their start and end apart: 79 -> 57, of which waited for: 27 -> 18; matrix products, arithmetic and copies ran while one was open for 25% -> 24% of each run, Pallas kernels for 1% -> 5%
where the time goes in v2:
time: 503 us; the launch traced here: 493 us
  waiting for transfers between devices  150 us (30%)
  starting transfers between devices  98.7 us (20%)
  Pallas kernels  84.1 us (17%)
  other arithmetic  67.1 us (13%)
  local copies, waits for them, and re-layouts  31 us (6%)
  matrix products  30.2 us (6%)
  blocking collectives  28.9 us (6%)
    ppermute x16, waiting for transfers between devices, halving_sum(): arrived = lax.ppermute(leaving, ('section', 'seq'), joint)  108 us
    ppermute x24, starting transfers between devices, section_send(): return lax.ppermute(x, ('section', 'seq'), joint)  53.2 us
    pallas_call x1, Pallas kernels, local_first(): pl.pallas_call(partial(local_first_kernel, count), in_specs=[SCALARS] + [...  38.3 us
    convert_element_type x14, other arithmetic, halving_sum(): sum((piece(entry, 1 - mine).astype(f32) for entry in held)).astype(bf16)  33.7 us
    ppermute x24, waiting for transfers between devices, section_send(): return lax.ppermute(x, ('section', 'seq'), joint)  22.8 us
    pallas_call x1, Pallas kernels, local_second(): pl.pallas_call(partial(local_second_kernel, count), in_specs=[SCALARS] +...  22.6 us
    all_to_all x1, blocking collectives, from_tasks(): lax.all_to_all(results.reshape(count, patch_rows, columns), 'seq', 0, 0)  15.6 us
    ppermute x16, starting transfers between devices, halving_sum(): arrived = lax.ppermute(leaving, ('section', 'seq'), joint)  15.2 us
  transfers between devices with their start and end apart: 57, of which 18 were waited for; matrix products, arithmetic and copies ran while one was open for 24% of the time, Pallas kernels for 5%

profile of v2, /device:TPU:0, one launch (start us, length us, event | category | flops | bytes accessed | tf_op | source)
XLA Modules:
  0.0 492.9 jit_solution(1891398441822558677)
XLA Ops:
  5.2 3.6 collective-permute-start.2
  28.1 3.5 collective-permute-done.7
  32.8 5.7 %collective-permute-start.10 = (bf16[96,768]{1,0:T(8,128)(2,1)S(1)}, bf16[96,768]{1,0:T(8,128)(2,1)S(1)}, u32[]{:S(2)}, u32[]{:S(2)}) collective-permute-start(bf16[96,768]{1,0:T(8,128)(2,1)S(1)} %get-tuple-element.92), channel_id=1, source_target_pairs={{0,12},{1,13},{2,14},{3,15},{4,8},{5,9},{6,10},{7,11},{8,4},{9,5},... | collective-permute-start | bytes 442376 | tf_op jit(solution)/shard_map/ppermute | solution.py:740
  51.5 3.5 convolution_convert_fusion
  59.3 3.6 collective-permute-start.11
  64.7 7.1 %all-to-all-start = ((bf16[16,32,384]{2,1,0:T(8,128)(2,1)}), bf16[16,32,384]{2,1,0:T(8,128)(2,1)S(1)}, u32[]{:S(2)}, u32[]{:S(2)}) async-start(bf16[16,32,384]{2,1,0:T(8,128)(2,1)} %slice_select_fusion), calls=%async_computation | async-start | bytes 786432 | tf_op jit(solution)/shard_map/all_to_all | solution.py:902
  71.9 12.9 %all-to-all-done = bf16[16,32,384]{2,1,0:T(8,128)(2,1)S(1)} async-done(((bf16[16,32,384]{2,1,0:T(8,128)(2,1)}), bf16[16,32,384]{2,1,0:T(8,128)(2,1)S(1)}, u32[]{:S(2)}, u32[]{:S(2)}) %all-to-all-start) | async-done | bytes 393248 | tf_op jit(solution)/shard_map/all_to_all | solution.py:902
  85.5 4.3 shard_map.178
  89.8 3.6 all-to-all-start.1
  94.3 6.9 %all-to-all-done.1 = bf16[16,32,128]{2,1,0:T(8,128)(2,1)S(1)} async-done(((bf16[16,32,128]{2,1,0:T(8,128)(2,1)}), bf16[16,32,128]{2,1,0:T(8,128)(2,1)S(1)}, u32[]{:S(2)}, u32[]{:S(2)}) %all-to-all-start.1) | async-done | bytes 131104 | tf_op jit(solution)/shard_map/all_to_all | solution.py:907
  109.0 4.5 multiply_convert_fusion
  113.5 3.5 fusion.3
  124.9 38.3 %shard_map.179 = (bf16[384,768]{1,0:T(8,128)(2,1)}, f32[384,768]{1,0:T(8,128)}, bf16[384,768]{1,0:T(8,128)(2,1)}, bf16[384,2304]{1,0:T(8,128)(2,1)}, bf16[384,76...) custom-call(s32[1]{0:T(128)} %bitcast.33.section_ref, ...), custom_call_target="tpu_custom_call" | custom-call | flops 12683575296 | bytes 40000000 | tf_op jit(solution)/shard_map/pallas_call | solution.py:484
  163.2 22.6 %shard_map.180 = (bf16[48,768]{1,0:T(8,128)(2,1)}, bf16[16,128,768]{2,1,0:T(8,128)(2,1)}, bf16[16,128,768]{2,1,0:T(8,128)(2,1)}) custom-call(s32[1]{0:T(128)} %bitcast.33.section_ref, s32[384,1]{1,0:T(8,128)} %bitcast.256, s32[48,1]{1,0:T(8,128)} %reshape.694.same_ref, f32[2,768]{1,0:T(2,128)} %get-tuple-element.97.gains_ref, ...), custom_call_target="tpu_custom_call" | custom-call | flops 4529848320 | bytes 20000000 | tf_op jit(solution)/shard_map/pallas_call | solution.py:544
  193.5 5.2 %fusion.upward_ref = bf16[96,3072]{1,0:T(8,128)(2,1)} fusion(bf16[96,768]{1,0:T(8,128)(2,1)S(1)} %bitcast.243, f32[96,3072]{1,0:T(8,128)} %get-tuple-element.122, bf16[1,3072,768]{2,1,0:T(8,128)(2,1)} %param.20), kind=kOutput, calls=%fused_computation.4 | convolution fusion | flops 457703424 | bytes 6635520 | tf_op jit(solution)/shard_map/dot_general | solution.py:38
  198.7 7.9 %shard_map.182 = (bf16[16,192,768]{2,1,0:T(8,128)(2,1)}, bf16[16,192,768]{2,1,0:T(8,128)(2,1)}) custom-call(bf16[96,3072]{1,0:T(8,128)(2,1)} %copy-done.8, bf16[96,768]{1,0:T(8,128)(2,1)} %bitcast.244, bf16[96,768]{1,0:T(8,128)(2,1)} %copy-done.21, bf16[96,3072]{1,0:T(8,128)(2,1)} %fusion.upward_ref), custom_call_target="tpu_custom_call" | custom-call | flops 905969664 | bytes 10000000 | tf_op jit(solution)/shard_map/pallas_call | solution.py:614
  206.6 4.1 multiply_reduce_fusion
  210.7 3.6 collective-permute-start.30
  219.7 13.4 %all_to_all.25 = bf16[16,32,128]{2,1,0:T(8,128)(2,1)} all-to-all(bf16[16,32,128]{2,1,0:T(8,128)(2,1)S(1)} %slice_select_fusion.1), channel_id=1, replica_groups=mesh['section'=2,'seq'=16] {'seq'}, dimensions={0} | all-to-all | bytes 262144 | tf_op jit(solution)/shard_map/all_to_all | solution.py:902
  233.1 5.8 %shard_map.181 = bf16[512,384]{1,0:T(8,128)(2,1)} custom-call(s32[512,1]{1,0:T(8,128)} %copy.74.column_ref, s32[1,512]{1,0:T(1,128)} %bitcast.266, bf16[512,384]{1,0:T(8,128)(2,1)} %bitcast.230, bf16[512,128]{1,0:T(8,128)(2,1)} %bitcast.253), custom_call_target="tpu_custom_call" | custom-call | tf_op jit(solution)/shard_map/pallas_call | solution.py:726
  238.9 15.6 %all_to_all.26 = bf16[16,32,384]{2,1,0:T(8,128)(2,1)S(1)} all-to-all(bf16[16,32,384]{2,1,0:T(8,128)(2,1)} %bitcast.233), channel_id=1, replica_groups=mesh['section'=2,'seq'=16] {'seq'}, dimensions={0} | all-to-all | bytes 786432 | tf_op jit(solution)/shard_map/all_to_all | solution.py:907
  258.8 3.5 multiply_reduce_fusion.1
  263.0 5.2 %shard_map.183 = (bf16[16,128,768]{2,1,0:T(8,128)(2,1)}, bf16[16,128,768]{2,1,0:T(8,128)(2,1)}) custom-call(bf16[96,768]{1,0:T(8,128)(2,1)} %copy-done.20, bf16[96,2304]{1,0:T(8,128)(2,1)} %copy-done.11, bf16[96,768]{1,0:T(8,128)(2,1)} %bitcast.248, bf16[96,768]{1,0:T(8,128)(2,1)} %copy-done.19, f32[4,768]{1,0:T(4,128)} %pad_maximum_fusion.7.small_ref), custom_call_target="tpu_custom_call" | custom-call | flops 452984832 | bytes 7000000 | tf_op jit(solution)/shard_map/pallas_call | solution.py:650
  268.2 4.1 collective-permute-start.35
  272.3 4.3 add_convert_fusion
  295.9 52.0 %collective-permute-done.46 = bf16[8,128,768]{2,1,0:T(8,128)(2,1)} collective-permute-done((bf16[8,128,768]{2,1,0:T(8,128)(2,1)}, bf16[8,128,768]{2,1,0:T(8,128)(2,1)}, u32[]{:S(2)}, u32[]{:S(2)}) %collective-permute-start.46) | collective-permute-done | bytes 1572896 | tf_op jit(solution)/shard_map/ppermute | solution.py:795
  360.7 5.6 %collective-permute-done.27 = bf16[96,768]{1,0:T(8,128)(2,1)S(1)} collective-permute-done((bf16[96,768]{1,0:T(8,128)(2,1)S(1)}, bf16[96,768]{1,0:T(8,128)(2,1)S(1)}, u32[]{:S(2)}, u32[]{:S(2)}) %collective-permute-start.27) | collective-permute-done | bytes 147488 | tf_op jit(solution)/shard_map/ppermute | solution.py:740
  394.8 14.6 %collective-permute-done.37 = bf16[4,128,768]{2,1,0:T(8,128)(2,1)} collective-permute-done((bf16[4,128,768]{2,1,0:T(8,128)(2,1)}, bf16[4,128,768]{2,1,0:T(8,128)(2,1)}, u32[]{:S(2)}, u32[]{:S(2)}) %collective-permute-start.37) | collective-permute-done | bytes 786464 | tf_op jit(solution)/shard_map/ppermute | solution.py:795
  423.3 3.6 all-to-all-start.4
  433.0 6.7 %collective-permute-done.43 = bf16[2,192,768]{2,1,0:T(8,128)(2,1)S(1)} collective-permute-done((bf16[2,192,768]{2,1,0:T(8,128)(2,1)}, bf16[2,192,768]{2,1,0:T(8,128)(2,1)S(1)}, u32[]{:S(2)}, u32[]{:S(2)}) %collective-permute-start.43) | collective-permute-done | bytes 589856 | tf_op jit(solution)/shard_map/ppermute | solution.py:795
  441.4 13.3 %collective-permute-done.33 = bf16[2,192,768]{2,1,0:T(8,128)(2,1)S(1)} collective-permute-done((bf16[2,192,768]{2,1,0:T(8,128)(2,1)}, bf16[2,192,768]{2,1,0:T(8,128)(2,1)S(1)}, u32[]{:S(2)}, u32[]{:S(2)}) %collective-permute-start.33) | collective-permute-done | bytes 589856 | tf_op jit(solution)/shard_map/ppermute | solution.py:795
  461.1 13.2 %collective-permute-done.44 = bf16[1,192,768]{2,1,0:T(8,128)(2,1)S(1)} collective-permute-done((bf16[1,192,768]{2,1,0:T(8,128)(2,1)S(1)}, bf16[1,192,768]{2,1,0:T(8,128)(2,1)S(1)}, u32[]{:S(2)}, u32[]{:S(2)}) %collective-permute-start.44) | collective-permute-done | bytes 294944 | tf_op jit(solution)/shard_map/ppermute | solution.py:795
  (383 shorter events, 185.0 us)
Async XLA Ops:
  0.7 19.7 %collective-permute-start.4 = (bf16[192,768]{1,0:T(8,128)(2,1)}, bf16[192,768]{1,0:T(8,128)(2,1)}, u32[]{:S(2)}, u32[]{:S(2)}) collective-permute-start(bf16[192,768]{1,0:T(8,128)(2,1)} %param.14), channel_id=1, source_target_pairs={{0,1},{1,0},{2,3},{3,2},{4,5},{5,4},{6,7},{7,6},{8,9},{9,8},{10,11... | collective-permute-start | bytes 884744 | tf_op jit(solution)/shard_map/ppermute | solution.py:863
  16.4 100.6 %collective-permute-start.15 = (f32[4,768]{1,0:T(4,128)}, f32[4,768]{1,0:T(4,128)}, u32[]{:S(2)}, u32[]{:S(2)}) collective-permute-start(f32[4,768]{1,0:T(4,128)} %pad_maximum_fusion.6), channel_id=1, source_target_pairs={{0,16},{16,0},{1,17},{17,1},{2,18},{18,2},{3,19},{19,3},{4,20},{20... | collective-permute-start | bytes 36872 | tf_op jit(solution)/shard_map/ppermute | solution.py:744
  20.4 104.4 %collective-permute-start.16 = (bf16[768,2304]{1,0:T(8,128)(2,1)}, bf16[768,2304]{1,0:T(8,128)(2,1)}, u32[]{:S(2)}, u32[]{:S(2)}) collective-permute-start(bf16[768,2304]{1,0:T(8,128)(2,1)} %bitcast.221), channel_id=1, source_target_pairs={{16,0},{17,1},{18,2},{19,3},{20,4},{21,5},{22,6},{23,7},{24,8},{25... | collective-permute-start | bytes 10616840 | tf_op jit(solution)/shard_map/ppermute | solution.py:740
  43.7 81.1 %collective-permute-start.18 = (bf16[768,3072]{1,0:T(8,128)(2,1)}, bf16[768,3072]{1,0:T(8,128)(2,1)}, u32[]{:S(2)}, u32[]{:S(2)}) collective-permute-start(bf16[768,3072]{1,0:T(8,128)(2,1)} %bitcast.219), channel_id=1, source_target_pairs={{16,0},{17,1},{18,2},{19,3},{20,4},{21,5},{22,6},{23,7},{24,8},{25... | collective-permute-start | bytes 14155784 | tf_op jit(solution)/shard_map/ppermute | solution.py:740
  45.6 79.3 %collective-permute-start.19 = (bf16[3072,768]{1,0:T(8,128)(2,1)}, bf16[3072,768]{1,0:T(8,128)(2,1)}, u32[]{:S(2)}, u32[]{:S(2)}) collective-permute-start(bf16[3072,768]{1,0:T(8,128)(2,1)} %bitcast.224), channel_id=1, source_target_pairs={{16,0},{17,1},{18,2},{19,3},{20,4},{21,5},{22,6},{23,7},{24,8},{25... | collective-permute-start | bytes 14155784 | tf_op jit(solution)/shard_map/ppermute | solution.py:740
  64.7 20.1 %all-to-all-start = ((bf16[16,32,384]{2,1,0:T(8,128)(2,1)}), bf16[16,32,384]{2,1,0:T(8,128)(2,1)S(1)}, u32[]{:S(2)}, u32[]{:S(2)}) async-start(bf16[16,32,384]{2,1,0:T(8,128)(2,1)} %slice_select_fusion), calls=%async_computation | async-start | bytes 786432 | tf_op jit(solution)/shard_map/all_to_all | solution.py:902
  105.4 19.5 %collective-permute-start.17 = (bf16[768,768]{1,0:T(8,128)(2,1)}, bf16[768,768]{1,0:T(8,128)(2,1)}, u32[]{:S(2)}, u32[]{:S(2)}) collective-permute-start(bf16[768,768]{1,0:T(8,128)(2,1)} %bitcast.226), channel_id=1, source_target_pairs={{16,0},{17,1},{18,2},{19,3},{20,4},{21,5},{22,6},{23,7},{24,8},{25... | collective-permute-start | bytes 3538952 | tf_op jit(solution)/shard_map/ppermute | solution.py:740
  190.1 82.2 %collective-permute-start.40 = (bf16[16,192,768]{2,1,0:T(8,128)(2,1)}, bf16[16,192,768]{2,1,0:T(8,128)(2,1)}, u32[]{:S(2)}, u32[]{:S(2)}) collective-permute-start(bf16[16,192,768]{2,1,0:T(8,128)(2,1)} %get-tuple-element.38), channel_id=1, source_target_pairs={{0,16},{16,0},{1,17},{17,1},{2,18},{18,2},{3,19},{19,3},{4,20},{20... | collective-permute-start | bytes 14155784 | tf_op jit(solution)/shard_map/ppermute | solution.py:744
  210.7 66.4 %collective-permute-start.30 = (bf16[16,192,768]{2,1,0:T(8,128)(2,1)}, bf16[16,192,768]{2,1,0:T(8,128)(2,1)}, u32[]{:S(2)}, u32[]{:S(2)}) collective-permute-start(bf16[16,192,768]{2,1,0:T(8,128)(2,1)} %get-tuple-element.34), channel_id=1, source_target_pairs={{0,16},{1,17},{2,18},{3,19},{4,20},{5,21},{6,22},{7,23},{8,24},{9,... | collective-permute-start | bytes 14155784 | tf_op jit(solution)/shard_map/ppermute | solution.py:740
  255.7 29.1 %collective-permute-start.45 = (bf16[16,128,768]{2,1,0:T(8,128)(2,1)}, bf16[16,128,768]{2,1,0:T(8,128)(2,1)}, u32[]{:S(2)}, u32[]{:S(2)}) collective-permute-start(bf16[16,128,768]{2,1,0:T(8,128)(2,1)} %get-tuple-element.40), channel_id=1, source_target_pairs={{0,16},{16,0},{1,17},{17,1},{2,18},{18,2},{3,19},{19,3},{4,20},{20... | collective-permute-start | bytes 9437192 | tf_op jit(solution)/shard_map/ppermute | solution.py:744
  268.2 20.7 %collective-permute-start.35 = (bf16[16,128,768]{2,1,0:T(8,128)(2,1)}, bf16[16,128,768]{2,1,0:T(8,128)(2,1)}, u32[]{:S(2)}, u32[]{:S(2)}) collective-permute-start(bf16[16,128,768]{2,1,0:T(8,128)(2,1)} %get-tuple-element.36), channel_id=1, source_target_pairs={{0,16},{1,17},{2,18},{3,19},{4,20},{5,21},{6,22},{7,23},{8,24},{9,... | collective-permute-start | bytes 9437192 | tf_op jit(solution)/shard_map/ppermute | solution.py:740
  276.6 91.8 %collective-permute-start.41 = (bf16[8,192,768]{2,1,0:T(8,128)(2,1)}, bf16[8,192,768]{2,1,0:T(8,128)(2,1)}, u32[]{:S(2)}, u32[]{:S(2)}) collective-permute-start(bf16[8,192,768]{2,1,0:T(8,128)(2,1)} %add_convert_fusion), channel_id=1, source_target_pairs={{0,1},{1,0},{2,3},{3,2},{4,5},{5,4},{6,7},{7,6},{8,9},{9,8},{10,11... | collective-permute-start | bytes 7077896 | tf_op jit(solution)/shard_map/ppermute | solution.py:795
  283.4 89.3 %collective-permute-start.31 = (bf16[8,192,768]{2,1,0:T(8,128)(2,1)}, bf16[8,192,768]{2,1,0:T(8,128)(2,1)}, u32[]{:S(2)}, u32[]{:S(2)}) collective-permute-start(bf16[8,192,768]{2,1,0:T(8,128)(2,1)} %constant_dynamic-slice_fusion.2), channel_id=1, source_target_pairs={{0,1},{1,0},{2,3},{3,2},{4,5},{5,4},{6,7},{7,6},{8,9},{9,8},{10,11... | collective-permute-start | bytes 7077896 | tf_op jit(solution)/shard_map/ppermute | solution.py:795
  288.1 59.8 %collective-permute-start.46 = (bf16[8,128,768]{2,1,0:T(8,128)(2,1)}, bf16[8,128,768]{2,1,0:T(8,128)(2,1)}, u32[]{:S(2)}, u32[]{:S(2)}) collective-permute-start(bf16[8,128,768]{2,1,0:T(8,128)(2,1)} %add_convert_fusion.1), channel_id=1, source_target_pairs={{0,1},{1,0},{2,3},{3,2},{4,5},{5,4},{6,7},{7,6},{8,9},{9,8},{10,11... | collective-permute-start | bytes 4718600 | tf_op jit(solution)/shard_map/ppermute | solution.py:795
  291.4 86.9 %collective-permute-start.36 = (bf16[8,128,768]{2,1,0:T(8,128)(2,1)}, bf16[8,128,768]{2,1,0:T(8,128)(2,1)}, u32[]{:S(2)}, u32[]{:S(2)}) collective-permute-start(bf16[8,128,768]{2,1,0:T(8,128)(2,1)} %constant_dynamic-slice_fusion.1), channel_id=1, source_target_pairs={{0,1},{1,0},{2,3},{3,2},{4,5},{5,4},{6,7},{7,6},{8,9},{9,8},{10,11... | collective-permute-start | bytes 4718600 | tf_op jit(solution)/shard_map/ppermute | solution.py:795
  292.8 60.3 %collective-permute-start.25 = (bf16[96,768]{1,0:T(8,128)(2,1)S(1)}, bf16[96,768]{1,0:T(8,128)(2,1)S(1)}, u32[]{:S(2)}, u32[]{:S(2)}) collective-permute-start(bf16[96,768]{1,0:T(8,128)(2,1)S(1)} %add_convert_fusion.14), channel_id=1, source_target_pairs={{0,4},{1,5},{2,6},{3,7},{4,0},{5,1},{6,2},{7,3},{8,12},{9,13},{10,... | collective-permute-start | bytes 442376 | tf_op jit(solution)/shard_map/ppermute | solution.py:740
  353.1 28.5 %collective-permute-start.47 = (bf16[4,128,768]{2,1,0:T(8,128)(2,1)}, bf16[4,128,768]{2,1,0:T(8,128)(2,1)S(1)}, u32[]{:S(2)}, u32[]{:S(2)}) collective-permute-start(bf16[4,128,768]{2,1,0:T(8,128)(2,1)} %add_convert_fusion.4), channel_id=1, source_target_pairs={{0,2},{1,3},{2,0},{3,1},{4,6},{5,7},{6,4},{7,5},{8,10},{9,11},{10,... | collective-permute-start | bytes 2359304 | tf_op jit(solution)/shard_map/ppermute | solution.py:795
  366.3 19.5 %collective-permute-start.28 = (bf16[384,768]{1,0:T(8,128)(2,1)S(1)}, bf16[384,768]{1,0:T(8,128)(2,1)}, u32[]{:S(2)}, u32[]{:S(2)}) collective-permute-start(bf16[384,768]{1,0:T(8,128)(2,1)S(1)} %pad_maximum_fusion.2), channel_id=1, source_target_pairs={{0,16},{1,17},{2,18},{3,19},{4,20},{5,21},{6,22},{7,23},{8,24},{9,... | collective-permute-start | bytes 1769480 | tf_op jit(solution)/shard_map/ppermute | solution.py:740
  371.8 39.0 %collective-permute-start.42 = (bf16[4,192,768]{2,1,0:T(8,128)(2,1)}, bf16[4,192,768]{2,1,0:T(8,128)(2,1)}, u32[]{:S(2)}, u32[]{:S(2)}) collective-permute-start(bf16[4,192,768]{2,1,0:T(8,128)(2,1)} %add_convert_fusion.2), channel_id=1, source_target_pairs={{0,2},{1,3},{2,0},{3,1},{4,6},{5,7},{6,4},{7,5},{8,10},{9,11},{10,... | collective-permute-start | bytes 3538952 | tf_op jit(solution)/shard_map/ppermute | solution.py:795
  375.6 40.0 %collective-permute-start.32 = (bf16[4,192,768]{2,1,0:T(8,128)(2,1)}, bf16[4,192,768]{2,1,0:T(8,128)(2,1)}, u32[]{:S(2)}, u32[]{:S(2)}) collective-permute-start(bf16[4,192,768]{2,1,0:T(8,128)(2,1)} %add_convert_fusion.3), channel_id=1, source_target_pairs={{0,2},{1,3},{2,0},{3,1},{4,6},{5,7},{6,4},{7,5},{8,10},{9,11},{10,... | collective-permute-start | bytes 3538952 | tf_op jit(solution)/shard_map/ppermute | solution.py:795
  380.7 28.7 %collective-permute-start.37 = (bf16[4,128,768]{2,1,0:T(8,128)(2,1)}, bf16[4,128,768]{2,1,0:T(8,128)(2,1)}, u32[]{:S(2)}, u32[]{:S(2)}) collective-permute-start(bf16[4,128,768]{2,1,0:T(8,128)(2,1)} %add_convert_fusion.5), channel_id=1, source_target_pairs={{0,2},{1,3},{2,0},{3,1},{4,6},{5,7},{6,4},{7,5},{8,10},{9,11},{10,... | collective-permute-start | bytes 2359304 | tf_op jit(solution)/shard_map/ppermute | solution.py:795
  387.7 31.3 %collective-permute-start.29 = (bf16[256,768]{1,0:T(8,128)(2,1)}, bf16[256,768]{1,0:T(8,128)(2,1)S(1)}, u32[]{:S(2)}, u32[]{:S(2)}) collective-permute-start(bf16[256,768]{1,0:T(8,128)(2,1)} %fusion.2), channel_id=1, source_target_pairs={{16,0},{17,1},{18,2},{19,3},{20,4},{21,5},{22,6},{23,7},{24,8},{25... | collective-permute-start | bytes 1179656 | tf_op jit(solution)/shard_map/ppermute | solution.py:740
  394.2 32.6 %collective-permute-start.49 = (bf16[1,128,768]{2,1,0:T(8,128)(2,1)S(1)}, bf16[1,128,768]{2,1,0:T(8,128)(2,1)S(1)}, u32[]{:S(2)}, u32[]{:S(2)}) collective-permute-start(bf16[1,128,768]{2,1,0:T(8,128)(2,1)S(1)} %add_convert_fusion.12), channel_id=1, source_target_pairs={{0,8},{1,9},{2,10},{3,11},{4,12},{5,13},{6,14},{7,15},{8,0},{9,1},... | collective-permute-start | bytes 589832 | tf_op jit(solution)/shard_map/ppermute | solution.py:795
  410.8 19.4 %collective-permute-start.38 = (bf16[2,128,768]{2,1,0:T(8,128)(2,1)S(1)}, bf16[2,128,768]{2,1,0:T(8,128)(2,1)}, u32[]{:S(2)}, u32[]{:S(2)}) collective-permute-start(bf16[2,128,768]{2,1,0:T(8,128)(2,1)S(1)} %add_convert_fusion.9), channel_id=1, source_target_pairs={{0,4},{1,5},{2,6},{3,7},{4,0},{5,1},{6,2},{7,3},{8,12},{9,13},{10,... | collective-permute-start | bytes 1179656 | tf_op jit(solution)/shard_map/ppermute | solution.py:795
  413.6 26.2 %collective-permute-start.43 = (bf16[2,192,768]{2,1,0:T(8,128)(2,1)}, bf16[2,192,768]{2,1,0:T(8,128)(2,1)S(1)}, u32[]{:S(2)}, u32[]{:S(2)}) collective-permute-start(bf16[2,192,768]{2,1,0:T(8,128)(2,1)} %add_convert_fusion.6), channel_id=1, source_target_pairs={{0,4},{1,5},{2,6},{3,7},{4,0},{5,1},{6,2},{7,3},{8,12},{9,13},{10,... | collective-permute-start | bytes 1769480 | tf_op jit(solution)/shard_map/ppermute | solution.py:795
  418.0 36.7 %collective-permute-start.33 = (bf16[2,192,768]{2,1,0:T(8,128)(2,1)}, bf16[2,192,768]{2,1,0:T(8,128)(2,1)S(1)}, u32[]{:S(2)}, u32[]{:S(2)}) collective-permute-start(bf16[2,192,768]{2,1,0:T(8,128)(2,1)} %add_convert_fusion.7), channel_id=1, source_target_pairs={{0,4},{1,5},{2,6},{3,7},{4,0},{5,1},{6,2},{7,3},{8,12},{9,13},{10,... | collective-permute-start | bytes 1769480 | tf_op jit(solution)/shard_map/ppermute | solution.py:795
  419.4 62.9 %collective-permute-start.20 = (bf16[3,128,768]{2,1,0:T(8,128)(2,1)S(1)}, bf16[3,128,768]{2,1,0:T(8,128)(2,1)}, u32[]{:S(2)}, u32[]{:S(2)}) collective-permute-start(bf16[3,128,768]{2,1,0:T(8,128)(2,1)S(1)} %bitcast.245), channel_id=1, source_target_pairs={{0,16},{1,17},{2,18},{3,19},{4,20},{5,21},{6,22},{7,23},{8,24},{9,... | collective-permute-start | bytes 1769480 | tf_op jit(solution)/shard_map/ppermute | solution.py:740
  423.3 63.4 %all-to-all-start.4 = ((bf16[16,16,768]{2,1,0:T(8,128)(2,1)}), bf16[16,16,768]{2,1,0:T(8,128)(2,1)S(1)}, u32[]{:S(2)}, u32[]{:S(2)}) async-start(bf16[16,16,768]{2,1,0:T(8,128)(2,1)} %bitcast.57), calls=%async_computation.4 | async-start | bytes 786432 | tf_op jit(solution)/shard_map/all_to_all | solution.py:1033
  426.9 57.9 %collective-permute-start.51 = (bf16[192,768]{1,0:T(8,128)(2,1)}, bf16[192,768]{1,0:T(8,128)(2,1)S(1)}, u32[]{:S(2)}, u32[]{:S(2)}) collective-permute-start(bf16[192,768]{1,0:T(8,128)(2,1)} %get-tuple-element.80), channel_id=1, source_target_pairs={{0,1},{1,0},{2,3},{3,2},{4,5},{5,4},{6,7},{7,6},{8,9},{9,8},{10,11... | collective-permute-start | bytes 884744 | tf_op jit(solution)/shard_map/ppermute | solution.py:1027
  430.2 54.6 %collective-permute-start.52 = (bf16[192,768]{1,0:T(8,128)(2,1)}, bf16[192,768]{1,0:T(8,128)(2,1)S(1)}, u32[]{:S(2)}, u32[]{:S(2)}) collective-permute-start(bf16[192,768]{1,0:T(8,128)(2,1)} %get-tuple-element.82), channel_id=1, source_target_pairs={{0,2},{1,3},{2,0},{3,1},{4,6},{5,7},{6,4},{7,5},{8,10},{9,11},{10,... | collective-permute-start | bytes 884744 | tf_op jit(solution)/shard_map/ppermute | solution.py:1027
  454.7 19.5 %collective-permute-start.44 = (bf16[1,192,768]{2,1,0:T(8,128)(2,1)S(1)}, bf16[1,192,768]{2,1,0:T(8,128)(2,1)S(1)}, u32[]{:S(2)}, u32[]{:S(2)}) collective-permute-start(bf16[1,192,768]{2,1,0:T(8,128)(2,1)S(1)} %add_convert_fusion.10), channel_id=1, source_target_pairs={{0,8},{1,9},{2,10},{3,11},{4,12},{5,13},{6,14},{7,15},{8,0},{9,1},... | collective-permute-start | bytes 884744 | tf_op jit(solution)/shard_map/ppermute | solution.py:795
  456.3 23.7 %collective-permute-start.34 = (bf16[1,192,768]{2,1,0:T(8,128)(2,1)S(1)}, bf16[1,192,768]{2,1,0:T(8,128)(2,1)S(1)}, u32[]{:S(2)}, u32[]{:S(2)}) collective-permute-start(bf16[1,192,768]{2,1,0:T(8,128)(2,1)S(1)} %add_convert_fusion.11), channel_id=1, source_target_pairs={{0,8},{1,9},{2,10},{3,11},{4,12},{5,13},{6,14},{7,15},{8,0},{9,1},... | collective-permute-start | bytes 884744 | tf_op jit(solution)/shard_map/ppermute | solution.py:795
  (97 other events, 798.3 us)

commit v3 on v2

--- a/solution.py
+++ b/solution.py
@@ -20,10 +20,15 @@
 BLOCK = 128
 TILE = 384
 GROUPS = 16
+SPAN = 4
 VMEM = 60 * 1024 * 1024
 
 bf16 = jnp.bfloat16
 f32 = jnp.float32
+
+
+def cost(micros):
+    return pl.CostEstimate(flops=int(micros * 2.2e9), bytes_accessed=1, transcendentals=0)
 
 
 def product(former, latter):
@@ -474,7 +479,6 @@
     hidden_width = own[3].shape[0]
     steps = rows // BLOCK
     shard = hidden_width // GROUPS
-    flops = 2 * rows * width * (4 * width + 2 * hidden_width) + 8 * rows * width * hidden_width
     live = live.astype(jnp.int32)
     sums = jax.ShapeDtypeStruct((GROUPS, shard, width), bf16)
 
@@ -513,9 +517,7 @@
             pltpu.SemaphoreType.DMA((2,)),
         ],
         compiler_params=pltpu.CompilerParams(vmem_limit_bytes=VMEM),
-        cost_estimate=pl.CostEstimate(
-            flops=flops, bytes_accessed=40_000_000, transcendentals=rows * hidden_width
-        ),
+        cost_estimate=cost(38),
     )(
         section,
         ids.reshape(rows, 1),
@@ -536,7 +538,6 @@
     rows, width = normed.shape
     steps = rows // BLOCK
     sums = jax.ShapeDtypeStruct((GROUPS, 2 * (width + VOCAB) // GROUPS, width), bf16)
-    flops = 2 * rows * width * 10 * width
 
     def vmem(*shape, kind=bf16):
         return pltpu.VMEM(shape, kind)
@@ -559,9 +560,7 @@
             pltpu.SemaphoreType.DMA((2,)),
         ],
         compiler_params=pltpu.CompilerParams(vmem_limit_bytes=VMEM),
-        cost_estimate=pl.CostEstimate(
-            flops=flops, bytes_accessed=20_000_000, transcendentals=rows * HEADS * BLOCK
-        ),
+        cost_estimate=cost(23),
     )(
         section,
         ids.reshape(rows, 1),
@@ -581,7 +580,9 @@
     )
 
 
-def global_feed_kernel(count, hidden_ref, branch_ref, normed_two_ref, upward_ref, first, second):
+def global_feed_kernel(
+    count, hidden_ref, branch_ref, normed_two_ref, upward_ref, first, second
+):
     hidden_width, width = hidden_ref.shape[1], branch_ref.shape[1]
     halves = width // TILE
     tile_rows = TILE // (hidden_width // GROUPS)
@@ -608,19 +609,18 @@
             )
 
 
-def global_feed(count, hidden, branch, normed_two, upward):
+def global_feed(count, hidden, branch, normed_two, upward, deps=()):
     hidden_width, width = hidden.shape[1], branch.shape[1]
     sums = jax.ShapeDtypeStruct((GROUPS, hidden_width // GROUPS, width), bf16)
-    return pl.pallas_call(
+    return call(
         partial(global_feed_kernel, count),
-        out_shape=[sums, sums],
-        compiler_params=pltpu.CompilerParams(vmem_limit_bytes=VMEM),
-        cost_estimate=pl.CostEstimate(
-            flops=4 * hidden.shape[0] * hidden_width * width,
-            bytes_accessed=10_000_000,
-            transcendentals=0,
-        ),
-    )(hidden, branch, normed_two, upward)
+        (hidden, branch, normed_two, upward),
+        [WHOLE] * 4,
+        [sums, sums],
+        [WHOLE] * 2,
+        deps=deps,
+        micros=8,
+    )
 
 
 def global_heads_kernel(
@@ -651,9 +651,7 @@
         partial(global_heads_kernel, count),
         out_shape=[sums, sums],
         compiler_params=pltpu.CompilerParams(vmem_limit_bytes=VMEM),
-        cost_estimate=pl.CostEstimate(
-            flops=8 * rows * width * width, bytes_accessed=7_000_000, transcendentals=0
-        ),
+        cost_estimate=cost(6),
     )(normed, grad_mixed, attended, branch, small)
 
 
@@ -705,7 +703,7 @@
         out_ref[:, 2 * PAIR : 3 * PAIR] = value_sum[...].astype(bf16)
 
 
-def global_attention(qkv, owners, grads=None):
+def global_attention(qkv, owners, grads=None, deps=()):
     count = qkv.shape[0]
     column, row = owners[:, None], owners[None, :]
     specs = [
@@ -722,16 +720,444 @@
             out_specs=blocks,
             out_shape=jax.ShapeDtypeStruct((count, PAIR), bf16),
             compiler_params=pltpu.CompilerParams(vmem_limit_bytes=VMEM),
+            cost_estimate=cost(15),
         )(column, row, qkv)
+
+    def body(*refs):
+        global_backward_kernel(*refs[:4], *refs[4 + len(deps) :])
+
     return pl.pallas_call(
-        global_backward_kernel,
+        body,
         grid=(count // BLOCK,),
-        in_specs=specs + [blocks],
+        in_specs=specs + [blocks] + [ANY] * len(deps),
         out_specs=pl.BlockSpec((count, 3 * PAIR), lambda i: (0, 0)),
         out_shape=jax.ShapeDtypeStruct((count, 3 * PAIR), bf16),
         scratch_shapes=[pltpu.VMEM((count, PAIR), f32), pltpu.VMEM((count, PAIR), f32)],
         compiler_params=pltpu.CompilerParams(vmem_limit_bytes=VMEM),
-    )(column, row, qkv, grads)
+        cost_estimate=cost(30),
+    )(column, row, qkv, grads, *deps)
+
+
+def call(kernel, args, specs, out_shape, out_specs, scratch=(), deps=(), micros=1):
+    count = len(args)
+
+    def body(*refs):
+        kernel(*refs[:count], *refs[count + len(deps) :])
+
+    return pl.pallas_call(
+        body,
+        in_specs=list(specs) + [ANY] * len(deps),
+        out_specs=out_specs,
+        out_shape=out_shape,
+        scratch_shapes=list(scratch),
+        compiler_params=pltpu.CompilerParams(vmem_limit_bytes=VMEM),
+        cost_estimate=cost(micros),
+    )(*args, *deps)
+
+
+def shaped(*shape, kind=bf16):
+    return jax.ShapeDtypeStruct(shape, kind)
+
+
+def patch_forward(member, ids, table, pieces, deps=()):
+    rows = ids.shape[0]
+    shard, width = pieces[0].shape
+    span = len(pieces)
+
+    def kernel(member_ref, ids_ref, table_ref, *rest):
+        piece_refs, (embedded_ref, weight_ref, share_ref, low_ref) = rest[:span], rest[span:]
+        member_now = member_ref[0]
+        for k in range(span):
+            start = pl.multiple_of((member_now ^ k) * shard, shard)
+            weight_ref[pl.ds(start, shard), :] = piece_refs[k][...]
+        vocabulary = lax.broadcasted_iota(jnp.int32, (rows, VOCAB), 1)
+        onehot = jnp.where(ids_ref[...] == vocabulary, 1.0, 0.0).astype(bf16)
+        embedded_ref[...] = product(onehot, table_ref[...]).astype(bf16)
+        share = product(embedded_ref[...], weight_ref[...])
+        share_ref[...] = share
+        low_ref[...] = share.astype(bf16)
+
+    return call(
+        kernel,
+        (member, ids.reshape(rows, 1), table, *pieces),
+        [SCALARS] + [WHOLE] * (2 + span),
+        [
+            shaped(rows, width),
+            shaped(span * shard, width),
+            shaped(rows, width, kind=f32),
+            shaped(rows, width),
+        ],
+        [WHOLE] * 4,
+        deps=deps,
+        micros=4,
+    )
+
+
+def split_heads(values, target, start, batches, part, width_of_task):
+    patch_rows = values.shape[0] // batches
+    for m in range(batches):
+        for pair in range(PAIRS):
+            target[m * PAIRS + pair, :, part * PAIR : (part + 1) * PAIR] = values[
+                m * patch_rows : (m + 1) * patch_rows, pair * PAIR : (pair + 1) * PAIR
+            ]
+
+
+def merge_heads(blocks, target, batches, parts):
+    patch_rows = target.shape[0] // batches
+    width = PAIRS * PAIR
+    for t in range(batches * PAIRS):
+        m, pair = t // PAIRS, t % PAIRS
+        first = blocks[0].shape[0]
+        block = blocks[0].at[t] if t < first else blocks[1].at[t - first]
+        for part in range(parts):
+            at = part * width + pair * PAIR
+            target[m * patch_rows : (m + 1) * patch_rows, at : at + PAIR] = block[
+                :, part * PAIR : (part + 1) * PAIR
+            ]
+
+
+def strided(values, target, span, offset):
+    size = values.shape[1] // (4 * span)
+    for k in range(span):
+        parts = [
+            values[:, (group * span + k) * size : (group * span + k + 1) * size]
+            for group in range(4)
+        ]
+        target[k, :, offset : offset + 4 * size] = jnp.concatenate(parts, axis=1)
+
+
+def global_start(batches, own, others, gains, biases, heads_in):
+    rows, width = own.shape
+    patch_rows = rows // batches
+
+    def kernel(own_ref, gains_ref, biases_ref, weight_hbm, *rest):
+        other_refs, (stream_ref, normed_ref, task_ref, share_ref, weight, sem) = (
+            rest[: len(others)],
+            rest[len(others) :],
+        )
+        load = pltpu.make_async_copy(weight_hbm, weight, sem)
+        load.start()
+        stream = own_ref[...]
+        for ref in other_refs:
+            stream = stream + ref[...].astype(f32)
+        stream_ref[...] = stream
+        normed = layer_norm(stream, gains_ref[0:1], biases_ref[0:1]).astype(bf16)
+        normed_ref[...] = normed
+        strided(normed, share_ref, SPAN, 0)
+        load.wait()
+        for part in range(3):
+            mixed = product(normed, weight[:, part * width : (part + 1) * width]).astype(bf16)
+            split_heads(mixed, task_ref, 0, batches, part, width)
+
+    return call(
+        kernel,
+        (own, gains, biases, heads_in, *others),
+        [WHOLE] * 3 + [ANY] + [WHOLE] * len(others),
+        [
+            shaped(rows, width, kind=f32),
+            shaped(rows, width),
+            shaped(batches * PAIRS, patch_rows, 3 * PAIR),
+            shaped(SPAN, rows, width // SPAN),
+        ],
+        [WHOLE] * 4,
+        [pltpu.VMEM(heads_in.shape, bf16), pltpu.SemaphoreType.DMA],
+        micros=5,
+    )
+
+
+def global_feed_forward(batches, blocks, stream, gains, biases, heads_out, expand, contract):
+    rows, width = stream.shape
+    hidden_width = expand.shape[1]
+    n = len(blocks)
+
+    def kernel(stream_ref, gains_ref, biases_ref, out_hbm, expand_hbm, contract_hbm, *rest):
+        block_refs, rest = rest[:n], rest[n:]
+        (attended_ref, middle_ref, normed_two_ref, slope_ref, hidden_ref, sent_ref) = rest[:6]
+        share_ref, w_out, w_expand, w_contract, sems = rest[6:]
+        loads = [
+            pltpu.make_async_copy(out_hbm, w_out, sems.at[0]),
+            pltpu.make_async_copy(expand_hbm, w_expand, sems.at[1]),
+            pltpu.make_async_copy(contract_hbm, w_contract, sems.at[2]),
+        ]
+        for load in loads:
+            load.start()
+        merge_heads(block_refs, attended_ref, batches, 1)
+        loads[0].wait()
+        middle = stream_ref[...] + product(attended_ref[...], w_out[...])
+        middle_ref[...] = middle
+        normed_two_ref[...] = layer_norm(middle, gains_ref[1:2], biases_ref[1:2]).astype(bf16)
+        loads[1].wait()
+
+        @pl.loop(0, hidden_width // width)
+        def _(i):
+            at = pl.ds(pl.multiple_of(i * width, 128), width)
+            hidden, slope = gelu_and_slope(product(normed_two_ref[...], w_expand[:, at]))
+            hidden_ref[:, at] = hidden.astype(bf16)
+            slope_ref[:, at] = slope.astype(bf16)
+
+        loads[2].wait()
+        result = middle_ref[...] + product(hidden_ref[...], w_contract[...])
+        sent_ref[...] = result.astype(bf16)
+        strided(hidden_ref[...], share_ref, SPAN, 0)
+        strided(normed_two_ref[...], share_ref, SPAN, hidden_width // SPAN)
+        strided(attended_ref[...], share_ref, SPAN, (hidden_width + width) // SPAN)
+
+    return call(
+        kernel,
+        (stream, gains, biases, heads_out, expand, contract, *blocks),
+        [WHOLE] * 3 + [ANY] * 3 + [WHOLE] * n,
+        [
+            shaped(rows, width),
+            shaped(rows, width, kind=f32),
+            shaped(rows, width),
+            shaped(rows, hidden_width),
+            shaped(rows, hidden_width),
+            shaped(rows, width),
+            shaped(SPAN, rows, (hidden_width + 2 * width) // SPAN),
+        ],
+        [WHOLE] * 7,
+        [
+            pltpu.VMEM(heads_out.shape, bf16),
+            pltpu.VMEM(expand.shape, bf16),
+            pltpu.VMEM(contract.shape, bf16),
+            pltpu.SemaphoreType.DMA((3,)),
+        ],
+        micros=8,
+    )
+
+
+def global_feed_backward(
+    batches, grad, middle, slope, gains, heads_out, expand, contract, member, share, deps=()
+):
+    rows, width = grad.shape
+    hidden_width = expand.shape[1]
+    patch_rows = rows // batches
+    own = share.shape[2]
+    whole = own + 2 * width + hidden_width
+
+    def kernel(
+        member_ref, grad_ref, middle_ref, slope_ref, gains_ref, share_ref,
+        out_hbm, expand_hbm, contract_hbm,
+        upward_ref, grad_middle_ref, branch_ref, task_ref, small_ref, *rest,
+    ):
+        sent_refs, (w_out, w_expand, w_contract, sems) = rest[:SPAN], rest[SPAN:]
+        loads = [
+            pltpu.make_async_copy(contract_hbm, w_contract, sems.at[2]),
+            pltpu.make_async_copy(expand_hbm, w_expand, sems.at[1]),
+            pltpu.make_async_copy(out_hbm, w_out, sems.at[0]),
+        ]
+        for load in loads:
+            load.start()
+        loads[0].wait()
+
+        @pl.loop(0, hidden_width // width)
+        def _(i):
+            at = pl.ds(pl.multiple_of(i * width, 128), width)
+            grad_hidden = product_transposed(grad_ref[...], w_contract[at, :])
+            upward_ref[:, at] = (grad_hidden * slope_ref[:, at].astype(f32)).astype(bf16)
+
+        loads[1].wait()
+        grad_normed = product_transposed(upward_ref[...], w_expand[...])
+        back, gain, bias = layer_norm_back(middle_ref[...], gains_ref[1:2], grad_normed)
+        grad_middle = back + grad_ref[...].astype(f32)
+        grad_middle_ref[...] = grad_middle
+        branch = grad_middle.astype(bf16)
+        branch_ref[...] = branch
+        small_ref[...] = jnp.concatenate([gain, bias], axis=0)
+        loads[2].wait()
+        attended = product_transposed(branch, w_out[...]).astype(bf16)
+        split_heads(attended, task_ref, 0, batches, 0, width)
+        for k in range(SPAN):
+            sent_refs[k][:, 0:own] = share_ref[member_ref[0] ^ k]
+            sent_refs[k][:, own : own + width] = grad_ref[...]
+            sent_refs[k][:, own + width : own + 2 * width] = branch
+            sent_refs[k][:, own + 2 * width :] = upward_ref[...]
+
+    return call(
+        kernel,
+        (member, grad, middle, slope, gains, share, heads_out, expand, contract),
+        [SCALARS] + [WHOLE] * 5 + [ANY] * 3,
+        [
+            shaped(rows, hidden_width),
+            shaped(rows, width, kind=f32),
+            shaped(rows, width),
+            shaped(batches * PAIRS, patch_rows, PAIR),
+            shaped(2, width, kind=f32),
+        ]
+        + [shaped(rows, whole)] * SPAN,
+        [WHOLE] * (5 + SPAN),
+        [
+            pltpu.VMEM(heads_out.shape, bf16),
+            pltpu.VMEM(expand.shape, bf16),
+            pltpu.VMEM(contract.shape, bf16),
+            pltpu.SemaphoreType.DMA((3,)),
+        ],
+        deps=deps,
+        micros=10,
+    )
+
+
+def global_end(
+    batches, blocks, stream, grad_middle, small, gains, heads_in, member, share, deps=()
+):
+    rows, width = stream.shape
+    n = len(blocks)
+    room = 16
+
+    def kernel(
+        member_ref, stream_ref, grad_middle_ref, small_ref, gains_ref, share_ref, weight_hbm, *rest
+    ):
+        block_refs, rest = rest[:n], rest[n:]
+        mixed_ref, low_ref, all_small_ref = rest[:3]
+        sent_refs, (weight, sem) = rest[3 : 3 + SPAN], rest[3 + SPAN :]
+        load = pltpu.make_async_copy(weight_hbm, weight, sem)
+        load.start()
+        merge_heads(block_refs, mixed_ref, batches, 3)
+        load.wait()
+        grad_normed = product_transposed(mixed_ref[...], weight[...])
+        back, gain, bias = layer_norm_back(stream_ref[...], gains_ref[0:1], grad_normed)
+        low_ref[...] = (back + grad_middle_ref[...]).astype(bf16)
+        smalls = jnp.concatenate([gain, small_ref[0:1], bias, small_ref[1:2]], axis=0)
+        all_small_ref[...] = smalls
+        tail = jnp.concatenate([smalls, jnp.zeros((room - 4, width), f32)], axis=0).astype(bf16)
+        for k in range(SPAN):
+            sent_refs[k][0:rows, 0 : 3 * width] = mixed_ref[...]
+            sent_refs[k][0:rows, 3 * width :] = share_ref[member_ref[0] ^ k]
+            sent_refs[k][rows:, 0:width] = tail
+            sent_refs[k][rows:, width:] = jnp.zeros((room, 2 * width + share_ref.shape[2]), bf16)
+
+    return call(
+        kernel,
+        (member, stream, grad_middle, small, gains, share, heads_in, *blocks),
+        [SCALARS] + [WHOLE] * 5 + [ANY] + [WHOLE] * n,
+        [shaped(rows, 3 * width), shaped(rows, width), shaped(4, width, kind=f32)]
+        + [shaped(rows + room, 3 * width + share.shape[2])] * SPAN,
+        [WHOLE] * (3 + SPAN),
+        [pltpu.VMEM(heads_in.shape, bf16), pltpu.SemaphoreType.DMA],
+        deps=deps,
+        micros=6,
+    )
+
+
+def patch_backward(section, ids, embedded, weight, own, crossed, deps=()):
+    rows, width = embedded.shape
+    block = own[0].shape[0]
+    n = len(own)
+
+    def kernel(section_ref, ids_ref, embedded_ref, weight_ref, crossed_ref, *rest):
+        own_refs, (patch_ref, table_ref, gathered) = rest[:n], rest[n:]
+
+        @pl.when(section_ref[0] == 0)
+        def _():
+            for k in range(n):
+                gathered[k * block : (k + 1) * block, :] = own_refs[k][...]
+
+        @pl.when(section_ref[0] != 0)
+        def _():
+            gathered[...] = crossed_ref[...]
+
+        patch_ref[...] = transposed_product(embedded_ref[...], gathered[...]).astype(bf16)
+        grad_embedded = product_transposed(gathered[...], weight_ref[...]).astype(bf16)
+        vocabulary = lax.broadcasted_iota(jnp.int32, (rows, VOCAB), 1)
+        onehot = jnp.where(ids_ref[...] == vocabulary, 1.0, 0.0).astype(bf16)
+        table_ref[...] = transposed_product(onehot, grad_embedded).astype(bf16)
+
+    return call(
+        kernel,
+        (section, ids.reshape(rows, 1), embedded, weight, crossed, *own),
+        [SCALARS] + [WHOLE] * (4 + n),
+        [shaped(weight.shape[0], width), shaped(VOCAB, width)],
+        [WHOLE] * 2,
+        [pltpu.VMEM((rows, width), bf16)],
+        deps=deps,
+        micros=6,
+    )
+
+
+def leave_by_group(group, buffer, targets, sems):
+    for j in range(len(targets)):
+        for k in range(len(targets)):
+
+            @pl.when((group ^ j) == k)
+            def _(j=j, k=k):
+                pltpu.make_async_copy(buffer.at[j], targets[k], sems.at[k]).start()
+
+    for k in range(len(targets)):
+        pltpu.make_async_copy(buffer.at[0], targets[k], sems.at[k]).wait()
+
+
+def feed_gradients(group, sent, own, width, deps=()):
+    rows = sent[0].shape[0]
+    hidden_width = sent[0].shape[1] - own - 2 * width
+    deep, thin = hidden_width // GROUPS, width // GROUPS
+    chunks = hidden_width // width
+    block = deep + (chunks + 1) * thin
+
+    def kernel(group_ref, *refs):
+        sent_refs, targets = refs[: len(sent)], refs[len(sent) : len(sent) + 4]
+        buffer, sems = refs[len(sent) + 4 :]
+
+        def columns(start, size):
+            return jnp.concatenate([ref[:, start : start + size] for ref in sent_refs], axis=0)
+
+        part = transposed_product(columns(0, 4 * deep), columns(own, width))
+        for j in range(4):
+            buffer[j, 0:deep, :] = part[j * deep : (j + 1) * deep].astype(bf16)
+        left = columns(4 * deep, 4 * thin)
+        for c in range(chunks):
+            part = transposed_product(left, columns(own + (2 + c) * width, width))
+            for j in range(4):
+                at = deep + c * thin
+                buffer[j, at : at + thin, :] = part[j * thin : (j + 1) * thin].astype(bf16)
+        part = transposed_product(columns(4 * (deep + thin), 4 * thin), columns(own + width, width))
+        for j in range(4):
+            buffer[j, block - thin : block, :] = part[j * thin : (j + 1) * thin].astype(bf16)
+        leave_by_group(group_ref[0], buffer, targets, sems)
+
+    return call(
+        kernel,
+        (group, *sent),
+        [SCALARS] + [WHOLE] * len(sent),
+        [shaped(block, width)] * 4,
+        [ANY] * 4,
+        [pltpu.VMEM((4, block, width), bf16), pltpu.SemaphoreType.DMA((4,))],
+        deps=deps,
+        micros=6,
+    )
+
+
+def heads_gradients(group, sent, rows, width, deps=()):
+    thin = width // GROUPS
+    room = sent[0].shape[0] - rows
+    block = 3 * thin + room
+
+    def kernel(group_ref, *refs):
+        sent_refs, targets = refs[: len(sent)], refs[len(sent) : len(sent) + 4]
+        buffer, sems = refs[len(sent) + 4 :]
+
+        def columns(start, size):
+            return jnp.concatenate([ref[0:rows, start : start + size] for ref in sent_refs], axis=0)
+
+        left = columns(3 * width, 4 * thin)
+        for c in range(3):
+            part = transposed_product(left, columns(c * width, width))
+            for j in range(4):
+                buffer[j, c * thin : (c + 1) * thin, :] = part[j * thin : (j + 1) * thin].astype(bf16)
+        small = sum(ref[rows:, 0:width].astype(f32) for ref in sent_refs).astype(bf16)
+        for j in range(4):
+            buffer[j, 3 * thin :, :] = small
+        leave_by_group(group_ref[0], buffer, targets, sems)
+
+    return call(
+        kernel,
+        (group, *sent),
+        [SCALARS] + [WHOLE] * len(sent),
+        [shaped(block, width)] * 4,
+        [ANY] * 4,
+        [pltpu.VMEM((4, block, width), bf16), pltpu.SemaphoreType.DMA((4,))],
+        deps=deps,
+        micros=4,
+    )
 
 
 def section_send(x, origin, target, pairs):
@@ -766,59 +1192,79 @@
     return bits.reshape(whole.shape)
 
 
-def halving_sum(parts):
-    count = lax.axis_size("seq")
-    place = lax.axis_index("seq")
-    section = lax.axis_index("section")
-    depth = count.bit_length() - 1
-    shape = parts[0].shape[1:]
-    held = [(part, 0) for part in parts]
-    half = count
-    for step in range(depth):
-        bits = [step, step]
-        if step < 2:
-            bits[1] = 1 - step
+def added(held, length, kind=bf16, deps=()):
+    count = len(held)
+    shape = held[0][0].shape[1:]
+    if not deps:
+        total = 0.0
+        for array, start, taken in held:
+            term = lax.dynamic_slice(array, (start, 0, 0), (length,) + shape).astype(f32)
+            total = total + (term if taken is None else jnp.where(taken > 0, term, 0.0))
+        return total.astype(kind)
+    size = max(1, length // 4)
+    scalars = [start for _, start, _ in held] + [1 if t is None else t for _, _, t in held]
+    scalars = jnp.stack([jnp.asarray(x, jnp.int32) for x in scalars])
+
+    def kernel(scalar_ref, *refs):
+        total = jnp.zeros((size,) + shape, f32)
+        for j in range(count):
+            term = refs[j][...].astype(f32)
+            if held[j][2] is not None:
+                term = jnp.where(scalar_ref[count + j] > 0, term, 0.0)
+            total = total + term
+        refs[-1][...] = total.astype(kind)
+
+    def spec(j):
+        return pl.BlockSpec((size,) + shape, lambda i, ref: (ref[j] // size + i, 0, 0))
+
+    return pl.pallas_call(
+        kernel,
+        grid_spec=pltpu.PrefetchScalarGridSpec(
+            num_scalar_prefetch=1,
+            grid=(length // size,),
+            in_specs=[spec(j) for j in range(count)] + [ANY] * len(deps),
+            out_specs=pl.BlockSpec((size,) + shape, lambda i, ref: (i, 0, 0)),
+        ),
+        out_shape=jax.ShapeDtypeStruct((length,) + shape, kind),
+        compiler_params=pltpu.CompilerParams(vmem_limit_bytes=VMEM),
+        cost_estimate=cost(4),
+    )(scalars, *[array for array, _, _ in held], *deps)
+
+
+class Halving:
+    def __init__(self, parts):
+        self.count = lax.axis_size("seq")
+        self.depth = self.count.bit_length() - 1
+        self.held = [(part, 0, taken) for part, taken in parts]
+        self.step = 0
+        self.leaving = None
+
+    def send(self, *deps):
+        place, section = lax.axis_index("seq"), lax.axis_index("section")
+        bits = [self.step, self.step]
+        if self.step < 2:
+            bits[1] = 1 - self.step
         mine = jnp.where(section == 0, (place >> bits[0]) & 1, (place >> bits[1]) & 1)
-        half //= 2
-
-        def piece(entry, which):
-            array, start = entry
-            return lax.dynamic_slice(array, (start + which * half, 0, 0), (half,) + shape)
-
-        leaving = sum(piece(entry, 1 - mine).astype(f32) for entry in held).astype(bf16)
-        joint = []
-        for origin in range(2):
-            joint += [
-                (origin * count + i, origin * count + (i ^ (1 << bits[origin])))
-                for i in range(count)
-            ]
-        arrived = lax.ppermute(leaving, ("section", "seq"), joint)
-        held = [(array, start + mine * half) for array, start in held] + [(arrived, 0)]
-    total = sum(
-        lax.dynamic_slice(array, (start, 0, 0), (1,) + shape).astype(f32) for array, start in held
-    )
-    return total[0]
-
-
-def feed_forward(stream, attended, gains, biases, heads_out, expand, contract):
-    middle = stream + product(attended, heads_out)
-    normed_two = layer_norm(middle, gains[1], biases[1]).astype(bf16)
-    hidden, slope = gelu_and_slope(product(normed_two, expand))
-    hidden = hidden.astype(bf16)
-    result = middle + product(hidden, contract)
-    return result, (middle, normed_two, slope, hidden)
-
-
-def feed_backward(grad_result, kept, gains, heads_out, expand, contract):
-    middle, normed_two, slope, hidden = kept
-    branch = grad_result.astype(bf16)
-    grad_upward = (slope * product_transposed(branch, contract)).astype(bf16)
-    grad_normed_two = product_transposed(grad_upward, expand)
-    grad_middle, gain_two, bias_two = layer_norm_back(middle, gains[1:2], grad_normed_two)
-    grad_middle = grad_middle + grad_result
-    attend_branch = grad_middle.astype(bf16)
-    grad_attended = product_transposed(attend_branch, heads_out).astype(bf16)
-    return grad_middle, attend_branch, grad_attended, branch, grad_upward, (gain_two, bias_two)
+        half = self.count >> (self.step + 1)
+        self.leaving = added(
+            [(array, start + (1 - mine) * half, taken) for array, start, taken in self.held],
+            half,
+            deps=deps,
+        )
+        joint = [
+            (origin * self.count + i, origin * self.count + (i ^ (1 << bits[origin])))
+            for origin in range(2)
+            for i in range(self.count)
+        ]
+        arrived = lax.ppermute(self.leaving, ("section", "seq"), joint)
+        self.held = [(array, start + mine * half, taken) for array, start, taken in self.held]
+        self.held.append((arrived, 0, None))
+        self.step += 1
+
+    def total(self):
+        while self.step < self.depth:
+            self.send()
+        return added(self.held, 1, f32)[0]
 
 
 def on_device(
@@ -848,20 +1294,14 @@
     expand, contract = expand_weight[0], contract_weight[0]
     own_table = embed_tables[0]
     straight = [(i, i) for i in range(count)]
-    vocabulary = jnp.arange(VOCAB, dtype=jnp.int32)
-
-    def onehot_of(ids):
-        return (ids[:, None] == vocabulary[None, :]).astype(bf16)
 
     quarters = PATCH // 2
     span = count // quarters
     group, member = place // span, place % span
     shard_rows = patch_weight.shape[0]
-    byte_weight = jnp.zeros((span * shard_rows, width), bf16)
-    byte_weight = lax.dynamic_update_slice(byte_weight, patch_weight, (member * shard_rows, 0))
+    pieces = [patch_weight]
     for k in range(1, span):
-        piece = lax.ppermute(patch_weight, "seq", [(i, i ^ k) for i in range(count)])
-        byte_weight = lax.dynamic_update_slice(byte_weight, piece, ((member ^ k) * shard_rows, 0))
+        pieces.append(lax.ppermute(patch_weight, "seq", [(i, i ^ k) for i in range(count)]))
     other_table = section_swap(own_table)
     global_table = jnp.where(is_global, own_table, other_table)
     local_table = jnp.where(is_global, other_table, own_table)
@@ -873,15 +1313,16 @@
             theirs = lax.ppermute(byte_values, "seq", [(i, i ^ (k * span)) for i in range(count)])
         theirs = theirs.reshape(rows, PATCH)
         byte_ids.append(lax.dynamic_index_in_dim(theirs, which_byte, 1, keepdims=False))
-    patch_onehot = onehot_of(jnp.concatenate(byte_ids))
-    embedded = product(patch_onehot, global_table).astype(bf16)
-    shares = product(embedded, byte_weight)
-    shares = shares + section_send(shares.astype(bf16), 1, 0, straight).astype(f32)
+    byte_ids = jnp.concatenate(byte_ids)
+    embedded, byte_weight, shares, low_shares = patch_forward(
+        member.reshape(1).astype(jnp.int32), byte_ids, global_table, pieces
+    )
+    shares = shares + section_send(low_shares, 1, 0, straight).astype(f32)
     shares = shares.reshape(quarters, rows, width)
-    stream = shares[0]
+    parts = []
     for k in range(1, quarters):
         pairs = [(i, i ^ (k * span)) for i in range(count)]
-        stream = stream + section_send(shares[k].astype(bf16), 0, 0, pairs).astype(f32)
+        parts.append(section_send(shares[k].astype(bf16), 0, 0, pairs))
 
     arrived = [section_send(w, 1, 0, straight) for w in (heads_in, heads_out, expand, contract)]
     other_norms = section_swap(jnp.concatenate([gains, biases]))
@@ -905,32 +1346,29 @@
     def from_tasks(results):
         columns = results.shape[1]
         slots = lax.all_to_all(results.reshape(count, patch_rows, columns), "seq", 0, 0)
-        blocks = slots[:first_tasks]
         if spare_tasks:
-            spare = section_send(slots[:spare_tasks], 1, 0, straight)
-            blocks = jnp.concatenate([blocks, spare])
-        return blocks
-
-    def by_pair(values, parts):
-        split = values.reshape(batches, patch_rows, parts, PAIRS, PAIR)
-        return jnp.transpose(split, (0, 3, 1, 2, 4)).reshape(tasks, patch_rows, parts * PAIR)
-
-    def from_pairs(blocks, parts):
-        split = blocks.reshape(batches, PAIRS, patch_rows, parts, PAIR)
-        return jnp.transpose(split, (0, 2, 3, 1, 4)).reshape(rows, parts * width)
+            return [slots, section_send(slots[:spare_tasks], 1, 0, straight)]
+        return [slots]
 
     task = jnp.minimum(jnp.where(is_global, place, first_tasks + place), tasks - 1)
     task_lengths = lax.dynamic_index_in_dim(item_lengths, task // PAIRS, 0, keepdims=False)
     task_owners = locate(jnp.arange(total_patches, dtype=jnp.int32) * PATCH, task_lengths)[0]
 
-    normed = layer_norm(stream, gains[0], biases[0]).astype(bf16)
-    mixed = product(normed, heads_in).astype(bf16)
-    qkv = to_tasks(by_pair(mixed, 3))
-    attended = from_pairs(from_tasks(global_attention(qkv, task_owners)), 1)
-    global_out, global_kept = feed_forward(
-        stream, attended, gains, biases, heads_out, expand, contract
-    )
-    sent = global_out.astype(bf16).reshape(batches, patch_rows, width)
+    stream, normed, tasks_out, normed_share = global_start(
+        batches, shares[0], parts, gains, biases, heads_in
+    )
+    qkv = to_tasks(tasks_out)
+    attended, middle, normed_two, slope, hidden, sent, feed_share = global_feed_forward(
+        batches,
+        from_tasks(global_attention(qkv, task_owners)),
+        stream,
+        gains,
+        biases,
+        heads_out,
+        expand,
+        contract,
+    )
+    sent = sent.reshape(batches, patch_rows, width)
 
     half = patch_rows // 2
     half_bytes = half * PATCH
@@ -999,40 +1437,6 @@
         is_global, own_sent, jnp.concatenate([other_out, local_out], axis=1)
     )
 
-    near_back = section_send(grad_shifted, 1, 0, straight)
-    edge_back = section_send(grad_shifted[:, :1], 0, 0, backward)
-    grad_sent = jnp.concatenate([grad_shifted[:, 1:], near_back, edge_back], axis=1)
-    grad_sent = grad_sent.reshape(rows, width).astype(f32)
-    grad_middle, attend_branch, grad_attended, branch, grad_upward, twos = feed_backward(
-        grad_sent, global_kept, gains, heads_out, expand, contract
-    )
-    task_grads = to_tasks(by_pair(grad_attended, 1))
-    grad_mixed = from_pairs(from_tasks(global_attention(qkv, task_owners, task_grads)), 3)
-    grad_normed = product_transposed(grad_mixed, heads_in)
-    back, gain_one, bias_one = layer_norm_back(stream, gains[0:1], grad_normed)
-    grad_stream = back + grad_middle
-
-    own_rows = grad_stream.astype(bf16)
-    gathered = [own_rows]
-    for k in range(1, quarters):
-        pairs = [(i, i ^ (k * span)) for i in range(count)]
-        gathered.append(section_send(own_rows, 0, 0, pairs))
-    gathered = jnp.concatenate(gathered)
-    gathered = jnp.where(is_global, gathered, section_send(gathered, 0, 1, straight))
-    patch_share = transposed_product(embedded, gathered).astype(bf16)
-    patch_share = patch_share.reshape(span, shard_rows, width)
-    patch_grads = lax.dynamic_index_in_dim(patch_share, member, 0, keepdims=False).astype(f32)
-    for k in range(1, span):
-        leaving = lax.dynamic_index_in_dim(patch_share, member ^ k, 0, keepdims=False)
-        patch_grads = patch_grads + lax.ppermute(
-            leaving, "seq", [(i, i ^ k) for i in range(count)]
-        ).astype(f32)
-    grad_embedded = product_transposed(gathered, byte_weight).astype(bf16)
-    table_share = transposed_product(patch_onehot, grad_embedded).astype(bf16)
-    table_share = table_share + section_send(table_share, 1, 0, straight)
-    table_parts = lax.all_to_all(table_share.reshape(count, VOCAB // count, width), "seq", 0, 0)
-    global_table_grad = jnp.sum(table_parts.astype(f32), axis=0)
-
     shard = width // count
     room = VOCAB // count
     group_shard, group_room = width // GROUPS, VOCAB // GROUPS
@@ -1055,41 +1459,165 @@
             by_slot(buffer, count, True, pieces[True]),
         )
 
-    def local_sum(entries, pieces):
+    def local_parts(entries, pieces):
         parts = []
         for keep, send in entries:
-            parts += [ordered(keep, pieces), ordered(section_swap(send), pieces)]
-        return halving_sum(parts)
-
-    def global_sum(first, second, pieces):
+            parts += [(ordered(keep, pieces), None), (ordered(section_swap(send), pieces), None)]
+        return parts
+
+    def global_parts(first, second, pieces):
         crossed = section_send(second, 0, 1, straight)
-        return halving_sum([ordered(jnp.where(is_global, first, crossed), pieces)])
-
-    local_feed = local_sum(feed_sums, feed_pieces)
-    local_heads = local_sum(heads_sums, heads_pieces)
-    global_feed_sum = global_sum(
-        *global_feed(count, global_kept[3], branch, global_kept[1], grad_upward), feed_pieces
-    )
-    small = jnp.concatenate([gain_one, twos[0], bias_one, twos[1]])
-    global_heads_sum = global_sum(
-        *global_heads(count, normed, grad_mixed, attended, attend_branch, small), heads_pieces
-    )
-    own_local = jnp.concatenate([local_feed, local_heads])
-    own_global = jnp.concatenate([global_feed_sum, global_heads_sum])
-    crossed = section_swap(jnp.where(is_global, own_local, own_global).astype(bf16)).astype(f32)
-    first = jnp.where(is_global, own_global, crossed)
-    second = jnp.where(is_global, crossed, own_local)
-
-    feed_rows = contract.shape[0] // count
-    contract_grad = first[:feed_rows]
-    expand_grad = jnp.concatenate(
-        [second[k * shard : (k + 1) * shard] for k in range(feed_rows // shard)], axis=1
-    )
-    first, second = first[feed_rows:], second[feed_rows:]
-    in_grad = jnp.concatenate([first[:shard], second[:shard], second[shard : 2 * shard]], axis=1)
-    out_grads = first[shard : 2 * shard]
-    table_grad = jnp.where(is_global, global_table_grad, first[2 * shard : 2 * shard + room])
-    small = lax.dynamic_slice_in_dim(first[2 * shard + room :][:4], place * shard, shard, 1)
+        if count != GROUPS:
+            return [(ordered(jnp.where(is_global, first, crossed), pieces), None)]
+        return [(first, is_global.astype(jnp.int32)), (crossed, section)]
+
+    near_back = section_send(grad_shifted, 1, 0, straight)
+    edge_back = section_send(grad_shifted[:, :1], 0, 0, backward)
+    grad_sent = jnp.concatenate([grad_shifted[:, 1:], near_back, edge_back], axis=1)
+    grad_sent = grad_sent.reshape(rows, width)
+
+    in_plane = span == SPAN and count == GROUPS
+    member_flag = (member % SPAN).reshape(1).astype(jnp.int32)
+    group_flag = group.reshape(1).astype(jnp.int32)
+
+    def plane_send(blocks):
+        return [blocks[0]] + [
+            section_send(blocks[k], 0, 0, [(i, i ^ k) for i in range(count)])
+            for k in range(1, SPAN)
+        ]
+
+    def group_sum(blocks):
+        return sum(
+            [blocks[0].astype(f32)]
+            + [
+                section_send(
+                    blocks[k], 0, 0, [(i, i ^ (k * span)) for i in range(count)]
+                ).astype(f32)
+                for k in range(1, quarters)
+            ]
+        )
+
+    local_feed = Halving(local_parts(feed_sums, feed_pieces))
+    local_heads = Halving(local_parts(heads_sums, heads_pieces))
+    local_feed.send(grad_sent)
+    local_heads.send(grad_sent)
+    grad_upward, grad_middle, attend_branch, task_grads, small, *feed_sent = global_feed_backward(
+        batches,
+        grad_sent,
+        middle,
+        slope,
+        gains,
+        heads_out,
+        expand,
+        contract,
+        member_flag,
+        feed_share,
+        [local_feed.leaving, local_heads.leaving],
+    )
+    if in_plane:
+        feed_sent = plane_send(feed_sent)
+    task_grads = to_tasks(task_grads)
+    local_feed.send()
+    grad_mixed = from_tasks(
+        global_attention(qkv, task_owners, task_grads, [local_feed.leaving])
+    )
+    local_heads.send()
+    local_feed.send()
+    grad_mixed, own_rows, small, *heads_sent = global_end(
+        batches,
+        grad_mixed,
+        stream,
+        grad_middle,
+        small,
+        gains,
+        heads_in,
+        member_flag,
+        normed_share,
+        [local_feed.leaving, local_heads.leaving],
+    )
+    if in_plane:
+        feed_blocks = feed_gradients(group_flag, feed_sent, feed_share.shape[2], width)
+        heads_blocks = heads_gradients(group_flag, plane_send(heads_sent), rows, width)
+
+    gathered = [own_rows]
+    for k in range(1, quarters):
+        pairs = [(i, i ^ (k * span)) for i in range(count)]
+        gathered.append(section_send(own_rows, 0, 0, pairs))
+    crossed = section_send(jnp.concatenate(gathered), 0, 1, straight)
+    local_feed.send()
+    local_heads.send()
+    patch_share, table_share = patch_backward(
+        flag,
+        byte_ids,
+        embedded,
+        byte_weight,
+        gathered,
+        crossed,
+        [local_feed.leaving, local_heads.leaving],
+    )
+    patch_share = patch_share.reshape(span, shard_rows, width)
+    patch_grads = lax.dynamic_index_in_dim(patch_share, member, 0, keepdims=False).astype(f32)
+    for k in range(1, span):
+        leaving = lax.dynamic_index_in_dim(patch_share, member ^ k, 0, keepdims=False)
+        patch_grads = patch_grads + lax.ppermute(
+            leaving, "seq", [(i, i ^ k) for i in range(count)]
+        ).astype(f32)
+    table_share = table_share + section_send(table_share, 1, 0, straight)
+    table_parts = lax.all_to_all(table_share.reshape(count, VOCAB // count, width), "seq", 0, 0)
+    global_table_grad = jnp.sum(table_parts.astype(f32), axis=0)
+
+    def ordered_rows(first, second):
+        feed_rows = contract.shape[0] // count
+        expand_sum = [second[k * shard : (k + 1) * shard] for k in range(feed_rows // shard)]
+        ins = [first[feed_rows :][:shard], second[feed_rows :][:shard]]
+        ins.append(second[feed_rows + shard :][:shard])
+        rest = first[feed_rows + shard :]
+        return (
+            first[:feed_rows],
+            jnp.concatenate(expand_sum, axis=1),
+            jnp.concatenate(ins, axis=1),
+            rest[:shard],
+            rest[shard : shard + room],
+            rest[shard + room : shard + room + 4],
+        )
+
+    own_local = jnp.concatenate([local_feed.total(), local_heads.total()])
+    if in_plane:
+        feed_block, heads_block = group_sum(feed_blocks), group_sum(heads_blocks)
+        deep = contract.shape[0] // count
+        chunks_of = [feed_block[deep + k * shard : deep + (k + 1) * shard] for k in range(5)]
+        ins = [heads_block[k * shard : (k + 1) * shard] for k in range(3)]
+        global_sums = (
+            feed_block[:deep],
+            jnp.concatenate(chunks_of[:4], axis=1),
+            jnp.concatenate(ins, axis=1),
+            chunks_of[4],
+            global_table_grad,
+            heads_block[3 * shard :][:4],
+        )
+        crossed = section_send(own_local.astype(bf16), 0, 1, straight).astype(f32)
+        local_sums = ordered_rows(crossed, own_local)
+    else:
+        feed_sum = Halving(
+            global_parts(
+                *global_feed(count, hidden, grad_sent, normed_two, grad_upward), feed_pieces
+            )
+        )
+        heads_sum = Halving(
+            global_parts(
+                *global_heads(count, normed, grad_mixed, attended, attend_branch, small),
+                heads_pieces,
+            )
+        )
+        own_global = jnp.concatenate([feed_sum.total(), heads_sum.total()])
+        crossed = section_swap(jnp.where(is_global, own_local, own_global).astype(bf16)).astype(f32)
+        global_sums = ordered_rows(own_global, crossed)
+        global_sums = global_sums[:4] + (global_table_grad, global_sums[5])
+        local_sums = ordered_rows(crossed, own_local)
+    contract_grad, expand_grad, in_grad, out_grads, table_grad, small = (
+        jnp.where(is_global, upper, lower) for upper, lower in zip(global_sums, local_sums)
+    )
+    small = lax.dynamic_slice_in_dim(small, place * shard, shard, 1)
     return (
         activations[None],
         table_grad[None],

time: 503 us -> 431 us (0.86)
  waiting for transfers between devices: 150 us -> 89 us
  starting transfers between devices: 98.7 us -> 142 us
  Pallas kernels: 84.1 us -> 126 us
  matrix products: 30.2 us -> 0 us
  blocking collectives: 28.9 us -> 0 us
  other arithmetic: 67.1 us -> 41.2 us
  local copies, waits for them, and re-layouts: 31 us -> 22.6 us
    ppermute x16 -> x8, waiting for transfers between devices: 108 us -> 18.3 us  [send(): arrived = lax.ppermute(self.leaving, ('section', 'seq'), joint)]
    pallas_call x3 -> x11, Pallas kernels: 18.9 us -> 60.8 us  [the longest x8 45.2 us: call(): pl.pallas_call(body, in_specs=list(specs) + [ANY] * len(deps), out_specs=...]
    ppermute x24 -> x35, starting transfers between devices: 53.2 us -> 92.2 us  [section_send(): return lax.ppermute(x, ('section', 'seq'), joint)]
    dot_general x12 -> x0, matrix products: 30.2 us -> none  [the longest x6 14.3 us: product(): return jnp.dot(former, latter, preferred_element_type=f32)]
    all_to_all x2 -> x0, blocking collectives: 28.9 us -> none  [the longest x1 15.6 us: from_tasks(): lax.all_to_all(results.reshape(count, patch_rows, columns), 'seq', 0, 0)]
    convert_element_type x19 -> x7, other arithmetic: 35.1 us -> 12.7 us  [the longest x6 12.7 us: added(): return total.astype(kind)]
    all_to_all x1 -> x2, waiting for transfers between devices: 12.9 us -> 32.8 us  [to_tasks(): landed = lax.all_to_all(slots, 'seq', 0, 0)]
    ppermute x24 -> x35, waiting for transfers between devices: 22.8 us -> 13.4 us  [section_send(): return lax.ppermute(x, ('section', 'seq'), joint)]
  transfers between devices with their start and end apart: 57 -> 61, of which waited for: 18 -> 15; matrix products, arithmetic and copies ran while one was open for 24% -> 14% of each run, Pallas kernels for 5% -> 15%
where the time goes in v3:
time: 431 us; the launch traced here: 423 us
  starting transfers between devices  142 us (33%)
  Pallas kernels  126 us (29%)
  waiting for transfers between devices  89 us (21%)
  other arithmetic  41.2 us (10%)
  local copies, waits for them, and re-layouts  22.6 us (5%)
    ppermute x35, starting transfers between devices, section_send(): return lax.ppermute(x, ('section', 'seq'), joint)  92.2 us
    pallas_call x8, Pallas kernels, call(): pl.pallas_call(body, in_specs=list(specs) + [ANY] * len(deps), out_specs=...  45.2 us
    pallas_call x1, Pallas kernels, local_first(): pl.pallas_call(partial(local_first_kernel, count), in_specs=[SCALARS] + [...  38.3 us
    all_to_all x2, waiting for transfers between devices, to_tasks(): landed = lax.all_to_all(slots, 'seq', 0, 0)  32.8 us
    pallas_call x1, Pallas kernels, local_second(): pl.pallas_call(partial(local_second_kernel, count), in_specs=[SCALARS] +...  22.6 us
    ppermute x8, waiting for transfers between devices, send(): arrived = lax.ppermute(self.leaving, ('section', 'seq'), joint)  18.3 us
    ppermute x35, waiting for transfers between devices, section_send(): return lax.ppermute(x, ('section', 'seq'), joint)  13.4 us
    convert_element_type x6, other arithmetic, added(): return total.astype(kind)  12.7 us
  transfers between devices with their start and end apart: 61, of which 15 were waited for; matrix products, arithmetic and copies ran while one was open for 14% of the time, Pallas kernels for 15%

profile of v3, /device:TPU:0, one launch (start us, length us, event | category | flops | bytes accessed | tf_op | source)
XLA Modules:
  0.0 422.8 jit_solution(13793737748539037109)
XLA Ops:
  0.7 5.1 %collective-permute-start.2 = (s32[3,256]{1,0:T(4,128)}, s32[3,256]{1,0:T(4,128)S(1)}, u32[]{:S(2)}, u32[]{:S(2)}) collective-permute-start(s32[3,256]{1,0:T(4,128)} %param.11), channel_id=1, source_target_pairs={{0,12},{1,13},{2,14},{3,15},{4,8},{5,9},{6,10},{7,11},{8,4},{9,5},... | collective-permute-start | bytes 9224 | tf_op jit(solution)/shard_map/ppermute | solution.py:1313
  18.4 8.7 %collective-permute-done.5.refs_5_ = bf16[192,768]{1,0:T(8,128)(2,1)S(1)} collective-permute-done((bf16[192,768]{1,0:T(8,128)(2,1)}, bf16[192,768]{1,0:T(8,128)(2,1)S(1)}, u32[]{:S(2)}, u32[]{:S(2)}) %collective-permute-start.5) | collective-permute-done | bytes 294944 | tf_op jit(solution)/shard_map/ppermute | solution.py:1304
  37.0 5.5 %collective-permute-start.10 = (bf16[96,768]{1,0:T(8,128)(2,1)S(1)}, bf16[96,768]{1,0:T(8,128)(2,1)S(1)}, u32[]{:S(2)}, u32[]{:S(2)}) collective-permute-start(bf16[96,768]{1,0:T(8,128)(2,1)S(1)} %get-tuple-element.141), channel_id=1, source_target_pairs={{0,12},{1,13},{2,14},{3,15},{4,8},{5,9},{6,10},{7,11},{8,4},{9,5},... | collective-permute-start | bytes 442376 | tf_op jit(solution)/shard_map/ppermute | solution.py:1166
  54.6 4.7 %shard_map.179 = (f32[96,768]{1,0:T(8,128)}, bf16[96,768]{1,0:T(8,128)(2,1)}, bf16[18,32,384]{2,1,0:T(8,128)(2,1)}, bf16[4,96,192]{2,1,0:T(8,128)(2,1)}) custom-call(f32[96,768]{1,0:T(8,128)} %slice.202.refs_0_, f32[2,768]{1,0:T(2,128)} %bitcast.204, f32[2,768]{1,0:T(2,128)} %bitcast.201, bf16[768,2304]{1,0:T(8,128)(2,1)} %bitcast.235, ...), custom_call_target="tpu_custom_call" | custom-call | flops 11000000512 | bytes 1 | tf_op jit(solution)/shard_map/pallas_call | solution.py:747
  60.1 4.0 collective-permute-start.11
  66.7 5.9 %all-to-all-start = ((bf16[16,32,384]{2,1,0:T(8,128)(2,1)}), bf16[16,32,384]{2,1,0:T(8,128)(2,1)S(1)}, u32[]{:S(2)}, u32[]{:S(2)}) async-start(bf16[16,32,384]{2,1,0:T(8,128)(2,1)} %pad_select_fusion), calls=%async_computation | async-start | bytes 786432 | tf_op jit(solution)/shard_map/all_to_all | solution.py:1343
  74.5 11.2 %all-to-all-done = bf16[16,32,384]{2,1,0:T(8,128)(2,1)S(1)} async-done(((bf16[16,32,384]{2,1,0:T(8,128)(2,1)}), bf16[16,32,384]{2,1,0:T(8,128)(2,1)S(1)}, u32[]{:S(2)}, u32[]{:S(2)}) %all-to-all-start) | async-done | bytes 393248 | tf_op jit(solution)/shard_map/all_to_all | solution.py:1343
  86.5 4.4 %shard_map.180 = bf16[512,128]{1,0:T(8,128)(2,1)} custom-call(s32[512,1]{1,0:T(8,128)} %copy.65.column_ref.refs_0_, s32[1,512]{1,0:T(1,128)} %bitcast.209, bf16[512,384]{1,0:T(8,128)(2,1)} %bitcast.184), custom_call_target="tpu_custom_call" | custom-call | flops 32999999488 | bytes 1 | tf_op jit(solution)/shard_map/pallas_call | solution.py:716
  94.5 7.8 %all-to-all-done.1.refs_6_ = bf16[16,32,128]{2,1,0:T(8,128)(2,1)S(1)} async-done(((bf16[16,32,128]{2,1,0:T(8,128)(2,1)}), bf16[16,32,128]{2,1,0:T(8,128)(2,1)S(1)}, u32[]{:S(2)}, u32[]{:S(2)}) %all-to-all-start.1) | async-done | bytes 131104 | tf_op jit(solution)/shard_map/all_to_all | solution.py:1348
  106.7 7.4 %shard_map.181 = (bf16[96,768]{1,0:T(8,128)(2,1)}, f32[96,768]{1,0:T(8,128)}, bf16[96,768]{1,0:T(8,128)(2,1)}, bf16[96,3072]{1,0:T(8,128)(2,1)}, bf16[96,3072]{1...) custom-call(f32[96,768]{1,0:T(8,128)} %get-tuple-element.56.refs_0_.refs_1_, f32[2,768]{1,0:T(2,128)} %bitcast.205, ...), custom_call_target="tpu_custom_call" | custom-call | flops 17600000000 | bytes 1 | tf_op jit(solution)/shard_map/pallas_call | solution.py:747
  125.9 38.3 %shard_map.182 = (bf16[384,768]{1,0:T(8,128)(2,1)}, f32[384,768]{1,0:T(8,128)}, bf16[384,768]{1,0:T(8,128)(2,1)}, bf16[384,2304]{1,0:T(8,128)(2,1)}, bf16[384,76...) custom-call(s32[1]{0:T(128)} %bitcast.33.section_ref.refs_0_, ...), custom_call_target="tpu_custom_call" | custom-call | flops 83599998976 | bytes 1 | tf_op jit(solution)/shard_map/pallas_call | solution.py:488
  164.2 22.6 %shard_map.183 = (bf16[48,768]{1,0:T(8,128)(2,1)}, bf16[16,128,768]{2,1,0:T(8,128)(2,1)}, bf16[16,128,768]{2,1,0:T(8,128)(2,1)}) custom-call(s32[1]{0:T(128)} %bitcast.33.section_ref.refs_0_, s32[384,1]{1,0:T(8,128)} %bitcast.189, s32[48,1]{1,0:T(8,128)} %reshape.814.same_ref, f32[2,768]{1,0:T(2,128)} %get-tuple-element.150.gains_ref, ...), custom_call_target="tpu_custom_call" | custom-call | flops 50600001536 | bytes 1 | tf_op jit(solution)/shard_map/pallas_call | solution.py:545
  195.7 4.7 %shard_map.185.refs_10_ = bf16[8,128,768]{2,1,0:T(8,128)(2,1)} custom-call(s32[4]{0:T(128)} %pad_add_fusion.3.scalar_ref, bf16[16,128,768]{2,1,0:T(8,128)(2,1)} %get-tuple-element.74.refs_0_, bf16[16,128,768]{2,1,0:T(8,128)(2,1)} %collective-permute-done.24.refs_1_, bf16[96,768]{1,0:T(8,128)(2,1)} %bitcast.191), custom_call_target="tpu_custom_call" | custom-call | flops 8800000000 | bytes 1 | tf_op jit(solution)/shard_map/pallas_call | solution.py:1220
  204.5 5.2 %shard_map.184.refs_9_ = bf16[8,192,768]{2,1,0:T(8,128)(2,1)} custom-call(s32[4]{0:T(128)} %pad_add_fusion.3.scalar_ref, bf16[16,192,768]{2,1,0:T(8,128)(2,1)} %get-tuple-element.72.refs_0_, bf16[16,192,768]{2,1,0:T(8,128)(2,1)} %collective-permute-done.23.refs_1_, bf16[96,768]{1,0:T(8,128)(2,1)} %bitcast.192), custom_call_target="tpu_custom_call" | custom-call | flops 8800000000 | bytes 1 | tf_op jit(solution)/shard_map/pallas_call | solution.py:1220
  209.7 11.4 %collective-permute-done.29 = bf16[8,128,768]{2,1,0:T(8,128)(2,1)} collective-permute-done((bf16[8,128,768]{2,1,0:T(8,128)(2,1)}, bf16[8,128,768]{2,1,0:T(8,128)(2,1)}, u32[]{:S(2)}, u32[]{:S(2)}) %collective-permute-start.29) | collective-permute-done | bytes 1572896 | tf_op jit(solution)/shard_map/ppermute | solution.py:1259
  225.0 10.8 %shard_map.186 = (bf16[96,3072]{1,0:T(8,128)(2,1)}, f32[96,768]{1,0:T(8,128)}, bf16[96,768]{1,0:T(8,128)(2,1)}, bf16[18,32,128]{2,1,0:T(8,128)(2,1)}, f32[2,768]...) custom-call(s32[1]{0:T(128)} %bitcast.42.refs_0_, ...), custom_call_target="tpu_custom_call" | custom-call | flops 22000001024 | bytes 1 | tf_op jit(solution)/shard_map/pallas_call | solution.py:747
  237.9 5.8 %collective-permute-done.35 = bf16[4,128,768]{2,1,0:T(8,128)(2,1)} collective-permute-done((bf16[4,128,768]{2,1,0:T(8,128)(2,1)S(1)}, bf16[4,128,768]{2,1,0:T(8,128)(2,1)}, u32[]{:S(2)}, u32[]{:S(2)}) %collective-permute-start.35) | collective-permute-done | bytes 786464 | tf_op jit(solution)/shard_map/ppermute | solution.py:1259
  252.6 3.9 collective-permute-start.51
  259.2 5.5 %all-to-all-start.2 = ((bf16[16,32,128]{2,1,0:T(8,128)(2,1)}), bf16[16,32,128]{2,1,0:T(8,128)(2,1)S(1)}, u32[]{:S(2)}, u32[]{:S(2)}) async-start(bf16[16,32,128]{2,1,0:T(8,128)(2,1)} %pad_select_fusion.1), calls=%async_computation.2 | async-start | bytes 262144 | tf_op jit(solution)/shard_map/all_to_all | solution.py:1343
  269.0 3.9 add_convert_fusion.refs_4_
  274.4 21.6 %all-to-all-done.2 = bf16[16,32,128]{2,1,0:T(8,128)(2,1)S(1)} async-done(((bf16[16,32,128]{2,1,0:T(8,128)(2,1)}), bf16[16,32,128]{2,1,0:T(8,128)(2,1)S(1)}, u32[]{:S(2)}, u32[]{:S(2)}) %all-to-all-start.2) | async-done | bytes 131104 | tf_op jit(solution)/shard_map/all_to_all | solution.py:1343
  296.6 5.8 %shard_map.187 = bf16[512,384]{1,0:T(8,128)(2,1)} custom-call(s32[512,1]{1,0:T(8,128)} %copy.65.column_ref.refs_0_, s32[1,512]{1,0:T(1,128)} %bitcast.210, bf16[512,384]{1,0:T(8,128)(2,1)} %bitcast.185, bf16[512,128]{1,0:T(8,128)(2,1)} %bitcast.194, bf16[4,192,768]{2,1,0:T(8,128)(2,1)} %add_convert_fusion.refs_4_), custom_call_target="tpu_custom_call" | custom-call | flops 65999998976 | bytes 1 | tf_op jit(solution)/shard_map/pallas_call | solution.py:729
  302.3 4.4 %all-to-all-start.3 = ((bf16[16,32,384]{2,1,0:T(8,128)(2,1)}), bf16[16,32,384]{2,1,0:T(8,128)(2,1)S(1)}, u32[]{:S(2)}, u32[]{:S(2)}) async-start(bf16[16,32,384]{2,1,0:T(8,128)(2,1)} %bitcast.186), calls=%async_computation.3 | async-start | bytes 786432 | tf_op jit(solution)/shard_map/all_to_all | solution.py:1348
  306.7 5.4 %shard_map.191 = (bf16[432,768]{1,0:T(8,128)(2,1)}, bf16[432,768]{1,0:T(8,128)(2,1)}, bf16[432,768]{1,0:T(8,128)(2,1)}, bf16[432,768]{1,0:T(8,128)(2,1)}) custom-call(s32[1]{0:T(128)} %bitcast.63.refs_0_, bf16[96,5760]{1,0:T(8,128)(2,1)} %get-tuple-element.91.refs_1_, bf16[96,5760]{1,0:T(8,128)(2,1)} %collective-permute-done.50.refs_2_, ...), custom_call_target="tpu_custom_call" | custom-call | flops 13200000000 | bytes 1 | tf_op jit(solution)/shard_map/pallas_call | solution.py:747
  315.9 4.3 %collective-permute-start.54 = (bf16[432,768]{1,0:T(8,128)(2,1)}, bf16[432,768]{1,0:T(8,128)(2,1)}, u32[]{:S(2)}, u32[]{:S(2)}) collective-permute-start(bf16[432,768]{1,0:T(8,128)(2,1)} %get-tuple-element.97), channel_id=1, source_target_pairs={{0,8},{1,9},{2,10},{3,11},{4,12},{5,13},{6,14},{7,15},{8,0},{9,1},... | collective-permute-start | bytes 1990664 | tf_op jit(solution)/shard_map/ppermute | solution.py:1166
  329.1 6.1 %shard_map.188 = (bf16[96,2304]{1,0:T(8,128)(2,1)}, bf16[96,768]{1,0:T(8,128)(2,1)}, f32[4,768]{1,0:T(4,128)}, bf16[112,2496]{1,0:T(8,128)(2,1)}, bf16[112,2496]...) custom-call(s32[1]{0:T(128)} %bitcast.42.refs_0_, f32[96,768]{1,0:T(8,128)} %get-tuple-element.56.refs_0_.refs_1_, ...), custom_call_target="tpu_custom_call" | custom-call | flops 13200000000 | bytes 1 | tf_op jit(solution)/shard_map/pallas_call | solution.py:747
  348.2 6.3 %collective-permute-start.31 = (bf16[96,768]{1,0:T(8,128)(2,1)}, bf16[96,768]{1,0:T(8,128)(2,1)S(1)}, u32[]{:S(2)}, u32[]{:S(2)}) collective-permute-start(bf16[96,768]{1,0:T(8,128)(2,1)} %get-tuple-element.80.refs_5_), channel_id=1, source_target_pairs={{0,8},{1,9},{2,10},{3,11},{4,12},{5,13},{6,14},{7,15},{8,0},{9,1},... | collective-permute-start | bytes 442376 | tf_op jit(solution)/shard_map/ppermute | solution.py:1166
  354.5 4.5 %collective-permute-start.32 = (bf16[96,768]{1,0:T(8,128)(2,1)}, bf16[96,768]{1,0:T(8,128)(2,1)S(1)}, u32[]{:S(2)}, u32[]{:S(2)}) collective-permute-start(bf16[96,768]{1,0:T(8,128)(2,1)} %get-tuple-element.80.refs_5_), channel_id=1, source_target_pairs={{0,12},{1,13},{2,14},{3,15},{4,8},{5,9},{6,10},{7,11},{8,4},{9,5},... | collective-permute-start | bytes 442376 | tf_op jit(solution)/shard_map/ppermute | solution.py:1166
  371.1 5.4 %collective-permute-start.48 = (bf16[160,768]{1,0:T(8,128)(2,1)}, bf16[160,768]{1,0:T(8,128)(2,1)S(1)}, u32[]{:S(2)}, u32[]{:S(2)}) collective-permute-start(bf16[160,768]{1,0:T(8,128)(2,1)} %get-tuple-element.89), channel_id=1, source_target_pairs={{0,8},{1,9},{2,10},{3,11},{4,12},{5,13},{6,14},{7,15},{8,0},{9,1},... | collective-permute-start | bytes 737288 | tf_op jit(solution)/shard_map/ppermute | solution.py:1166
  381.4 4.1 shard_map.189
  402.2 6.3 %all-to-all-start.4 = ((bf16[16,16,768]{2,1,0:T(8,128)(2,1)}), bf16[16,16,768]{2,1,0:T(8,128)(2,1)}, u32[]{:S(2)}, u32[]{:S(2)}) async-start(bf16[16,16,768]{2,1,0:T(8,128)(2,1)} %bitcast.54), calls=%async_computation.4 | async-start | bytes 786432 | tf_op jit(solution)/shard_map/all_to_all | solution.py:1566
  412.6 8.0 %all-to-all-done.4 = bf16[16,16,768]{2,1,0:T(8,128)(2,1)} async-done(((bf16[16,16,768]{2,1,0:T(8,128)(2,1)}), bf16[16,16,768]{2,1,0:T(8,128)(2,1)}, u32[]{:S(2)}, u32[]{:S(2)}) %all-to-all-start.4) | async-done | bytes 393248 | tf_op jit(solution)/shard_map/all_to_all | solution.py:1566
  (293 shorter events, 161.7 us)
Async XLA Ops:
  11.3 15.7 %collective-permute-start.5 = (bf16[192,768]{1,0:T(8,128)(2,1)}, bf16[192,768]{1,0:T(8,128)(2,1)S(1)}, u32[]{:S(2)}, u32[]{:S(2)}) collective-permute-start(bf16[192,768]{1,0:T(8,128)(2,1)} %refs_3_.1), channel_id=1, source_target_pairs={{0,2},{1,3},{2,0},{3,1},{4,6},{5,7},{6,4},{7,5},{8,10},{9,11},{10,... | collective-permute-start | bytes 884744 | tf_op jit(solution)/shard_map/ppermute | solution.py:1304
  13.5 101.4 %collective-permute-start.15 = (f32[4,768]{1,0:T(4,128)S(1)}, f32[4,768]{1,0:T(4,128)S(1)}, u32[]{:S(2)}, u32[]{:S(2)}) collective-permute-start(f32[4,768]{1,0:T(4,128)S(1)} %pad_maximum_fusion.3), channel_id=1, source_target_pairs={{0,16},{16,0},{1,17},{17,1},{2,18},{18,2},{3,19},{19,3},{4,20},{20... | collective-permute-start | bytes 36872 | tf_op jit(solution)/shard_map/ppermute | solution.py:1170
  15.2 110.8 %collective-permute-start.16 = (bf16[768,2304]{1,0:T(8,128)(2,1)}, bf16[768,2304]{1,0:T(8,128)(2,1)}, u32[]{:S(2)}, u32[]{:S(2)}) collective-permute-start(bf16[768,2304]{1,0:T(8,128)(2,1)} %bitcast.234), channel_id=1, source_target_pairs={{16,0},{17,1},{18,2},{19,3},{20,4},{21,5},{22,6},{23,7},{24,8},{25... | collective-permute-start | bytes 10616840 | tf_op jit(solution)/shard_map/ppermute | solution.py:1166
  48.0 77.9 %collective-permute-start.18 = (bf16[768,3072]{1,0:T(8,128)(2,1)}, bf16[768,3072]{1,0:T(8,128)(2,1)}, u32[]{:S(2)}, u32[]{:S(2)}) collective-permute-start(bf16[768,3072]{1,0:T(8,128)(2,1)} %bitcast.226), channel_id=1, source_target_pairs={{16,0},{17,1},{18,2},{19,3},{20,4},{21,5},{22,6},{23,7},{24,8},{25... | collective-permute-start | bytes 14155784 | tf_op jit(solution)/shard_map/ppermute | solution.py:1166
  49.5 76.4 %collective-permute-start.19 = (bf16[3072,768]{1,0:T(8,128)(2,1)}, bf16[3072,768]{1,0:T(8,128)(2,1)}, u32[]{:S(2)}, u32[]{:S(2)}) collective-permute-start(bf16[3072,768]{1,0:T(8,128)(2,1)} %bitcast.230), channel_id=1, source_target_pairs={{16,0},{17,1},{18,2},{19,3},{20,4},{21,5},{22,6},{23,7},{24,8},{25... | collective-permute-start | bytes 14155784 | tf_op jit(solution)/shard_map/ppermute | solution.py:1166
  66.7 19.0 %all-to-all-start = ((bf16[16,32,384]{2,1,0:T(8,128)(2,1)}), bf16[16,32,384]{2,1,0:T(8,128)(2,1)S(1)}, u32[]{:S(2)}, u32[]{:S(2)}) async-start(bf16[16,32,384]{2,1,0:T(8,128)(2,1)} %pad_select_fusion), calls=%async_computation | async-start | bytes 786432 | tf_op jit(solution)/shard_map/all_to_all | solution.py:1343
  105.4 20.5 %collective-permute-start.17 = (bf16[768,768]{1,0:T(8,128)(2,1)S(1)}, bf16[768,768]{1,0:T(8,128)(2,1)}, u32[]{:S(2)}, u32[]{:S(2)}) collective-permute-start(bf16[768,768]{1,0:T(8,128)(2,1)S(1)} %bitcast.243), channel_id=1, source_target_pairs={{16,0},{17,1},{18,2},{19,3},{20,4},{21,5},{22,6},{23,7},{24,8},{25... | collective-permute-start | bytes 3538952 | tf_op jit(solution)/shard_map/ppermute | solution.py:1166
  186.9 17.6 %collective-permute-start.23 = (bf16[16,192,768]{2,1,0:T(8,128)(2,1)}, bf16[16,192,768]{2,1,0:T(8,128)(2,1)}, u32[]{:S(2)}, u32[]{:S(2)}) collective-permute-start(bf16[16,192,768]{2,1,0:T(8,128)(2,1)} %get-tuple-element.73), channel_id=1, source_target_pairs={{0,16},{16,0},{1,17},{17,1},{2,18},{18,2},{3,19},{19,3},{4,20},{20... | collective-permute-start | bytes 14155784 | tf_op jit(solution)/shard_map/ppermute | solution.py:1170
  200.4 20.7 %collective-permute-start.29 = (bf16[8,128,768]{2,1,0:T(8,128)(2,1)}, bf16[8,128,768]{2,1,0:T(8,128)(2,1)}, u32[]{:S(2)}, u32[]{:S(2)}) collective-permute-start(bf16[8,128,768]{2,1,0:T(8,128)(2,1)} %shard_map.185.refs_10_), channel_id=1, source_target_pairs={{0,1},{1,0},{2,3},{3,2},{4,5},{5,4},{6,7},{7,6},{8,9},{9,8},{10,11... | collective-permute-start | bytes 4718600 | tf_op jit(solution)/shard_map/ppermute | solution.py:1259
  202.4 43.9 %collective-permute-start.20 = (bf16[3,128,768]{2,1,0:T(8,128)(2,1)}, bf16[3,128,768]{2,1,0:T(8,128)(2,1)}, u32[]{:S(2)}, u32[]{:S(2)}) collective-permute-start(bf16[3,128,768]{2,1,0:T(8,128)(2,1)} %bitcast.39), channel_id=1, source_target_pairs={{0,16},{1,17},{2,18},{3,19},{4,20},{5,21},{6,22},{7,23},{8,24},{9,... | collective-permute-start | bytes 1769480 | tf_op jit(solution)/shard_map/ppermute | solution.py:1166
  209.7 59.3 %collective-permute-start.26 = (bf16[8,192,768]{2,1,0:T(8,128)(2,1)}, bf16[8,192,768]{2,1,0:T(8,128)(2,1)S(1)}, u32[]{:S(2)}, u32[]{:S(2)}) collective-permute-start(bf16[8,192,768]{2,1,0:T(8,128)(2,1)} %shard_map.184.refs_9_), channel_id=1, source_target_pairs={{0,1},{1,0},{2,3},{3,2},{4,5},{5,4},{6,7},{7,6},{8,9},{9,8},{10,11... | collective-permute-start | bytes 7077896 | tf_op jit(solution)/shard_map/ppermute | solution.py:1259
  223.0 20.6 %collective-permute-start.35 = (bf16[4,128,768]{2,1,0:T(8,128)(2,1)S(1)}, bf16[4,128,768]{2,1,0:T(8,128)(2,1)}, u32[]{:S(2)}, u32[]{:S(2)}) collective-permute-start(bf16[4,128,768]{2,1,0:T(8,128)(2,1)S(1)} %add_convert_fusion.1.refs_10_), channel_id=1, source_target_pairs={{0,2},{1,3},{2,0},{3,1},{4,6},{5,7},{6,4},{7,5},{8,10},{9,11},{10,... | collective-permute-start | bytes 2359304 | tf_op jit(solution)/shard_map/ppermute | solution.py:1259
  236.6 19.9 %collective-permute-start.25 = (bf16[2,32,128]{2,1,0:T(8,128)(2,1)S(1)}, bf16[2,32,128]{2,1,0:T(8,128)(2,1)S(1)}, u32[]{:S(2)}, u32[]{:S(2)}) collective-permute-start(bf16[2,32,128]{2,1,0:T(8,128)(2,1)S(1)} %slice.177), channel_id=1, source_target_pairs={{0,16},{1,17},{2,18},{3,19},{4,20},{5,21},{6,22},{7,23},{8,24},{9,... | collective-permute-start | bytes 49160 | tf_op jit(solution)/shard_map/ppermute | solution.py:1166
  245.2 19.5 %collective-permute-start.38 = (bf16[2,128,768]{2,1,0:T(8,128)(2,1)S(1)}, bf16[2,128,768]{2,1,0:T(8,128)(2,1)S(1)}, u32[]{:S(2)}, u32[]{:S(2)}) collective-permute-start(bf16[2,128,768]{2,1,0:T(8,128)(2,1)S(1)} %add_convert_fusion.3.refs_10_), channel_id=1, source_target_pairs={{0,4},{1,5},{2,6},{3,7},{4,0},{5,1},{6,2},{7,3},{8,12},{9,13},{10,... | collective-permute-start | bytes 1179656 | tf_op jit(solution)/shard_map/ppermute | solution.py:1259
  249.0 57.8 %collective-permute-start.50 = (bf16[96,5760]{1,0:T(8,128)(2,1)}, bf16[96,5760]{1,0:T(8,128)(2,1)}, u32[]{:S(2)}, u32[]{:S(2)}) collective-permute-start(bf16[96,5760]{1,0:T(8,128)(2,1)} %get-tuple-element.92), channel_id=1, source_target_pairs={{0,1},{1,0},{2,3},{3,2},{4,5},{5,4},{6,7},{7,6},{8,9},{9,8},{10,11... | collective-permute-start | bytes 3317768 | tf_op jit(solution)/shard_map/ppermute | solution.py:1166
  252.6 54.1 %collective-permute-start.51 = (bf16[96,5760]{1,0:T(8,128)(2,1)}, bf16[96,5760]{1,0:T(8,128)(2,1)}, u32[]{:S(2)}, u32[]{:S(2)}) collective-permute-start(bf16[96,5760]{1,0:T(8,128)(2,1)} %get-tuple-element.93), channel_id=1, source_target_pairs={{0,2},{1,3},{2,0},{3,1},{4,6},{5,7},{6,4},{7,5},{8,10},{9,11},{10,... | collective-permute-start | bytes 3317768 | tf_op jit(solution)/shard_map/ppermute | solution.py:1166
  256.6 50.2 %collective-permute-start.52 = (bf16[96,5760]{1,0:T(8,128)(2,1)}, bf16[96,5760]{1,0:T(8,128)(2,1)}, u32[]{:S(2)}, u32[]{:S(2)}) collective-permute-start(bf16[96,5760]{1,0:T(8,128)(2,1)} %get-tuple-element.94), channel_id=1, source_target_pairs={{0,3},{1,2},{2,1},{3,0},{4,7},{5,6},{6,5},{7,4},{8,11},{9,10},{10,... | collective-permute-start | bytes 3317768 | tf_op jit(solution)/shard_map/ppermute | solution.py:1166
  259.2 36.8 %all-to-all-start.2 = ((bf16[16,32,128]{2,1,0:T(8,128)(2,1)}), bf16[16,32,128]{2,1,0:T(8,128)(2,1)S(1)}, u32[]{:S(2)}, u32[]{:S(2)}) async-start(bf16[16,32,128]{2,1,0:T(8,128)(2,1)} %pad_select_fusion.1), calls=%async_computation.2 | async-start | bytes 262144 | tf_op jit(solution)/shard_map/all_to_all | solution.py:1343
  266.1 56.2 %collective-permute-start.39 = (bf16[1,128,768]{2,1,0:T(8,128)(2,1)S(1)}, bf16[1,128,768]{2,1,0:T(8,128)(2,1)}, u32[]{:S(2)}, u32[]{:S(2)}) collective-permute-start(bf16[1,128,768]{2,1,0:T(8,128)(2,1)S(1)} %add_convert_fusion.5), channel_id=1, source_target_pairs={{0,8},{1,9},{2,10},{3,11},{4,12},{5,13},{6,14},{7,15},{8,0},{9,1},... | collective-permute-start | bytes 589832 | tf_op jit(solution)/shard_map/ppermute | solution.py:1259
  272.9 53.0 %collective-permute-start.28 = (bf16[4,192,768]{2,1,0:T(8,128)(2,1)}, bf16[4,192,768]{2,1,0:T(8,128)(2,1)}, u32[]{:S(2)}, u32[]{:S(2)}) collective-permute-start(bf16[4,192,768]{2,1,0:T(8,128)(2,1)} %add_convert_fusion.refs_4_), channel_id=1, source_target_pairs={{0,2},{1,3},{2,0},{3,1},{4,6},{5,7},{6,4},{7,5},{8,10},{9,11},{10,... | collective-permute-start | bytes 3538952 | tf_op jit(solution)/shard_map/ppermute | solution.py:1259
  302.3 22.0 %all-to-all-start.3 = ((bf16[16,32,384]{2,1,0:T(8,128)(2,1)}), bf16[16,32,384]{2,1,0:T(8,128)(2,1)S(1)}, u32[]{:S(2)}, u32[]{:S(2)}) async-start(bf16[16,32,384]{2,1,0:T(8,128)(2,1)} %bitcast.186), calls=%async_computation.3 | async-start | bytes 786432 | tf_op jit(solution)/shard_map/all_to_all | solution.py:1348
  312.1 30.3 %collective-permute-start.53 = (bf16[432,768]{1,0:T(8,128)(2,1)}, bf16[432,768]{1,0:T(8,128)(2,1)}, u32[]{:S(2)}, u32[]{:S(2)}) collective-permute-start(bf16[432,768]{1,0:T(8,128)(2,1)} %get-tuple-element.96), channel_id=1, source_target_pairs={{0,4},{1,5},{2,6},{3,7},{4,0},{5,1},{6,2},{7,3},{8,12},{9,13},{10,... | collective-permute-start | bytes 1990664 | tf_op jit(solution)/shard_map/ppermute | solution.py:1166
  315.9 28.5 %collective-permute-start.54 = (bf16[432,768]{1,0:T(8,128)(2,1)}, bf16[432,768]{1,0:T(8,128)(2,1)}, u32[]{:S(2)}, u32[]{:S(2)}) collective-permute-start(bf16[432,768]{1,0:T(8,128)(2,1)} %get-tuple-element.97), channel_id=1, source_target_pairs={{0,8},{1,9},{2,10},{3,11},{4,12},{5,13},{6,14},{7,15},{8,0},{9,1},... | collective-permute-start | bytes 1990664 | tf_op jit(solution)/shard_map/ppermute | solution.py:1166
  320.3 27.9 %collective-permute-start.55 = (bf16[432,768]{1,0:T(8,128)(2,1)}, bf16[432,768]{1,0:T(8,128)(2,1)}, u32[]{:S(2)}, u32[]{:S(2)}) collective-permute-start(bf16[432,768]{1,0:T(8,128)(2,1)} %get-tuple-element.98), channel_id=1, source_target_pairs={{0,12},{1,13},{2,14},{3,15},{4,8},{5,9},{6,10},{7,11},{8,4},{9,5},... | collective-permute-start | bytes 1990664 | tf_op jit(solution)/shard_map/ppermute | solution.py:1166
  335.2 30.6 %collective-permute-start.44 = (bf16[112,2496]{1,0:T(8,128)(2,1)}, bf16[112,2496]{1,0:T(8,128)(2,1)}, u32[]{:S(2)}, u32[]{:S(2)}) collective-permute-start(bf16[112,2496]{1,0:T(8,128)(2,1)} %get-tuple-element.84), channel_id=1, source_target_pairs={{0,1},{1,0},{2,3},{3,2},{4,5},{5,4},{6,7},{7,6},{8,9},{9,8},{10,11... | collective-permute-start | bytes 1677320 | tf_op jit(solution)/shard_map/ppermute | solution.py:1166
  339.0 26.8 %collective-permute-start.45 = (bf16[112,2496]{1,0:T(8,128)(2,1)}, bf16[112,2496]{1,0:T(8,128)(2,1)}, u32[]{:S(2)}, u32[]{:S(2)}) collective-permute-start(bf16[112,2496]{1,0:T(8,128)(2,1)} %get-tuple-element.85), channel_id=1, source_target_pairs={{0,2},{1,3},{2,0},{3,1},{4,6},{5,7},{6,4},{7,5},{8,10},{9,11},{10,... | collective-permute-start | bytes 1677320 | tf_op jit(solution)/shard_map/ppermute | solution.py:1166
  342.4 23.4 %collective-permute-start.46 = (bf16[112,2496]{1,0:T(8,128)(2,1)}, bf16[112,2496]{1,0:T(8,128)(2,1)}, u32[]{:S(2)}, u32[]{:S(2)}) collective-permute-start(bf16[112,2496]{1,0:T(8,128)(2,1)} %get-tuple-element.86), channel_id=1, source_target_pairs={{0,3},{1,2},{2,1},{3,0},{4,7},{5,6},{6,5},{7,4},{8,11},{9,10},{10,... | collective-permute-start | bytes 1677320 | tf_op jit(solution)/shard_map/ppermute | solution.py:1166
  360.9 18.4 %collective-permute-start.34 = (bf16[2,192,768]{2,1,0:T(8,128)(2,1)}, bf16[2,192,768]{2,1,0:T(8,128)(2,1)S(1)}, u32[]{:S(2)}, u32[]{:S(2)}) collective-permute-start(bf16[2,192,768]{2,1,0:T(8,128)(2,1)} %add_convert_fusion.2.refs_9_), channel_id=1, source_target_pairs={{0,4},{1,5},{2,6},{3,7},{4,0},{5,1},{6,2},{7,3},{8,12},{9,13},{10,... | collective-permute-start | bytes 1769480 | tf_op jit(solution)/shard_map/ppermute | solution.py:1259
  363.7 17.6 %collective-permute-start.33 = (bf16[384,768]{1,0:T(8,128)(2,1)S(1)}, bf16[384,768]{1,0:T(8,128)(2,1)}, u32[]{:S(2)}, u32[]{:S(2)}) collective-permute-start(bf16[384,768]{1,0:T(8,128)(2,1)S(1)} %pad_maximum_fusion), channel_id=1, source_target_pairs={{0,16},{1,17},{2,18},{3,19},{4,20},{5,21},{6,22},{7,23},{8,24},{9,... | collective-permute-start | bytes 1769480 | tf_op jit(solution)/shard_map/ppermute | solution.py:1166
  369.1 19.2 %collective-permute-start.47 = (bf16[160,768]{1,0:T(8,128)(2,1)}, bf16[160,768]{1,0:T(8,128)(2,1)S(1)}, u32[]{:S(2)}, u32[]{:S(2)}) collective-permute-start(bf16[160,768]{1,0:T(8,128)(2,1)} %get-tuple-element.88), channel_id=1, source_target_pairs={{0,4},{1,5},{2,6},{3,7},{4,0},{5,1},{6,2},{7,3},{8,12},{9,13},{10,... | collective-permute-start | bytes 737288 | tf_op jit(solution)/shard_map/ppermute | solution.py:1166
  371.1 18.7 %collective-permute-start.48 = (bf16[160,768]{1,0:T(8,128)(2,1)}, bf16[160,768]{1,0:T(8,128)(2,1)S(1)}, u32[]{:S(2)}, u32[]{:S(2)}) collective-permute-start(bf16[160,768]{1,0:T(8,128)(2,1)} %get-tuple-element.89), channel_id=1, source_target_pairs={{0,8},{1,9},{2,10},{3,11},{4,12},{5,13},{6,14},{7,15},{8,0},{9,1},... | collective-permute-start | bytes 737288 | tf_op jit(solution)/shard_map/ppermute | solution.py:1166
  402.2 18.5 %all-to-all-start.4 = ((bf16[16,16,768]{2,1,0:T(8,128)(2,1)}), bf16[16,16,768]{2,1,0:T(8,128)(2,1)}, u32[]{:S(2)}, u32[]{:S(2)}) async-start(bf16[16,16,768]{2,1,0:T(8,128)(2,1)} %bitcast.54), calls=%async_computation.4 | async-start | bytes 786432 | tf_op jit(solution)/shard_map/all_to_all | solution.py:1566
  (77 other events, 716.6 us)

commit v4 on v3

v4 whole, which is shorter than its diff:
```python
from functools import partial

import jax
import jax.numpy as jnp
from jax import lax
from jax.experimental import pallas as pl
from jax.experimental.pallas import tpu as pltpu
from jax.sharding import PartitionSpec as P

HEADS = 12
HEAD_SIZE = 64
VOCAB = 256
PATCH = 8
ITEMS = 4
PAIRS = HEADS // 2
PAIR = 2 * HEAD_SIZE
SCALE = HEAD_SIZE ** (-0.5)
EPSILON = 1e-05
MASKED = -1e30
BLOCK = 128
TILE = 384
GROUPS = 16
SPAN = 4
VMEM = 60 * 1024 * 1024

bf16 = jnp.bfloat16
f32 = jnp.float32


def cost(micros):
    return pl.CostEstimate(flops=int(micros * 1.1e9), bytes_accessed=1, transcendentals=0)


def product(former, latter):
    return jnp.dot(former, latter, preferred_element_type=f32)


def transposed_product(former, latter):
    return lax.dot_general(former, latter, (((0,), (0,)), ((), ())), preferred_element_type=f32)


def product_transposed(former, latter):
    return lax.dot_general(former, latter, (((1,), (1,)), ((), ())), preferred_element_type=f32)


def normalise(values):
    average = jnp.mean(values, axis=-1, keepdims=True)
    centered = values - average
    inverse_root = lax.rsqrt(jnp.mean(centered * centered, axis=-1, keepdims=True) + EPSILON)
    return centered * inverse_root, inverse_root


def layer_norm(values, gain, bias):
    return normalise(values)[0] * gain + bias


def layer_norm_back(values, gain, grad):
    unit, inverse_root = normalise(values)
    scaled = grad * gain
    grad_values = inverse_root * (
        scaled
        - jnp.mean(scaled, axis=-1, keepdims=True)
        - unit * jnp.mean(scaled * unit, axis=-1, keepdims=True)
    )
    return (
        grad_values,
        jnp.sum(grad * unit, axis=0, keepdims=True),
        jnp.sum(grad, axis=0, keepdims=True),
    )


def locate(positions, lengths_row):
    padded = (lengths_row + PATCH - 1) // PATCH * PATCH
    item_ends = jnp.cumsum(padded)
    starts = item_ends - padded
    inside = (positions[:, None] >= starts[None, :]) & (positions[:, None] < item_ends[None, :])
    offsets = jnp.arange(ITEMS, dtype=jnp.int32)[None, :] - ITEMS
    owners = jnp.sum(jnp.where(inside, offsets, 0), axis=1) + ITEMS
    live_mask = jnp.any(inside & (positions[:, None] < (starts + lengths_row)[None, :]), axis=1)
    return (owners, live_mask)


def slot_of(q, count):
    if count != GROUPS:
        return q
    return (q % SPAN) * (GROUPS // SPAN) + q // SPAN


def store_rows(buffer, value, count, start, columns=slice(None)):
    rows = value.shape[0] // GROUPS
    for q in range(GROUPS):
        buffer[slot_of(q, count), pl.ds(start, rows), columns] = value[
            q * rows : (q + 1) * rows
        ].astype(bf16)


def patch_bias(live_row):
    rows = lax.broadcasted_iota(jnp.int32, (BLOCK, BLOCK), 0)
    columns = lax.broadcasted_iota(jnp.int32, (BLOCK, BLOCK), 1)
    same = (rows // PATCH) == (columns // PATCH)
    allowed = same & (columns <= rows) & ((live_row > 0) | (columns == rows))
    bias = jnp.where(allowed, 0.0, MASKED)
    return jnp.concatenate([bias, bias], axis=0)


def softmax_rows(scores):
    peak = jnp.max(scores, axis=-1, keepdims=True)
    exponents = jnp.exp(scores - peak)
    return exponents * (1.0 / jnp.sum(exponents, axis=-1, keepdims=True))


def lane_masks():
    lanes = lax.broadcasted_iota(jnp.int32, (1, PAIR), 1)
    low = jnp.where(lanes < HEAD_SIZE, 1.0, 0.0)
    return lanes < HEAD_SIZE, low.astype(bf16), (1.0 - low).astype(bf16)


def stacked(values, low, high, scale=1.0):
    return jnp.concatenate([values * (low * scale), values * (high * scale)], axis=0)


def unstacked(values, is_low):
    half = values.shape[0] // 2
    return jnp.where(is_low, values[:half], values[half:])


def pair_probabilities(queries, keys, bias, masks):
    _, low, high = masks
    return softmax_rows(product_transposed(stacked(queries, low, high, SCALE), keys) + bias)


def pair_forward(queries, keys, values, bias, masks):
    probabilities = pair_probabilities(queries, keys, bias, masks)
    return unstacked(product(probabilities.astype(bf16), values), masks[0])


def pair_backward(queries, keys, values, grads, probabilities, masks):
    is_low, low, high = masks
    both = stacked(queries, low, high, SCALE)
    both_grads = stacked(grads, low, high)
    prob_grads = product_transposed(both_grads, values)
    delta = jnp.sum(probabilities * prob_grads, axis=-1, keepdims=True)
    score_grads = (probabilities * (prob_grads - delta)).astype(bf16)
    return (
        unstacked(product(score_grads, keys), is_low) * SCALE,
        transposed_product(score_grads, both),
        transposed_product(probabilities.astype(bf16), both_grads),
    )


def gelu_and_slope(x):
    root = 0.7978845608028654
    cubic = 0.044715
    square = x * x
    bent = jnp.tanh(x * (root + (root * cubic) * square))
    half = 0.5 * (1.0 + bent)
    slope = half + (0.5 * x) * (1.0 - bent * bent) * (root + (3.0 * root * cubic) * square)
    return x * half, slope


def fetch(section, own, arrived, target, sem):
    @pl.when(section == 0)
    def _():
        pltpu.make_async_copy(arrived, target, sem).start()

    @pl.when(section != 0)
    def _():
        pltpu.make_async_copy(own, target, sem).start()


def section_columns(hidden_width, width):
    tables = []
    for names in (
        ("hidden", "branch", "attended", "attend_branch", "normed", "queries", "stream"),
        ("upward", "normed_two", "normed", "keys", "values"),
    ):
        table, start = {}, 0
        for name in names:
            size = hidden_width if start == 0 else width
            table[name] = slice(start, start + size)
            start += size
        tables.append((table, start))
    return tables


SMALL_ROWS = 16


def item_spans(numbers_ref, first, batch):
    spans, start = [], 0
    for k in range(ITEMS):
        length = numbers_ref[first + batch * ITEMS + k]
        stop = start + (length + PATCH - 1) // PATCH * PATCH
        spans.append((start, start + length, stop))
        start = stop
    return spans


def is_live(positions, spans):
    live = jnp.zeros(positions.shape, jnp.bool_)
    for start, live_end, _ in spans:
        live = live | ((positions >= start) & (positions < live_end))
    return live


def owner_of(positions, spans):
    owner = jnp.full(positions.shape, ITEMS, jnp.int32)
    for k, (start, _, stop) in enumerate(spans):
        owner = jnp.where((positions >= start) & (positions < stop), k, owner)
    return owner


def local_kernel(
    patch_rows,
    numbers_ref,
    ids_ref,
    table_ref,
    sent_ref,
    edge_ref,
    near_ref,
    gains_ref,
    biases_ref,
    out_grad_hbm,
    own_in,
    own_out,
    own_expand,
    own_contract,
    new_in,
    new_out,
    new_expand,
    new_contract,
    act_ref,
    grad_shifted_ref,
    grad_edge_ref,
    keep_ref,
    send_ref,
    w_in,
    w_out,
    w_expand,
    w_contract,
    first,
    second,
    out_grad_ref,
    source_ref,
    stream_ref,
    mixed_ref,
    middle_ref,
    slope_ref,
    grad_middle_ref,
    grad_attended_ref,
    grad_stream_ref,
    probability_ref,
    sems,
    out_sems,
):
    section, offset, chunk = numbers_ref[0], numbers_ref[1], numbers_ref[2]
    rows, width = act_ref.shape
    batches = rows // BLOCK
    hidden_width = w_expand.shape[1]
    half = patch_rows // 2
    block_patches = BLOCK // PATCH
    lane = pl.multiple_of(section * (half * PATCH) + chunk * BLOCK, BLOCK)
    base = offset + lane
    grads_in = [
        pltpu.make_async_copy(
            out_grad_hbm.at[m, pl.ds(lane, BLOCK)],
            out_grad_ref.at[m * BLOCK : (m + 1) * BLOCK],
            sems.at[4 + m],
        )
        for m in range(batches)
    ]
    fetch(section, own_in, new_in, w_in, sems.at[0])
    for copy in grads_in:
        copy.start()
    fetch(section, own_out, new_out, w_out, sems.at[1])
    fetch(section, own_expand, new_expand, w_expand, sems.at[2])
    fetch(section, own_contract, new_contract, w_contract, sems.at[3])
    (to_first, first_width), (to_second, second_width) = section_columns(hidden_width, width)
    body = slice(0, rows)
    out_count = [0]

    def leave(from_first, columns, at_rows=body):
        source = first if from_first else second
        sem = out_sems.at[out_count[0]]
        out_count[0] += 1
        part = source.at[at_rows, columns]

        @pl.when(section == (0 if from_first else 1))
        def _():
            pltpu.make_async_copy(part, keep_ref.at[at_rows, columns], sem).start()

        @pl.when(section != (0 if from_first else 1))
        def _():
            pltpu.make_async_copy(part, send_ref.at[at_rows, columns], sem).start()

        return pltpu.make_async_copy(part, keep_ref.at[at_rows, columns], sem)

    blocks = [slice(m * BLOCK, (m + 1) * BLOCK) for m in range(batches)]
    spans = [item_spans(numbers_ref, 3, m) for m in range(batches)]
    column = lax.broadcasted_iota(jnp.int32, (BLOCK, 1), 0)
    row = lax.broadcasted_iota(jnp.int32, (1, BLOCK), 1)
    live_columns = [is_live(base + column, span) for span in spans]
    biases_of = [
        patch_bias(jnp.where(is_live(base + row, span), 1, 0)) for span in spans
    ]
    sent_rows, edge_rows = sent_ref.shape[0], edge_ref.shape[0]
    source_ref[0:sent_rows, :] = sent_ref[...]
    source_ref[sent_rows : sent_rows + edge_rows, :] = edge_ref[...]
    source_ref[sent_rows + edge_rows :, :] = near_ref[...]

    for copy in grads_in:
        copy.wait()
    for m, at in enumerate(blocks):
        vocabulary = lax.broadcasted_iota(jnp.int32, (VOCAB, BLOCK), 0)
        ids = ids_ref[m : m + 1, pl.ds(lane, BLOCK)]
        onehot = jnp.where(ids == vocabulary, 1.0, 0.0).astype(bf16)
        patch = column // PATCH
        place = chunk * block_patches + patch
        start = base + patch * PATCH
        same = owner_of(start, spans[m]) == owner_of(start - PATCH, spans[m])
        inside = jnp.where(place == 0, sent_rows + m, m * patch_rows + place - 1)
        chosen = jnp.where(section == 0, inside, sent_rows + edge_rows + m * half + place)
        chosen = jnp.where(same, chosen, -1)
        columns = lax.broadcasted_iota(jnp.int32, (BLOCK, source_ref.shape[0]), 1)
        spread = jnp.where(columns == chosen, 1.0, 0.0).astype(bf16)
        stream = transposed_product(onehot, table_ref[...]) + product(spread, source_ref[...])
        stream_ref[at, :] = stream
        normed = layer_norm(stream, gains_ref[0:1], biases_ref[0:1]).astype(bf16)
        first[at, to_first["normed"]] = normed
        second[at, to_second["normed"]] = normed
        first[at, to_first["branch"]] = jnp.where(
            live_columns[m], out_grad_ref[at, :].astype(f32), 0.0
        ).astype(bf16)

    pltpu.make_async_copy(own_in, w_in, sems.at[0]).wait()
    for i in range(3 * width // TILE):
        at = slice(i * TILE, (i + 1) * TILE)
        mixed_ref[:, at] = product(first[body, to_first["normed"]], w_in[:, at]).astype(bf16)

    masks = lane_masks()

    def pair_columns(pair, start=0):
        return slice(start + pair * PAIR, start + (pair + 1) * PAIR)

    for m, at in enumerate(blocks):
        for pair in range(PAIRS):
            probabilities = pair_probabilities(
                mixed_ref[at, pair_columns(pair)],
                mixed_ref[at, pair_columns(pair, width)],
                biases_of[m],
                masks,
            )
            probability_ref[m * PAIRS + pair] = probabilities
            attended = product(
                probabilities.astype(bf16), mixed_ref[at, pair_columns(pair, 2 * width)]
            )
            first[at, pair_columns(pair, to_first["attended"].start)] = unstacked(
                attended, masks[0]
            ).astype(bf16)

    pltpu.make_async_copy(own_out, w_out, sems.at[1]).wait()
    for at in blocks:
        middle = stream_ref[at, :] + product(first[at, to_first["attended"]], w_out[...])
        middle_ref[at, :] = middle
        normed_two = layer_norm(middle, gains_ref[1:2], biases_ref[1:2]).astype(bf16)
        second[at, to_second["normed_two"]] = normed_two

    pltpu.make_async_copy(own_expand, w_expand, sems.at[2]).wait()
    for i in range(hidden_width // TILE):
        at = slice(i * TILE, (i + 1) * TILE)
        hidden, slope = gelu_and_slope(
            product(second[body, to_second["normed_two"]], w_expand[:, at])
        )
        first[body, at] = hidden.astype(bf16)
        slope_ref[:, at] = slope.astype(bf16)

    copies = [leave(True, slice(0, to_first["attended"].stop))]
    pltpu.make_async_copy(own_contract, w_contract, sems.at[3]).wait()
    live_column = jnp.concatenate([jnp.where(x, 1, 0) for x in live_columns], axis=0)
    for i in range(width // 256):
        at = slice(i * 256, (i + 1) * 256)
        result = middle_ref[:, at] + product(first[body, to_first["hidden"]], w_contract[:, at])
        act_ref[:, at] = jnp.where(live_column > 0, result, 0.0).astype(bf16)

    for i in range(hidden_width // TILE):
        at = slice(i * TILE, (i + 1) * TILE)
        grad_hidden = product_transposed(first[body, to_first["branch"]], w_contract[at, :])
        second[body, at] = (grad_hidden * slope_ref[:, at].astype(f32)).astype(bf16)

    copies.append(leave(False, slice(0, to_second["normed"].stop)))
    for i in range(width // 256):
        at = slice(i * 256, (i + 1) * 256)
        grad_middle_ref[:, at] = product_transposed(
            second[body, to_second["upward"]], w_expand[at, :]
        )

    gain_two = bias_two = gain_one = bias_one = jnp.zeros((1, width), f32)
    for at in blocks:
        back, gain, bias = layer_norm_back(
            middle_ref[at, :], gains_ref[1:2], grad_middle_ref[at, :]
        )
        grad_middle = back + first[at, to_first["branch"]].astype(f32)
        grad_middle_ref[at, :] = grad_middle
        branch = grad_middle.astype(bf16)
        first[at, to_first["attend_branch"]] = branch
        grad_attended_ref[at, :] = product_transposed(branch, w_out[...]).astype(bf16)
        gain_two, bias_two = gain_two + gain, bias_two + bias

    copies.append(leave(True, slice(to_first["attend_branch"].start, to_first["normed"].stop)))
    for m, at in enumerate(blocks):
        for pair in range(PAIRS):
            parts = pair_backward(
                mixed_ref[at, pair_columns(pair)],
                mixed_ref[at, pair_columns(pair, width)],
                mixed_ref[at, pair_columns(pair, 2 * width)],
                grad_attended_ref[at, pair_columns(pair)],
                probability_ref[m * PAIRS + pair],
                masks,
            )
            first[at, pair_columns(pair, to_first["queries"].start)] = parts[0].astype(bf16)
            second[at, pair_columns(pair, to_second["keys"].start)] = parts[1].astype(bf16)
            second[at, pair_columns(pair, to_second["values"].start)] = parts[2].astype(bf16)

    keys_values = slice(to_second["keys"].start, to_second["values"].stop)
    copies.append(leave(False, keys_values))
    for i in range(width // 256):
        at = slice(i * 256, (i + 1) * 256)
        grad_stream_ref[:, at] = product_transposed(
            first[body, to_first["queries"]], w_in[at, 0:width]
        ) + product_transposed(second[body, keys_values], w_in[at, width:])

    for m, at in enumerate(blocks):
        back, gain, bias = layer_norm_back(
            stream_ref[at, :], gains_ref[0:1], grad_stream_ref[at, :]
        )
        grad_stream = back + grad_middle_ref[at, :]
        first[at, to_first["stream"]] = grad_stream.astype(bf16)
        gain_one, bias_one = gain_one + gain, bias_one + bias
        summed = jnp.sum(grad_stream.reshape(block_patches, PATCH, width), axis=1)
        start = base + PATCH * lax.broadcasted_iota(jnp.int32, (block_patches, 1), 0)
        same = owner_of(start, spans[m]) == owner_of(start - PATCH, spans[m])
        summed = jnp.where(same, summed, 0.0).astype(bf16)
        grad_shifted_ref[m * block_patches : (m + 1) * block_patches, :] = summed
        grad_edge_ref[m : m + 1, :] = summed[0:1]

    grad_edge_ref[batches:, :] = jnp.zeros((SMALL_ROWS - batches, width), bf16)
    small = jnp.concatenate(
        [gain_one, gain_two, bias_one, bias_two, jnp.zeros((SMALL_ROWS - 4, width), f32)], axis=0
    )
    second[rows:, 0:width] = small.astype(bf16)
    copies.append(leave(False, slice(0, width), slice(rows, rows + SMALL_ROWS)))
    copies.append(leave(True, slice(to_first["queries"].start, first_width)))
    for copy in copies:
        copy.wait()


ANY = pl.BlockSpec(memory_space=pl.ANY)
WHOLE = pl.BlockSpec(memory_space=pltpu.VMEM)
SCALARS = pl.BlockSpec(memory_space=pltpu.SMEM)


def vmem(*shape, kind=bf16):
    return pltpu.VMEM(shape, kind)


def local_block(numbers, ids, table, sent, edge, near, gains, biases, out_grad, patch_rows, own, new):
    batches, width = out_grad.shape[0], out_grad.shape[2]
    rows = batches * BLOCK
    hidden_width = own[3].shape[0]
    (_, first_width), (_, second_width) = section_columns(hidden_width, width)
    part = jax.ShapeDtypeStruct((rows + SMALL_ROWS, first_width), bf16)
    return pl.pallas_call(
        partial(local_kernel, patch_rows),
        in_specs=[SCALARS] + [WHOLE] * 7 + [ANY] * 9,
        out_specs=[WHOLE] * 3 + [ANY] * 2,
        out_shape=[
            jax.ShapeDtypeStruct((rows, width), bf16),
            jax.ShapeDtypeStruct((rows // PATCH, width), bf16),
            jax.ShapeDtypeStruct((SMALL_ROWS, width), bf16),
            part,
            part,
        ],
        scratch_shapes=[
            vmem(*own[0].shape),
            vmem(*own[1].shape),
            vmem(*own[2].shape),
            vmem(*own[3].shape),
            vmem(*part.shape),
            vmem(part.shape[0], second_width),
            vmem(rows, width),
            vmem(sent.shape[0] + edge.shape[0] + near.shape[0], width),
            vmem(rows, width, kind=f32),
            vmem(rows, 3 * width),
            vmem(rows, width, kind=f32),
            vmem(rows, hidden_width),
            vmem(rows, width, kind=f32),
            vmem(rows, width),
            vmem(rows, width, kind=f32),
            vmem(batches * PAIRS, 2 * BLOCK, BLOCK, kind=f32),
            pltpu.SemaphoreType.DMA((4 + batches,)),
            pltpu.SemaphoreType.DMA((6,)),
        ],
        compiler_params=pltpu.CompilerParams(vmem_limit_bytes=VMEM),
        cost_estimate=cost(35),
    )(numbers, ids, table, sent, edge, near, gains, biases, out_grad, *own, *new)


def local_gradients(count, numbers, ids, keep, arrived, hidden_width, width, half, deps=()):
    rows = keep.shape[0] - SMALL_ROWS
    (to_first, first_width), (to_second, _) = section_columns(hidden_width, width)
    deep, shard, room = hidden_width // GROUPS, width // GROUPS, VOCAB // GROUPS
    block = deep + 2 * shard + room
    cuts = (slice(0, hidden_width + width), slice(hidden_width + width, first_width))

    def kernel(numbers_ref, ids_ref, keep_ref, new_ref, *rest):
        out_ref, held, smalls, sums, sems, out_sems = rest[len(deps) :]
        copies = []
        for k, cut in enumerate(cuts):
            for j, ref in enumerate((keep_ref, new_ref)):
                copies.append(
                    pltpu.make_async_copy(
                        ref.at[0:rows, cut], held.at[j * rows : (j + 1) * rows, cut], sems.at[2 * k + j]
                    )
                )
        for j, ref in enumerate((keep_ref, new_ref)):
            copies.append(
                pltpu.make_async_copy(
                    ref.at[rows : rows + SMALL_ROWS, 0:width], smalls.at[j], sems.at[4 + j]
                )
            )
        for copy in copies:
            copy.start()
        section_now, chunk = numbers_ref[0], numbers_ref[2]
        tile_shards = TILE // deep

        copies[0].wait()
        copies[1].wait()

        @pl.when(section_now == 0)
        def _():
            for i in range(hidden_width // TILE):
                part = transposed_product(
                    held[:, i * TILE : (i + 1) * TILE], held[:, to_first["branch"]]
                )
                for k in range(tile_shards):
                    slot = slot_of(i * tile_shards + k, count)
                    sums[slot, 0:deep, :] = part[k * deep : (k + 1) * deep].astype(bf16)

        @pl.when(section_now != 0)
        def _():
            for i in range(hidden_width // TILE):
                part = transposed_product(
                    held[:, to_second["normed_two"]], held[:, i * TILE : (i + 1) * TILE]
                )
                chunk, at = i * TILE // width, i * TILE % width
                store_rows(sums, part, count, chunk * shard, slice(at, at + TILE))

        feed = pl.ds(0, deep)
        pltpu.make_async_copy(sums.at[:, feed], out_ref.at[:, feed], out_sems.at[0]).start()
        for copy in copies[2:]:
            copy.wait()

        @pl.when(section_now == 0)
        def _():
            part = transposed_product(
                held[:, to_first["attended"]], held[:, to_first["attend_branch"]]
            )
            store_rows(sums, part, count, deep)
            part = transposed_product(held[:, to_first["normed"]], held[:, to_first["queries"]])
            store_rows(sums, part, count, deep + shard)
            vocabulary = lax.broadcasted_iota(jnp.int32, (VOCAB, BLOCK), 0)
            onehots = []
            for where in (section_now, 1 - section_now):
                lane = pl.multiple_of(where * half + chunk * BLOCK, BLOCK)
                for m in range(rows // BLOCK):
                    ids_row = ids_ref[m : m + 1, pl.ds(lane, BLOCK)]
                    onehots.append(jnp.where(ids_row == vocabulary, 1.0, 0.0).astype(bf16))
            part = product(jnp.concatenate(onehots, axis=1), held[:, to_first["stream"]])
            store_rows(sums, part, count, deep + 2 * shard)

        @pl.when(section_now != 0)
        def _():
            for k, name in enumerate(("keys", "values")):
                part = transposed_product(held[:, to_second["normed"]], held[:, to_second[name]])
                store_rows(sums, part, count, deep + k * shard)
            small = (smalls[0].astype(f32) + smalls[1].astype(f32)).astype(bf16)
            for q in range(GROUPS):
                sums[q, deep + 2 * shard :, :] = small

        heads = pl.ds(deep, block - deep)
        pltpu.make_async_copy(sums.at[:, heads], out_ref.at[:, heads], out_sems.at[1]).start()
        pltpu.make_async_copy(sums.at[:, feed], out_ref.at[:, feed], out_sems.at[0]).wait()
        pltpu.make_async_copy(sums.at[:, heads], out_ref.at[:, heads], out_sems.at[1]).wait()

    return pl.pallas_call(
        kernel,
        in_specs=[SCALARS, WHOLE, ANY, ANY] + [ANY] * len(deps),
        out_specs=ANY,
        out_shape=jax.ShapeDtypeStruct((GROUPS, block, width), bf16),
        scratch_shapes=[
            vmem(2 * rows, first_width),
            vmem(2, SMALL_ROWS, width),
            vmem(GROUPS, block, width),
            pltpu.SemaphoreType.DMA((6,)),
            pltpu.SemaphoreType.DMA((2,)),
        ],
        compiler_params=pltpu.CompilerParams(vmem_limit_bytes=VMEM),
        cost_estimate=cost(12),
    )(numbers, ids, keep, arrived, *deps)


def global_sums_kernel(
    count, hidden_ref, branch_ref, normed_two_ref, upward_ref, normed_ref, grad_mixed_ref,
    attended_ref, attend_branch_ref, small_ref, first, second,
):
    hidden_width, width = hidden_ref.shape[1], branch_ref.shape[1]
    deep, shard, room = hidden_width // GROUPS, width // GROUPS, VOCAB // GROUPS
    tile_shards = TILE // deep
    for i in range(hidden_width // TILE):
        columns = slice(i * TILE, (i + 1) * TILE)
        part = transposed_product(hidden_ref[:, columns], branch_ref[...])
        for k in range(tile_shards):
            slot = slot_of(i * tile_shards + k, count)
            first[slot, 0:deep, :] = part[k * deep : (k + 1) * deep].astype(bf16)
        part = transposed_product(normed_two_ref[...], upward_ref[:, columns])
        chunk, at = i * TILE // width, i * TILE % width
        store_rows(second, part, count, chunk * shard, slice(at, at + TILE))
    part = transposed_product(attended_ref[...], attend_branch_ref[...])
    store_rows(first, part, count, deep)
    targets = ((first, deep + shard), (second, deep), (second, deep + shard))
    for chunk, (target, start) in enumerate(targets):
        columns = slice(chunk * width, (chunk + 1) * width)
        part = transposed_product(normed_ref[...], grad_mixed_ref[:, columns])
        store_rows(target, part, count, start)
    small = jnp.concatenate([small_ref[...], jnp.zeros((room - 4, width), f32)], axis=0)
    for q in range(GROUPS):
        first[q, deep + 2 * shard :, :] = jnp.zeros((room, width), bf16)
        second[q, deep + 2 * shard :, :] = small.astype(bf16)


def global_sums_of(count, *arrays):
    hidden, branch = arrays[:2]
    hidden_width, width = hidden.shape[1], branch.shape[1]
    block = hidden_width // GROUPS + (2 * width + VOCAB) // GROUPS
    sums = jax.ShapeDtypeStruct((GROUPS, block, width), bf16)
    return pl.pallas_call(
        partial(global_sums_kernel, count),
        out_shape=[sums, sums],
        compiler_params=pltpu.CompilerParams(vmem_limit_bytes=VMEM),
        cost_estimate=cost(14),
    )(*arrays)


def causal_bias(start, owner_column, owner_row):
    shape = (BLOCK, owner_row.shape[1])
    rows = lax.broadcasted_iota(jnp.int32, shape, 0) + start
    columns = lax.broadcasted_iota(jnp.int32, shape, 1)
    bias = jnp.where((columns <= rows) & (owner_column == owner_row), 0.0, MASKED)
    return jnp.concatenate([bias, bias], axis=0)


def global_forward_kernel(column_ref, row_ref, qkv_ref, out_ref):
    start = pl.multiple_of(pl.program_id(0) * BLOCK, BLOCK)
    bias = causal_bias(start, column_ref[...], row_ref[...])
    out_ref[...] = pair_forward(
        qkv_ref[pl.ds(start, BLOCK), 0:PAIR],
        qkv_ref[:, PAIR : 2 * PAIR],
        qkv_ref[:, 2 * PAIR : 3 * PAIR],
        bias,
        lane_masks(),
    ).astype(bf16)


def global_backward_kernel(column_ref, row_ref, qkv_ref, grad_ref, out_ref, key_sum, value_sum):
    step = pl.program_id(0)
    start = pl.multiple_of(step * BLOCK, BLOCK)
    bias = causal_bias(start, column_ref[...], row_ref[...])

    @pl.when(step == 0)
    def _():
        key_sum[...] = jnp.zeros_like(key_sum)
        value_sum[...] = jnp.zeros_like(value_sum)

    queries, keys = qkv_ref[pl.ds(start, BLOCK), 0:PAIR], qkv_ref[:, PAIR : 2 * PAIR]
    masks = lane_masks()
    grad_queries, grad_keys, grad_values = pair_backward(
        queries,
        keys,
        qkv_ref[:, 2 * PAIR : 3 * PAIR],
        grad_ref[...],
        pair_probabilities(queries, keys, bias, masks),
        masks,
    )
    out_ref[pl.ds(start, BLOCK), 0:PAIR] = grad_queries.astype(bf16)
    key_sum[...] += grad_keys
    value_sum[...] += grad_values

    @pl.when(step == pl.num_programs(0) - 1)
    def _():
        out_ref[:, PAIR : 2 * PAIR] = key_sum[...].astype(bf16)
        out_ref[:, 2 * PAIR : 3 * PAIR] = value_sum[...].astype(bf16)


def global_attention(qkv, owners, grads=None, deps=()):
    count = qkv.shape[0]
    column, row = owners[:, None], owners[None, :]
    specs = [
        pl.BlockSpec((BLOCK, 1), lambda i: (i, 0)),
        pl.BlockSpec((1, count), lambda i: (0, 0)),
        pl.BlockSpec((count, 3 * PAIR), lambda i: (0, 0)),
    ]
    blocks = pl.BlockSpec((BLOCK, PAIR), lambda i: (i, 0))
    if grads is None:
        return pl.pallas_call(
            global_forward_kernel,
            grid=(count // BLOCK,),
            in_specs=specs,
            out_specs=blocks,
            out_shape=jax.ShapeDtypeStruct((count, PAIR), bf16),
            compiler_params=pltpu.CompilerParams(vmem_limit_bytes=VMEM),
            cost_estimate=cost(15),
        )(column, row, qkv)

    def body(*refs):
        global_backward_kernel(*refs[:4], *refs[4 + len(deps) :])

    return pl.pallas_call(
        body,
        grid=(count // BLOCK,),
        in_specs=specs + [blocks] + [ANY] * len(deps),
        out_specs=pl.BlockSpec((count, 3 * PAIR), lambda i: (0, 0)),
        out_shape=jax.ShapeDtypeStruct((count, 3 * PAIR), bf16),
        scratch_shapes=[pltpu.VMEM((count, PAIR), f32), pltpu.VMEM((count, PAIR), f32)],
        compiler_params=pltpu.CompilerParams(vmem_limit_bytes=VMEM),
        cost_estimate=cost(30),
    )(column, row, qkv, grads, *deps)


def call(kernel, args, specs, out_shape, out_specs, scratch=(), deps=(), micros=1):
    count = len(args)

    def body(*refs):
        kernel(*refs[:count], *refs[count + len(deps) :])

    return pl.pallas_call(
        body,
        in_specs=list(specs) + [ANY] * len(deps),
        out_specs=out_specs,
        out_shape=out_shape,
        scratch_shapes=list(scratch),
        compiler_params=pltpu.CompilerParams(vmem_limit_bytes=VMEM),
        cost_estimate=cost(micros),
    )(*args, *deps)


def shaped(*shape, kind=bf16):
    return jax.ShapeDtypeStruct(shape, kind)


def patch_forward(member, ids, table, pieces, deps=()):
    rows = ids.shape[0]
    shard, width = pieces[0].shape
    span = len(pieces)

    def kernel(member_ref, ids_ref, table_ref, *rest):
        piece_refs, (embedded_ref, weight_ref, share_ref, low_ref) = rest[:span], rest[span:]
        member_now = member_ref[0]
        for k in range(span):
            start = pl.multiple_of((member_now ^ k) * shard, shard)
            weight_ref[pl.ds(start, shard), :] = piece_refs[k][...]
        vocabulary = lax.broadcasted_iota(jnp.int32, (rows, VOCAB), 1)
        onehot = jnp.where(ids_ref[...] == vocabulary, 1.0, 0.0).astype(bf16)
        embedded_ref[...] = product(onehot, table_ref[...]).astype(bf16)
        share = product(embedded_ref[...], weight_ref[...])
        share_ref[...] = share
        low_ref[...] = share.astype(bf16)

    return call(
        kernel,
        (member, ids.reshape(rows, 1), table, *pieces),
        [SCALARS] + [WHOLE] * (2 + span),
        [
            shaped(rows, width),
            shaped(span * shard, width),
            shaped(rows, width, kind=f32),
            shaped(rows, width),
        ],
        [WHOLE] * 4,
        deps=deps,
        micros=4,
    )


def split_heads(values, target, start, batches, part, width_of_task):
    patch_rows = values.shape[0] // batches
    for m in range(batches):
        for pair in range(PAIRS):
            target[m * PAIRS + pair, :, part * PAIR : (part + 1) * PAIR] = values[
                m * patch_rows : (m + 1) * patch_rows, pair * PAIR : (pair + 1) * PAIR
            ]


def merge_heads(blocks, target, batches, parts):
    patch_rows = target.shape[0] // batches
    width = PAIRS * PAIR
    for t in range(batches * PAIRS):
        m, pair = t // PAIRS, t % PAIRS
        first = blocks[0].shape[0]
        block = blocks[0].at[t] if t < first else blocks[1].at[t - first]
        for part in range(parts):
            at = part * width + pair * PAIR
            target[m * patch_rows : (m + 1) * patch_rows, at : at + PAIR] = block[
                :, part * PAIR : (part + 1) * PAIR
            ]


def strided(values, target, span, offset):
    size = values.shape[1] // (4 * span)
    for k in range(span):
        parts = [
            values[:, (group * span + k) * size : (group * span + k + 1) * size]
            for group in range(4)
        ]
        target[k, :, offset : offset + 4 * size] = jnp.concatenate(parts, axis=1)


def global_start(batches, own, others, gains, biases, heads_in):
    rows, width = own.shape
    patch_rows = rows // batches

    def kernel(own_ref, gains_ref, biases_ref, weight_hbm, *rest):
        other_refs, (stream_ref, normed_ref, task_ref, share_ref, weight, sem) = (
            rest[: len(others)],
            rest[len(others) :],
        )
        load = pltpu.make_async_copy(weight_hbm, weight, sem)
        load.start()
        stream = own_ref[...]
        for ref in other_refs:
            stream = stream + ref[...].astype(f32)
        stream_ref[...] = stream
        normed = layer_norm(stream, gains_ref[0:1], biases_ref[0:1]).astype(bf16)
        normed_ref[...] = normed
        strided(normed, share_ref, SPAN, 0)
        load.wait()
        for part in range(3):
            mixed = product(normed, weight[:, part * width : (part + 1) * width]).astype(bf16)
            split_heads(mixed, task_ref, 0, batches, part, width)

    return call(
        kernel,
        (own, gains, biases, heads_in, *others),
        [WHOLE] * 3 + [ANY] + [WHOLE] * len(others),
        [
            shaped(rows, width, kind=f32),
            shaped(rows, width),
            shaped(batches * PAIRS, patch_rows, 3 * PAIR),
            shaped(SPAN, rows, width // SPAN),
        ],
        [WHOLE] * 4,
        [pltpu.VMEM(heads_in.shape, bf16), pltpu.SemaphoreType.DMA],
        micros=5,
    )


def global_feed_forward(batches, blocks, stream, gains, biases, heads_out, expand, contract):
    rows, width = stream.shape
    hidden_width = expand.shape[1]
    n = len(blocks)
    patch_rows = rows // batches
    half = patch_rows // 2

    def kernel(stream_ref, gains_ref, biases_ref, out_hbm, expand_hbm, contract_hbm, *rest):
        block_refs, rest = rest[:n], rest[n:]
        (attended_ref, middle_ref, normed_two_ref, slope_ref, hidden_ref, sent_ref) = rest[:6]
        share_ref, edge_ref, near_ref, w_out, w_expand, w_contract, sems = rest[6:]
        loads = [
            pltpu.make_async_copy(out_hbm, w_out, sems.at[0]),
            pltpu.make_async_copy(expand_hbm, w_expand, sems.at[1]),
            pltpu.make_async_copy(contract_hbm, w_contract, sems.at[2]),
        ]
        for load in loads:
            load.start()
        merge_heads(block_refs, attended_ref, batches, 1)
        loads[0].wait()
        middle = stream_ref[...] + product(attended_ref[...], w_out[...])
        middle_ref[...] = middle
        normed_two_ref[...] = layer_norm(middle, gains_ref[1:2], biases_ref[1:2]).astype(bf16)
        loads[1].wait()

        @pl.loop(0, hidden_width // width)
        def _(i):
            at = pl.ds(pl.multiple_of(i * width, 128), width)
            hidden, slope = gelu_and_slope(product(normed_two_ref[...], w_expand[:, at]))
            hidden_ref[:, at] = hidden.astype(bf16)
            slope_ref[:, at] = slope.astype(bf16)

        loads[2].wait()
        result = middle_ref[...] + product(hidden_ref[...], w_contract[...])
        sent = result.astype(bf16)
        sent_ref[...] = sent
        edge_ref[...] = jnp.zeros(edge_ref.shape, bf16)
        for m in range(batches):
            stop = (m + 1) * patch_rows
            edge_ref[m : m + 1, :] = sent[stop - 1 : stop]
            near_ref[m * half : (m + 1) * half, :] = sent[stop - half - 1 : stop - 1]
        strided(hidden_ref[...], share_ref, SPAN, 0)
        strided(normed_two_ref[...], share_ref, SPAN, hidden_width // SPAN)
        strided(attended_ref[...], share_ref, SPAN, (hidden_width + width) // SPAN)

    return call(
        kernel,
        (stream, gains, biases, heads_out, expand, contract, *blocks),
        [WHOLE] * 3 + [ANY] * 3 + [WHOLE] * n,
        [
            shaped(rows, width),
            shaped(rows, width, kind=f32),
            shaped(rows, width),
            shaped(rows, hidden_width),
            shaped(rows, hidden_width),
            shaped(rows, width),
            shaped(SPAN, rows, (hidden_width + 2 * width) // SPAN),
            shaped(SMALL_ROWS, width),
            shaped(batches * half, width),
        ],
        [WHOLE] * 9,
        [
            pltpu.VMEM(heads_out.shape, bf16),
            pltpu.VMEM(expand.shape, bf16),
            pltpu.VMEM(contract.shape, bf16),
            pltpu.SemaphoreType.DMA((3,)),
        ],
        micros=8,
    )


def global_feed_backward(
    batches, own, near, edge, middle, slope, gains, heads_out, expand, contract, deps=()
):
    rows, width = middle.shape
    hidden_width = expand.shape[1]
    patch_rows = rows // batches
    half = patch_rows // 2

    def kernel(
        own_ref, near_ref, edge_ref, middle_ref, slope_ref, gains_ref, out_hbm, expand_hbm,
        contract_hbm, upward_ref, grad_middle_ref, branch_ref, task_ref, small_ref, grad_ref,
        w_out, w_expand, w_contract, sems,
    ):
        loads = [
            pltpu.make_async_copy(contract_hbm, w_contract, sems.at[2]),
            pltpu.make_async_copy(expand_hbm, w_expand, sems.at[1]),
            pltpu.make_async_copy(out_hbm, w_out, sems.at[0]),
        ]
        for load in loads:
            load.start()
        source = jnp.concatenate([own_ref[...], near_ref[...], edge_ref[...]], axis=0)
        index = lax.broadcasted_iota(jnp.int32, (rows, 1), 0)
        batch, place = index // patch_rows, index % patch_rows
        chosen = jnp.where(
            place < half - 1,
            batch * half + place + 1,
            jnp.where(
                place < patch_rows - 1,
                batches * half + batch * half + place - (half - 1),
                2 * batches * half + batch,
            ),
        )
        columns = lax.broadcasted_iota(jnp.int32, (rows, source.shape[0]), 1)
        picked = jnp.where(columns == chosen, 1.0, 0.0).astype(bf16)
        grad_ref[...] = product(picked, source).astype(bf16)
        loads[0].wait()

        @pl.loop(0, hidden_width // width)
        def _(i):
            at = pl.ds(pl.multiple_of(i * width, 128), width)
            grad_hidden = product_transposed(grad_ref[...], w_contract[at, :])
            upward_ref[:, at] = (grad_hidden * slope_ref[:, at].astype(f32)).astype(bf16)

        loads[1].wait()
        grad_normed = product_transposed(upward_ref[...], w_expand[...])
        back, gain, bias = layer_norm_back(middle_ref[...], gains_ref[1:2], grad_normed)
        grad_middle = back + grad_ref[...].astype(f32)
        grad_middle_ref[...] = grad_middle
        branch = grad_middle.astype(bf16)
        branch_ref[...] = branch
        small_ref[...] = jnp.concatenate([gain, bias], axis=0)
        loads[2].wait()
        attended = product_transposed(branch, w_out[...]).astype(bf16)
        split_heads(attended, task_ref, 0, batches, 0, width)

    return call(
        kernel,
        (own, near, edge, middle, slope, gains, heads_out, expand, contract),
        [WHOLE] * 6 + [ANY] * 3,
        [
            shaped(rows, hidden_width),
            shaped(rows, width, kind=f32),
            shaped(rows, width),
            shaped(batches * PAIRS, patch_rows, PAIR),
            shaped(2, width, kind=f32),
            shaped(rows, width),
        ],
        [WHOLE] * 6,
        [
            pltpu.VMEM(heads_out.shape, bf16),
            pltpu.VMEM(expand.shape, bf16),
            pltpu.VMEM(contract.shape, bf16),
            pltpu.SemaphoreType.DMA((3,)),
        ],
        deps=deps,
        micros=10,
    )


def global_end(batches, blocks, stream, grad_middle, small, gains, heads_in, deps=()):
    rows, width = stream.shape
    n = len(blocks)

    def kernel(stream_ref, grad_middle_ref, small_ref, gains_ref, weight_hbm, *rest):
        block_refs, (mixed_ref, low_ref, all_small_ref, weight, sem) = rest[:n], rest[n:]
        load = pltpu.make_async_copy(weight_hbm, weight, sem)
        load.start()
        merge_heads(block_refs, mixed_ref, batches, 3)
        load.wait()
        grad_normed = product_transposed(mixed_ref[...], weight[...])
        back, gain, bias = layer_norm_back(stream_ref[...], gains_ref[0:1], grad_normed)
        low_ref[0:rows, :] = (back + grad_middle_ref[...]).astype(bf16)
        smalls = jnp.concatenate([gain, small_ref[0:1], bias, small_ref[1:2]], axis=0)
        all_small_ref[...] = smalls
        rest = jnp.zeros((SMALL_ROWS - 4, width), f32)
        low_ref[rows:, :] = jnp.concatenate([smalls, rest], axis=0).astype(bf16)

    return call(
        kernel,
        (stream, grad_middle, small, gains, heads_in, *blocks),
        [WHOLE] * 4 + [ANY] + [WHOLE] * n,
        [
            shaped(rows, 3 * width),
            shaped(rows + SMALL_ROWS, width),
            shaped(4, width, kind=f32),
        ],
        [WHOLE] * 3,
        [pltpu.VMEM(heads_in.shape, bf16), pltpu.SemaphoreType.DMA],
        deps=deps,
        micros=6,
    )


def patch_backward(section, ids, embedded, weight, own, crossed, span, deps=()):
    rows, width = embedded.shape
    block = own[0].shape[0]
    n = len(own)
    used = rows // n
    shard = weight.shape[0] // span

    def kernel(section_ref, ids_ref, embedded_ref, weight_ref, crossed_ref, *rest):
        own_refs, (patch_ref, table_ref, gathered, small) = rest[:n], rest[n:]

        @pl.when(section_ref[0] == 0)
        def _():
            for k in range(n):
                gathered[k * used : (k + 1) * used, :] = own_refs[k][0:used, :]
            total = sum(ref[used:, :].astype(f32) for ref in own_refs)
            small[...] = total.astype(bf16)

        @pl.when(section_ref[0] != 0)
        def _():
            for k in range(n):
                gathered[k * used : (k + 1) * used, :] = crossed_ref[k * block : k * block + used, :]
            small[...] = jnp.zeros_like(small)

        part = transposed_product(embedded_ref[...], gathered[...]).astype(bf16)
        for k in range(span):
            patch_ref[k, 0:shard, :] = part[k * shard : (k + 1) * shard]
            patch_ref[k, shard:, :] = small[...]
        grad_embedded = product_transposed(gathered[...], weight_ref[...]).astype(bf16)
        vocabulary = lax.broadcasted_iota(jnp.int32, (rows, VOCAB), 1)
        onehot = jnp.where(ids_ref[...] == vocabulary, 1.0, 0.0).astype(bf16)
        table_ref[...] = transposed_product(onehot, grad_embedded).astype(bf16)

    return call(
        kernel,
        (section, ids.reshape(rows, 1), embedded, weight, crossed, *own),
        [SCALARS] + [WHOLE] * (4 + n),
        [shaped(span, shard + SMALL_ROWS, width), shaped(VOCAB, width)],
        [WHOLE] * 2,
        [pltpu.VMEM((rows, width), bf16), pltpu.VMEM((SMALL_ROWS, width), bf16)],
        deps=deps,
        micros=6,
    )


def leave_by_group(group, buffer, targets, sems):
    for j in range(len(targets)):
        for k in range(len(targets)):

            @pl.when((group ^ j) == k)
            def _(j=j, k=k):
                pltpu.make_async_copy(buffer.at[j], targets[k], sems.at[k]).start()

    for k in range(len(targets)):
        pltpu.make_async_copy(buffer.at[0], targets[k], sems.at[k]).wait()


def plane_parts(hidden_width, width):
    starts, start = {}, 0
    for name, size in (
        ("hidden", hidden_width // SPAN),
        ("normed_two", width // SPAN),
        ("attended", width // SPAN),
        ("branch", width),
        ("attend_branch", width),
        ("upward", hidden_width),
        ("mixed", 3 * width),
        ("normed", width // SPAN),
    ):
        starts[name] = slice(start, start + size)
        start += size
    return starts, start


def pack(member, feed_share, normed_share, branch, attend_branch, upward, mixed, deps=()):
    rows, width = branch.shape
    hidden_width = upward.shape[1]
    parts, whole = plane_parts(hidden_width, width)
    own = slice(0, feed_share.shape[2])

    def kernel(member_ref, feed_ref, normed_ref, branch_ref, attend_ref, upward_ref, mixed_ref, *sent_refs):
        for k in range(SPAN):
            sent_refs[k][0:rows, own] = feed_ref[member_ref[0] ^ k]
            sent_refs[k][0:rows, parts["branch"]] = branch_ref[...]
            sent_refs[k][0:rows, parts["attend_branch"]] = attend_ref[...]
            sent_refs[k][0:rows, parts["upward"]] = upward_ref[...]
            sent_refs[k][0:rows, parts["mixed"]] = mixed_ref[...]
            sent_refs[k][0:rows, parts["normed"]] = normed_ref[member_ref[0] ^ k]

    return call(
        kernel,
        (member, feed_share, normed_share, branch, attend_branch, upward, mixed),
        [SCALARS] + [WHOLE] * 6,
        [shaped(rows, whole)] * SPAN,
        [WHOLE] * SPAN,
        deps=deps,
        micros=4,
    )


def plane_gradients(group, sent, rows, hidden_width, width, deps=()):
    parts, _ = plane_parts(hidden_width, width)
    deep, thin = hidden_width // GROUPS, width // GROUPS
    chunks = hidden_width // width
    block = deep + (chunks + 4) * thin

    def kernel(group_ref, *refs):
        sent_refs, (keep_ref, leave_ref, buffer, sems) = refs[: len(sent)], refs[len(sent) :]

        def columns(name, chunk=None):
            at = parts[name]
            if chunk is not None:
                at = slice(at.start + chunk * width, at.start + (chunk + 1) * width)
            return jnp.concatenate([ref[0:rows, at] for ref in sent_refs], axis=0)

        def store(part, start, size):
            for j in range(4):
                buffer[j, start : start + size, :] = part[j * size : (j + 1) * size].astype(bf16)

        store(transposed_product(columns("hidden"), columns("branch")), 0, deep)
        left, at = columns("normed_two"), deep
        for c in range(chunks):
            store(transposed_product(left, columns("upward", c)), at, thin)
            at += thin
        store(transposed_product(columns("attended"), columns("attend_branch")), at, thin)
        left = columns("normed")
        for c in range(3):
            at += thin
            store(transposed_product(left, columns("mixed", c)), at, thin)
        for j in range(4):
            mine = ((group_ref[0] ^ j) & 1) == 0

            @pl.when(mine)
            def _(j=j):
                pltpu.make_async_copy(buffer.at[j], keep_ref.at[j >> 1], sems.at[j]).start()

            @pl.when(jnp.logical_not(mine))
            def _(j=j):
                pltpu.make_async_copy(buffer.at[j], leave_ref.at[j >> 1], sems.at[j]).start()

        for j in range(4):
            pltpu.make_async_copy(buffer.at[j], keep_ref.at[j >> 1], sems.at[j]).wait()

    return call(
        kernel,
        (group, *sent),
        [SCALARS] + [WHOLE] * len(sent),
        [shaped(2, block, width)] * 2,
        [ANY] * 2,
        [pltpu.VMEM((4, block, width), bf16), pltpu.SemaphoreType.DMA((4,))],
        deps=deps,
        micros=8,
    )


def half_sum(which, kept, near, deps=()):
    shape = kept.shape[1:]

    def kernel(which_ref, kept_ref, near_ref, out_ref):
        total = kept_ref[0].astype(f32) + near_ref[0].astype(f32)
        out_ref[...] = total.astype(bf16)

    count = len(deps)

    def body(*refs):
        kernel(*refs[:3], refs[-1])

    steps = 1 if shape[0] % 32 else 2
    size = shape[0] // steps
    spec = pl.BlockSpec((1, size, shape[1]), lambda i, ref: (ref[0], i, 0))
    return pl.pallas_call(
        body,
        grid_spec=pltpu.PrefetchScalarGridSpec(
            num_scalar_prefetch=1,
            grid=(steps,),
            in_specs=[spec, spec] + [ANY] * count,
            out_specs=pl.BlockSpec((size, shape[1]), lambda i, ref: (i, 0)),
        ),
        out_shape=shaped(*shape),
        compiler_params=pltpu.CompilerParams(vmem_limit_bytes=VMEM),
        cost_estimate=cost(2),
    )(which, kept, near, *deps)


def finish(section, upper, deep, shard, room, block, own, crossed, table_parts, patch_parts):
    width = own.shape[1]
    chunks = deep // shard
    p = len(patch_parts)

    def kernel(section_ref, upper_ref, kept_ref, near_ref, far_ref, own_ref, crossed_ref, table_ref, *refs):
        patch_refs = refs[:p]
        contract, expand, ins, out, table, small, patch = refs[p:]
        heads_start = deep + (chunks + 1) * shard
        mine = upper_ref[0]

        def total(start, size):
            at = slice(start, start + size)
            return kept_ref[mine, at].astype(f32) + near_ref[mine, at].astype(f32) + far_ref[at].astype(f32)

        def taken(ref, start, size):
            return ref[start : start + size, :]

        total_patch = sum(ref[...].astype(f32) for ref in patch_refs)
        patch[...] = total_patch[: patch.shape[0]]

        @pl.when(section_ref[0] == 0)
        def _():
            contract[...] = total(0, deep)
            for c in range(chunks):
                expand[:, c * width : (c + 1) * width] = total(deep + c * shard, shard)
            out[...] = total(deep + chunks * shard, shard)
            for c in range(3):
                ins[:, c * width : (c + 1) * width] = total(heads_start + c * shard, shard)
            small[...] = total_patch[patch.shape[0] :]
            sums = jnp.zeros((room, width), f32)
            for k in range(table_ref.shape[0]):
                sums = sums + table_ref[k].astype(f32)
            table[...] = sums

        @pl.when(section_ref[0] != 0)
        def _():
            contract[...] = taken(crossed_ref, 0, deep)
            for c in range(chunks):
                expand[:, c * width : (c + 1) * width] = taken(own_ref, c * shard, shard)
            out[...] = taken(crossed_ref, deep, shard)
            ins[:, 0:width] = taken(crossed_ref, deep + shard, shard)
            for c in range(2):
                ins[:, (c + 1) * width : (c + 2) * width] = taken(own_ref, deep + c * shard, shard)
            small[...] = taken(own_ref, deep + 2 * shard, small.shape[0])
            table[...] = taken(crossed_ref, deep + 2 * shard, room)

    return call(
        kernel,
        (section, upper, *block, own, crossed, table_parts, *patch_parts),
        [SCALARS] * 2 + [WHOLE] * (6 + p),
        [
            shaped(deep, width, kind=f32),
            shaped(shard, chunks * width, kind=f32),
            shaped(shard, 3 * width, kind=f32),
            shaped(shard, width, kind=f32),
            shaped(room, width, kind=f32),
            shaped(SMALL_ROWS, width, kind=f32),
            shaped(patch_parts[0].shape[0] - SMALL_ROWS, width, kind=f32),
        ],
        [WHOLE] * 7,
        micros=4,
    )


SEQ = ("group", "member")


def section_send(x, origin, target, pairs):
    count = lax.axis_size(SEQ)
    joint = [(origin * count + i, target * count + j) for i, j in pairs]
    return lax.ppermute(x, ("section",) + SEQ, joint)


def section_swap(x):
    return lax.ppermute(x, "section", [(0, 1), (1, 0)])


def by_slot(buffer, count, pieces):
    split = count // GROUPS
    parts, start = [], 0
    for size, shared in pieces:
        part = buffer[:, start : start + size]
        start += size
        kept = shared or size // split
        if shared:
            part = jnp.broadcast_to(part[:, None, :shared], (GROUPS, split, shared, part.shape[2]))
        parts.append(part.reshape(count, kept, part.shape[-1]))
    whole = jnp.concatenate(parts, axis=1)
    turned = whole.reshape((4, count // 4) + whole.shape[1:])
    return jnp.swapaxes(turned, 0, 1).reshape(whole.shape)


def place_sum(shares):
    shares = lax.psum_scatter(shares, "member", scatter_dimension=0, tiled=True)
    return lax.psum_scatter(shares, "group", scatter_dimension=0, tiled=True)[0]


def on_device(
    byte_values,
    item_lengths,
    embed_tables,
    patch_weight,
    norm_gains,
    norm_biases,
    heads_in,
    heads_out,
    expand_weight,
    contract_weight,
    out_grad,
):
    place = lax.axis_index(SEQ)
    count = lax.axis_size(SEQ)
    section = lax.axis_index("section")
    is_global = section == 0
    batches, byte_rows = byte_values.shape
    patch_rows = byte_rows // PATCH
    width = heads_out.shape[2]
    rows = batches * patch_rows
    total_patches = patch_rows * count
    gains, biases = norm_gains[0], norm_biases[0]
    heads_in, heads_out = heads_in[0], heads_out[0]
    expand, contract = expand_weight[0], contract_weight[0]
    own_table = embed_tables[0]
    straight = [(i, i) for i in range(count)]

    quarters = PATCH // 2
    span = count // quarters
    group, member = place // span, place % span
    shard_rows = patch_weight.shape[0]
    pieces = [patch_weight]
    for k in range(1, span):
        pieces.append(lax.ppermute(patch_weight, SEQ, [(i, i ^ k) for i in range(count)]))
    other_table = section_swap(own_table)
    global_table = jnp.where(is_global, own_table, other_table)
    local_table = jnp.where(is_global, other_table, own_table)
    which_byte = section * quarters + group
    byte_ids = []
    for k in range(quarters):
        theirs = byte_values
        if k:
            theirs = lax.ppermute(byte_values, SEQ, [(i, i ^ (k * span)) for i in range(count)])
        theirs = theirs.reshape(rows, PATCH)
        byte_ids.append(lax.dynamic_index_in_dim(theirs, which_byte, 1, keepdims=False))
    byte_ids = jnp.concatenate(byte_ids)
    embedded, byte_weight, shares, low_shares = patch_forward(
        member.reshape(1).astype(jnp.int32), byte_ids, global_table, pieces
    )
    shares = shares + section_send(low_shares, 1, 0, straight).astype(f32)
    shares = shares.reshape(quarters, rows, width)
    parts = []
    for k in range(1, quarters):
        pairs = [(i, i ^ (k * span)) for i in range(count)]
        parts.append(section_send(shares[k].astype(bf16), 0, 0, pairs))

    arrived = [section_send(w, 1, 0, straight) for w in (heads_in, heads_out, expand, contract)]
    other_norms = section_swap(jnp.concatenate([gains, biases]))
    local_gains = jnp.where(is_global, other_norms[:2], gains)
    local_biases = jnp.where(is_global, other_norms[2:], biases)

    tasks = batches * PAIRS
    first_tasks = min(tasks, count)
    spare_tasks = tasks - first_tasks

    def to_tasks(blocks):
        columns = blocks.shape[2]
        slots = jnp.pad(blocks[:first_tasks], ((0, count - first_tasks), (0, 0), (0, 0)))
        if spare_tasks:
            spare = section_send(blocks[first_tasks:], 0, 1, straight)
            spare = jnp.pad(spare, ((0, count - spare_tasks), (0, 0), (0, 0)))
            slots = jnp.where(is_global, slots, spare)
        landed = lax.all_to_all(slots, SEQ, 0, 0)
        return landed.reshape(total_patches, columns)

    def from_tasks(results):
        columns = results.shape[1]
        slots = lax.all_to_all(results.reshape(count, patch_rows, columns), SEQ, 0, 0)
        if spare_tasks:
            return [slots, section_send(slots[:spare_tasks], 1, 0, straight)]
        return [slots]

    task = jnp.minimum(jnp.where(is_global, place, first_tasks + place), tasks - 1)
    task_lengths = lax.dynamic_index_in_dim(item_lengths, task // PAIRS, 0, keepdims=False)
    task_owners = locate(jnp.arange(total_patches, dtype=jnp.int32) * PATCH, task_lengths)[0]

    stream, normed, tasks_out, normed_share = global_start(
        batches, shares[0], parts, gains, biases, heads_in
    )
    qkv = to_tasks(tasks_out)
    attended, middle, normed_two, slope, hidden, sent, feed_share, edge, near = global_feed_forward(
        batches,
        from_tasks(global_attention(qkv, task_owners)),
        stream,
        gains,
        biases,
        heads_out,
        expand,
        contract,
    )
    half = patch_rows // 2
    half_bytes = half * PATCH
    chunks = half_bytes // BLOCK
    onward = [(i, i + 1) for i in range(count - 1)]
    backward = [(i + 1, i) for i in range(count - 1)]
    near = section_send(near, 0, 1, straight)
    edge = section_send(edge, 0, 0, onward)
    weights = (heads_in, heads_out, expand, contract)
    flag = section.reshape(1).astype(jnp.int32)
    block_patches = BLOCK // PATCH
    local_outs, activations_of, grads_shifted, grads_edge = [], [], [], []
    for c in range(chunks):
        numbers = jnp.concatenate(
            [
                jnp.stack([section, place * byte_rows, jnp.int32(c)]).astype(jnp.int32),
                item_lengths.reshape(-1),
            ]
        )
        act, grad_shifted, grad_edge, keep, send = local_block(
            numbers,
            byte_values,
            local_table,
            sent,
            edge,
            near,
            local_gains,
            local_biases,
            out_grad,
            patch_rows,
            weights,
            arrived,
        )
        local_outs.append(act.reshape(batches, BLOCK, width))
        grads_shifted.append(grad_shifted.reshape(batches, block_patches, width))
        grads_edge.append(grad_edge)
        activations_of.append((numbers, keep, section_swap(send)))
    local_out = jnp.concatenate(local_outs, axis=1)
    grad_shifted = jnp.concatenate(grads_shifted, axis=1).reshape(batches * half, width)

    other_out = section_send(local_out, 0, 1, straight)
    byte_places = place * byte_rows + jnp.arange(byte_rows, dtype=jnp.int32)
    live_bytes = jnp.stack([locate(byte_places, item_lengths[m])[1] for m in range(batches)])
    own_sent = jnp.broadcast_to(
        sent.reshape(batches, patch_rows, 1, width), (batches, patch_rows, PATCH, width)
    ).reshape(batches, byte_rows, width)
    own_sent = jnp.where(live_bytes[:, :, None], own_sent, jnp.zeros((), bf16))
    activations = jnp.where(
        is_global, own_sent, jnp.concatenate([other_out, local_out], axis=1)
    )

    shard = width // count
    room = VOCAB // count
    group_shard, group_room = width // GROUPS, VOCAB // GROUPS
    small_rows = max(4, room)
    pieces = {
        False: [(contract.shape[0] // GROUPS, 0), (group_shard, 0), (group_shard, 0), (group_room, 0)],
        True: [(group_shard, 0)] * (expand.shape[1] // width + 2) + [(group_room, small_rows)],
    }

    def ordered(buffer):
        if count == GROUPS:
            return buffer
        upper, lower = by_slot(buffer, count, pieces[False]), by_slot(buffer, count, pieces[True])
        rows_of = max(upper.shape[1], lower.shape[1])
        upper, lower = (
            jnp.pad(x, ((0, 0), (0, rows_of - x.shape[1]), (0, 0))) for x in (upper, lower)
        )
        return jnp.where(is_global, upper, lower)

    near_back = section_send(grad_shifted, 1, 0, straight)
    edge_back = section_send(grads_edge[0], 0, 0, backward)
    in_plane = span == SPAN and count == GROUPS
    member_flag = (member % SPAN).reshape(1).astype(jnp.int32)
    group_flag = group.reshape(1).astype(jnp.int32)

    def plane_send(blocks):
        return [blocks[0]] + [
            section_send(blocks[k], 0, 0, [(i, i ^ k) for i in range(count)])
            for k in range(1, SPAN)
        ]

    upper = (group >> 1) & 1
    upper_flag = upper.reshape(1).astype(jnp.int32)

    def group_pairs(step):
        return [(i, i ^ (step * span)) for i in range(count)]

    def both_send(x, pairs):
        joint = [(s * count + i, s * count + j) for s in range(2) for i, j in pairs]
        return lax.ppermute(x, ("section",) + SEQ, joint)

    grad_upward, grad_middle, attend_branch, task_grads, small, grad_sent = global_feed_backward(
        batches,
        grad_shifted,
        near_back,
        edge_back,
        middle,
        slope,
        gains,
        heads_out,
        expand,
        contract,
    )
    half_locals = [
        ordered(
            local_gradients(
                count,
                numbers,
                byte_values,
                keep,
                crossed,
                contract.shape[0],
                width,
                half_bytes,
                [grad_sent],
            )
        )
        for numbers, keep, crossed in activations_of
    ]
    if chunks > 1:
        half_locals = [sum(x.astype(f32) for x in half_locals).astype(bf16)]
    half_locals = half_locals[0]
    task_grads = to_tasks(task_grads)
    task_mixed = global_attention(qkv, task_owners, task_grads)
    grad_mixed, own_rows, small = global_end(
        batches,
        from_tasks(task_mixed),
        stream,
        grad_middle,
        small,
        gains,
        heads_in,
    )

    gathered = [own_rows]
    for k in range(1, quarters):
        pairs = [(i, i ^ (k * span)) for i in range(count)]
        gathered.append(section_send(own_rows, 0, 0, pairs))
    crossed = section_send(jnp.concatenate(gathered), 0, 1, straight)
    patch_share, table_share = patch_backward(
        flag,
        byte_ids,
        embedded,
        byte_weight,
        gathered,
        crossed,
        span,
    )
    if in_plane:
        in_planes = lax.psum_scatter(half_locals, "member", scatter_dimension=0, tiled=True)
        in_planes = in_planes.reshape((2, 2) + in_planes.shape[1:])
        parity = group & 1
        local_near = both_send(
            lax.dynamic_index_in_dim(in_planes, 1 - parity, 1, keepdims=False), group_pairs(1)
        )
        local_kept = lax.dynamic_index_in_dim(in_planes, parity, 1, keepdims=False)
    else:
        own_local = place_sum(half_locals)
    patch_parts = [lax.dynamic_index_in_dim(patch_share, member, 0, keepdims=False)]
    for k in range(1, span):
        leaving = lax.dynamic_index_in_dim(patch_share, member ^ k, 0, keepdims=False)
        patch_parts.append(lax.ppermute(leaving, SEQ, [(i, i ^ k) for i in range(count)]))
    table_share = table_share + section_send(table_share, 1, 0, straight)
    table_parts = lax.all_to_all(table_share.reshape(count, VOCAB // count, width), SEQ, 0, 0)

    def ordered_rows(first, second):
        feed_rows = contract.shape[0] // count
        expand_sum = [second[k * shard : (k + 1) * shard] for k in range(feed_rows // shard)]
        rest, others = first[feed_rows:], second[feed_rows:]
        ins = [rest[shard : 2 * shard], others[:shard], others[shard : 2 * shard]]
        return (
            first[:feed_rows],
            jnp.concatenate(expand_sum, axis=1),
            jnp.concatenate(ins, axis=1),
            rest[:shard],
            rest[2 * shard : 2 * shard + room],
            others[2 * shard : 2 * shard + 4],
        )

    if in_plane:
        sent_parts = pack(
            member_flag, feed_share, normed_share, grad_sent, attend_branch, grad_upward, grad_mixed,
        )
        kept, leaving = plane_gradients(
            group_flag, plane_send(sent_parts), rows, contract.shape[0], width, [patch_share]
        )
        local_far = both_send(
            half_sum(1 - upper_flag, local_kept, local_near), group_pairs(2)
        )
        near = section_send(leaving, 0, 0, group_pairs(1))
        far = section_send(
            half_sum(1 - upper_flag, kept, near, patch_parts[1:]), 0, 0, group_pairs(2)
        )
        own_local = sum(
            lax.dynamic_index_in_dim(x, upper, 0, keepdims=False).astype(f32)
            for x in (local_kept, local_near)
        ) + local_far.astype(f32)
        crossed = section_send(own_local, 0, 1, straight)
        contract_grad, expand_grad, in_grad, out_grads, table_grad, small, patch_grads = finish(
            flag,
            upper_flag,
            contract.shape[0] // count,
            shard,
            room,
            (kept, near, far),
            own_local,
            crossed,
            table_parts,
            patch_parts,
        )
        small = small[:4]
    else:
        upper, lower = global_sums_of(
            count, hidden, grad_sent, normed_two, grad_upward, normed, grad_mixed, attended,
            attend_branch, small,
        )
        own_global = ordered(jnp.where(is_global, upper, section_send(lower, 0, 1, straight)))
        own_global = place_sum(own_global)
        crossed = section_swap(jnp.where(is_global, own_local, own_global)).astype(f32)
        global_sums = ordered_rows(own_global.astype(f32), crossed)
        global_table = jnp.sum(table_parts.astype(f32), axis=0)
        global_sums = global_sums[:4] + (global_table, global_sums[5])
        local_sums = ordered_rows(crossed, own_local.astype(f32))
        contract_grad, expand_grad, in_grad, out_grads, table_grad, small = (
            jnp.where(is_global, upper, lower) for upper, lower in zip(global_sums, local_sums)
        )
        patch_grads = sum(x.astype(f32) for x in patch_parts)[:shard_rows]
    small = lax.dynamic_slice_in_dim(small, place * shard, shard, 1)
    return (
        activations[None],
        table_grad[None],
        patch_grads,
        small[None, 0:2],
        small[None, 2:4],
        in_grad[None],
        out_grads[None],
        expand_grad[None],
        contract_grad[None],
    )


def solution(mesh):
    devices = mesh.devices
    groups = PATCH // 2
    split = jax.sharding.Mesh(
        devices.reshape(devices.shape[0], groups, devices.shape[1] // groups), ("section",) + SEQ
    )
    both = ("section",) + SEQ
    placed = (
        P(None, SEQ),
        P(),
        P("section", None, None),
        P(both, None),
        P("section", None, None),
        P("section", None, None),
        P("section", None, None),
        P("section", None, None),
        P("section", None, None),
        P("section", None, None),
        P(None, SEQ, None),
    )
    return jax.shard_map(
        on_device,
        mesh=split,
        in_specs=placed,
        out_specs=(
            P("section", None, SEQ, None),
            P("section", SEQ, None),
            P(both, None),
            P("section", None, SEQ),
            P("section", None, SEQ),
            P("section", SEQ, None),
            P("section", SEQ, None),
            P("section", SEQ, None),
            P("section", SEQ, None),
        ),
        check_vma=False,
    )
```

time: 431 us -> 411 us (0.954)
  starting transfers between devices: 142 us -> 107 us
  other arithmetic: 41.2 us -> 11.7 us
  blocking collectives: 0 us -> 29.2 us
  waiting for transfers between devices: 89 us -> 114 us
  Pallas kernels: 126 us -> 109 us
  between operations: 2.32 us -> 15.5 us
  local copies, waits for them, and re-layouts: 22.6 us -> 16.9 us
    all_to_all x0 -> x2, blocking collectives: none -> 29.2 us  [the longest x1 15.6 us: from_tasks(): lax.all_to_all(results.reshape(count, patch_rows, columns), SEQ, 0, 0)]
    pallas_call x4, Pallas kernels: 70.7 us -> 47.4 us  [the longest x1 31.5 us: local_block(): pl.pallas_call(partial(local_kernel, patch_rows), in_specs=[SCALARS] + [W...]
    ppermute x52 -> x39, waiting for transfers between devices: 40.5 us -> 63.3 us  [the longest x28 39.4 us: section_send(): return lax.ppermute(x, ('section',) + SEQ, joint)]
    ppermute x52 -> x39, starting transfers between devices: 115 us -> 93.3 us  [the longest x28 74.3 us: section_send(): return lax.ppermute(x, ('section',) + SEQ, joint)]
    reduce_scatter x0 -> x1, waiting for transfers between devices: none -> 12.9 us  [on_device(): lax.psum_scatter(half_locals, 'member', scatter_dimension=0, tiled=True)]
    convert_element_type x8 -> x0, other arithmetic: 12.8 us -> none  [the longest x6 12.7 us: added(): return total.astype(kind)]
    all_to_all x5 -> x3, starting transfers between devices: 25.7 us -> 13.3 us  [the longest x1 5.89 us: to_tasks(): landed = lax.all_to_all(slots, SEQ, 0, 0)]
    all_to_all x5 -> x3, waiting for transfers between devices: 48.5 us -> 37.7 us  [the longest x1 20.6 us: on_device(): lax.all_to_all(table_share.reshape(count, VOCAB // count, width), SEQ, 0, 0)]
  transfers between devices with their start and end apart: 61 -> 46, of which waited for: 15 -> 19; matrix products, arithmetic and copies ran while one was open for 14% -> 5% of each run, Pallas kernels for 15% -> 14%
where the time goes in v4:
time: 411 us; the launch traced here: 404 us
  waiting for transfers between devices  114 us (28%)
  Pallas kernels  109 us (27%)
  starting transfers between devices  107 us (26%)
  blocking collectives  29.2 us (7%)
  local copies, waits for them, and re-layouts  16.9 us (4%)
  between operations  15.5 us (4%)
  other arithmetic  11.7 us (3%)
    ppermute x28, starting transfers between devices, section_send(): return lax.ppermute(x, ('section',) + SEQ, joint)  74.3 us
    pallas_call x9, Pallas kernels, call(): pl.pallas_call(body, in_specs=list(specs) + [ANY] * len(deps), out_specs=...  51.5 us
    ppermute x28, waiting for transfers between devices, section_send(): return lax.ppermute(x, ('section',) + SEQ, joint)  39.4 us
    pallas_call x1, Pallas kernels, local_block(): pl.pallas_call(partial(local_kernel, patch_rows), in_specs=[SCALARS] + [W...  31.5 us
    all_to_all x1, waiting for transfers between devices, on_device(): lax.all_to_all(table_share.reshape(count, VOCAB // count, width), SEQ, 0, 0)  20.6 us
    ppermute x2, waiting for transfers between devices, both_send(): return lax.ppermute(x, ('section',) + SEQ, joint)  16.4 us
    all_to_all x1, blocking collectives, from_tasks(): lax.all_to_all(results.reshape(count, patch_rows, columns), SEQ, 0, 0)  15.6 us
    all_to_all x1, blocking collectives, to_tasks(): landed = lax.all_to_all(slots, SEQ, 0, 0)  13.6 us
  transfers between devices with their start and end apart: 46, of which 19 were waited for; matrix products, arithmetic and copies ran while one was open for 5% of the time, Pallas kernels for 14%

profile of v4, /device:TPU:0, one launch (start us, length us, event | category | flops | bytes accessed | tf_op | source)
XLA Modules:
  0.0 403.7 jit_solution(8562319977680829366)
XLA Ops:
  7.7 4.7 %collective-permute-start.2 = (s32[3,256]{1,0:T(4,128)}, s32[3,256]{1,0:T(4,128)S(1)}, u32[]{:S(2)}, u32[]{:S(2)}) collective-permute-start(s32[3,256]{1,0:T(4,128)} %ids_ref.3), channel_id=1, source_target_pairs={{0,12},{1,13},{2,14},{3,15},{4,8},{5,9},{6,10},{7,11},{8,4},{9,5},... | collective-permute-start | bytes 9224 | tf_op jit(solution)/shard_map/ppermute | solution.py:1374
  23.1 7.4 %collective-permute-done.5.refs_5_ = bf16[192,768]{1,0:T(8,128)(2,1)S(1)} collective-permute-done((bf16[192,768]{1,0:T(8,128)(2,1)}, bf16[192,768]{1,0:T(8,128)(2,1)S(1)}, u32[]{:S(2)}, u32[]{:S(2)}) %collective-permute-start.5) | collective-permute-done | bytes 294944 | tf_op jit(solution)/shard_map/ppermute | solution.py:1365
  40.5 5.5 %collective-permute-start.10 = (bf16[96,768]{1,0:T(8,128)(2,1)S(1)}, bf16[96,768]{1,0:T(8,128)(2,1)S(1)}, u32[]{:S(2)}, u32[]{:S(2)}) collective-permute-start(bf16[96,768]{1,0:T(8,128)(2,1)S(1)} %get-tuple-element.110), channel_id=1, source_target_pairs={{0,12},{1,13},{2,14},{3,15},{4,8},{5,9},{6,10},{7,11},{8,4},{9,5},... | collective-permute-start | bytes 442376 | tf_op jit(solution)/shard_map/ppermute | solution.py:1304
  58.0 4.7 %shard_map.179 = (f32[96,768]{1,0:T(8,128)}, bf16[96,768]{1,0:T(8,128)(2,1)}, bf16[18,32,384]{2,1,0:T(8,128)(2,1)}, bf16[4,96,192]{2,1,0:T(8,128)(2,1)}) custom-call(f32[96,768]{1,0:T(8,128)} %slice.79.refs_0_, f32[2,768]{1,0:T(2,128)} %bitcast.143, f32[2,768]{1,0:T(2,128)} %bitcast.140, bf16[768,2304]{1,0:T(8,128)(2,1)} %bitcast.167, ...), custom_call_target="tpu_custom_call" | custom-call | flops 5500000256 | bytes 1 | tf_op jit(solution)/shard_map/pallas_call | solution.py:745
  63.5 7.1 %collective-permute-start.11 = (bf16[2,32,384]{2,1,0:T(8,128)(2,1)S(1)}, bf16[2,32,384]{2,1,0:T(8,128)(2,1)S(1)}, u32[]{:S(2)}, u32[]{:S(2)}) collective-permute-start(bf16[2,32,384]{2,1,0:T(8,128)(2,1)S(1)} %slice.69), channel_id=1, source_target_pairs={{0,16},{1,17},{2,18},{3,19},{4,20},{5,21},{6,22},{7,23},{8,24},{9,... | collective-permute-start | bytes 147464 | tf_op jit(solution)/shard_map/ppermute | solution.py:1304
  73.2 5.9 %all-to-all-start = ((bf16[16,32,384]{2,1,0:T(8,128)(2,1)}), bf16[16,32,384]{2,1,0:T(8,128)(2,1)S(1)}, u32[]{:S(2)}, u32[]{:S(2)}) async-start(bf16[16,32,384]{2,1,0:T(8,128)(2,1)} %pad_select_fusion), calls=%async_computation | async-start | bytes 786432 | tf_op jit(solution)/shard_map/all_to_all | solution.py:1404
  81.5 10.8 %all-to-all-done = bf16[16,32,384]{2,1,0:T(8,128)(2,1)S(1)} async-done(((bf16[16,32,384]{2,1,0:T(8,128)(2,1)}), bf16[16,32,384]{2,1,0:T(8,128)(2,1)S(1)}, u32[]{:S(2)}, u32[]{:S(2)}) %all-to-all-start) | async-done | bytes 393248 | tf_op jit(solution)/shard_map/all_to_all | solution.py:1404
  93.0 4.4 %shard_map.180 = bf16[512,128]{1,0:T(8,128)(2,1)} custom-call(s32[512,1]{1,0:T(8,128)} %copy.33.column_ref.refs_0_, s32[1,512]{1,0:T(1,128)} %bitcast.149, bf16[512,384]{1,0:T(8,128)(2,1)} %bitcast.133), custom_call_target="tpu_custom_call" | custom-call | flops 16499999744 | bytes 1 | tf_op jit(solution)/shard_map/pallas_call | solution.py:714
  97.3 3.6 all-to-all-start.1
  102.4 6.3 %all-to-all-done.1.refs_6_ = bf16[16,32,128]{2,1,0:T(8,128)(2,1)S(1)} async-done(((bf16[16,32,128]{2,1,0:T(8,128)(2,1)}), bf16[16,32,128]{2,1,0:T(8,128)(2,1)S(1)}, u32[]{:S(2)}, u32[]{:S(2)}) %all-to-all-start.1) | async-done | bytes 131104 | tf_op jit(solution)/shard_map/all_to_all | solution.py:1409
  112.5 7.4 %shard_map.181 = (bf16[96,768]{1,0:T(8,128)(2,1)}, f32[96,768]{1,0:T(8,128)}, bf16[96,768]{1,0:T(8,128)(2,1)}, bf16[96,3072]{1,0:T(8,128)(2,1)}, bf16[96,3072]{1...) custom-call(f32[96,768]{1,0:T(8,128)} %get-tuple-element.52.refs_0_,, ...), custom_call_target="tpu_custom_call" | custom-call | flops 8800000000 | bytes 1 | tf_op jit(solution)/shard_map/pallas_call | solution.py:745
  127.4 31.5 %shard_map.182 = (bf16[384,768]{1,0:T(8,128)(2,1)}, bf16[48,768]{1,0:T(8,128)(2,1)}, bf16[16,768]{1,0:T(8,128)(2,1)}, bf16[400,7680]{1,0:T(8,128)(2,1)}, bf16[400,7680]{1,0:T(8,128)(2,1)}) custom-call(s32[15]{0:T(128)} %pad_add_fusion.2.numbers_ref, s32[3,256]{1,0:T(4,128)} %ids_ref.3, bf16[256,768]{1,0:T(8,128)(2,1)} %get-tuple-element.109.table_ref, ...), custom_call_target="tpu_custom_call" | custom-call | flops 38499999744 | bytes 1 | tf_op jit(solution)/shard_map/pallas_call | solution.py:472
  161.5 4.9 %collective-permute-done.22.refs_2_ = bf16[16,768]{1,0:T(8,128)(2,1)S(1)} collective-permute-done((bf16[16,768]{1,0:T(8,128)(2,1)}, bf16[16,768]{1,0:T(8,128)(2,1)S(1)}, u32[]{:S(2)}, u32[]{:S(2)}) %collective-permute-start.22) | collective-permute-done | bytes 24608 | tf_op jit(solution)/shard_map/ppermute | solution.py:1304
  169.8 9.1 %shard_map.183 = (bf16[96,3072]{1,0:T(8,128)(2,1)}, f32[96,768]{1,0:T(8,128)}, bf16[96,768]{1,0:T(8,128)(2,1)}, bf16[18,32,128]{2,1,0:T(8,128)(2,1)}, f32[2,768]{1,0:T(2,128)}, /*index=5*/bf16[96,768]{1,0:T(8,128)(2,1)}) custom-call(bf16[48,768]{1,0:T(8,128)(2,1)} %get-tuple-element.60.refs_0_, bf16[48,768]{1,0:T(8,128)(2,1)} %copy-done.44, ...), custom_call_target="tpu_custom_call" | custom-call | flops 11000000512 | bytes 1 | tf_op jit(solution)/shard_map/pallas_call | solution.py:745
  178.9 11.4 %shard_map.190 = bf16[16,304,768]{2,1,0:T(8,128)(2,1)} custom-call(s32[15]{0:T(128)} %pad_add_fusion.2.numbers_ref, s32[3,256]{1,0:T(4,128)} %ids_ref.3, bf16[400,7680]{1,0:T(8,128)(2,1)} %get-tuple-element.81.keep_ref, bf16[400,7680]{1,0:T(8,128)(2,1)} %collective-permute-done.37.new_ref, bf16[96,768]{1,0:T(8,128)(2,1)} %get-tuple-element.64.refs_3_.rest_0_), custom_call_target="tpu_custom_call" | custom-call | flops 13200000000 | bytes 1 | tf_op jit(solution)/shard_map/pallas_call | solution.py:595
  195.0 13.6 %all_to_all.25 = bf16[16,32,128]{2,1,0:T(8,128)(2,1)} all-to-all(bf16[16,32,128]{2,1,0:T(8,128)(2,1)S(1)} %pad_select_fusion.1), channel_id=1, replica_groups=mesh['section'=2,'group'=4,'member'=4] {'group','member'}, dimensions={0} | all-to-all | bytes 262144 | tf_op jit(solution)/shard_map/all_to_all | solution.py:1404
  208.6 5.8 %shard_map.184 = bf16[512,384]{1,0:T(8,128)(2,1)} custom-call(s32[512,1]{1,0:T(8,128)} %copy.33.column_ref.refs_0_, s32[1,512]{1,0:T(1,128)} %bitcast.150, bf16[512,384]{1,0:T(8,128)(2,1)} %bitcast.134, bf16[512,128]{1,0:T(8,128)(2,1)} %bitcast.139), custom_call_target="tpu_custom_call" | custom-call | flops 32999999488 | bytes 1 | tf_op jit(solution)/shard_map/pallas_call | solution.py:727
  214.4 15.6 %all_to_all.26.refs_5_ = bf16[16,32,384]{2,1,0:T(8,128)(2,1)S(1)} all-to-all(bf16[16,32,384]{2,1,0:T(8,128)(2,1)} %bitcast.135), channel_id=1, replica_groups=mesh['section'=2,'group'=4,'member'=4] {'group','member'}, dimensions={0} | all-to-all | bytes 786432 | tf_op jit(solution)/shard_map/all_to_all | solution.py:1409
  233.8 5.2 %shard_map.185 = (bf16[96,2304]{1,0:T(8,128)(2,1)}, bf16[112,768]{1,0:T(8,128)(2,1)}, f32[4,768]{1,0:T(4,128)}) custom-call(f32[96,768]{1,0:T(8,128)} %get-tuple-element.52.refs_0_, f32[96,768]{1,0:T(8,128)} %get-tuple-element.67.refs_1_, f32[2,768]{1,0:T(2,128)} %get-tuple-element.68.refs_2_, f32[2,768]{1,0:T(2,128)} %bitcast.146, ...), custom_call_target="tpu_custom_call" | custom-call | flops 6600000000 | bytes 1 | tf_op jit(solution)/shard_map/pallas_call | solution.py:745
  245.2 4.0 collective-permute-start.30
  249.1 5.1 %shard_map.186 = (bf16[96,8256]{1,0:T(8,128)(2,1)}, bf16[96,8256]{1,0:T(8,128)(2,1)}, bf16[96,8256]{1,0:T(8,128)(2,1)}, bf16[96,8256]{1,0:T(8,128)(2,1)}) custom-call(s32[1]{0:T(128)} %bitcast.40.refs_0_, bf16[4,96,1152]{2,1,0:T(8,128)(2,1)} %get-tuple-element.58.refs_1_, bf16[4,96,192]{2,1,0:T(8,128)(2,1)} %get-tuple-element.59.refs_2_, ...), custom_call_target="tpu_custom_call" | custom-call | flops 4400000000 | bytes 1 | tf_op jit(solution)/shard_map/pallas_call | solution.py:745
  259.1 4.5 %collective-permute-start.27 = (bf16[96,8256]{1,0:T(8,128)(2,1)}, bf16[96,8256]{1,0:T(8,128)(2,1)}, u32[]{:S(2)}, u32[]{:S(2)}) collective-permute-start(bf16[96,8256]{1,0:T(8,128)(2,1)} %get-tuple-element.74), channel_id=1, source_target_pairs={{0,3},{1,2},{2,1},{3,0},{4,7},{5,6},{6,5},{7,4},{8,11},{9,10},{10,... | collective-permute-start | bytes 4755464 | tf_op jit(solution)/shard_map/ppermute | solution.py:1304
  266.8 4.5 %shard_map.187 = (bf16[4,208,768]{2,1,0:T(8,128)(2,1)}, bf16[256,768]{1,0:T(8,128)(2,1)}) custom-call(s32[1]{0:T(128)} %bitcast.33.refs_0_, s32[384,1]{1,0:T(8,128)} %reshape.458.refs_1_, bf16[384,768]{1,0:T(8,128)(2,1)} %get-tuple-element.75.refs_2_, bf16[768,768]{1,0:T(8,128)(2,1)} %get-tuple-element.76.refs_3_, ...), custom_call_target="tpu_custom_call" | custom-call | flops 6600000000 | bytes 1 | tf_op jit(solution)/shard_map/pallas_call | solution.py:745
  271.3 12.9 %reduce-scatter.2.cloned.1.call-done = bf16[4,304,768]{2,1,0:T(8,128)(2,1)} async-done(((bf16[16,304,768]{2,1,0:T(8,128)(2,1)}), bf16[4,304,768]{2,1,0:T(8,128)(2,1)}) %reduce-scatter.2.cloned.1.call-update) | async-done | bytes 1867792 | tf_op jit(solution)/shard_map/reduce_scatter | solution.py:1581
  292.0 18.0 %collective-permute-done.27.refs_4_ = bf16[96,8256]{1,0:T(8,128)(2,1)} collective-permute-done((bf16[96,8256]{1,0:T(8,128)(2,1)}, bf16[96,8256]{1,0:T(8,128)(2,1)}, u32[]{:S(2)}, u32[]{:S(2)}) %collective-permute-start.27) | collective-permute-done | bytes 1585184 | tf_op jit(solution)/shard_map/ppermute | solution.py:1304
  310.1 6.7 %shard_map.188 = (bf16[2,576,768]{2,1,0:T(8,128)(2,1)}, bf16[2,576,768]{2,1,0:T(8,128)(2,1)}) custom-call(s32[1]{0:T(128)} %bitcast.39.refs_0_, bf16[96,8256]{1,0:T(8,128)(2,1)} %get-tuple-element.71.refs_1_, bf16[96,8256]{1,0:T(8,128)(2,1)} %copy-done.32, bf16[96,8256]{1,0:T(8,128)(2,1)} %collective-permute-done.26.refs_3_, ...), custom_call_target="tpu_custom_call" | custom-call | flops 8800000000 | bytes 1 | tf_op jit(solution)/shard_map/pallas_call | solution.py:745
  329.1 16.4 %collective-permute-done.39 = bf16[304,768]{1,0:T(8,128)(2,1)S(1)} collective-permute-done((bf16[304,768]{1,0:T(8,128)(2,1)}, bf16[304,768]{1,0:T(8,128)(2,1)S(1)}, u32[]{:S(2)}, u32[]{:S(2)}) %collective-permute-start.39) | collective-permute-done | bytes 466976 | tf_op jit(solution)/shard_map/ppermute | solution.py:1521
  348.2 4.0 collective-permute-start.40
  355.4 5.3 %collective-permute-start.36 = (bf16[576,768]{1,0:T(8,128)(2,1)}, bf16[576,768]{1,0:T(8,128)(2,1)}, u32[]{:S(2)}, u32[]{:S(2)}) collective-permute-start(bf16[576,768]{1,0:T(8,128)(2,1)} %shard_map.189), channel_id=1, source_target_pairs={{0,8},{1,9},{2,10},{3,11},{4,12},{5,13},{6,14},{7,15},{8,0},{9,1},... | collective-permute-start | bytes 2654216 | tf_op jit(solution)/shard_map/ppermute | solution.py:1304
  362.9 3.8 all-to-all-start.4
  368.5 20.6 %all-to-all-done.4.refs_7_ = bf16[16,16,768]{2,1,0:T(8,128)(2,1)S(1)} async-done(((bf16[16,16,768]{2,1,0:T(8,128)(2,1)}), bf16[16,16,768]{2,1,0:T(8,128)(2,1)S(1)}, u32[]{:S(2)}, u32[]{:S(2)}) %all-to-all-start.4) | async-done | bytes 393248 | tf_op jit(solution)/shard_map/all_to_all | solution.py:1595
  389.9 5.2 %shard_map.192 = (f32[192,768]{1,0:T(8,128)}, f32[48,3072]{1,0:T(8,128)}, f32[48,2304]{1,0:T(8,128)}, f32[48,768]{1,0:T(8,128)}, f32[16,768]{1,0:T(8,128)}, /*index=5*/f32[16,768]{1,0:T(8,128)}, f32[192,768]{1,0:T(8,128)}) custom-call(s32[1]{0:T(128)} %bitcast.33.refs_0_, s32[1]{0:T(128)} %bitcast.38.refs_1_, ...), custom_call_target="tpu_custom_call" | custom-call | flops 4400000000 | bytes 1 | tf_op jit(solution)/shard_map/pallas_call | solution.py:745
  (226 shorter events, 112.3 us)
Async XLA Ops:
  7.2 14.0 %collective-permute-start.3 = (bf16[256,768]{1,0:T(8,128)(2,1)}, bf16[256,768]{1,0:T(8,128)(2,1)S(1)}, u32[]{:S(2)}, u32[]{:S(2)}) collective-permute-start(bf16[256,768]{1,0:T(8,128)(2,1)} %bitcast.136), channel_id=1, source_target_pairs={{0,16},{16,0},{1,17},{17,1},{2,18},{18,2},{3,19},{19,3},{4,20},{20... | collective-permute-start | bytes 1179656 | tf_op jit(solution)/shard_map/ppermute | solution.py:1308
  13.0 10.1 %collective-permute-start.4 = (bf16[192,768]{1,0:T(8,128)(2,1)}, bf16[192,768]{1,0:T(8,128)(2,1)S(1)}, u32[]{:S(2)}, u32[]{:S(2)}) collective-permute-start(bf16[192,768]{1,0:T(8,128)(2,1)} %refs_3_.1), channel_id=1, source_target_pairs={{0,1},{1,0},{2,3},{3,2},{4,5},{5,4},{6,7},{7,6},{8,9},{9,8},{10,11... | collective-permute-start | bytes 884744 | tf_op jit(solution)/shard_map/ppermute | solution.py:1365
  15.7 14.9 %collective-permute-start.5 = (bf16[192,768]{1,0:T(8,128)(2,1)}, bf16[192,768]{1,0:T(8,128)(2,1)S(1)}, u32[]{:S(2)}, u32[]{:S(2)}) collective-permute-start(bf16[192,768]{1,0:T(8,128)(2,1)} %refs_3_.1), channel_id=1, source_target_pairs={{0,2},{1,3},{2,0},{3,1},{4,6},{5,7},{6,4},{7,5},{8,10},{9,11},{10,... | collective-permute-start | bytes 884744 | tf_op jit(solution)/shard_map/ppermute | solution.py:1365
  17.3 13.2 %collective-permute-start.6 = (bf16[192,768]{1,0:T(8,128)(2,1)}, bf16[192,768]{1,0:T(8,128)(2,1)S(1)}, u32[]{:S(2)}, u32[]{:S(2)}) collective-permute-start(bf16[192,768]{1,0:T(8,128)(2,1)} %refs_3_.1), channel_id=1, source_target_pairs={{0,3},{1,2},{2,1},{3,0},{4,7},{5,6},{6,5},{7,4},{8,11},{9,10},{10,... | collective-permute-start | bytes 884744 | tf_op jit(solution)/shard_map/ppermute | solution.py:1365
  40.5 13.5 %collective-permute-start.10 = (bf16[96,768]{1,0:T(8,128)(2,1)S(1)}, bf16[96,768]{1,0:T(8,128)(2,1)S(1)}, u32[]{:S(2)}, u32[]{:S(2)}) collective-permute-start(bf16[96,768]{1,0:T(8,128)(2,1)S(1)} %get-tuple-element.110), channel_id=1, source_target_pairs={{0,12},{1,13},{2,14},{3,15},{4,8},{5,9},{6,10},{7,11},{8,4},{9,5},... | collective-permute-start | bytes 442376 | tf_op jit(solution)/shard_map/ppermute | solution.py:1304
  45.9 9.3 %collective-permute-start.8 = (bf16[96,768]{1,0:T(8,128)(2,1)S(1)}, bf16[96,768]{1,0:T(8,128)(2,1)S(1)}, u32[]{:S(2)}, u32[]{:S(2)}) collective-permute-start(bf16[96,768]{1,0:T(8,128)(2,1)S(1)} %get-tuple-element.112), channel_id=1, source_target_pairs={{0,4},{1,5},{2,6},{3,7},{4,0},{5,1},{6,2},{7,3},{8,12},{9,13},{10,... | collective-permute-start | bytes 442376 | tf_op jit(solution)/shard_map/ppermute | solution.py:1304
  47.9 9.5 %collective-permute-start.9 = (bf16[96,768]{1,0:T(8,128)(2,1)S(1)}, bf16[96,768]{1,0:T(8,128)(2,1)S(1)}, u32[]{:S(2)}, u32[]{:S(2)}) collective-permute-start(bf16[96,768]{1,0:T(8,128)(2,1)S(1)} %get-tuple-element.111), channel_id=1, source_target_pairs={{0,8},{1,9},{2,10},{3,11},{4,12},{5,13},{6,14},{7,15},{8,0},{9,1},... | collective-permute-start | bytes 442376 | tf_op jit(solution)/shard_map/ppermute | solution.py:1304
  50.6 76.1 %collective-permute-start.18 = (bf16[768,3072]{1,0:T(8,128)(2,1)}, bf16[768,3072]{1,0:T(8,128)(2,1)}, u32[]{:S(2)}, u32[]{:S(2)}) collective-permute-start(bf16[768,3072]{1,0:T(8,128)(2,1)} %bitcast.158), channel_id=1, source_target_pairs={{16,0},{17,1},{18,2},{19,3},{20,4},{21,5},{22,6},{23,7},{24,8},{25... | collective-permute-start | bytes 14155784 | tf_op jit(solution)/shard_map/ppermute | solution.py:1304
  51.9 74.9 %collective-permute-start.19 = (bf16[3072,768]{1,0:T(8,128)(2,1)}, bf16[3072,768]{1,0:T(8,128)(2,1)}, u32[]{:S(2)}, u32[]{:S(2)}) collective-permute-start(bf16[3072,768]{1,0:T(8,128)(2,1)} %bitcast.162), channel_id=1, source_target_pairs={{16,0},{17,1},{18,2},{19,3},{20,4},{21,5},{22,6},{23,7},{24,8},{25... | collective-permute-start | bytes 14155784 | tf_op jit(solution)/shard_map/ppermute | solution.py:1304
  54.0 72.8 %collective-permute-start.16 = (bf16[768,2304]{1,0:T(8,128)(2,1)}, bf16[768,2304]{1,0:T(8,128)(2,1)}, u32[]{:S(2)}, u32[]{:S(2)}) collective-permute-start(bf16[768,2304]{1,0:T(8,128)(2,1)} %bitcast.166), channel_id=1, source_target_pairs={{16,0},{17,1},{18,2},{19,3},{20,4},{21,5},{22,6},{23,7},{24,8},{25... | collective-permute-start | bytes 10616840 | tf_op jit(solution)/shard_map/ppermute | solution.py:1304
  73.2 19.0 %all-to-all-start = ((bf16[16,32,384]{2,1,0:T(8,128)(2,1)}), bf16[16,32,384]{2,1,0:T(8,128)(2,1)S(1)}, u32[]{:S(2)}, u32[]{:S(2)}) async-start(bf16[16,32,384]{2,1,0:T(8,128)(2,1)} %pad_select_fusion), calls=%async_computation | async-start | bytes 786432 | tf_op jit(solution)/shard_map/all_to_all | solution.py:1404
  97.3 11.4 %all-to-all-start.1 = ((bf16[16,32,128]{2,1,0:T(8,128)(2,1)}), bf16[16,32,128]{2,1,0:T(8,128)(2,1)S(1)}, u32[]{:S(2)}, u32[]{:S(2)}) async-start(bf16[16,32,128]{2,1,0:T(8,128)(2,1)} %bitcast.138), calls=%async_computation.1 | async-start | bytes 262144 | tf_op jit(solution)/shard_map/all_to_all | solution.py:1409
  101.0 183.3 %reduce-scatter.2.cloned.1.call-start = ((), (), s32[]{:S(2)}) async-start(), calls=%async_computation.6 | async-start | bytes 9338880 | tf_op jit(solution)/shard_map/reduce_scatter | solution.py:1581
  101.0 20.9 %collective-permute-start.17 = (bf16[768,768]{1,0:T(8,128)(2,1)S(1)}, bf16[768,768]{1,0:T(8,128)(2,1)S(1)}, u32[]{:S(2)}, u32[]{:S(2)}) collective-permute-start(bf16[768,768]{1,0:T(8,128)(2,1)S(1)} %bitcast.173), channel_id=1, source_target_pairs={{16,0},{17,1},{18,2},{19,3},{20,4},{21,5},{22,6},{23,7},{24,8},{25... | collective-permute-start | bytes 3538952 | tf_op jit(solution)/shard_map/ppermute | solution.py:1304
  158.8 20.1 %collective-permute-start.37 = (bf16[400,7680]{1,0:T(8,128)(2,1)}, bf16[400,7680]{1,0:T(8,128)(2,1)}, u32[]{:S(2)}, u32[]{:S(2)}) collective-permute-start(bf16[400,7680]{1,0:T(8,128)(2,1)} %get-tuple-element.82), channel_id=1, source_target_pairs={{0,16},{16,0},{1,17},{17,1},{2,18},{18,2},{3,19},{19,3},{4,20},{20... | collective-permute-start | bytes 18432008 | tf_op jit(solution)/shard_map/ppermute | solution.py:1308
  158.9 10.2 %collective-permute-start.21 = (bf16[48,768]{1,0:T(8,128)(2,1)}, bf16[48,768]{1,0:T(8,128)(2,1)S(1)}, u32[]{:S(2)}, u32[]{:S(2)}) collective-permute-start(bf16[48,768]{1,0:T(8,128)(2,1)} %get-tuple-element.60.refs_0_), channel_id=1, source_target_pairs={{16,0},{17,1},{18,2},{19,3},{20,4},{21,5},{22,6},{23,7},{24,8},{25... | collective-permute-start | bytes 221192 | tf_op jit(solution)/shard_map/ppermute | solution.py:1304
  239.0 20.0 %collective-permute-start.28 = (bf16[112,768]{1,0:T(8,128)(2,1)}, bf16[112,768]{1,0:T(8,128)(2,1)S(1)}, u32[]{:S(2)}, u32[]{:S(2)}) collective-permute-start(bf16[112,768]{1,0:T(8,128)(2,1)} %get-tuple-element.77.refs_5_), channel_id=1, source_target_pairs={{0,4},{1,5},{2,6},{3,7},{4,0},{5,1},{6,2},{7,3},{8,12},{9,13},{10,... | collective-permute-start | bytes 516104 | tf_op jit(solution)/shard_map/ppermute | solution.py:1304
  242.0 21.5 %collective-permute-start.29 = (bf16[112,768]{1,0:T(8,128)(2,1)}, bf16[112,768]{1,0:T(8,128)(2,1)S(1)}, u32[]{:S(2)}, u32[]{:S(2)}) collective-permute-start(bf16[112,768]{1,0:T(8,128)(2,1)} %get-tuple-element.77.refs_5_), channel_id=1, source_target_pairs={{0,8},{1,9},{2,10},{3,11},{4,12},{5,13},{6,14},{7,15},{8,0},{9,1},... | collective-permute-start | bytes 516104 | tf_op jit(solution)/shard_map/ppermute | solution.py:1304
  245.2 18.4 %collective-permute-start.30 = (bf16[112,768]{1,0:T(8,128)(2,1)}, bf16[112,768]{1,0:T(8,128)(2,1)S(1)}, u32[]{:S(2)}, u32[]{:S(2)}) collective-permute-start(bf16[112,768]{1,0:T(8,128)(2,1)} %get-tuple-element.77.refs_5_), channel_id=1, source_target_pairs={{0,12},{1,13},{2,14},{3,15},{4,8},{5,9},{6,10},{7,11},{8,4},{9,5},... | collective-permute-start | bytes 516104 | tf_op jit(solution)/shard_map/ppermute | solution.py:1304
  254.3 37.7 %collective-permute-start.25 = (bf16[96,8256]{1,0:T(8,128)(2,1)}, bf16[96,8256]{1,0:T(8,128)(2,1)S(1)}, u32[]{:S(2)}, u32[]{:S(2)}) collective-permute-start(bf16[96,8256]{1,0:T(8,128)(2,1)} %get-tuple-element.72), channel_id=1, source_target_pairs={{0,1},{1,0},{2,3},{3,2},{4,5},{5,4},{6,7},{7,6},{8,9},{9,8},{10,11... | collective-permute-start | bytes 4755464 | tf_op jit(solution)/shard_map/ppermute | solution.py:1304
  256.2 35.8 %collective-permute-start.26 = (bf16[96,8256]{1,0:T(8,128)(2,1)}, bf16[96,8256]{1,0:T(8,128)(2,1)}, u32[]{:S(2)}, u32[]{:S(2)}) collective-permute-start(bf16[96,8256]{1,0:T(8,128)(2,1)} %get-tuple-element.73), channel_id=1, source_target_pairs={{0,2},{1,3},{2,0},{3,1},{4,6},{5,7},{6,4},{7,5},{8,10},{9,11},{10,... | collective-permute-start | bytes 4755464 | tf_op jit(solution)/shard_map/ppermute | solution.py:1304
  259.1 51.0 %collective-permute-start.27 = (bf16[96,8256]{1,0:T(8,128)(2,1)}, bf16[96,8256]{1,0:T(8,128)(2,1)}, u32[]{:S(2)}, u32[]{:S(2)}) collective-permute-start(bf16[96,8256]{1,0:T(8,128)(2,1)} %get-tuple-element.74), channel_id=1, source_target_pairs={{0,3},{1,2},{2,1},{3,0},{4,7},{5,6},{6,5},{7,4},{8,11},{9,10},{10,... | collective-permute-start | bytes 4755464 | tf_op jit(solution)/shard_map/ppermute | solution.py:1304
  286.8 33.4 %collective-permute-start.38 = (bf16[2,304,768]{2,1,0:T(8,128)(2,1)S(1)}, bf16[2,304,768]{2,1,0:T(8,128)(2,1)}, u32[]{:S(2)}, u32[]{:S(2)}) collective-permute-start(bf16[2,304,768]{2,1,0:T(8,128)(2,1)S(1)} %get-tuple-element.102), channel_id=1, source_target_pairs={{0,4},{1,5},{2,6},{3,7},{4,0},{5,1},{6,2},{7,3},{8,12},{9,13},{10,... | collective-permute-start | bytes 2801672 | tf_op jit(solution)/shard_map/ppermute | solution.py:1521
  316.8 35.4 %collective-permute-start.32 = (bf16[2,576,768]{2,1,0:T(8,128)(2,1)}, bf16[2,576,768]{2,1,0:T(8,128)(2,1)}, u32[]{:S(2)}, u32[]{:S(2)}) collective-permute-start(bf16[2,576,768]{2,1,0:T(8,128)(2,1)} %get-tuple-element.80), channel_id=1, source_target_pairs={{0,4},{1,5},{2,6},{3,7},{4,0},{5,1},{6,2},{7,3},{8,12},{9,13},{10,... | collective-permute-start | bytes 5308424 | tf_op jit(solution)/shard_map/ppermute | solution.py:1304
  322.3 23.2 %collective-permute-start.39 = (bf16[304,768]{1,0:T(8,128)(2,1)}, bf16[304,768]{1,0:T(8,128)(2,1)S(1)}, u32[]{:S(2)}, u32[]{:S(2)}) collective-permute-start(bf16[304,768]{1,0:T(8,128)(2,1)} %shard_map.191), channel_id=1, source_target_pairs={{0,8},{1,9},{2,10},{3,11},{4,12},{5,13},{6,14},{7,15},{8,0},{9,1},... | collective-permute-start | bytes 1400840 | tf_op jit(solution)/shard_map/ppermute | solution.py:1521
  325.6 22.6 %collective-permute-start.33 = (bf16[208,768]{1,0:T(8,128)(2,1)S(1)}, bf16[208,768]{1,0:T(8,128)(2,1)S(1)}, u32[]{:S(2)}, u32[]{:S(2)}) collective-permute-start(bf16[208,768]{1,0:T(8,128)(2,1)S(1)} %get-tuple-element.107), channel_id=1, source_target_pairs={{0,1},{1,0},{2,3},{3,2},{4,5},{5,4},{6,7},{7,6},{8,9},{9,8},{10,11... | collective-permute-start | bytes 958472 | tf_op jit(solution)/shard_map/ppermute | solution.py:1593
  326.1 26.0 %collective-permute-start.34 = (bf16[208,768]{1,0:T(8,128)(2,1)S(1)}, bf16[208,768]{1,0:T(8,128)(2,1)S(1)}, u32[]{:S(2)}, u32[]{:S(2)}) collective-permute-start(bf16[208,768]{1,0:T(8,128)(2,1)S(1)} %get-tuple-element.106), channel_id=1, source_target_pairs={{0,2},{1,3},{2,0},{3,1},{4,6},{5,7},{6,4},{7,5},{8,10},{9,11},{10,... | collective-permute-start | bytes 958472 | tf_op jit(solution)/shard_map/ppermute | solution.py:1593
  326.7 25.5 %collective-permute-start.35 = (bf16[208,768]{1,0:T(8,128)(2,1)S(1)}, bf16[208,768]{1,0:T(8,128)(2,1)}, u32[]{:S(2)}, u32[]{:S(2)}) collective-permute-start(bf16[208,768]{1,0:T(8,128)(2,1)S(1)} %get-tuple-element.105), channel_id=1, source_target_pairs={{0,3},{1,2},{2,1},{3,0},{4,7},{5,6},{6,5},{7,4},{8,11},{9,10},{10,... | collective-permute-start | bytes 958472 | tf_op jit(solution)/shard_map/ppermute | solution.py:1593
  345.5 16.6 %collective-permute-start.41 = (bf16[256,768]{1,0:T(8,128)(2,1)S(1)}, bf16[256,768]{1,0:T(8,128)(2,1)S(1)}, u32[]{:S(2)}, u32[]{:S(2)}) collective-permute-start(bf16[256,768]{1,0:T(8,128)(2,1)S(1)} %copy-done.6), channel_id=1, source_target_pairs={{16,0},{17,1},{18,2},{19,3},{20,4},{21,5},{22,6},{23,7},{24,8},{25... | collective-permute-start | bytes 1179656 | tf_op jit(solution)/shard_map/ppermute | solution.py:1304
  348.2 40.9 %collective-permute-start.40 = (f32[304,768]{1,0:T(8,128)S(1)}, f32[304,768]{1,0:T(8,128)}, u32[]{:S(2)}, u32[]{:S(2)}) collective-permute-start(f32[304,768]{1,0:T(8,128)S(1)} %fusion.refs_5_), channel_id=1, source_target_pairs={{0,16},{1,17},{2,18},{3,19},{4,20},{5,21},{6,22},{7,23},{8,24},{9,... | collective-permute-start | bytes 2801672 | tf_op jit(solution)/shard_map/ppermute | solution.py:1304
  355.4 33.7 %collective-permute-start.36 = (bf16[576,768]{1,0:T(8,128)(2,1)}, bf16[576,768]{1,0:T(8,128)(2,1)}, u32[]{:S(2)}, u32[]{:S(2)}) collective-permute-start(bf16[576,768]{1,0:T(8,128)(2,1)} %shard_map.189), channel_id=1, source_target_pairs={{0,8},{1,9},{2,10},{3,11},{4,12},{5,13},{6,14},{7,15},{8,0},{9,1},... | collective-permute-start | bytes 2654216 | tf_op jit(solution)/shard_map/ppermute | solution.py:1304
  362.9 26.1 %all-to-all-start.4 = ((bf16[16,16,768]{2,1,0:T(8,128)(2,1)}), bf16[16,16,768]{2,1,0:T(8,128)(2,1)S(1)}, u32[]{:S(2)}, u32[]{:S(2)}) async-start(bf16[16,16,768]{2,1,0:T(8,128)(2,1)} %bitcast.51), calls=%async_computation.5 | async-start | bytes 786432 | tf_op jit(solution)/shard_map/all_to_all | solution.py:1595
  (63 other events, 435.5 us)
Sparse Core Ops, SparseCore 0:
  190.5 93.7 reduce-scatter.1

commit v5 on v4

--- a/solution.py
+++ b/solution.py
@@ -873,7 +873,7 @@
     def kernel(stream_ref, gains_ref, biases_ref, out_hbm, expand_hbm, contract_hbm, *rest):
         block_refs, rest = rest[:n], rest[n:]
         (attended_ref, middle_ref, normed_two_ref, slope_ref, hidden_ref, sent_ref) = rest[:6]
-        share_ref, edge_ref, near_ref, w_out, w_expand, w_contract, sems = rest[6:]
+        share_ref, other_share_ref, edge_ref, near_ref, w_out, w_expand, w_contract, sems = rest[6:]
         loads = [
             pltpu.make_async_copy(out_hbm, w_out, sems.at[0]),
             pltpu.make_async_copy(expand_hbm, w_expand, sems.at[1]),
@@ -905,8 +905,8 @@
             edge_ref[m : m + 1, :] = sent[stop - 1 : stop]
             near_ref[m * half : (m + 1) * half, :] = sent[stop - half - 1 : stop - 1]
         strided(hidden_ref[...], share_ref, SPAN, 0)
-        strided(normed_two_ref[...], share_ref, SPAN, hidden_width // SPAN)
-        strided(attended_ref[...], share_ref, SPAN, (hidden_width + width) // SPAN)
+        strided(normed_two_ref[...], other_share_ref, SPAN, 0)
+        strided(attended_ref[...], other_share_ref, SPAN, width // SPAN)
 
     return call(
         kernel,
@@ -919,11 +919,12 @@
             shaped(rows, hidden_width),
             shaped(rows, hidden_width),
             shaped(rows, width),
-            shaped(SPAN, rows, (hidden_width + 2 * width) // SPAN),
+            shaped(SPAN, rows, hidden_width // SPAN),
+            shaped(SPAN, rows, 2 * width // SPAN),
             shaped(SMALL_ROWS, width),
             shaped(batches * half, width),
         ],
-        [WHOLE] * 9,
+        [WHOLE] * 10,
         [
             pltpu.VMEM(heads_out.shape, bf16),
             pltpu.VMEM(expand.shape, bf16),
@@ -1103,78 +1104,123 @@
         pltpu.make_async_copy(buffer.at[0], targets[k], sems.at[k]).wait()
 
 
-def plane_parts(hidden_width, width):
-    starts, start = {}, 0
-    for name, size in (
-        ("hidden", hidden_width // SPAN),
-        ("normed_two", width // SPAN),
-        ("attended", width // SPAN),
-        ("branch", width),
-        ("attend_branch", width),
-        ("upward", hidden_width),
-        ("mixed", 3 * width),
-        ("normed", width // SPAN),
-    ):
-        starts[name] = slice(start, start + size)
-        start += size
-    return starts, start
-
-
-def pack(member, feed_share, normed_share, branch, attend_branch, upward, mixed, deps=()):
-    rows, width = branch.shape
-    hidden_width = upward.shape[1]
-    parts, whole = plane_parts(hidden_width, width)
-    own = slice(0, feed_share.shape[2])
-
-    def kernel(member_ref, feed_ref, normed_ref, branch_ref, attend_ref, upward_ref, mixed_ref, *sent_refs):
+def pack_columns(hidden_width, width):
+    deep, thin = hidden_width // SPAN, width // SPAN
+    first = [
+        (slice(0, deep), slice(deep, deep + width)),
+        (slice(deep + width, deep + width + thin), slice(deep + width + thin, deep + 4 * width + thin)),
+    ]
+    right = 2 * thin
+    second = [
+        (slice(0, thin), slice(right, right + hidden_width)),
+        (slice(thin, right), slice(right + hidden_width, right + hidden_width + width)),
+    ]
+    return first, second, max(first[-1][1].stop, second[-1][1].stop)
+
+
+def pack_second(member, share, attend_branch, upward, whole, deps=()):
+    rows, width = attend_branch.shape
+    own, hidden_width = share.shape[2], upward.shape[1]
+
+    def kernel(member_ref, share_ref, attend_ref, upward_ref, out_ref):
         for k in range(SPAN):
-            sent_refs[k][0:rows, own] = feed_ref[member_ref[0] ^ k]
-            sent_refs[k][0:rows, parts["branch"]] = branch_ref[...]
-            sent_refs[k][0:rows, parts["attend_branch"]] = attend_ref[...]
-            sent_refs[k][0:rows, parts["upward"]] = upward_ref[...]
-            sent_refs[k][0:rows, parts["mixed"]] = mixed_ref[...]
-            sent_refs[k][0:rows, parts["normed"]] = normed_ref[member_ref[0] ^ k]
+            out_ref[k, :, 0:own] = share_ref[member_ref[0] ^ k]
+            out_ref[k, :, own : own + hidden_width] = upward_ref[...]
+            out_ref[k, :, own + hidden_width : own + hidden_width + width] = attend_ref[...]
 
     return call(
         kernel,
-        (member, feed_share, normed_share, branch, attend_branch, upward, mixed),
-        [SCALARS] + [WHOLE] * 6,
-        [shaped(rows, whole)] * SPAN,
-        [WHOLE] * SPAN,
+        (member, share, attend_branch, upward),
+        [SCALARS] + [WHOLE] * 3,
+        shaped(SPAN, rows, whole),
+        WHOLE,
+        deps=deps,
+        micros=3,
+    )
+
+
+def pack(section, member, share, normed_share, branch, mixed, second, passed, deps=()):
+    rows, width = branch.shape
+    deep, thin, whole = share.shape[2], normed_share.shape[2], second.shape[2]
+
+    def kernel(
+        section_ref, member_ref, share_ref, normed_ref, branch_ref, mixed_ref, passed_ref,
+        second_ref, *rest,
+    ):
+        sent_refs, same_ref, sems = rest[:SPAN], rest[SPAN], rest[SPAN + 1]
+        same_ref[...] = passed_ref[...]
+
+        @pl.when(section_ref[0] == 0)
+        def _():
+            for k in range(SPAN):
+                sent_refs[k][:, 0:deep] = share_ref[member_ref[0] ^ k]
+                sent_refs[k][:, deep : deep + width] = branch_ref[...]
+                sent_refs[k][:, deep + width : deep + width + thin] = normed_ref[member_ref[0] ^ k]
+                sent_refs[k][:, deep + width + thin : deep + 4 * width + thin] = mixed_ref[...]
+
+        @pl.when(section_ref[0] != 0)
+        def _():
+            copies = [
+                pltpu.make_async_copy(second_ref.at[k], sent_refs[k], sems.at[k])
+                for k in range(SPAN)
+            ]
+            for copy in copies:
+                copy.start()
+            for copy in copies:
+                copy.wait()
+
+    return call(
+        kernel,
+        (section, member, share, normed_share, branch, mixed, passed, second),
+        [SCALARS] * 2 + [WHOLE] * 5 + [ANY],
+        [shaped(rows, whole)] * SPAN + [shaped(*passed.shape)],
+        [WHOLE] * (SPAN + 1),
+        [pltpu.SemaphoreType.DMA((SPAN,))],
         deps=deps,
         micros=4,
     )
 
 
-def plane_gradients(group, sent, rows, hidden_width, width, deps=()):
-    parts, _ = plane_parts(hidden_width, width)
-    deep, thin = hidden_width // GROUPS, width // GROUPS
-    chunks = hidden_width // width
-    block = deep + (chunks + 4) * thin
-
-    def kernel(group_ref, *refs):
+def plane_gradients(section, group, sent, hidden_width, width, deps=()):
+    halves = pack_columns(hidden_width, width)[:2]
+    rows_of = [
+        sum(
+            (left.stop - left.start) // 4 * ((right.stop - right.start) // width)
+            for left, right in pairs
+        )
+        for pairs in halves
+    ]
+    block = max(rows_of)
+
+    def kernel(section_ref, group_ref, *refs):
         sent_refs, (keep_ref, leave_ref, buffer, sems) = refs[: len(sent)], refs[len(sent) :]
 
-        def columns(name, chunk=None):
-            at = parts[name]
-            if chunk is not None:
-                at = slice(at.start + chunk * width, at.start + (chunk + 1) * width)
-            return jnp.concatenate([ref[0:rows, at] for ref in sent_refs], axis=0)
-
-        def store(part, start, size):
-            for j in range(4):
-                buffer[j, start : start + size, :] = part[j * size : (j + 1) * size].astype(bf16)
-
-        store(transposed_product(columns("hidden"), columns("branch")), 0, deep)
-        left, at = columns("normed_two"), deep
-        for c in range(chunks):
-            store(transposed_product(left, columns("upward", c)), at, thin)
-            at += thin
-        store(transposed_product(columns("attended"), columns("attend_branch")), at, thin)
-        left = columns("normed")
-        for c in range(3):
-            at += thin
-            store(transposed_product(left, columns("mixed", c)), at, thin)
+        def columns(at):
+            return jnp.concatenate([ref[:, at] for ref in sent_refs], axis=0)
+
+        def fill(pairs):
+            start = 0
+            for left, right in pairs:
+                former, size = columns(left), (left.stop - left.start) // 4
+                for first in range(right.start, right.stop, width):
+                    part = transposed_product(former, columns(slice(first, first + width)))
+                    for j in range(4):
+                        buffer[j, start : start + size, :] = part[
+                            j * size : (j + 1) * size
+                        ].astype(bf16)
+                    start += size
+            if start < block:
+                for j in range(4):
+                    buffer[j, start:block, :] = jnp.zeros((block - start, width), bf16)
+
+        @pl.when(section_ref[0] == 0)
+        def _():
+            fill(halves[0])
+
+        @pl.when(section_ref[0] != 0)
+        def _():
+            fill(halves[1])
+
         for j in range(4):
             mine = ((group_ref[0] ^ j) & 1) == 0
 
@@ -1191,13 +1237,32 @@
 
     return call(
         kernel,
-        (group, *sent),
-        [SCALARS] + [WHOLE] * len(sent),
+        (section, group, *sent),
+        [SCALARS] * 2 + [WHOLE] * len(sent),
         [shaped(2, block, width)] * 2,
         [ANY] * 2,
         [pltpu.VMEM((4, block, width), bf16), pltpu.SemaphoreType.DMA((4,))],
         deps=deps,
-        micros=8,
+        micros=6,
+    )
+
+
+def by_parity(parity, sums, deps=()):
+    count, rows, width = sums.shape
+
+    def kernel(parity_ref, sums_ref, kept_ref, leaving_ref):
+        for k in range(count // 2):
+            kept_ref[k] = sums_ref[2 * k + parity_ref[0]]
+            leaving_ref[k] = sums_ref[2 * k + 1 - parity_ref[0]]
+
+    return call(
+        kernel,
+        (parity, sums),
+        [SCALARS, WHOLE],
+        [shaped(count // 2, rows, width)] * 2,
+        [WHOLE] * 2,
+        deps=deps,
+        micros=3,
     )
 
 
@@ -1230,35 +1295,31 @@
     )(which, kept, near, *deps)
 
 
-def finish(section, upper, deep, shard, room, block, own, crossed, table_parts, patch_parts):
-    width = own.shape[1]
+def finish(section, deep, shard, room, own_global, own_local, crossed, fars, table_parts, patch_parts):
+    width = own_local.shape[1]
     chunks = deep // shard
     p = len(patch_parts)
 
-    def kernel(section_ref, upper_ref, kept_ref, near_ref, far_ref, own_ref, crossed_ref, table_ref, *refs):
+    def kernel(section_ref, global_ref, local_ref, crossed_ref, table_ref, *refs):
+        (global_one, global_two, local_one, local_two), refs = refs[:4], refs[4:]
         patch_refs = refs[:p]
         contract, expand, ins, out, table, small, patch = refs[p:]
-        heads_start = deep + (chunks + 1) * shard
-        mine = upper_ref[0]
-
-        def total(start, size):
-            at = slice(start, start + size)
-            return kept_ref[mine, at].astype(f32) + near_ref[mine, at].astype(f32) + far_ref[at].astype(f32)
-
-        def taken(ref, start, size):
-            return ref[start : start + size, :]
+
+        def total(some, start, size):
+            return sum(ref[start : start + size, :].astype(f32) for ref in some)
 
         total_patch = sum(ref[...].astype(f32) for ref in patch_refs)
         patch[...] = total_patch[: patch.shape[0]]
 
         @pl.when(section_ref[0] == 0)
         def _():
-            contract[...] = total(0, deep)
+            one, two = (global_ref, global_one), (crossed_ref, global_two)
+            contract[...] = total(one, 0, deep)
+            for c in range(3):
+                ins[:, c * width : (c + 1) * width] = total(one, deep + c * shard, shard)
             for c in range(chunks):
-                expand[:, c * width : (c + 1) * width] = total(deep + c * shard, shard)
-            out[...] = total(deep + chunks * shard, shard)
-            for c in range(3):
-                ins[:, c * width : (c + 1) * width] = total(heads_start + c * shard, shard)
+                expand[:, c * width : (c + 1) * width] = total(two, c * shard, shard)
+            out[...] = total(two, chunks * shard, shard)
             small[...] = total_patch[patch.shape[0] :]
             sums = jnp.zeros((room, width), f32)
             for k in range(table_ref.shape[0]):
@@ -1267,20 +1328,21 @@
 
         @pl.when(section_ref[0] != 0)
         def _():
-            contract[...] = taken(crossed_ref, 0, deep)
+            one, two = (crossed_ref, local_one), (local_ref, local_two)
+            contract[...] = total(one, 0, deep)
+            out[...] = total(one, deep, shard)
+            ins[:, 0:width] = total(one, deep + shard, shard)
+            table[...] = total(one, deep + 2 * shard, room)
             for c in range(chunks):
-                expand[:, c * width : (c + 1) * width] = taken(own_ref, c * shard, shard)
-            out[...] = taken(crossed_ref, deep, shard)
-            ins[:, 0:width] = taken(crossed_ref, deep + shard, shard)
+                expand[:, c * width : (c + 1) * width] = total(two, c * shard, shard)
             for c in range(2):
-                ins[:, (c + 1) * width : (c + 2) * width] = taken(own_ref, deep + c * shard, shard)
-            small[...] = taken(own_ref, deep + 2 * shard, small.shape[0])
-            table[...] = taken(crossed_ref, deep + 2 * shard, room)
+                ins[:, (c + 1) * width : (c + 2) * width] = total(two, deep + c * shard, shard)
+            small[...] = total(two, deep + 2 * shard, small.shape[0])
 
     return call(
         kernel,
-        (section, upper, *block, own, crossed, table_parts, *patch_parts),
-        [SCALARS] * 2 + [WHOLE] * (6 + p),
+        (section, own_global, own_local, crossed, table_parts, *fars, *patch_parts),
+        [SCALARS] + [WHOLE] * (8 + p),
         [
             shaped(deep, width, kind=f32),
             shaped(shard, chunks * width, kind=f32),
@@ -1419,7 +1481,7 @@
         batches, shares[0], parts, gains, biases, heads_in
     )
     qkv = to_tasks(tasks_out)
-    attended, middle, normed_two, slope, hidden, sent, feed_share, edge, near = global_feed_forward(
+    attended, middle, normed_two, slope, hidden, sent, feed_share, other_share, edge, near = global_feed_forward(
         batches,
         from_tasks(global_attention(qkv, task_owners)),
         stream,
@@ -1506,8 +1568,7 @@
 
     def plane_send(blocks):
         return [blocks[0]] + [
-            section_send(blocks[k], 0, 0, [(i, i ^ k) for i in range(count)])
-            for k in range(1, SPAN)
+            both_send(blocks[k], [(i, i ^ k) for i in range(count)]) for k in range(1, SPAN)
         ]
 
     upper = (group >> 1) & 1
@@ -1520,6 +1581,25 @@
         joint = [(s * count + i, s * count + j) for s in range(2) for i, j in pairs]
         return lax.ppermute(x, ("section",) + SEQ, joint)
 
+    half_locals = [
+        ordered(
+            local_gradients(
+                count,
+                numbers,
+                byte_values,
+                keep,
+                crossed,
+                contract.shape[0],
+                width,
+                half_bytes,
+                [near_back, edge_back],
+            )
+        )
+        for numbers, keep, crossed in activations_of
+    ]
+    if chunks > 1:
+        half_locals = [sum(x.astype(f32) for x in half_locals).astype(bf16)]
+    half_locals = half_locals[0]
     grad_upward, grad_middle, attend_branch, task_grads, small, grad_sent = global_feed_backward(
         batches,
         grad_shifted,
@@ -1531,26 +1611,13 @@
         heads_out,
         expand,
         contract,
-    )
-    half_locals = [
-        ordered(
-            local_gradients(
-                count,
-                numbers,
-                byte_values,
-                keep,
-                crossed,
-                contract.shape[0],
-                width,
-                half_bytes,
-                [grad_sent],
-            )
-        )
-        for numbers, keep, crossed in activations_of
-    ]
-    if chunks > 1:
-        half_locals = [sum(x.astype(f32) for x in half_locals).astype(bf16)]
-    half_locals = half_locals[0]
+        [half_locals],
+    )
+    if in_plane:
+        whole = pack_columns(contract.shape[0], width)[2]
+        second_parts = section_send(
+            pack_second(member_flag, other_share, attend_branch, grad_upward, whole), 0, 1, straight
+        )
     task_grads = to_tasks(task_grads)
     task_mixed = global_attention(qkv, task_owners, task_grads)
     grad_mixed, own_rows, small = global_end(
@@ -1562,6 +1629,12 @@
         gains,
         heads_in,
     )
+
+    if in_plane:
+        *sent_parts, own_rows = pack(
+            flag, member_flag, feed_share, normed_share, grad_sent, grad_mixed, second_parts, own_rows
+        )
+        arrived_parts = plane_send(sent_parts)
 
     gathered = [own_rows]
     for k in range(1, quarters):
@@ -1576,15 +1649,13 @@
         gathered,
         crossed,
         span,
+        arrived_parts[1:] if in_plane else (),
     )
     if in_plane:
         in_planes = lax.psum_scatter(half_locals, "member", scatter_dimension=0, tiled=True)
-        in_planes = in_planes.reshape((2, 2) + in_planes.shape[1:])
-        parity = group & 1
-        local_near = both_send(
-            lax.dynamic_index_in_dim(in_planes, 1 - parity, 1, keepdims=False), group_pairs(1)
-        )
-        local_kept = lax.dynamic_index_in_dim(in_planes, parity, 1, keepdims=False)
+        parity_flag = (group & 1).reshape(1).astype(jnp.int32)
+        local_kept, local_leaving = by_parity(parity_flag, in_planes, [crossed])
+        local_near = both_send(local_leaving, group_pairs(1))
     else:
         own_local = place_sum(half_locals)
     patch_parts = [lax.dynamic_index_in_dim(patch_share, member, 0, keepdims=False)]
@@ -1609,33 +1680,42 @@
         )
 
     if in_plane:
-        sent_parts = pack(
-            member_flag, feed_share, normed_share, grad_sent, attend_branch, grad_upward, grad_mixed,
-        )
+        local_far = half_sum(1 - upper_flag, local_kept, local_near)
+        local_mine = half_sum(upper_flag, local_kept, local_near)
+        across = group_pairs(2)
+        local_fars = [
+            section_send(local_far, 0, 1, across),
+            section_send(local_far, 1, 1, across),
+        ]
         kept, leaving = plane_gradients(
-            group_flag, plane_send(sent_parts), rows, contract.shape[0], width, [patch_share]
-        )
-        local_far = both_send(
-            half_sum(1 - upper_flag, local_kept, local_near), group_pairs(2)
-        )
-        near = section_send(leaving, 0, 0, group_pairs(1))
-        far = section_send(
-            half_sum(1 - upper_flag, kept, near, patch_parts[1:]), 0, 0, group_pairs(2)
-        )
-        own_local = sum(
-            lax.dynamic_index_in_dim(x, upper, 0, keepdims=False).astype(f32)
-            for x in (local_kept, local_near)
-        ) + local_far.astype(f32)
-        crossed = section_send(own_local, 0, 1, straight)
+            flag,
+            group_flag,
+            arrived_parts,
+            contract.shape[0],
+            width,
+            [patch_share, *local_fars],
+        )
+        near = both_send(leaving, group_pairs(1))
+        far = half_sum(1 - upper_flag, kept, near, patch_parts[1:])
+        mine = half_sum(upper_flag, kept, near, [far])
+        extra = mine.shape[0] - local_mine.shape[0]
+        crossed = section_swap(
+            jnp.where(is_global, jnp.pad(local_mine, ((0, extra), (0, 0))), mine)
+        )
+        fars = [
+            section_send(far, 0, 0, across),
+            section_send(far, 1, 0, across),
+            *local_fars,
+        ]
         contract_grad, expand_grad, in_grad, out_grads, table_grad, small, patch_grads = finish(
             flag,
-            upper_flag,
             contract.shape[0] // count,
             shard,
             room,
-            (kept, near, far),
-            own_local,
+            mine,
+            local_mine,
             crossed,
+            fars,
             table_parts,
             patch_parts,
         )

time: 411 us -> 402 us (0.978)
  blocking collectives: 29.2 us -> 16 us
  waiting for transfers between devices: 114 us -> 105 us
  Pallas kernels: 109 us -> 116 us
  starting transfers between devices: 107 us -> 113 us
    all_to_all x1, waiting for transfers between devices: 20.6 us -> 0.01 us  [on_device(): lax.all_to_all(table_share.reshape(count, VOCAB // count, width), SEQ, 0, 0)]
    all_to_all x1 -> x0, blocking collectives: 13.6 us -> none  [to_tasks(): landed = lax.all_to_all(slots, SEQ, 0, 0)]
    ppermute x2 -> x5, waiting for transfers between devices: 16.4 us -> 29 us  [both_send(): return lax.ppermute(x, ('section',) + SEQ, joint)]
    reduce_scatter x1, waiting for transfers between devices: 12.9 us -> 0.62 us  [on_device(): lax.psum_scatter(half_locals, 'member', scatter_dimension=0, tiled=True)]
    ppermute x28 -> x27, starting transfers between devices: 74.3 us -> 65.2 us  [section_send(): return lax.ppermute(x, ('section',) + SEQ, joint)]
    ppermute x3, waiting for transfers between devices: 0.01 us -> 7.18 us  [on_device(): lax.ppermute(leaving, SEQ, [(i, i ^ k) for i in range(count)])]
    ppermute x2 -> x5, starting transfers between devices: 4.82 us -> 11.5 us  [both_send(): return lax.ppermute(x, ('section',) + SEQ, joint)]
    all_to_all x1 -> x2, starting transfers between devices: 5.89 us -> 10.7 us  [to_tasks(): landed = lax.all_to_all(slots, SEQ, 0, 0)]
  transfers between devices with their start and end apart: 46 -> 50, of which waited for: 19 -> 24; matrix products, arithmetic and copies ran while one was open for 5% -> 5% of each run, Pallas kernels for 14% -> 15%
where the time goes in v5:
time: 402 us; the launch traced here: 395 us
  Pallas kernels  116 us (29%)
  starting transfers between devices  113 us (28%)
  waiting for transfers between devices  105 us (26%)
  local copies, waits for them, and re-layouts  17.3 us (4%)
  blocking collectives  16 us (4%)
  between operations  15.5 us (4%)
  other arithmetic  13 us (3%)
    ppermute x27, starting transfers between devices, section_send(): return lax.ppermute(x, ('section',) + SEQ, joint)  65.2 us
    pallas_call x11, Pallas kernels, call(): pl.pallas_call(body, in_specs=list(specs) + [ANY] * len(deps), out_specs=...  54.3 us
    ppermute x27, waiting for transfers between devices, section_send(): return lax.ppermute(x, ('section',) + SEQ, joint)  39 us
    pallas_call x1, Pallas kernels, local_block(): pl.pallas_call(partial(local_kernel, patch_rows), in_specs=[SCALARS] + [W...  31.5 us
    ppermute x5, waiting for transfers between devices, both_send(): return lax.ppermute(x, ('section',) + SEQ, joint)  29 us
    all_to_all x1, blocking collectives, from_tasks(): lax.all_to_all(results.reshape(count, patch_rows, columns), SEQ, 0, 0)  16 us
    all_to_all x2, waiting for transfers between devices, to_tasks(): landed = lax.all_to_all(slots, SEQ, 0, 0)  13.4 us
    pallas_call x1, Pallas kernels, local_gradients(): pl.pallas_call(kernel, in_specs=[SCALARS, WHOLE, ANY, ANY] + [ANY] * len(...  11.5 us
  transfers between devices with their start and end apart: 50, of which 24 were waited for; matrix products, arithmetic and copies ran while one was open for 5% of the time, Pallas kernels for 15%

profile of v5, /device:TPU:0, one launch (start us, length us, event | category | flops | bytes accessed | tf_op | source)
XLA Modules:
  0.0 394.8 jit_solution(8607422288513608287)
XLA Ops:
  7.7 4.7 %collective-permute-start.2 = (s32[3,256]{1,0:T(4,128)}, s32[3,256]{1,0:T(4,128)S(1)}, u32[]{:S(2)}, u32[]{:S(2)}) collective-permute-start(s32[3,256]{1,0:T(4,128)} %ids_ref.3), channel_id=1, source_target_pairs={{0,12},{1,13},{2,14},{3,15},{4,8},{5,9},{6,10},{7,11},{8,4},{9,5},... | collective-permute-start | bytes 9224 | tf_op jit(solution)/shard_map/ppermute | solution.py:1436
  26.4 5.3 %collective-permute-done.6.refs_6_ = bf16[192,768]{1,0:T(8,128)(2,1)S(1)} collective-permute-done((bf16[192,768]{1,0:T(8,128)(2,1)}, bf16[192,768]{1,0:T(8,128)(2,1)S(1)}, u32[]{:S(2)}, u32[]{:S(2)}) %collective-permute-start.6) | collective-permute-done | bytes 294944 | tf_op jit(solution)/shard_map/ppermute | solution.py:1427
  41.4 4.6 %collective-permute-start.10 = (bf16[96,768]{1,0:T(8,128)(2,1)S(1)}, bf16[96,768]{1,0:T(8,128)(2,1)S(1)}, u32[]{:S(2)}, u32[]{:S(2)}) collective-permute-start(bf16[96,768]{1,0:T(8,128)(2,1)S(1)} %get-tuple-element.116), channel_id=1, source_target_pairs={{0,12},{1,13},{2,14},{3,15},{4,8},{5,9},{6,10},{7,11},{8,4},{9,5},... | collective-permute-start | bytes 442376 | tf_op jit(solution)/shard_map/ppermute | solution.py:1366
  48.0 3.6 collective-permute-start.8
  57.1 4.7 %shard_map.179 = (f32[96,768]{1,0:T(8,128)}, bf16[96,768]{1,0:T(8,128)(2,1)}, bf16[18,32,384]{2,1,0:T(8,128)(2,1)}, bf16[4,96,192]{2,1,0:T(8,128)(2,1)}) custom-call(f32[96,768]{1,0:T(8,128)} %slice.79.refs_0_, f32[2,768]{1,0:T(2,128)} %bitcast.131, f32[2,768]{1,0:T(2,128)} %bitcast.128, bf16[768,2304]{1,0:T(8,128)(2,1)} %bitcast.19.refs_3_.own_in.refs_4_, ...), custom_call_target="tpu_custom_call" | custom-call | flops 5500000256 | bytes 1 | tf_op jit(solution)/shard_map/pallas_call | solution.py:745
  62.6 8.9 %collective-permute-start.11 = (bf16[2,32,384]{2,1,0:T(8,128)(2,1)S(1)}, bf16[2,32,384]{2,1,0:T(8,128)(2,1)S(1)}, u32[]{:S(2)}, u32[]{:S(2)}) collective-permute-start(bf16[2,32,384]{2,1,0:T(8,128)(2,1)S(1)} %slice.69), channel_id=1, source_target_pairs={{0,16},{1,17},{2,18},{3,19},{4,20},{5,21},{6,22},{7,23},{8,24},{9,... | collective-permute-start | bytes 147464 | tf_op jit(solution)/shard_map/ppermute | solution.py:1366
  74.2 5.7 %all-to-all-start = ((bf16[16,32,384]{2,1,0:T(8,128)(2,1)}), bf16[16,32,384]{2,1,0:T(8,128)(2,1)S(1)}, u32[]{:S(2)}, u32[]{:S(2)}) async-start(bf16[16,32,384]{2,1,0:T(8,128)(2,1)} %pad_select_fusion.1), calls=%async_computation | async-start | bytes 786432 | tf_op jit(solution)/shard_map/all_to_all | solution.py:1466
  82.2 10.8 %all-to-all-done = bf16[16,32,384]{2,1,0:T(8,128)(2,1)S(1)} async-done(((bf16[16,32,384]{2,1,0:T(8,128)(2,1)}), bf16[16,32,384]{2,1,0:T(8,128)(2,1)S(1)}, u32[]{:S(2)}, u32[]{:S(2)}) %all-to-all-start) | async-done | bytes 393248 | tf_op jit(solution)/shard_map/all_to_all | solution.py:1466
  93.8 4.4 %shard_map.180 = bf16[512,128]{1,0:T(8,128)(2,1)} custom-call(s32[512,1]{1,0:T(8,128)} %copy.33.column_ref.refs_0_, s32[1,512]{1,0:T(1,128)} %bitcast.137, bf16[512,384]{1,0:T(8,128)(2,1)} %bitcast.121), custom_call_target="tpu_custom_call" | custom-call | flops 16499999744 | bytes 1 | tf_op jit(solution)/shard_map/pallas_call | solution.py:714
  98.1 3.6 all-to-all-start.1
  103.2 6.3 %all-to-all-done.1.refs_6_ = bf16[16,32,128]{2,1,0:T(8,128)(2,1)S(1)} async-done(((bf16[16,32,128]{2,1,0:T(8,128)(2,1)}), bf16[16,32,128]{2,1,0:T(8,128)(2,1)S(1)}, u32[]{:S(2)}, u32[]{:S(2)}) %all-to-all-start.1) | async-done | bytes 131104 | tf_op jit(solution)/shard_map/all_to_all | solution.py:1471
  113.2 7.5 %shard_map.181 = (bf16[96,768]{1,0:T(8,128)(2,1)}, f32[96,768]{1,0:T(8,128)}, bf16[96,768]{1,0:T(8,128)(2,1)}, bf16[96,3072]{1,0:T(8,128)(2,1)}, bf16[96,3072]{1...) custom-call(f32[96,768]{1,0:T(8,128)} %get-tuple-element.56.refs_0_,, ...), custom_call_target="tpu_custom_call" | custom-call | flops 8800000000 | bytes 1 | tf_op jit(solution)/shard_map/pallas_call | solution.py:745
  126.8 31.5 %shard_map.182 = (bf16[384,768]{1,0:T(8,128)(2,1)}, bf16[48,768]{1,0:T(8,128)(2,1)}, bf16[16,768]{1,0:T(8,128)(2,1)}, bf16[400,7680]{1,0:T(8,128)(2,1)}, bf16[400,7680]{1,0:T(8,128)(2,1)}) custom-call(s32[15]{0:T(128)} %pad_add_fusion.2.numbers_ref, s32[3,256]{1,0:T(4,128)} %ids_ref.3, bf16[256,768]{1,0:T(8,128)(2,1)} %get-tuple-element.115.table_ref, ...), custom_call_target="tpu_custom_call" | custom-call | flops 38499999744 | bytes 1 | tf_op jit(solution)/shard_map/pallas_call | solution.py:472
  161.3 4.6 %collective-permute-done.22.rest_1_.refs_2_ = bf16[16,768]{1,0:T(8,128)(2,1)S(1)} collective-permute-done((bf16[16,768]{1,0:T(8,128)(2,1)}, bf16[16,768]{1,0:T(8,128)(2,1)S(1)}, u32[]{:S(2)}, u32[]{:S(2)}) %collective-permute-start.22) | collective-permute-done | bytes 24608 | tf_op jit(solution)/shard_map/ppermute | solution.py:1366
  169.2 11.5 %shard_map.183.refs_9_ = bf16[16,304,768]{2,1,0:T(8,128)(2,1)} custom-call(s32[15]{0:T(128)} %pad_add_fusion.2.numbers_ref, s32[3,256]{1,0:T(4,128)} %ids_ref.3, bf16[400,7680]{1,0:T(8,128)(2,1)} %get-tuple-element.68.keep_ref, bf16[400,7680]{1,0:T(8,128)(2,1)} %collective-permute-done.23.new_ref, bf16[48,768]{1,0:T(8,128)(2,1)} %copy-done.49, ...), custom_call_target="tpu_custom_call" | custom-call | flops 13200000000 | bytes 1 | tf_op jit(solution)/shard_map/pallas_call | solution.py:595
  180.8 9.1 %shard_map.184 = (bf16[96,3072]{1,0:T(8,128)(2,1)}, f32[96,768]{1,0:T(8,128)}, bf16[96,768]{1,0:T(8,128)(2,1)}, bf16[18,32,128]{2,1,0:T(8,128)(2,1)}, f32[2,768]{1,0:T(2,128)}, /*index=5*/bf16[96,768]{1,0:T(8,128)(2,1)}) custom-call(bf16[48,768]{1,0:T(8,128)(2,1)} %get-tuple-element.64.refs_0_, bf16[48,768]{1,0:T(8,128)(2,1)} %copy-done.49, ...), custom_call_target="tpu_custom_call" | custom-call | flops 11000000512 | bytes 1 | tf_op jit(solution)/shard_map/pallas_call | solution.py:745
  195.9 5.0 %all-to-all-start.2 = ((bf16[16,32,128]{2,1,0:T(8,128)(2,1)}), bf16[16,32,128]{2,1,0:T(8,128)(2,1)S(1)}, u32[]{:S(2)}, u32[]{:S(2)}) async-start(bf16[16,32,128]{2,1,0:T(8,128)(2,1)} %pad_select_fusion.2), calls=%async_computation.2 | async-start | bytes 262144 | tf_op jit(solution)/shard_map/all_to_all | solution.py:1466
  209.6 5.7 %shard_map.185 = bf16[512,384]{1,0:T(8,128)(2,1)} custom-call(s32[512,1]{1,0:T(8,128)} %copy.33.column_ref.refs_0_, s32[1,512]{1,0:T(1,128)} %bitcast.138, bf16[512,384]{1,0:T(8,128)(2,1)} %bitcast.122, bf16[512,128]{1,0:T(8,128)(2,1)} %bitcast.126), custom_call_target="tpu_custom_call" | custom-call | flops 32999999488 | bytes 1 | tf_op jit(solution)/shard_map/pallas_call | solution.py:727
  215.4 16.0 %all_to_all.25.refs_5_ = bf16[16,32,384]{2,1,0:T(8,128)(2,1)S(1)} all-to-all(bf16[16,32,384]{2,1,0:T(8,128)(2,1)} %bitcast.123), channel_id=1, replica_groups=mesh['section'=2,'group'=4,'member'=4] {'group','member'}, dimensions={0} | all-to-all | bytes 786432 | tf_op jit(solution)/shard_map/all_to_all | solution.py:1471
  235.1 5.3 %shard_map.186 = (bf16[96,2304]{1,0:T(8,128)(2,1)}, bf16[112,768]{1,0:T(8,128)(2,1)}, f32[4,768]{1,0:T(4,128)}) custom-call(f32[96,768]{1,0:T(8,128)} %get-tuple-element.56.refs_0_, f32[96,768]{1,0:T(8,128)} %get-tuple-element.71.refs_1_, f32[2,768]{1,0:T(2,128)} %get-tuple-element.72.refs_2_, f32[2,768]{1,0:T(2,128)} %bitcast.134, ...), custom_call_target="tpu_custom_call" | custom-call | flops 6600000000 | bytes 1 | tf_op jit(solution)/shard_map/pallas_call | solution.py:745
  242.1 4.4 %shard_map.188 = (bf16[96,4224]{1,0:T(8,128)(2,1)}, bf16[96,4224]{1,0:T(8,128)(2,1)}, bf16[96,4224]{1,0:T(8,128)(2,1)}, bf16[96,4224]{1,0:T(8,128)(2,1)}, bf16[112,768]{1,0:T(8,128)(2,1)}) custom-call(s32[1]{0:T(128)} %bitcast.33.refs_0_, s32[1]{0:T(128)} %bitcast.40.refs_0_.refs_1_, bf16[4,96,768]{2,1,0:T(8,128)(2,1)} %get-tuple-element.62.refs_2_, ...), custom_call_target="tpu_custom_call" | custom-call | flops 4400000000 | bytes 1 | tf_op jit(solution)/shard_map/pallas_call | solution.py:745
  252.9 3.8 collective-permute-start.30
  274.7 18.5 %collective-permute-done.34.refs_2_ = bf16[2,304,768]{2,1,0:T(8,128)(2,1)S(1)} collective-permute-done((bf16[2,304,768]{2,1,0:T(8,128)(2,1)}, bf16[2,304,768]{2,1,0:T(8,128)(2,1)S(1)}, u32[]{:S(2)}, u32[]{:S(2)}) %collective-permute-start.34) | collective-permute-done | bytes 933920 | tf_op jit(solution)/shard_map/ppermute | solution.py:1582
  296.9 5.1 %collective-permute-start.35 = (bf16[304,768]{1,0:T(8,128)(2,1)}, bf16[304,768]{1,0:T(8,128)(2,1)S(1)}, u32[]{:S(2)}, u32[]{:S(2)}) collective-permute-start(bf16[304,768]{1,0:T(8,128)(2,1)} %shard_map.191), channel_id=1, source_target_pairs={{0,24},{1,25},{2,26},{3,27},{4,28},{5,29},{6,30},{7,31},{8,16},{9,... | collective-permute-start | bytes 1400840 | tf_op jit(solution)/shard_map/ppermute | solution.py:1366
  302.0 7.3 %collective-permute-done.29.refs_11_.refs_5_ = bf16[96,4224]{1,0:T(8,128)(2,1)} collective-permute-done((bf16[96,4224]{1,0:T(8,128)(2,1)S(1)}, bf16[96,4224]{1,0:T(8,128)(2,1)}, u32[]{:S(2)}, u32[]{:S(2)}) %collective-permute-start.29) | collective-permute-done | bytes 811040 | tf_op jit(solution)/shard_map/ppermute | solution.py:1582
  309.2 4.5 %shard_map.189 = (bf16[4,208,768]{2,1,0:T(8,128)(2,1)}, bf16[256,768]{1,0:T(8,128)(2,1)}) custom-call(s32[1]{0:T(128)} %bitcast.33.refs_0_, s32[384,1]{1,0:T(8,128)} %reshape.450.refs_1_, bf16[384,768]{1,0:T(8,128)(2,1)} %get-tuple-element.83.refs_2_, bf16[768,768]{1,0:T(8,128)(2,1)} %get-tuple-element.84.refs_3_, bf16[448,768]{1,0:T(8,128)(2,1)} %copy-done.37, ...), custom_call_target="tpu_custom_call" | custom-call | flops 6600000000 | bytes 1 | tf_op jit(solution)/shard_map/pallas_call | solution.py:745
  314.8 4.6 %shard_map.192 = (bf16[2,336,768]{2,1,0:T(8,128)(2,1)}, bf16[2,336,768]{2,1,0:T(8,128)(2,1)}) custom-call(s32[1]{0:T(128)} %bitcast.33.refs_0_, s32[1]{0:T(128)} %bitcast.39.refs_1_, bf16[96,4224]{1,0:T(8,128)(2,1)} %get-tuple-element.79.refs_2_, bf16[96,4224]{1,0:T(8,128)(2,1)} %collective-permute-done.27.refs_9_.refs_3_, ...), custom_call_target="tpu_custom_call" | custom-call | flops 6600000000 | bytes 1 | tf_op jit(solution)/shard_map/pallas_call | solution.py:745
  319.4 6.7 %collective-permute-start.37 = (bf16[2,336,768]{2,1,0:T(8,128)(2,1)}, bf16[2,336,768]{2,1,0:T(8,128)(2,1)}, u32[]{:S(2)}, u32[]{:S(2)}) collective-permute-start(bf16[2,336,768]{2,1,0:T(8,128)(2,1)} %get-tuple-element.90), channel_id=1, source_target_pairs={{0,4},{1,5},{2,6},{3,7},{4,0},{5,1},{6,2},{7,3},{8,12},{9,13},{10,... | collective-permute-start | bytes 3096584 | tf_op jit(solution)/shard_map/ppermute | solution.py:1582
  335.0 3.7 all-to-all-start.4
  340.8 7.2 %collective-permute-done.39.refs_4_.refs_11_ = bf16[208,768]{1,0:T(8,128)(2,1)S(1)} collective-permute-done((bf16[208,768]{1,0:T(8,128)(2,1)S(1)}, bf16[208,768]{1,0:T(8,128)(2,1)S(1)}, u32[]{:S(2)}, u32[]{:S(2)}) %collective-permute-start.39) | collective-permute-done | bytes 319520 | tf_op jit(solution)/shard_map/ppermute | solution.py:1664
  364.5 16.6 %collective-permute-done.44.refs_6_ = bf16[336,768]{1,0:T(8,128)(2,1)S(1)} collective-permute-done((bf16[336,768]{1,0:T(8,128)(2,1)}, bf16[336,768]{1,0:T(8,128)(2,1)S(1)}, u32[]{:S(2)}, u32[]{:S(2)}) %collective-permute-start.44) | collective-permute-done | bytes 516128 | tf_op jit(solution)/shard_map/ppermute | solution.py:1366
  381.9 4.2 %shard_map.196 = (f32[192,768]{1,0:T(8,128)}, f32[48,3072]{1,0:T(8,128)}, f32[48,2304]{1,0:T(8,128)}, f32[48,768]{1,0:T(8,128)}, f32[16,768]{1,0:T(8,128)}, /*index=5*/f32[16,768]{1,0:T(8,128)}, f32[192,768]{1,0:T(8,128)}) custom-call(s32[1]{0:T(128)} %bitcast.33.refs_0_, bf16[336,768]{1,0:T(8,128)(2,1)} %shard_map.194.refs_1_, ...), custom_call_target="tpu_custom_call" | custom-call | flops 4400000000 | bytes 1 | tf_op jit(solution)/shard_map/pallas_call | solution.py:745
  (248 shorter events, 133.9 us)
Async XLA Ops:
  7.2 14.0 %collective-permute-start.3 = (bf16[256,768]{1,0:T(8,128)(2,1)}, bf16[256,768]{1,0:T(8,128)(2,1)S(1)}, u32[]{:S(2)}, u32[]{:S(2)}) collective-permute-start(bf16[256,768]{1,0:T(8,128)(2,1)} %bitcast.124), channel_id=1, source_target_pairs={{0,16},{16,0},{1,17},{17,1},{2,18},{18,2},{3,19},{19,3},{4,20},{20... | collective-permute-start | bytes 1179656 | tf_op jit(solution)/shard_map/ppermute | solution.py:1370
  7.7 11.9 %collective-permute-start.2 = (s32[3,256]{1,0:T(4,128)}, s32[3,256]{1,0:T(4,128)S(1)}, u32[]{:S(2)}, u32[]{:S(2)}) collective-permute-start(s32[3,256]{1,0:T(4,128)} %ids_ref.3), channel_id=1, source_target_pairs={{0,12},{1,13},{2,14},{3,15},{4,8},{5,9},{6,10},{7,11},{8,4},{9,5},... | collective-permute-start | bytes 9224 | tf_op jit(solution)/shard_map/ppermute | solution.py:1436
  16.2 10.2 %collective-permute-start.4 = (bf16[192,768]{1,0:T(8,128)(2,1)}, bf16[192,768]{1,0:T(8,128)(2,1)S(1)}, u32[]{:S(2)}, u32[]{:S(2)}) collective-permute-start(bf16[192,768]{1,0:T(8,128)(2,1)} %refs_3_.1), channel_id=1, source_target_pairs={{0,1},{1,0},{2,3},{3,2},{4,5},{5,4},{6,7},{7,6},{8,9},{9,8},{10,11... | collective-permute-start | bytes 884744 | tf_op jit(solution)/shard_map/ppermute | solution.py:1427
  17.8 13.8 %collective-permute-start.6 = (bf16[192,768]{1,0:T(8,128)(2,1)}, bf16[192,768]{1,0:T(8,128)(2,1)S(1)}, u32[]{:S(2)}, u32[]{:S(2)}) collective-permute-start(bf16[192,768]{1,0:T(8,128)(2,1)} %refs_3_.1), channel_id=1, source_target_pairs={{0,3},{1,2},{2,1},{3,0},{4,7},{5,6},{6,5},{7,4},{8,11},{9,10},{10,... | collective-permute-start | bytes 884744 | tf_op jit(solution)/shard_map/ppermute | solution.py:1427
  41.4 13.5 %collective-permute-start.10 = (bf16[96,768]{1,0:T(8,128)(2,1)S(1)}, bf16[96,768]{1,0:T(8,128)(2,1)S(1)}, u32[]{:S(2)}, u32[]{:S(2)}) collective-permute-start(bf16[96,768]{1,0:T(8,128)(2,1)S(1)} %get-tuple-element.116), channel_id=1, source_target_pairs={{0,12},{1,13},{2,14},{3,15},{4,8},{5,9},{6,10},{7,11},{8,4},{9,5},... | collective-permute-start | bytes 442376 | tf_op jit(solution)/shard_map/ppermute | solution.py:1366
  46.0 10.2 %collective-permute-start.9 = (bf16[96,768]{1,0:T(8,128)(2,1)S(1)}, bf16[96,768]{1,0:T(8,128)(2,1)S(1)}, u32[]{:S(2)}, u32[]{:S(2)}) collective-permute-start(bf16[96,768]{1,0:T(8,128)(2,1)S(1)} %get-tuple-element.117), channel_id=1, source_target_pairs={{0,8},{1,9},{2,10},{3,11},{4,12},{5,13},{6,14},{7,15},{8,0},{9,1},... | collective-permute-start | bytes 442376 | tf_op jit(solution)/shard_map/ppermute | solution.py:1366
  51.6 74.6 %collective-permute-start.16 = (bf16[768,2304]{1,0:T(8,128)(2,1)}, bf16[768,2304]{1,0:T(8,128)(2,1)}, u32[]{:S(2)}, u32[]{:S(2)}) collective-permute-start(bf16[768,2304]{1,0:T(8,128)(2,1)} %bitcast.19.refs_3_.own_in.refs_4_), channel_id=1, source_target_pairs={{16,0},{17,1},{18,2},{19,3},{20,4},{21,5},{22,6},{23,7},{24,8},{25... | collective-permute-start | bytes 10616840 | tf_op jit(solution)/shard_map/ppermute | solution.py:1366
  52.9 73.3 %collective-permute-start.18 = (bf16[768,3072]{1,0:T(8,128)(2,1)}, bf16[768,3072]{1,0:T(8,128)(2,1)}, u32[]{:S(2)}, u32[]{:S(2)}) collective-permute-start(bf16[768,3072]{1,0:T(8,128)(2,1)} %bitcast.146), channel_id=1, source_target_pairs={{16,0},{17,1},{18,2},{19,3},{20,4},{21,5},{22,6},{23,7},{24,8},{25... | collective-permute-start | bytes 14155784 | tf_op jit(solution)/shard_map/ppermute | solution.py:1366
  54.9 71.3 %collective-permute-start.19 = (bf16[3072,768]{1,0:T(8,128)(2,1)}, bf16[3072,768]{1,0:T(8,128)(2,1)}, u32[]{:S(2)}, u32[]{:S(2)}) collective-permute-start(bf16[3072,768]{1,0:T(8,128)(2,1)} %bitcast.150), channel_id=1, source_target_pairs={{16,0},{17,1},{18,2},{19,3},{20,4},{21,5},{22,6},{23,7},{24,8},{25... | collective-permute-start | bytes 14155784 | tf_op jit(solution)/shard_map/ppermute | solution.py:1366
  74.2 18.8 %all-to-all-start = ((bf16[16,32,384]{2,1,0:T(8,128)(2,1)}), bf16[16,32,384]{2,1,0:T(8,128)(2,1)S(1)}, u32[]{:S(2)}, u32[]{:S(2)}) async-start(bf16[16,32,384]{2,1,0:T(8,128)(2,1)} %pad_select_fusion.1), calls=%async_computation | async-start | bytes 786432 | tf_op jit(solution)/shard_map/all_to_all | solution.py:1466
  98.1 11.4 %all-to-all-start.1 = ((bf16[16,32,128]{2,1,0:T(8,128)(2,1)}), bf16[16,32,128]{2,1,0:T(8,128)(2,1)S(1)}, u32[]{:S(2)}, u32[]{:S(2)}) async-start(bf16[16,32,128]{2,1,0:T(8,128)(2,1)} %bitcast.127), calls=%async_computation.1 | async-start | bytes 262144 | tf_op jit(solution)/shard_map/all_to_all | solution.py:1471
  101.8 164.9 %reduce-scatter.2.cloned.1.call-start = ((), (), s32[]{:S(2)}) async-start(), calls=%async_computation.6 | async-start | bytes 9338880 | tf_op jit(solution)/shard_map/reduce_scatter | solution.py:1655
  101.8 21.9 %collective-permute-start.17 = (bf16[768,768]{1,0:T(8,128)(2,1)S(1)}, bf16[768,768]{1,0:T(8,128)(2,1)S(1)}, u32[]{:S(2)}, u32[]{:S(2)}) collective-permute-start(bf16[768,768]{1,0:T(8,128)(2,1)S(1)} %bitcast.157), channel_id=1, source_target_pairs={{16,0},{17,1},{18,2},{19,3},{20,4},{21,5},{22,6},{23,7},{24,8},{25... | collective-permute-start | bytes 3538952 | tf_op jit(solution)/shard_map/ppermute | solution.py:1366
  158.3 10.4 %collective-permute-start.23 = (bf16[400,7680]{1,0:T(8,128)(2,1)}, bf16[400,7680]{1,0:T(8,128)(2,1)}, u32[]{:S(2)}, u32[]{:S(2)}) collective-permute-start(bf16[400,7680]{1,0:T(8,128)(2,1)} %get-tuple-element.69), channel_id=1, source_target_pairs={{0,16},{16,0},{1,17},{17,1},{2,18},{18,2},{3,19},{19,3},{4,20},{20... | collective-permute-start | bytes 18432008 | tf_op jit(solution)/shard_map/ppermute | solution.py:1370
  195.9 13.0 %all-to-all-start.2 = ((bf16[16,32,128]{2,1,0:T(8,128)(2,1)}), bf16[16,32,128]{2,1,0:T(8,128)(2,1)S(1)}, u32[]{:S(2)}, u32[]{:S(2)}) async-start(bf16[16,32,128]{2,1,0:T(8,128)(2,1)} %pad_select_fusion.2), calls=%async_computation.2 | async-start | bytes 262144 | tf_op jit(solution)/shard_map/all_to_all | solution.py:1466
  204.2 36.2 %collective-permute-start.26 = (bf16[4,96,4224]{2,1,0:T(8,128)(2,1)}, bf16[4,96,4224]{2,1,0:T(8,128)(2,1)S(1)}, u32[]{:S(2)}, u32[]{:S(2)}) collective-permute-start(bf16[4,96,4224]{2,1,0:T(8,128)(2,1)} %shard_map.187), channel_id=1, source_target_pairs={{0,16},{1,17},{2,18},{3,19},{4,20},{5,21},{6,22},{7,23},{8,24},{9,... | collective-permute-start | bytes 9732104 | tf_op jit(solution)/shard_map/ppermute | solution.py:1366
  246.6 10.1 %collective-permute-start.32 = (bf16[112,768]{1,0:T(8,128)(2,1)}, bf16[112,768]{1,0:T(8,128)(2,1)S(1)}, u32[]{:S(2)}, u32[]{:S(2)}) collective-permute-start(bf16[112,768]{1,0:T(8,128)(2,1)} %get-tuple-element.85.refs_5_), channel_id=1, source_target_pairs={{0,12},{1,13},{2,14},{3,15},{4,8},{5,9},{6,10},{7,11},{8,4},{9,5},... | collective-permute-start | bytes 516104 | tf_op jit(solution)/shard_map/ppermute | solution.py:1366
  249.7 10.5 %collective-permute-start.31 = (bf16[112,768]{1,0:T(8,128)(2,1)}, bf16[112,768]{1,0:T(8,128)(2,1)S(1)}, u32[]{:S(2)}, u32[]{:S(2)}) collective-permute-start(bf16[112,768]{1,0:T(8,128)(2,1)} %get-tuple-element.85.refs_5_), channel_id=1, source_target_pairs={{0,8},{1,9},{2,10},{3,11},{4,12},{5,13},{6,14},{7,15},{8,0},{9,1},... | collective-permute-start | bytes 516104 | tf_op jit(solution)/shard_map/ppermute | solution.py:1366
  270.0 23.3 %collective-permute-start.34 = (bf16[2,304,768]{2,1,0:T(8,128)(2,1)}, bf16[2,304,768]{2,1,0:T(8,128)(2,1)S(1)}, u32[]{:S(2)}, u32[]{:S(2)}) collective-permute-start(bf16[2,304,768]{2,1,0:T(8,128)(2,1)} %get-tuple-element.88), channel_id=1, source_target_pairs={{0,4},{1,5},{2,6},{3,7},{4,0},{5,1},{6,2},{7,3},{8,12},{9,13},{10,... | collective-permute-start | bytes 2801672 | tf_op jit(solution)/shard_map/ppermute | solution.py:1582
  271.2 30.7 %collective-permute-start.27 = (bf16[96,4224]{1,0:T(8,128)(2,1)}, bf16[96,4224]{1,0:T(8,128)(2,1)}, u32[]{:S(2)}, u32[]{:S(2)}) collective-permute-start(bf16[96,4224]{1,0:T(8,128)(2,1)} %get-tuple-element.80), channel_id=1, source_target_pairs={{0,1},{1,0},{2,3},{3,2},{4,5},{5,4},{6,7},{7,6},{8,9},{9,8},{10,11... | collective-permute-start | bytes 2433032 | tf_op jit(solution)/shard_map/ppermute | solution.py:1582
  272.5 29.4 %collective-permute-start.28 = (bf16[96,4224]{1,0:T(8,128)(2,1)S(1)}, bf16[96,4224]{1,0:T(8,128)(2,1)}, u32[]{:S(2)}, u32[]{:S(2)}) collective-permute-start(bf16[96,4224]{1,0:T(8,128)(2,1)S(1)} %copy-done.36), channel_id=1, source_target_pairs={{0,2},{1,3},{2,0},{3,1},{4,6},{5,7},{6,4},{7,5},{8,10},{9,11},{10,... | collective-permute-start | bytes 2433032 | tf_op jit(solution)/shard_map/ppermute | solution.py:1582
  273.3 36.0 %collective-permute-start.29 = (bf16[96,4224]{1,0:T(8,128)(2,1)S(1)}, bf16[96,4224]{1,0:T(8,128)(2,1)}, u32[]{:S(2)}, u32[]{:S(2)}) collective-permute-start(bf16[96,4224]{1,0:T(8,128)(2,1)S(1)} %copy-done.35), channel_id=1, source_target_pairs={{0,3},{1,2},{2,1},{3,0},{4,7},{5,6},{6,5},{7,4},{8,11},{9,10},{10,... | collective-permute-start | bytes 2433032 | tf_op jit(solution)/shard_map/ppermute | solution.py:1582
  296.2 17.6 %collective-permute-start.36 = (bf16[304,768]{1,0:T(8,128)(2,1)}, bf16[304,768]{1,0:T(8,128)(2,1)S(1)}, u32[]{:S(2)}, u32[]{:S(2)}) collective-permute-start(bf16[304,768]{1,0:T(8,128)(2,1)} %shard_map.191), channel_id=1, source_target_pairs={{16,24},{17,25},{18,26},{19,27},{20,28},{21,29},{22,30},{23,31},{2... | collective-permute-start | bytes 1400840 | tf_op jit(solution)/shard_map/ppermute | solution.py:1366
  296.9 16.9 %collective-permute-start.35 = (bf16[304,768]{1,0:T(8,128)(2,1)}, bf16[304,768]{1,0:T(8,128)(2,1)S(1)}, u32[]{:S(2)}, u32[]{:S(2)}) collective-permute-start(bf16[304,768]{1,0:T(8,128)(2,1)} %shard_map.191), channel_id=1, source_target_pairs={{0,24},{1,25},{2,26},{3,27},{4,28},{5,29},{6,30},{7,31},{8,16},{9,... | collective-permute-start | bytes 1400840 | tf_op jit(solution)/shard_map/ppermute | solution.py:1366
  319.4 31.8 %collective-permute-start.37 = (bf16[2,336,768]{2,1,0:T(8,128)(2,1)}, bf16[2,336,768]{2,1,0:T(8,128)(2,1)}, u32[]{:S(2)}, u32[]{:S(2)}) collective-permute-start(bf16[2,336,768]{2,1,0:T(8,128)(2,1)} %get-tuple-element.90), channel_id=1, source_target_pairs={{0,4},{1,5},{2,6},{3,7},{4,0},{5,1},{6,2},{7,3},{8,12},{9,13},{10,... | collective-permute-start | bytes 3096584 | tf_op jit(solution)/shard_map/ppermute | solution.py:1582
  328.4 12.4 %collective-permute-start.40 = (bf16[208,768]{1,0:T(8,128)(2,1)}, bf16[208,768]{1,0:T(8,128)(2,1)S(1)}, u32[]{:S(2)}, u32[]{:S(2)}) collective-permute-start(bf16[208,768]{1,0:T(8,128)(2,1)} %get-tuple-element.111), channel_id=1, source_target_pairs={{0,3},{1,2},{2,1},{3,0},{4,7},{5,6},{6,5},{7,4},{8,11},{9,10},{10,... | collective-permute-start | bytes 958472 | tf_op jit(solution)/shard_map/ppermute | solution.py:1664
  329.9 18.1 %collective-permute-start.39 = (bf16[208,768]{1,0:T(8,128)(2,1)S(1)}, bf16[208,768]{1,0:T(8,128)(2,1)S(1)}, u32[]{:S(2)}, u32[]{:S(2)}) collective-permute-start(bf16[208,768]{1,0:T(8,128)(2,1)S(1)} %get-tuple-element.112), channel_id=1, source_target_pairs={{0,2},{1,3},{2,0},{3,1},{4,6},{5,7},{6,4},{7,5},{8,10},{9,11},{10,... | collective-permute-start | bytes 958472 | tf_op jit(solution)/shard_map/ppermute | solution.py:1664
  331.2 16.8 %collective-permute-start.38 = (bf16[208,768]{1,0:T(8,128)(2,1)S(1)}, bf16[208,768]{1,0:T(8,128)(2,1)}, u32[]{:S(2)}, u32[]{:S(2)}) collective-permute-start(bf16[208,768]{1,0:T(8,128)(2,1)S(1)} %get-tuple-element.113), channel_id=1, source_target_pairs={{0,1},{1,0},{2,3},{3,2},{4,5},{5,4},{6,7},{7,6},{8,9},{9,8},{10,11... | collective-permute-start | bytes 958472 | tf_op jit(solution)/shard_map/ppermute | solution.py:1664
  331.9 31.1 %collective-permute-start.20 = (bf16[3,128,768]{2,1,0:T(8,128)(2,1)S(1)}, bf16[3,128,768]{2,1,0:T(8,128)(2,1)S(1)}, u32[]{:S(2)}, u32[]{:S(2)}) collective-permute-start(bf16[3,128,768]{2,1,0:T(8,128)(2,1)S(1)} %bitcast.118), channel_id=1, source_target_pairs={{0,16},{1,17},{2,18},{3,19},{4,20},{5,21},{6,22},{7,23},{8,24},{9,... | collective-permute-start | bytes 1769480 | tf_op jit(solution)/shard_map/ppermute | solution.py:1366
  335.0 29.5 %all-to-all-start.4 = ((bf16[16,16,768]{2,1,0:T(8,128)(2,1)}), bf16[16,16,768]{2,1,0:T(8,128)(2,1)S(1)}, u32[]{:S(2)}, u32[]{:S(2)}) async-start(bf16[16,16,768]{2,1,0:T(8,128)(2,1)} %bitcast.47), calls=%async_computation.5 | async-start | bytes 786432 | tf_op jit(solution)/shard_map/all_to_all | solution.py:1666
  353.3 27.7 %collective-permute-start.44 = (bf16[336,768]{1,0:T(8,128)(2,1)}, bf16[336,768]{1,0:T(8,128)(2,1)S(1)}, u32[]{:S(2)}, u32[]{:S(2)}) collective-permute-start(bf16[336,768]{1,0:T(8,128)(2,1)} %shard_map.193.refs_3_), channel_id=1, source_target_pairs={{16,8},{17,9},{18,10},{19,11},{20,12},{21,13},{22,14},{23,15},{24,... | collective-permute-start | bytes 1548296 | tf_op jit(solution)/shard_map/ppermute | solution.py:1366
  354.7 26.9 %collective-permute-start.43 = (bf16[336,768]{1,0:T(8,128)(2,1)}, bf16[336,768]{1,0:T(8,128)(2,1)}, u32[]{:S(2)}, u32[]{:S(2)}) collective-permute-start(bf16[336,768]{1,0:T(8,128)(2,1)} %shard_map.193.refs_3_), channel_id=1, source_target_pairs={{0,8},{1,9},{2,10},{3,11},{4,12},{5,13},{6,14},{7,15},{8,0},{9,1},... | collective-permute-start | bytes 1548296 | tf_op jit(solution)/shard_map/ppermute | solution.py:1366
  (73 other events, 398.1 us)
Sparse Core Ops, SparseCore 0:
  180.9 85.6 reduce-scatter.1

commit v6 on v5

--- a/solution.py
+++ b/solution.py
@@ -69,17 +69,6 @@
     )
 
 
-def locate(positions, lengths_row):
-    padded = (lengths_row + PATCH - 1) // PATCH * PATCH
-    item_ends = jnp.cumsum(padded)
-    starts = item_ends - padded
-    inside = (positions[:, None] >= starts[None, :]) & (positions[:, None] < item_ends[None, :])
-    offsets = jnp.arange(ITEMS, dtype=jnp.int32)[None, :] - ITEMS
-    owners = jnp.sum(jnp.where(inside, offsets, 0), axis=1) + ITEMS
-    live_mask = jnp.any(inside & (positions[:, None] < (starts + lengths_row)[None, :]), axis=1)
-    return (owners, live_mask)
-
-
 def slot_of(q, count):
     if count != GROUPS:
         return q
@@ -214,12 +203,13 @@
     patch_rows,
     numbers_ref,
     ids_ref,
-    table_ref,
+    own_table_ref,
+    new_table_ref,
     sent_ref,
     edge_ref,
     near_ref,
-    gains_ref,
-    biases_ref,
+    own_norms_ref,
+    new_norms_ref,
     out_grad_hbm,
     own_in,
     own_out,
@@ -250,6 +240,7 @@
     grad_attended_ref,
     grad_stream_ref,
     probability_ref,
+    table_ref,
     sems,
     out_sems,
 ):
@@ -277,6 +268,17 @@
     fetch(section, own_contract, new_contract, w_contract, sems.at[3])
     (to_first, first_width), (to_second, second_width) = section_columns(hidden_width, width)
     body = slice(0, rows)
+    norms = jnp.where(section == 0, new_norms_ref[...], own_norms_ref[...])
+    gains, biases = norms[0:2], norms[2:4]
+
+    @pl.when(section == 0)
+    def _():
+        table_ref[...] = new_table_ref[...]
+
+    @pl.when(section != 0)
+    def _():
+        table_ref[...] = own_table_ref[...]
+
     out_count = [0]
 
     def leave(from_first, columns, at_rows=body):
@@ -325,7 +327,7 @@
         spread = jnp.where(columns == chosen, 1.0, 0.0).astype(bf16)
         stream = transposed_product(onehot, table_ref[...]) + product(spread, source_ref[...])
         stream_ref[at, :] = stream
-        normed = layer_norm(stream, gains_ref[0:1], biases_ref[0:1]).astype(bf16)
+        normed = layer_norm(stream, gains[0:1], biases[0:1]).astype(bf16)
         first[at, to_first["normed"]] = normed
         second[at, to_second["normed"]] = normed
         first[at, to_first["branch"]] = jnp.where(
@@ -362,7 +364,7 @@
     for at in blocks:
         middle = stream_ref[at, :] + product(first[at, to_first["attended"]], w_out[...])
         middle_ref[at, :] = middle
-        normed_two = layer_norm(middle, gains_ref[1:2], biases_ref[1:2]).astype(bf16)
+        normed_two = layer_norm(middle, gains[1:2], biases[1:2]).astype(bf16)
         second[at, to_second["normed_two"]] = normed_two
 
     pltpu.make_async_copy(own_expand, w_expand, sems.at[2]).wait()
@@ -397,7 +399,7 @@
     gain_two = bias_two = gain_one = bias_one = jnp.zeros((1, width), f32)
     for at in blocks:
         back, gain, bias = layer_norm_back(
-            middle_ref[at, :], gains_ref[1:2], grad_middle_ref[at, :]
+            middle_ref[at, :], gains[1:2], grad_middle_ref[at, :]
         )
         grad_middle = back + first[at, to_first["branch"]].astype(f32)
         grad_middle_ref[at, :] = grad_middle
@@ -431,7 +433,7 @@
 
     for m, at in enumerate(blocks):
         back, gain, bias = layer_norm_back(
-            stream_ref[at, :], gains_ref[0:1], grad_stream_ref[at, :]
+            stream_ref[at, :], gains[0:1], grad_stream_ref[at, :]
         )
         grad_stream = back + grad_middle_ref[at, :]
         first[at, to_first["stream"]] = grad_stream.astype(bf16)
@@ -463,7 +465,7 @@
     return pltpu.VMEM(shape, kind)
 
 
-def local_block(numbers, ids, table, sent, edge, near, gains, biases, out_grad, patch_rows, own, new):
+def local_block(numbers, ids, tables, sent, edge, near, norms, out_grad, patch_rows, own, new):
     batches, width = out_grad.shape[0], out_grad.shape[2]
     rows = batches * BLOCK
     hidden_width = own[3].shape[0]
@@ -471,7 +473,7 @@
     part = jax.ShapeDtypeStruct((rows + SMALL_ROWS, first_width), bf16)
     return pl.pallas_call(
         partial(local_kernel, patch_rows),
-        in_specs=[SCALARS] + [WHOLE] * 7 + [ANY] * 9,
+        in_specs=[SCALARS] + [WHOLE] * 8 + [ANY] * 9,
         out_specs=[WHOLE] * 3 + [ANY] * 2,
         out_shape=[
             jax.ShapeDtypeStruct((rows, width), bf16),
@@ -497,12 +499,13 @@
             vmem(rows, width),
             vmem(rows, width, kind=f32),
             vmem(batches * PAIRS, 2 * BLOCK, BLOCK, kind=f32),
+            vmem(*tables[0].shape),
             pltpu.SemaphoreType.DMA((4 + batches,)),
             pltpu.SemaphoreType.DMA((6,)),
         ],
         compiler_params=pltpu.CompilerParams(vmem_limit_bytes=VMEM),
         cost_estimate=cost(35),
-    )(numbers, ids, table, sent, edge, near, gains, biases, out_grad, *own, *new)
+    )(numbers, ids, *tables, sent, edge, near, *norms, out_grad, *own, *new)
 
 
 def local_gradients(count, numbers, ids, keep, arrived, hidden_width, width, half, deps=()):
@@ -651,17 +654,18 @@
     )(*arrays)
 
 
-def causal_bias(start, owner_column, owner_row):
-    shape = (BLOCK, owner_row.shape[1])
-    rows = lax.broadcasted_iota(jnp.int32, shape, 0) + start
-    columns = lax.broadcasted_iota(jnp.int32, shape, 1)
-    bias = jnp.where((columns <= rows) & (owner_column == owner_row), 0.0, MASKED)
+def causal_bias(start, count, numbers_ref):
+    spans = item_spans(numbers_ref, 1, numbers_ref[0])
+    rows = lax.broadcasted_iota(jnp.int32, (BLOCK, 1), 0) + start
+    columns = lax.broadcasted_iota(jnp.int32, (1, count), 1)
+    same = owner_of(rows * PATCH, spans) == owner_of(columns * PATCH, spans)
+    bias = jnp.where((columns <= rows) & same, 0.0, MASKED)
     return jnp.concatenate([bias, bias], axis=0)
 
 
-def global_forward_kernel(column_ref, row_ref, qkv_ref, out_ref):
+def global_forward_kernel(numbers_ref, qkv_ref, out_ref):
     start = pl.multiple_of(pl.program_id(0) * BLOCK, BLOCK)
-    bias = causal_bias(start, column_ref[...], row_ref[...])
+    bias = causal_bias(start, qkv_ref.shape[0], numbers_ref)
     out_ref[...] = pair_forward(
         qkv_ref[pl.ds(start, BLOCK), 0:PAIR],
         qkv_ref[:, PAIR : 2 * PAIR],
@@ -671,10 +675,10 @@
     ).astype(bf16)
 
 
-def global_backward_kernel(column_ref, row_ref, qkv_ref, grad_ref, out_ref, key_sum, value_sum):
+def global_backward_kernel(numbers_ref, qkv_ref, grad_ref, out_ref, key_sum, value_sum):
     step = pl.program_id(0)
     start = pl.multiple_of(step * BLOCK, BLOCK)
-    bias = causal_bias(start, column_ref[...], row_ref[...])
+    bias = causal_bias(start, qkv_ref.shape[0], numbers_ref)
 
     @pl.when(step == 0)
     def _():
@@ -701,12 +705,10 @@
         out_ref[:, 2 * PAIR : 3 * PAIR] = value_sum[...].astype(bf16)
 
 
-def global_attention(qkv, owners, grads=None, deps=()):
+def global_attention(qkv, numbers, grads=None, deps=()):
     count = qkv.shape[0]
-    column, row = owners[:, None], owners[None, :]
     specs = [
-        pl.BlockSpec((BLOCK, 1), lambda i: (i, 0)),
-        pl.BlockSpec((1, count), lambda i: (0, 0)),
+        SCALARS,
         pl.BlockSpec((count, 3 * PAIR), lambda i: (0, 0)),
     ]
     blocks = pl.BlockSpec((BLOCK, PAIR), lambda i: (i, 0))
@@ -719,10 +721,10 @@
             out_shape=jax.ShapeDtypeStruct((count, PAIR), bf16),
             compiler_params=pltpu.CompilerParams(vmem_limit_bytes=VMEM),
             cost_estimate=cost(15),
-        )(column, row, qkv)
+        )(numbers, qkv)
 
     def body(*refs):
-        global_backward_kernel(*refs[:4], *refs[4 + len(deps) :])
+        global_backward_kernel(*refs[:3], *refs[3 + len(deps) :])
 
     return pl.pallas_call(
         body,
@@ -733,7 +735,7 @@
         scratch_shapes=[pltpu.VMEM((count, PAIR), f32), pltpu.VMEM((count, PAIR), f32)],
         compiler_params=pltpu.CompilerParams(vmem_limit_bytes=VMEM),
         cost_estimate=cost(30),
-    )(column, row, qkv, grads, *deps)
+    )(numbers, qkv, grads, *deps)
 
 
 def call(kernel, args, specs, out_shape, out_specs, scratch=(), deps=(), micros=1):
@@ -757,47 +759,80 @@
     return jax.ShapeDtypeStruct(shape, kind)
 
 
-def patch_forward(member, ids, table, pieces, deps=()):
-    rows = ids.shape[0]
-    shard, width = pieces[0].shape
-    span = len(pieces)
-
-    def kernel(member_ref, ids_ref, table_ref, *rest):
-        piece_refs, (embedded_ref, weight_ref, share_ref, low_ref) = rest[:span], rest[span:]
-        member_now = member_ref[0]
+def patch_forward(numbers, patch_rows, byte_rows, own_table, new_table, pieces, deps=()):
+    batches, width = byte_rows[0].shape[0], own_table.shape[1]
+    segments = len(byte_rows) * batches
+    rows = segments * patch_rows
+    shard = pieces[0].shape[0]
+    span, count = len(pieces), len(byte_rows)
+    room = (segments + 15) // 16 * 16
+
+    def kernel(numbers_ref, own_ref, new_ref, *rest):
+        byte_refs, piece_refs, rest = rest[:count], rest[count : count + span], rest[count + span :]
+        embedded_ref, weight_ref, share_ref, low_ref, onehot_ref, table_ref = rest
+        member_now = numbers_ref[1]
         for k in range(span):
             start = pl.multiple_of((member_now ^ k) * shard, shard)
             weight_ref[pl.ds(start, shard), :] = piece_refs[k][...]
-        vocabulary = lax.broadcasted_iota(jnp.int32, (rows, VOCAB), 1)
-        onehot = jnp.where(ids_ref[...] == vocabulary, 1.0, 0.0).astype(bf16)
-        embedded_ref[...] = product(onehot, table_ref[...]).astype(bf16)
+
+        @pl.when(numbers_ref[0] == 0)
+        def _():
+            table_ref[...] = own_ref[...]
+
+        @pl.when(numbers_ref[0] != 0)
+        def _():
+            table_ref[...] = new_ref[...]
+
+        some = [ref[...].astype(f32) for ref in byte_refs]
+        some.append(jnp.zeros((room - segments, some[0].shape[1]), f32))
+        some = jnp.concatenate(some, axis=0).astype(bf16)
+        shape = (some.shape[1], rows)
+        place = lax.broadcasted_iota(jnp.int32, shape, 1) % patch_rows * PATCH + numbers_ref[2]
+        picked = lax.broadcasted_iota(jnp.int32, shape, 0) == place
+        wide = product(some, jnp.where(picked, 1.0, 0.0).astype(bf16))
+        segment = lax.broadcasted_iota(jnp.int32, (room, rows), 1) // patch_rows
+        here = lax.broadcasted_iota(jnp.int32, (room, rows), 0) == segment
+        ids = jnp.sum(jnp.where(here, wide, 0.0), axis=0, keepdims=True).astype(jnp.int32)
+        vocabulary = lax.broadcasted_iota(jnp.int32, (VOCAB, rows), 0)
+        onehot = jnp.where(ids == vocabulary, 1.0, 0.0).astype(bf16)
+        onehot_ref[...] = onehot
+        embedded_ref[...] = transposed_product(onehot, table_ref[...]).astype(bf16)
         share = product(embedded_ref[...], weight_ref[...])
         share_ref[...] = share
         low_ref[...] = share.astype(bf16)
 
     return call(
         kernel,
-        (member, ids.reshape(rows, 1), table, *pieces),
-        [SCALARS] + [WHOLE] * (2 + span),
+        (numbers, own_table, new_table, *byte_rows, *pieces),
+        [SCALARS] + [WHOLE] * (2 + count + span),
         [
             shaped(rows, width),
             shaped(span * shard, width),
             shaped(rows, width, kind=f32),
             shaped(rows, width),
+            shaped(VOCAB, rows),
         ],
-        [WHOLE] * 4,
+        [WHOLE] * 5,
+        [pltpu.VMEM(own_table.shape, bf16)],
         deps=deps,
         micros=4,
     )
 
 
-def split_heads(values, target, start, batches, part, width_of_task):
+def split_heads(values, targets, batches, part):
     patch_rows = values.shape[0] // batches
-    for m in range(batches):
-        for pair in range(PAIRS):
-            target[m * PAIRS + pair, :, part * PAIR : (part + 1) * PAIR] = values[
-                m * patch_rows : (m + 1) * patch_rows, pair * PAIR : (pair + 1) * PAIR
-            ]
+    first = targets[0].shape[0]
+    for t in range(batches * PAIRS):
+        m, pair = t // PAIRS, t % PAIRS
+        target = targets[0].at[t] if t < first else targets[1].at[t - first]
+        target[:, part * PAIR : (part + 1) * PAIR] = values[
+            m * patch_rows : (m + 1) * patch_rows, pair * PAIR : (pair + 1) * PAIR
+        ]
+
+
+def task_shapes(batches, first, patch_rows, columns):
+    rest = batches * PAIRS - first
+    return [shaped(first, patch_rows, columns)] + ([shaped(rest, patch_rows, columns)] if rest else [])
 
 
 def merge_heads(blocks, target, batches, parts):
@@ -824,15 +859,15 @@
         target[k, :, offset : offset + 4 * size] = jnp.concatenate(parts, axis=1)
 
 
-def global_start(batches, own, others, gains, biases, heads_in):
+def global_start(batches, first_tasks, own, others, gains, biases, heads_in):
     rows, width = own.shape
     patch_rows = rows // batches
+    tasks = task_shapes(batches, first_tasks, patch_rows, 3 * PAIR)
 
     def kernel(own_ref, gains_ref, biases_ref, weight_hbm, *rest):
-        other_refs, (stream_ref, normed_ref, task_ref, share_ref, weight, sem) = (
-            rest[: len(others)],
-            rest[len(others) :],
-        )
+        other_refs, rest = rest[: len(others)], rest[len(others) :]
+        (stream_ref, normed_ref, share_ref), task_refs = rest[:3], rest[3 : 3 + len(tasks)]
+        weight, sem = rest[3 + len(tasks) :]
         load = pltpu.make_async_copy(weight_hbm, weight, sem)
         load.start()
         stream = own_ref[...]
@@ -845,7 +880,7 @@
         load.wait()
         for part in range(3):
             mixed = product(normed, weight[:, part * width : (part + 1) * width]).astype(bf16)
-            split_heads(mixed, task_ref, 0, batches, part, width)
+            split_heads(mixed, task_refs, batches, part)
 
     return call(
         kernel,
@@ -854,10 +889,10 @@
         [
             shaped(rows, width, kind=f32),
             shaped(rows, width),
-            shaped(batches * PAIRS, patch_rows, 3 * PAIR),
             shaped(SPAN, rows, width // SPAN),
+            *tasks,
         ],
-        [WHOLE] * 4,
+        [WHOLE] * (3 + len(tasks)),
         [pltpu.VMEM(heads_in.shape, bf16), pltpu.SemaphoreType.DMA],
         micros=5,
     )
@@ -936,18 +971,19 @@
 
 
 def global_feed_backward(
-    batches, own, near, edge, middle, slope, gains, heads_out, expand, contract, deps=()
+    batches, first_tasks, own, near, edge, middle, slope, gains, heads_out, expand, contract, deps=()
 ):
     rows, width = middle.shape
     hidden_width = expand.shape[1]
     patch_rows = rows // batches
     half = patch_rows // 2
+    tasks = task_shapes(batches, first_tasks, patch_rows, PAIR)
 
     def kernel(
         own_ref, near_ref, edge_ref, middle_ref, slope_ref, gains_ref, out_hbm, expand_hbm,
-        contract_hbm, upward_ref, grad_middle_ref, branch_ref, task_ref, small_ref, grad_ref,
-        w_out, w_expand, w_contract, sems,
+        contract_hbm, upward_ref, grad_middle_ref, branch_ref, small_ref, grad_ref, *rest,
     ):
+        task_refs, (w_out, w_expand, w_contract, sems) = rest[: len(tasks)], rest[len(tasks) :]
         loads = [
             pltpu.make_async_copy(contract_hbm, w_contract, sems.at[2]),
             pltpu.make_async_copy(expand_hbm, w_expand, sems.at[1]),
@@ -988,7 +1024,7 @@
         small_ref[...] = jnp.concatenate([gain, bias], axis=0)
         loads[2].wait()
         attended = product_transposed(branch, w_out[...]).astype(bf16)
-        split_heads(attended, task_ref, 0, batches, 0, width)
+        split_heads(attended, task_refs, batches, 0)
 
     return call(
         kernel,
@@ -998,11 +1034,11 @@
             shaped(rows, hidden_width),
             shaped(rows, width, kind=f32),
             shaped(rows, width),
-            shaped(batches * PAIRS, patch_rows, PAIR),
             shaped(2, width, kind=f32),
             shaped(rows, width),
+            *tasks,
         ],
-        [WHOLE] * 6,
+        [WHOLE] * (5 + len(tasks)),
         [
             pltpu.VMEM(heads_out.shape, bf16),
             pltpu.VMEM(expand.shape, bf16),
@@ -1048,14 +1084,14 @@
     )
 
 
-def patch_backward(section, ids, embedded, weight, own, crossed, span, deps=()):
+def patch_backward(section, onehot, embedded, weight, own, crossed, span, deps=()):
     rows, width = embedded.shape
     block = own[0].shape[0]
     n = len(own)
     used = rows // n
     shard = weight.shape[0] // span
 
-    def kernel(section_ref, ids_ref, embedded_ref, weight_ref, crossed_ref, *rest):
+    def kernel(section_ref, onehot_ref, embedded_ref, weight_ref, crossed_ref, *rest):
         own_refs, (patch_ref, table_ref, gathered, small) = rest[:n], rest[n:]
 
         @pl.when(section_ref[0] == 0)
@@ -1076,13 +1112,11 @@
             patch_ref[k, 0:shard, :] = part[k * shard : (k + 1) * shard]
             patch_ref[k, shard:, :] = small[...]
         grad_embedded = product_transposed(gathered[...], weight_ref[...]).astype(bf16)
-        vocabulary = lax.broadcasted_iota(jnp.int32, (rows, VOCAB), 1)
-        onehot = jnp.where(ids_ref[...] == vocabulary, 1.0, 0.0).astype(bf16)
-        table_ref[...] = transposed_product(onehot, grad_embedded).astype(bf16)
+        table_ref[...] = product(onehot_ref[...], grad_embedded).astype(bf16)
 
     return call(
         kernel,
-        (section, ids.reshape(rows, 1), embedded, weight, crossed, *own),
+        (section, onehot, embedded, weight, crossed, *own),
         [SCALARS] + [WHOLE] * (4 + n),
         [shaped(span, shard + SMALL_ROWS, width), shaped(VOCAB, width)],
         [WHOLE] * 2,
@@ -1266,33 +1300,30 @@
     )
 
 
-def half_sum(which, kept, near, deps=()):
+def half_sums(upper, kept, near, deps=()):
     shape = kept.shape[1:]
 
-    def kernel(which_ref, kept_ref, near_ref, out_ref):
-        total = kept_ref[0].astype(f32) + near_ref[0].astype(f32)
-        out_ref[...] = total.astype(bf16)
-
-    count = len(deps)
-
-    def body(*refs):
-        kernel(*refs[:3], refs[-1])
-
-    steps = 1 if shape[0] % 32 else 2
-    size = shape[0] // steps
-    spec = pl.BlockSpec((1, size, shape[1]), lambda i, ref: (ref[0], i, 0))
-    return pl.pallas_call(
-        body,
-        grid_spec=pltpu.PrefetchScalarGridSpec(
-            num_scalar_prefetch=1,
-            grid=(steps,),
-            in_specs=[spec, spec] + [ANY] * count,
-            out_specs=pl.BlockSpec((size, shape[1]), lambda i, ref: (i, 0)),
-        ),
-        out_shape=shaped(*shape),
-        compiler_params=pltpu.CompilerParams(vmem_limit_bytes=VMEM),
-        cost_estimate=cost(2),
-    )(which, kept, near, *deps)
+    def kernel(upper_ref, kept_ref, near_ref, far_ref, mine_ref):
+        for k in range(2):
+            total = (kept_ref[k].astype(f32) + near_ref[k].astype(f32)).astype(bf16)
+
+            @pl.when(upper_ref[0] == k)
+            def _():
+                mine_ref[...] = total
+
+            @pl.when(upper_ref[0] != k)
+            def _():
+                far_ref[...] = total
+
+    return call(
+        kernel,
+        (upper, kept, near),
+        [SCALARS, WHOLE, WHOLE],
+        [shaped(*shape)] * 2,
+        [WHOLE] * 2,
+        deps=deps,
+        micros=2,
+    )
 
 
 def finish(section, deep, shard, room, own_global, own_local, crossed, fars, table_parts, patch_parts):
@@ -1354,6 +1385,40 @@
         ],
         [WHOLE] * 7,
         micros=4,
+    )
+
+
+def activation_rows(numbers, sent, other, own, deps=()):
+    batches, half, width = own.shape
+    patch_rows = sent.shape[0] // batches
+    byte_rows = patch_rows * PATCH
+
+    def kernel(numbers_ref, sent_ref, other_ref, own_ref, out_ref):
+        @pl.when(numbers_ref[0] == 0)
+        def _():
+            rows = lax.broadcasted_iota(jnp.int32, (byte_rows, 1), 0)
+            columns = lax.broadcasted_iota(jnp.int32, (byte_rows, patch_rows), 1)
+            for m in range(batches):
+                live = is_live(numbers_ref[1] + rows, item_spans(numbers_ref, 3, m))
+                chosen = jnp.where(live, rows // PATCH, -1)
+                spread = jnp.where(columns == chosen, 1.0, 0.0).astype(bf16)
+                part = sent_ref[m * patch_rows : (m + 1) * patch_rows, :]
+                out_ref[m] = product(spread, part).astype(bf16)
+
+        @pl.when(numbers_ref[0] != 0)
+        def _():
+            for m in range(batches):
+                out_ref[m, 0:half, :] = other_ref[m]
+                out_ref[m, half:, :] = own_ref[m]
+
+    return call(
+        kernel,
+        (numbers, sent, other, own),
+        [SCALARS] + [WHOLE] * 3,
+        shaped(batches, byte_rows, width),
+        WHOLE,
+        deps=deps,
+        micros=2,
     )
 
 
@@ -1426,19 +1491,14 @@
     for k in range(1, span):
         pieces.append(lax.ppermute(patch_weight, SEQ, [(i, i ^ k) for i in range(count)]))
     other_table = section_swap(own_table)
-    global_table = jnp.where(is_global, own_table, other_table)
-    local_table = jnp.where(is_global, other_table, own_table)
-    which_byte = section * quarters + group
-    byte_ids = []
-    for k in range(quarters):
-        theirs = byte_values
-        if k:
-            theirs = lax.ppermute(byte_values, SEQ, [(i, i ^ (k * span)) for i in range(count)])
-        theirs = theirs.reshape(rows, PATCH)
-        byte_ids.append(lax.dynamic_index_in_dim(theirs, which_byte, 1, keepdims=False))
-    byte_ids = jnp.concatenate(byte_ids)
-    embedded, byte_weight, shares, low_shares = patch_forward(
-        member.reshape(1).astype(jnp.int32), byte_ids, global_table, pieces
+    theirs = [byte_values]
+    for k in range(1, quarters):
+        theirs.append(
+            lax.ppermute(byte_values, SEQ, [(i, i ^ (k * span)) for i in range(count)])
+        )
+    place_numbers = jnp.stack([section, member, section * quarters + group]).astype(jnp.int32)
+    embedded, byte_weight, shares, low_shares, byte_onehot = patch_forward(
+        place_numbers, patch_rows, theirs, own_table, other_table, pieces
     )
     shares = shares + section_send(low_shares, 1, 0, straight).astype(f32)
     shares = shares.reshape(quarters, rows, width)
@@ -1448,19 +1508,18 @@
         parts.append(section_send(shares[k].astype(bf16), 0, 0, pairs))
 
     arrived = [section_send(w, 1, 0, straight) for w in (heads_in, heads_out, expand, contract)]
-    other_norms = section_swap(jnp.concatenate([gains, biases]))
-    local_gains = jnp.where(is_global, other_norms[:2], gains)
-    local_biases = jnp.where(is_global, other_norms[2:], biases)
+    own_norms = jnp.concatenate([gains, biases])
+    other_norms = section_swap(own_norms)
 
     tasks = batches * PAIRS
     first_tasks = min(tasks, count)
     spare_tasks = tasks - first_tasks
 
-    def to_tasks(blocks):
-        columns = blocks.shape[2]
-        slots = jnp.pad(blocks[:first_tasks], ((0, count - first_tasks), (0, 0), (0, 0)))
+    def to_tasks(first, spare=None):
+        columns = first.shape[2]
+        slots = jnp.pad(first, ((0, count - first_tasks), (0, 0), (0, 0)))
         if spare_tasks:
-            spare = section_send(blocks[first_tasks:], 0, 1, straight)
+            spare = section_send(spare, 0, 1, straight)
             spare = jnp.pad(spare, ((0, count - spare_tasks), (0, 0), (0, 0)))
             slots = jnp.where(is_global, slots, spare)
         landed = lax.all_to_all(slots, SEQ, 0, 0)
@@ -1474,16 +1533,16 @@
         return [slots]
 
     task = jnp.minimum(jnp.where(is_global, place, first_tasks + place), tasks - 1)
-    task_lengths = lax.dynamic_index_in_dim(item_lengths, task // PAIRS, 0, keepdims=False)
-    task_owners = locate(jnp.arange(total_patches, dtype=jnp.int32) * PATCH, task_lengths)[0]
-
-    stream, normed, tasks_out, normed_share = global_start(
-        batches, shares[0], parts, gains, biases, heads_in
-    )
-    qkv = to_tasks(tasks_out)
+    lengths = item_lengths.reshape(-1)
+    task_numbers = jnp.concatenate([(task // PAIRS).reshape(1).astype(jnp.int32), lengths])
+
+    stream, normed, normed_share, *tasks_out = global_start(
+        batches, first_tasks, shares[0], parts, gains, biases, heads_in
+    )
+    qkv = to_tasks(*tasks_out)
     attended, middle, normed_two, slope, hidden, sent, feed_share, other_share, edge, near = global_feed_forward(
         batches,
-        from_tasks(global_attention(qkv, task_owners)),
+        from_tasks(global_attention(qkv, task_numbers)),
         stream,
         gains,
         biases,
@@ -1506,18 +1565,17 @@
         numbers = jnp.concatenate(
             [
                 jnp.stack([section, place * byte_rows, jnp.int32(c)]).astype(jnp.int32),
-                item_lengths.reshape(-1),
+                lengths,
             ]
         )
         act, grad_shifted, grad_edge, keep, send = local_block(
             numbers,
             byte_values,
-            local_table,
+            (own_table, other_table),
             sent,
             edge,
             near,
-            local_gains,
-            local_biases,
+            (own_norms, other_norms),
             out_grad,
             patch_rows,
             weights,
@@ -1531,15 +1589,7 @@
     grad_shifted = jnp.concatenate(grads_shifted, axis=1).reshape(batches * half, width)
 
     other_out = section_send(local_out, 0, 1, straight)
-    byte_places = place * byte_rows + jnp.arange(byte_rows, dtype=jnp.int32)
-    live_bytes = jnp.stack([locate(byte_places, item_lengths[m])[1] for m in range(batches)])
-    own_sent = jnp.broadcast_to(
-        sent.reshape(batches, patch_rows, 1, width), (batches, patch_rows, PATCH, width)
-    ).reshape(batches, byte_rows, width)
-    own_sent = jnp.where(live_bytes[:, :, None], own_sent, jnp.zeros((), bf16))
-    activations = jnp.where(
-        is_global, own_sent, jnp.concatenate([other_out, local_out], axis=1)
-    )
+    activations = activation_rows(numbers, sent, other_out, local_out)
 
     shard = width // count
     room = VOCAB // count
@@ -1600,8 +1650,9 @@
     if chunks > 1:
         half_locals = [sum(x.astype(f32) for x in half_locals).astype(bf16)]
     half_locals = half_locals[0]
-    grad_upward, grad_middle, attend_branch, task_grads, small, grad_sent = global_feed_backward(
+    grad_upward, grad_middle, attend_branch, small, grad_sent, *task_grads = global_feed_backward(
         batches,
+        first_tasks,
         grad_shifted,
         near_back,
         edge_back,
@@ -1618,8 +1669,8 @@
         second_parts = section_send(
             pack_second(member_flag, other_share, attend_branch, grad_upward, whole), 0, 1, straight
         )
-    task_grads = to_tasks(task_grads)
-    task_mixed = global_attention(qkv, task_owners, task_grads)
+    task_grads = to_tasks(*task_grads)
+    task_mixed = global_attention(qkv, task_numbers, task_grads)
     grad_mixed, own_rows, small = global_end(
         batches,
         from_tasks(task_mixed),
@@ -1643,7 +1694,7 @@
     crossed = section_send(jnp.concatenate(gathered), 0, 1, straight)
     patch_share, table_share = patch_backward(
         flag,
-        byte_ids,
+        byte_onehot,
         embedded,
         byte_weight,
         gathered,
@@ -1680,8 +1731,7 @@
         )
 
     if in_plane:
-        local_far = half_sum(1 - upper_flag, local_kept, local_near)
-        local_mine = half_sum(upper_flag, local_kept, local_near)
+        local_far, local_mine = half_sums(upper_flag, local_kept, local_near)
         across = group_pairs(2)
         local_fars = [
             section_send(local_far, 0, 1, across),
@@ -1696,8 +1746,7 @@
             [patch_share, *local_fars],
         )
         near = both_send(leaving, group_pairs(1))
-        far = half_sum(1 - upper_flag, kept, near, patch_parts[1:])
-        mine = half_sum(upper_flag, kept, near, [far])
+        far, mine = half_sums(upper_flag, kept, near, patch_parts[1:])
         extra = mine.shape[0] - local_mine.shape[0]
         crossed = section_swap(
             jnp.where(is_global, jnp.pad(local_mine, ((0, extra), (0, 0))), mine)

time: 402 us -> 398 us (0.990)
  waiting for transfers between devices: 105 us -> 118 us
  starting transfers between devices: 113 us -> 104 us
  other arithmetic: 13 us -> 8.7 us
    ppermute x27, starting transfers between devices: 65.2 us -> 54.3 us  [section_send(): return lax.ppermute(x, ('section',) + SEQ, joint)]
    ppermute x27, waiting for transfers between devices: 39 us -> 48.7 us  [section_send(): return lax.ppermute(x, ('section',) + SEQ, joint)]
    ppermute x3, waiting for transfers between devices: 8.49 us -> 0.01 us  [on_device(): lax.ppermute(patch_weight, SEQ, [(i, i ^ k) for i in range(count)])]
    pallas_call x11 -> x14, Pallas kernels: 54.3 us -> 62.7 us  [call(): pl.pallas_call(body, in_specs=list(specs) + [ANY] * len(deps), out_specs=...]
    pallas_call x4 -> x0, Pallas kernels: 8.29 us -> none  [half_sum(): pl.pallas_call(body, grid_spec=pltpu.PrefetchScalarGridSpec(num_scalar_pr...]
    ppermute x3, waiting for transfers between devices: 0.53 us -> 4.72 us  [on_device(): lax.ppermute(byte_values, SEQ, [(i, i ^ k * span) for i in range(count)])]
    unnamed x110 -> x96, local copies, waits for them, and re-layouts: 9.21 us -> 10.9 us
  transfers between devices with their start and end apart: 50 -> 50, of which waited for: 24 -> 26; matrix products, arithmetic and copies ran while one was open for 5% -> 3% of each run, Pallas kernels for 15% -> 15%
where the time goes in v6:
time: 398 us; the launch traced here: 391 us
  waiting for transfers between devices  118 us (30%)
  Pallas kernels  116 us (29%)
  starting transfers between devices  104 us (26%)
  blocking collectives  15.4 us (4%)
  between operations  15.2 us (4%)
  local copies, waits for them, and re-layouts  14 us (4%)
  other arithmetic  8.7 us (2%)
    pallas_call x14, Pallas kernels, call(): pl.pallas_call(body, in_specs=list(specs) + [ANY] * len(deps), out_specs=...  62.7 us
    ppermute x27, starting transfers between devices, section_send(): return lax.ppermute(x, ('section',) + SEQ, joint)  54.3 us
    ppermute x27, waiting for transfers between devices, section_send(): return lax.ppermute(x, ('section',) + SEQ, joint)  48.7 us
    ppermute x5, waiting for transfers between devices, both_send(): return lax.ppermute(x, ('section',) + SEQ, joint)  32.3 us
    pallas_call x1, Pallas kernels, local_block(): pl.pallas_call(partial(local_kernel, patch_rows), in_specs=[SCALARS] + [W...  31.6 us
    all_to_all x1, blocking collectives, from_tasks(): lax.all_to_all(results.reshape(count, patch_rows, columns), SEQ, 0, 0)  15.4 us
    all_to_all x2, waiting for transfers between devices, to_tasks(): landed = lax.all_to_all(slots, SEQ, 0, 0)  13.4 us
    ppermute x5, starting transfers between devices, both_send(): return lax.ppermute(x, ('section',) + SEQ, joint)  13.2 us
  transfers between devices with their start and end apart: 50, of which 26 were waited for; matrix products, arithmetic and copies ran while one was open for 3% of the time, Pallas kernels for 15%

profile of v6, /device:TPU:0, one launch (start us, length us, event | category | flops | bytes accessed | tf_op | source)
XLA Modules:
  0.0 390.8 jit_solution(7322023291656777787)
XLA Ops:
  20.5 3.9 %collective-permute-start.3 = (s32[3,256]{1,0:T(4,128)}, s32[3,256]{1,0:T(4,128)S(1)}, u32[]{:S(2)}, u32[]{:S(2)}) collective-permute-start(s32[3,256]{1,0:T(4,128)} %ids_ref.3), channel_id=1, source_target_pairs={{0,12},{1,13},{2,14},{3,15},{4,8},{5,9},{6,10},{7,11},{8,4},{9,5},... | collective-permute-start | bytes 9224 | tf_op jit(solution)/shard_map/ppermute | solution.py:1497
  27.9 4.0 %shard_map.178 = (bf16[384,768]{1,0:T(8,128)(2,1)}, bf16[768,768]{1,0:T(8,128)(2,1)}, f32[384,768]{1,0:T(8,128)}, bf16[384,768]{1,0:T(8,128)(2,1)}, bf16[256,384]{1,0:T(8,128)(2,1)}) custom-call(s32[3]{0:T(128)} %pad_add_fusion.1.refs_0_, bf16[256,768]{1,0:T(8,128)(2,1)} %bitcast.72, bf16[256,768]{1,0:T(8,128)(2,1)} %copy-done.29, s32[3,256]{1,0:T(4,128)} %ids_ref.3, ...), custom_call_target="tpu_custom_call" | custom-call | flops 4400000000 | bytes 1 | tf_op jit(solution)/shard_map/pallas_call | solution.py:747
  37.4 5.7 %collective-permute-start.10 = (bf16[96,768]{1,0:T(8,128)(2,1)S(1)}, bf16[96,768]{1,0:T(8,128)(2,1)S(1)}, u32[]{:S(2)}, u32[]{:S(2)}) collective-permute-start(bf16[96,768]{1,0:T(8,128)(2,1)S(1)} %get-tuple-element.119), channel_id=1, source_target_pairs={{0,12},{1,13},{2,14},{3,15},{4,8},{5,9},{6,10},{7,11},{8,4},{9,5},... | collective-permute-start | bytes 442376 | tf_op jit(solution)/shard_map/ppermute | solution.py:1431
  50.2 4.4 %collective-permute-done.9.refs_5_ = bf16[96,768]{1,0:T(8,128)(2,1)S(1)} collective-permute-done((bf16[96,768]{1,0:T(8,128)(2,1)S(1)}, bf16[96,768]{1,0:T(8,128)(2,1)S(1)}, u32[]{:S(2)}, u32[]{:S(2)}) %collective-permute-start.9) | collective-permute-done | bytes 147488 | tf_op jit(solution)/shard_map/ppermute | solution.py:1431
  55.2 4.6 %shard_map.179 = (f32[96,768]{1,0:T(8,128)}, bf16[96,768]{1,0:T(8,128)(2,1)}, bf16[4,96,192]{2,1,0:T(8,128)(2,1)}, bf16[16,32,384]{2,1,0:T(8,128)(2,1)}, bf16[2,32,384]{2,1,0:T(8,128)(2,1)}) custom-call(f32[96,768]{1,0:T(8,128)} %slice.43.refs_0_, f32[2,768]{1,0:T(2,128)} %bitcast.48, f32[2,768]{1,0:T(2,128)} %bitcast.45, bf16[768,2304]{1,0:T(8,128)(2,1)} %bitcast.61, ...), custom_call_target="tpu_custom_call" | custom-call | flops 5500000256 | bytes 1 | tf_op jit(solution)/shard_map/pallas_call | solution.py:747
  64.1 4.7 %all-to-all-start = ((bf16[16,32,384]{2,1,0:T(8,128)(2,1)}), bf16[16,32,384]{2,1,0:T(8,128)(2,1)S(1)}, u32[]{:S(2)}, u32[]{:S(2)}) async-start(bf16[16,32,384]{2,1,0:T(8,128)(2,1)} %pad_select_fusion.1), calls=%async_computation | async-start | bytes 786432 | tf_op jit(solution)/shard_map/all_to_all | solution.py:1525
  70.8 10.1 %all-to-all-done = bf16[16,32,384]{2,1,0:T(8,128)(2,1)S(1)} async-done(((bf16[16,32,384]{2,1,0:T(8,128)(2,1)}), bf16[16,32,384]{2,1,0:T(8,128)(2,1)S(1)}, u32[]{:S(2)}, u32[]{:S(2)}) %all-to-all-start) | async-done | bytes 393248 | tf_op jit(solution)/shard_map/all_to_all | solution.py:1525
  81.7 4.1 %shard_map.180 = bf16[512,128]{1,0:T(8,128)(2,1)} custom-call(s32[13]{0:T(128)} %pad_add_fusion.2.numbers_ref.refs_0_, bf16[512,384]{1,0:T(8,128)(2,1)} %bitcast.40), custom_call_target="tpu_custom_call" | custom-call | flops 16499999744 | bytes 1 | tf_op jit(solution)/shard_map/pallas_call | solution.py:716
  85.8 3.6 all-to-all-start.1
  90.8 6.4 %all-to-all-done.1.refs_6_ = bf16[16,32,128]{2,1,0:T(8,128)(2,1)S(1)} async-done(((bf16[16,32,128]{2,1,0:T(8,128)(2,1)}), bf16[16,32,128]{2,1,0:T(8,128)(2,1)S(1)}, u32[]{:S(2)}, u32[]{:S(2)}) %all-to-all-start.1) | async-done | bytes 131104 | tf_op jit(solution)/shard_map/all_to_all | solution.py:1530
  100.9 7.4 %shard_map.181 = (bf16[96,768]{1,0:T(8,128)(2,1)}, f32[96,768]{1,0:T(8,128)}, bf16[96,768]{1,0:T(8,128)(2,1)}, bf16[96,3072]{1,0:T(8,128)(2,1)}, bf16[96,3072]{1...) custom-call(f32[96,768]{1,0:T(8,128)} %get-tuple-element.63.refs_0_,, ...), custom_call_target="tpu_custom_call" | custom-call | flops 8800000000 | bytes 1 | tf_op jit(solution)/shard_map/pallas_call | solution.py:747
  115.8 31.6 %shard_map.182 = (bf16[384,768]{1,0:T(8,128)(2,1)}, bf16[48,768]{1,0:T(8,128)(2,1)}, bf16[16,768]{1,0:T(8,128)(2,1)}, bf16[400,7680]{1,0:T(8,128)(2,1)}, bf16[400,7680]{1,0:T(8,128)(2,1)}) custom-call(s32[15]{0:T(128)} %pad_add_fusion.numbers_ref.refs_0_, s32[3,256]{1,0:T(4,128)} %ids_ref.3, bf16[256,768]{1,0:T(8,128)(2,1)} %bitcast.73, ...), custom_call_target="tpu_custom_call" | custom-call | flops 38499999744 | bytes 1 | tf_op jit(solution)/shard_map/pallas_call | solution.py:474
  150.1 4.9 %collective-permute-done.22.rest_1_.refs_2_ = bf16[16,768]{1,0:T(8,128)(2,1)S(1)} collective-permute-done((bf16[16,768]{1,0:T(8,128)(2,1)}, bf16[16,768]{1,0:T(8,128)(2,1)S(1)}, u32[]{:S(2)}, u32[]{:S(2)}) %collective-permute-start.22) | collective-permute-done | bytes 24608 | tf_op jit(solution)/shard_map/ppermute | solution.py:1431
  158.3 11.6 %shard_map.184.refs_9_ = bf16[16,304,768]{2,1,0:T(8,128)(2,1)} custom-call(s32[15]{0:T(128)} %pad_add_fusion.numbers_ref.refs_0_, s32[3,256]{1,0:T(4,128)} %ids_ref.3, bf16[400,7680]{1,0:T(8,128)(2,1)} %get-tuple-element.76.keep_ref, bf16[400,7680]{1,0:T(8,128)(2,1)} %collective-permute-done.23.new_ref, bf16[48,768]{1,0:T(8,128)(2,1)} %copy-done.39, ...), custom_call_target="tpu_custom_call" | custom-call | flops 13200000000 | bytes 1 | tf_op jit(solution)/shard_map/pallas_call | solution.py:598
  170.0 9.1 %shard_map.185 = (bf16[96,3072]{1,0:T(8,128)(2,1)}, f32[96,768]{1,0:T(8,128)}, bf16[96,768]{1,0:T(8,128)(2,1)}, f32[2,768]{1,0:T(2,128)}, bf16[96,768]{1,0:T(8,1...) custom-call(bf16[48,768]{1,0:T(8,128)(2,1)} %get-tuple-element.72.refs_0_, ...), custom_call_target="tpu_custom_call" | custom-call | flops 11000000512 | bytes 1 | tf_op jit(solution)/shard_map/pallas_call | solution.py:747
  184.6 5.7 %all-to-all-start.2 = ((bf16[16,32,128]{2,1,0:T(8,128)(2,1)}), bf16[16,32,128]{2,1,0:T(8,128)(2,1)S(1)}, u32[]{:S(2)}, u32[]{:S(2)}) async-start(bf16[16,32,128]{2,1,0:T(8,128)(2,1)} %pad_select_fusion.2), calls=%async_computation.2 | async-start | bytes 262144 | tf_op jit(solution)/shard_map/all_to_all | solution.py:1525
  194.9 3.3 all-to-all-done.2
  198.8 5.8 %shard_map.186 = bf16[512,384]{1,0:T(8,128)(2,1)} custom-call(s32[13]{0:T(128)} %pad_add_fusion.2.numbers_ref.refs_0_, bf16[512,384]{1,0:T(8,128)(2,1)} %bitcast.41, bf16[512,128]{1,0:T(8,128)(2,1)} %bitcast.43), custom_call_target="tpu_custom_call" | custom-call | flops 32999999488 | bytes 1 | tf_op jit(solution)/shard_map/pallas_call | solution.py:729
  204.6 15.4 %all_to_all.25.refs_5_ = bf16[16,32,384]{2,1,0:T(8,128)(2,1)S(1)} all-to-all(bf16[16,32,384]{2,1,0:T(8,128)(2,1)} %bitcast.42), channel_id=1, replica_groups=mesh['section'=2,'group'=4,'member'=4] {'group','member'}, dimensions={0} | all-to-all | bytes 786432 | tf_op jit(solution)/shard_map/all_to_all | solution.py:1530
  223.8 5.3 %shard_map.187 = (bf16[96,2304]{1,0:T(8,128)(2,1)}, bf16[112,768]{1,0:T(8,128)(2,1)}, f32[4,768]{1,0:T(4,128)}) custom-call(f32[96,768]{1,0:T(8,128)} %get-tuple-element.63.refs_0_, f32[96,768]{1,0:T(8,128)} %get-tuple-element.79.refs_1_, f32[2,768]{1,0:T(2,128)} %get-tuple-element.80.refs_2_, f32[2,768]{1,0:T(2,128)} %bitcast.51, ...), custom_call_target="tpu_custom_call" | custom-call | flops 6600000000 | bytes 1 | tf_op jit(solution)/shard_map/pallas_call | solution.py:747
  230.8 4.0 %shard_map.189 = (bf16[96,4224]{1,0:T(8,128)(2,1)}, bf16[96,4224]{1,0:T(8,128)(2,1)}, bf16[96,4224]{1,0:T(8,128)(2,1)}, bf16[96,4224]{1,0:T(8,128)(2,1)}, bf16[112,768]{1,0:T(8,128)(2,1)}) custom-call(s32[1]{0:T(128)} %bitcast.refs_0_, s32[1]{0:T(128)} %bitcast.18.refs_0_.refs_1_, bf16[4,96,768]{2,1,0:T(8,128)(2,1)} %get-tuple-element.70.refs_2_, ...), custom_call_target="tpu_custom_call" | custom-call | flops 4400000000 | bytes 1 | tf_op jit(solution)/shard_map/pallas_call | solution.py:747
  240.9 4.0 %collective-permute-start.32 = (bf16[112,768]{1,0:T(8,128)(2,1)}, bf16[112,768]{1,0:T(8,128)(2,1)S(1)}, u32[]{:S(2)}, u32[]{:S(2)}) collective-permute-start(bf16[112,768]{1,0:T(8,128)(2,1)} %get-tuple-element.95.refs_5_), channel_id=1, source_target_pairs={{0,12},{1,13},{2,14},{3,15},{4,8},{5,9},{6,10},{7,11},{8,4},{9,5},... | collective-permute-start | bytes 516104 | tf_op jit(solution)/shard_map/ppermute | solution.py:1431
  264.6 17.7 %collective-permute-done.34.refs_2_ = bf16[2,304,768]{2,1,0:T(8,128)(2,1)S(1)} collective-permute-done((bf16[2,304,768]{2,1,0:T(8,128)(2,1)}, bf16[2,304,768]{2,1,0:T(8,128)(2,1)S(1)}, u32[]{:S(2)}, u32[]{:S(2)}) %collective-permute-start.34) | collective-permute-done | bytes 933920 | tf_op jit(solution)/shard_map/ppermute | solution.py:1632
  289.8 9.3 %collective-permute-done.28.refs_10_.refs_4_ = bf16[96,4224]{1,0:T(8,128)(2,1)} collective-permute-done((bf16[96,4224]{1,0:T(8,128)(2,1)S(1)}, bf16[96,4224]{1,0:T(8,128)(2,1)}, u32[]{:S(2)}, u32[]{:S(2)}) %collective-permute-start.28) | collective-permute-done | bytes 811040 | tf_op jit(solution)/shard_map/ppermute | solution.py:1632
  299.2 4.5 %shard_map.190 = (bf16[4,208,768]{2,1,0:T(8,128)(2,1)}, bf16[256,768]{1,0:T(8,128)(2,1)}) custom-call(s32[1]{0:T(128)} %bitcast.refs_0_, bf16[256,384]{1,0:T(8,128)(2,1)} %get-tuple-element.92.refs_1_, bf16[384,768]{1,0:T(8,128)(2,1)} %get-tuple-element.93.refs_2_, bf16[768,768]{1,0:T(8,128)(2,1)} %get-tuple-element.94.refs_3_, bf16[448,768]{1,0:T(8,128)(2,1)} %copy-done.22, ...), custom_call_target="tpu_custom_call" | custom-call | flops 6600000000 | bytes 1 | tf_op jit(solution)/shard_map/pallas_call | solution.py:747
  304.6 4.6 %shard_map.193 = (bf16[2,336,768]{2,1,0:T(8,128)(2,1)}, bf16[2,336,768]{2,1,0:T(8,128)(2,1)}) custom-call(s32[1]{0:T(128)} %bitcast.refs_0_, s32[1]{0:T(128)} %bitcast.17.refs_1_, bf16[96,4224]{1,0:T(8,128)(2,1)} %get-tuple-element.88.refs_2_, bf16[96,4224]{1,0:T(8,128)(2,1)} %collective-permute-done.27.refs_9_.refs_3_, ...), custom_call_target="tpu_custom_call" | custom-call | flops 6600000000 | bytes 1 | tf_op jit(solution)/shard_map/pallas_call | solution.py:747
  309.3 8.2 %collective-permute-start.37 = (bf16[2,336,768]{2,1,0:T(8,128)(2,1)}, bf16[2,336,768]{2,1,0:T(8,128)(2,1)}, u32[]{:S(2)}, u32[]{:S(2)}) collective-permute-start(bf16[2,336,768]{2,1,0:T(8,128)(2,1)} %get-tuple-element.101), channel_id=1, source_target_pairs={{0,4},{1,5},{2,6},{3,7},{4,0},{5,1},{6,2},{7,3},{8,12},{9,13},{10,... | collective-permute-start | bytes 3096584 | tf_op jit(solution)/shard_map/ppermute | solution.py:1632
  326.2 3.6 all-to-all-start.4
  329.8 9.9 %collective-permute-done.39.refs_4_.refs_11_ = bf16[208,768]{1,0:T(8,128)(2,1)S(1)} collective-permute-done((bf16[208,768]{1,0:T(8,128)(2,1)S(1)}, bf16[208,768]{1,0:T(8,128)(2,1)S(1)}, u32[]{:S(2)}, u32[]{:S(2)}) %collective-permute-start.39) | collective-permute-done | bytes 319520 | tf_op jit(solution)/shard_map/ppermute | solution.py:1715
  339.7 5.3 %collective-permute-done.37.refs_2_ = bf16[2,336,768]{2,1,0:T(8,128)(2,1)} collective-permute-done((bf16[2,336,768]{2,1,0:T(8,128)(2,1)}, bf16[2,336,768]{2,1,0:T(8,128)(2,1)}, u32[]{:S(2)}, u32[]{:S(2)}) %collective-permute-start.37) | collective-permute-done | bytes 1032224 | tf_op jit(solution)/shard_map/ppermute | solution.py:1632
  356.6 20.6 %collective-permute-done.43.refs_5_ = bf16[336,768]{1,0:T(8,128)(2,1)S(1)} collective-permute-done((bf16[336,768]{1,0:T(8,128)(2,1)}, bf16[336,768]{1,0:T(8,128)(2,1)S(1)}, u32[]{:S(2)}, u32[]{:S(2)}) %collective-permute-start.43) | collective-permute-done | bytes 516128 | tf_op jit(solution)/shard_map/ppermute | solution.py:1431
  377.9 4.2 %shard_map.195 = (f32[192,768]{1,0:T(8,128)}, f32[48,3072]{1,0:T(8,128)}, f32[48,2304]{1,0:T(8,128)}, f32[48,768]{1,0:T(8,128)}, f32[16,768]{1,0:T(8,128)}, /*index=5*/f32[16,768]{1,0:T(8,128)}, f32[192,768]{1,0:T(8,128)}) custom-call(s32[1]{0:T(128)} %bitcast.refs_0_, bf16[336,768]{1,0:T(8,128)(2,1)} %get-tuple-element.102.refs_1_, ...), custom_call_target="tpu_custom_call" | custom-call | flops 4400000000 | bytes 1 | tf_op jit(solution)/shard_map/pallas_call | solution.py:747
  (203 shorter events, 128.0 us)
Async XLA Ops:
  7.2 19.1 %collective-permute-start = (bf16[256,768]{1,0:T(8,128)(2,1)}, bf16[256,768]{1,0:T(8,128)(2,1)S(1)}, u32[]{:S(2)}, u32[]{:S(2)}) collective-permute-start(bf16[256,768]{1,0:T(8,128)(2,1)} %bitcast.71), channel_id=1, source_target_pairs={{0,16},{16,0},{1,17},{17,1},{2,18},{18,2},{3,19},{19,3},{4,20},{20... | collective-permute-start | bytes 1179656 | tf_op jit(solution)/shard_map/ppermute | solution.py:1435
  7.7 18.5 %collective-permute-start.4 = (bf16[192,768]{1,0:T(8,128)(2,1)}, bf16[192,768]{1,0:T(8,128)(2,1)S(1)}, u32[]{:S(2)}, u32[]{:S(2)}) collective-permute-start(bf16[192,768]{1,0:T(8,128)(2,1)} %refs_7_.1), channel_id=1, source_target_pairs={{0,1},{1,0},{2,3},{3,2},{4,5},{5,4},{6,7},{7,6},{8,9},{9,8},{10,11... | collective-permute-start | bytes 884744 | tf_op jit(solution)/shard_map/ppermute | solution.py:1492
  10.3 15.9 %collective-permute-start.5 = (bf16[192,768]{1,0:T(8,128)(2,1)}, bf16[192,768]{1,0:T(8,128)(2,1)S(1)}, u32[]{:S(2)}, u32[]{:S(2)}) collective-permute-start(bf16[192,768]{1,0:T(8,128)(2,1)} %refs_7_.1), channel_id=1, source_target_pairs={{0,2},{1,3},{2,0},{3,1},{4,6},{5,7},{6,4},{7,5},{8,10},{9,11},{10,... | collective-permute-start | bytes 884744 | tf_op jit(solution)/shard_map/ppermute | solution.py:1492
  11.8 14.4 %collective-permute-start.6 = (bf16[192,768]{1,0:T(8,128)(2,1)}, bf16[192,768]{1,0:T(8,128)(2,1)S(1)}, u32[]{:S(2)}, u32[]{:S(2)}) collective-permute-start(bf16[192,768]{1,0:T(8,128)(2,1)} %refs_7_.1), channel_id=1, source_target_pairs={{0,3},{1,2},{2,1},{3,0},{4,7},{5,6},{6,5},{7,4},{8,11},{9,10},{10,... | collective-permute-start | bytes 884744 | tf_op jit(solution)/shard_map/ppermute | solution.py:1492
  33.1 82.1 %collective-permute-start.18 = (bf16[768,3072]{1,0:T(8,128)(2,1)}, bf16[768,3072]{1,0:T(8,128)(2,1)}, u32[]{:S(2)}, u32[]{:S(2)}) collective-permute-start(bf16[768,3072]{1,0:T(8,128)(2,1)} %bitcast.53), channel_id=1, source_target_pairs={{16,0},{17,1},{18,2},{19,3},{20,4},{21,5},{22,6},{23,7},{24,8},{25... | collective-permute-start | bytes 14155784 | tf_op jit(solution)/shard_map/ppermute | solution.py:1431
  34.4 80.8 %collective-permute-start.19 = (bf16[3072,768]{1,0:T(8,128)(2,1)}, bf16[3072,768]{1,0:T(8,128)(2,1)}, u32[]{:S(2)}, u32[]{:S(2)}) collective-permute-start(bf16[3072,768]{1,0:T(8,128)(2,1)} %bitcast.57), channel_id=1, source_target_pairs={{16,0},{17,1},{18,2},{19,3},{20,4},{21,5},{22,6},{23,7},{24,8},{25... | collective-permute-start | bytes 14155784 | tf_op jit(solution)/shard_map/ppermute | solution.py:1431
  37.4 10.9 %collective-permute-start.10 = (bf16[96,768]{1,0:T(8,128)(2,1)S(1)}, bf16[96,768]{1,0:T(8,128)(2,1)S(1)}, u32[]{:S(2)}, u32[]{:S(2)}) collective-permute-start(bf16[96,768]{1,0:T(8,128)(2,1)S(1)} %get-tuple-element.119), channel_id=1, source_target_pairs={{0,12},{1,13},{2,14},{3,15},{4,8},{5,9},{6,10},{7,11},{8,4},{9,5},... | collective-permute-start | bytes 442376 | tf_op jit(solution)/shard_map/ppermute | solution.py:1431
  64.1 16.8 %all-to-all-start = ((bf16[16,32,384]{2,1,0:T(8,128)(2,1)}), bf16[16,32,384]{2,1,0:T(8,128)(2,1)S(1)}, u32[]{:S(2)}, u32[]{:S(2)}) async-start(bf16[16,32,384]{2,1,0:T(8,128)(2,1)} %pad_select_fusion.1), calls=%async_computation | async-start | bytes 786432 | tf_op jit(solution)/shard_map/all_to_all | solution.py:1525
  68.8 46.4 %collective-permute-start.16 = (bf16[768,2304]{1,0:T(8,128)(2,1)}, bf16[768,2304]{1,0:T(8,128)(2,1)}, u32[]{:S(2)}, u32[]{:S(2)}) collective-permute-start(bf16[768,2304]{1,0:T(8,128)(2,1)} %bitcast.62), channel_id=1, source_target_pairs={{16,0},{17,1},{18,2},{19,3},{20,4},{21,5},{22,6},{23,7},{24,8},{25... | collective-permute-start | bytes 10616840 | tf_op jit(solution)/shard_map/ppermute | solution.py:1431
  85.8 11.4 %all-to-all-start.1 = ((bf16[16,32,128]{2,1,0:T(8,128)(2,1)}), bf16[16,32,128]{2,1,0:T(8,128)(2,1)S(1)}, u32[]{:S(2)}, u32[]{:S(2)}) async-start(bf16[16,32,128]{2,1,0:T(8,128)(2,1)} %bitcast.44), calls=%async_computation.1 | async-start | bytes 262144 | tf_op jit(solution)/shard_map/all_to_all | solution.py:1530
  89.4 167.1 %reduce-scatter.2.cloned.1.call-start = ((), (), s32[]{:S(2)}) async-start(), calls=%async_computation.6 | async-start | bytes 9338880 | tf_op jit(solution)/shard_map/reduce_scatter | solution.py:1706
  89.5 21.0 %collective-permute-start.17 = (bf16[768,768]{1,0:T(8,128)(2,1)S(1)}, bf16[768,768]{1,0:T(8,128)(2,1)S(1)}, u32[]{:S(2)}, u32[]{:S(2)}) collective-permute-start(bf16[768,768]{1,0:T(8,128)(2,1)S(1)} %bitcast.68), channel_id=1, source_target_pairs={{16,0},{17,1},{18,2},{19,3},{20,4},{21,5},{22,6},{23,7},{24,8},{25... | collective-permute-start | bytes 3538952 | tf_op jit(solution)/shard_map/ppermute | solution.py:1431
  147.4 10.4 %collective-permute-start.23 = (bf16[400,7680]{1,0:T(8,128)(2,1)}, bf16[400,7680]{1,0:T(8,128)(2,1)}, u32[]{:S(2)}, u32[]{:S(2)}) collective-permute-start(bf16[400,7680]{1,0:T(8,128)(2,1)} %get-tuple-element.77), channel_id=1, source_target_pairs={{0,16},{16,0},{1,17},{17,1},{2,18},{18,2},{3,19},{19,3},{4,20},{20... | collective-permute-start | bytes 18432008 | tf_op jit(solution)/shard_map/ppermute | solution.py:1435
  147.5 10.2 %collective-permute-start.21 = (bf16[48,768]{1,0:T(8,128)(2,1)}, bf16[48,768]{1,0:T(8,128)(2,1)S(1)}, u32[]{:S(2)}, u32[]{:S(2)}) collective-permute-start(bf16[48,768]{1,0:T(8,128)(2,1)} %get-tuple-element.72.refs_0_), channel_id=1, source_target_pairs={{16,0},{17,1},{18,2},{19,3},{20,4},{21,5},{22,6},{23,7},{24,8},{25... | collective-permute-start | bytes 221192 | tf_op jit(solution)/shard_map/ppermute | solution.py:1431
  184.6 13.6 %all-to-all-start.2 = ((bf16[16,32,128]{2,1,0:T(8,128)(2,1)}), bf16[16,32,128]{2,1,0:T(8,128)(2,1)S(1)}, u32[]{:S(2)}, u32[]{:S(2)}) async-start(bf16[16,32,128]{2,1,0:T(8,128)(2,1)} %pad_select_fusion.2), calls=%async_computation.2 | async-start | bytes 262144 | tf_op jit(solution)/shard_map/all_to_all | solution.py:1525
  193.4 35.8 %collective-permute-start.26 = (bf16[4,96,4224]{2,1,0:T(8,128)(2,1)}, bf16[4,96,4224]{2,1,0:T(8,128)(2,1)S(1)}, u32[]{:S(2)}, u32[]{:S(2)}) collective-permute-start(bf16[4,96,4224]{2,1,0:T(8,128)(2,1)} %shard_map.188), channel_id=1, source_target_pairs={{0,16},{1,17},{2,18},{3,19},{4,20},{5,21},{6,22},{7,23},{8,24},{9,... | collective-permute-start | bytes 9732104 | tf_op jit(solution)/shard_map/ppermute | solution.py:1431
  234.8 10.1 %collective-permute-start.30 = (bf16[112,768]{1,0:T(8,128)(2,1)}, bf16[112,768]{1,0:T(8,128)(2,1)S(1)}, u32[]{:S(2)}, u32[]{:S(2)}) collective-permute-start(bf16[112,768]{1,0:T(8,128)(2,1)} %get-tuple-element.95.refs_5_), channel_id=1, source_target_pairs={{0,4},{1,5},{2,6},{3,7},{4,0},{5,1},{6,2},{7,3},{8,12},{9,13},{10,... | collective-permute-start | bytes 516104 | tf_op jit(solution)/shard_map/ppermute | solution.py:1431
  237.8 10.3 %collective-permute-start.31 = (bf16[112,768]{1,0:T(8,128)(2,1)}, bf16[112,768]{1,0:T(8,128)(2,1)S(1)}, u32[]{:S(2)}, u32[]{:S(2)}) collective-permute-start(bf16[112,768]{1,0:T(8,128)(2,1)} %get-tuple-element.95.refs_5_), channel_id=1, source_target_pairs={{0,8},{1,9},{2,10},{3,11},{4,12},{5,13},{6,14},{7,15},{8,0},{9,1},... | collective-permute-start | bytes 516104 | tf_op jit(solution)/shard_map/ppermute | solution.py:1431
  259.6 22.7 %collective-permute-start.34 = (bf16[2,304,768]{2,1,0:T(8,128)(2,1)}, bf16[2,304,768]{2,1,0:T(8,128)(2,1)S(1)}, u32[]{:S(2)}, u32[]{:S(2)}) collective-permute-start(bf16[2,304,768]{2,1,0:T(8,128)(2,1)} %get-tuple-element.98), channel_id=1, source_target_pairs={{0,4},{1,5},{2,6},{3,7},{4,0},{5,1},{6,2},{7,3},{8,12},{9,13},{10,... | collective-permute-start | bytes 2801672 | tf_op jit(solution)/shard_map/ppermute | solution.py:1632
  261.1 28.7 %collective-permute-start.27 = (bf16[96,4224]{1,0:T(8,128)(2,1)S(1)}, bf16[96,4224]{1,0:T(8,128)(2,1)}, u32[]{:S(2)}, u32[]{:S(2)}) collective-permute-start(bf16[96,4224]{1,0:T(8,128)(2,1)S(1)} %copy-done.21), channel_id=1, source_target_pairs={{0,1},{1,0},{2,3},{3,2},{4,5},{5,4},{6,7},{7,6},{8,9},{9,8},{10,11... | collective-permute-start | bytes 2433032 | tf_op jit(solution)/shard_map/ppermute | solution.py:1632
  262.4 36.7 %collective-permute-start.28 = (bf16[96,4224]{1,0:T(8,128)(2,1)S(1)}, bf16[96,4224]{1,0:T(8,128)(2,1)}, u32[]{:S(2)}, u32[]{:S(2)}) collective-permute-start(bf16[96,4224]{1,0:T(8,128)(2,1)S(1)} %copy-done.20), channel_id=1, source_target_pairs={{0,2},{1,3},{2,0},{3,1},{4,6},{5,7},{6,4},{7,5},{8,10},{9,11},{10,... | collective-permute-start | bytes 2433032 | tf_op jit(solution)/shard_map/ppermute | solution.py:1632
  263.2 36.0 %collective-permute-start.29 = (bf16[96,4224]{1,0:T(8,128)(2,1)S(1)}, bf16[96,4224]{1,0:T(8,128)(2,1)}, u32[]{:S(2)}, u32[]{:S(2)}) collective-permute-start(bf16[96,4224]{1,0:T(8,128)(2,1)S(1)} %copy-done.19), channel_id=1, source_target_pairs={{0,3},{1,2},{2,1},{3,0},{4,7},{5,6},{6,5},{7,4},{8,11},{9,10},{10,... | collective-permute-start | bytes 2433032 | tf_op jit(solution)/shard_map/ppermute | solution.py:1632
  286.1 17.6 %collective-permute-start.35 = (bf16[304,768]{1,0:T(8,128)(2,1)}, bf16[304,768]{1,0:T(8,128)(2,1)S(1)}, u32[]{:S(2)}, u32[]{:S(2)}) collective-permute-start(bf16[304,768]{1,0:T(8,128)(2,1)} %get-tuple-element.99), channel_id=1, source_target_pairs={{0,24},{1,25},{2,26},{3,27},{4,28},{5,29},{6,30},{7,31},{8,16},{9,... | collective-permute-start | bytes 1400840 | tf_op jit(solution)/shard_map/ppermute | solution.py:1431
  289.1 14.6 %collective-permute-start.36 = (bf16[304,768]{1,0:T(8,128)(2,1)}, bf16[304,768]{1,0:T(8,128)(2,1)S(1)}, u32[]{:S(2)}, u32[]{:S(2)}) collective-permute-start(bf16[304,768]{1,0:T(8,128)(2,1)} %get-tuple-element.99), channel_id=1, source_target_pairs={{16,24},{17,25},{18,26},{19,27},{20,28},{21,29},{22,30},{23,31},{2... | collective-permute-start | bytes 1400840 | tf_op jit(solution)/shard_map/ppermute | solution.py:1431
  309.3 35.7 %collective-permute-start.37 = (bf16[2,336,768]{2,1,0:T(8,128)(2,1)}, bf16[2,336,768]{2,1,0:T(8,128)(2,1)}, u32[]{:S(2)}, u32[]{:S(2)}) collective-permute-start(bf16[2,336,768]{2,1,0:T(8,128)(2,1)} %get-tuple-element.101), channel_id=1, source_target_pairs={{0,4},{1,5},{2,6},{3,7},{4,0},{5,1},{6,2},{7,3},{8,12},{9,13},{10,... | collective-permute-start | bytes 3096584 | tf_op jit(solution)/shard_map/ppermute | solution.py:1632
  319.6 10.2 %collective-permute-start.38 = (bf16[208,768]{1,0:T(8,128)(2,1)S(1)}, bf16[208,768]{1,0:T(8,128)(2,1)S(1)}, u32[]{:S(2)}, u32[]{:S(2)}) collective-permute-start(bf16[208,768]{1,0:T(8,128)(2,1)S(1)} %get-tuple-element.118), channel_id=1, source_target_pairs={{0,1},{1,0},{2,3},{3,2},{4,5},{5,4},{6,7},{7,6},{8,9},{9,8},{10,11... | collective-permute-start | bytes 958472 | tf_op jit(solution)/shard_map/ppermute | solution.py:1715
  320.9 18.8 %collective-permute-start.39 = (bf16[208,768]{1,0:T(8,128)(2,1)S(1)}, bf16[208,768]{1,0:T(8,128)(2,1)S(1)}, u32[]{:S(2)}, u32[]{:S(2)}) collective-permute-start(bf16[208,768]{1,0:T(8,128)(2,1)S(1)} %get-tuple-element.117), channel_id=1, source_target_pairs={{0,2},{1,3},{2,0},{3,1},{4,6},{5,7},{6,4},{7,5},{8,10},{9,11},{10,... | collective-permute-start | bytes 958472 | tf_op jit(solution)/shard_map/ppermute | solution.py:1715
  321.6 18.1 %collective-permute-start.40 = (bf16[208,768]{1,0:T(8,128)(2,1)S(1)}, bf16[208,768]{1,0:T(8,128)(2,1)}, u32[]{:S(2)}, u32[]{:S(2)}) collective-permute-start(bf16[208,768]{1,0:T(8,128)(2,1)S(1)} %get-tuple-element.116), channel_id=1, source_target_pairs={{0,3},{1,2},{2,1},{3,0},{4,7},{5,6},{6,5},{7,4},{8,11},{9,10},{10,... | collective-permute-start | bytes 958472 | tf_op jit(solution)/shard_map/ppermute | solution.py:1715
  323.1 29.7 %collective-permute-start.20 = (bf16[3,128,768]{2,1,0:T(8,128)(2,1)S(1)}, bf16[3,128,768]{2,1,0:T(8,128)(2,1)S(1)}, u32[]{:S(2)}, u32[]{:S(2)}) collective-permute-start(bf16[3,128,768]{2,1,0:T(8,128)(2,1)S(1)} %bitcast.70), channel_id=1, source_target_pairs={{0,16},{1,17},{2,18},{3,19},{4,20},{5,21},{6,22},{7,23},{8,24},{9,... | collective-permute-start | bytes 1769480 | tf_op jit(solution)/shard_map/ppermute | solution.py:1431
  326.2 30.4 %all-to-all-start.4 = ((bf16[16,16,768]{2,1,0:T(8,128)(2,1)}), bf16[16,16,768]{2,1,0:T(8,128)(2,1)S(1)}, u32[]{:S(2)}, u32[]{:S(2)}) async-start(bf16[16,16,768]{2,1,0:T(8,128)(2,1)} %bitcast.25), calls=%async_computation.5 | async-start | bytes 786432 | tf_op jit(solution)/shard_map/all_to_all | solution.py:1717
  349.6 27.6 %collective-permute-start.43 = (bf16[336,768]{1,0:T(8,128)(2,1)}, bf16[336,768]{1,0:T(8,128)(2,1)S(1)}, u32[]{:S(2)}, u32[]{:S(2)}) collective-permute-start(bf16[336,768]{1,0:T(8,128)(2,1)} %get-tuple-element.105), channel_id=1, source_target_pairs={{0,8},{1,9},{2,10},{3,11},{4,12},{5,13},{6,14},{7,15},{8,0},{9,1},... | collective-permute-start | bytes 1548296 | tf_op jit(solution)/shard_map/ppermute | solution.py:1431
  351.5 25.9 %collective-permute-start.44 = (bf16[336,768]{1,0:T(8,128)(2,1)}, bf16[336,768]{1,0:T(8,128)(2,1)}, u32[]{:S(2)}, u32[]{:S(2)}) collective-permute-start(bf16[336,768]{1,0:T(8,128)(2,1)} %get-tuple-element.105), channel_id=1, source_target_pairs={{16,8},{17,9},{18,10},{19,11},{20,12},{21,13},{22,14},{23,15},{24,... | collective-permute-start | bytes 1548296 | tf_op jit(solution)/shard_map/ppermute | solution.py:1431
  (66 other events, 384.8 us)
Sparse Core Ops, SparseCore 0:
  170.1 86.3 reduce-scatter.1

commit v7 on v6

--- a/solution.py
+++ b/solution.py
@@ -923,7 +923,7 @@
         normed_two_ref[...] = layer_norm(middle, gains_ref[1:2], biases_ref[1:2]).astype(bf16)
         loads[1].wait()
 
-        @pl.loop(0, hidden_width // width)
+        @pl.loop(0, hidden_width // width, unroll=True)
         def _(i):
             at = pl.ds(pl.multiple_of(i * width, 128), width)
             hidden, slope = gelu_and_slope(product(normed_two_ref[...], w_expand[:, at]))
@@ -1008,7 +1008,7 @@
         grad_ref[...] = product(picked, source).astype(bf16)
         loads[0].wait()
 
-        @pl.loop(0, hidden_width // width)
+        @pl.loop(0, hidden_width // width, unroll=True)
         def _(i):
             at = pl.ds(pl.multiple_of(i * width, 128), width)
             grad_hidden = product_transposed(grad_ref[...], w_contract[at, :])
@@ -1284,40 +1284,45 @@
 def by_parity(parity, sums, deps=()):
     count, rows, width = sums.shape
 
-    def kernel(parity_ref, sums_ref, kept_ref, leaving_ref):
-        for k in range(count // 2):
-            kept_ref[k] = sums_ref[2 * k + parity_ref[0]]
-            leaving_ref[k] = sums_ref[2 * k + 1 - parity_ref[0]]
+    def kernel(parity_ref, sums_ref, *rest):
+        rest[-1][...] = sums_ref[...]
+
+    block = (1, rows, width)
+    return pl.pallas_call(
+        kernel,
+        grid_spec=pltpu.PrefetchScalarGridSpec(
+            num_scalar_prefetch=1,
+            grid=(count // 2,),
+            in_specs=[pl.BlockSpec(block, lambda i, ref: (2 * i + 1 - ref[0], 0, 0))]
+            + [ANY] * len(deps),
+            out_specs=pl.BlockSpec(block, lambda i, ref: (i, 0, 0)),
+        ),
+        out_shape=shaped(count // 2, rows, width),
+        compiler_params=pltpu.CompilerParams(vmem_limit_bytes=VMEM),
+        cost_estimate=cost(3),
+    )(parity, sums, *deps)
+
+
+def half_sums(flags, kept, near, deps=()):
+    shape = kept.shape[1:]
+    every = kept.shape[0] == 4
+
+    def kernel(flags_ref, kept_ref, near_ref, far_ref, mine_ref):
+        for k in range(2):
+            own = kept_ref[2 * k + flags_ref[2]] if every else kept_ref[k]
+            total = (own.astype(f32) + near_ref[k].astype(f32)).astype(bf16)
+
+            @pl.when(flags_ref[1] == k)
+            def _():
+                mine_ref[...] = total
+
+            @pl.when(flags_ref[1] != k)
+            def _():
+                far_ref[...] = total
 
     return call(
         kernel,
-        (parity, sums),
-        [SCALARS, WHOLE],
-        [shaped(count // 2, rows, width)] * 2,
-        [WHOLE] * 2,
-        deps=deps,
-        micros=3,
-    )
-
-
-def half_sums(upper, kept, near, deps=()):
-    shape = kept.shape[1:]
-
-    def kernel(upper_ref, kept_ref, near_ref, far_ref, mine_ref):
-        for k in range(2):
-            total = (kept_ref[k].astype(f32) + near_ref[k].astype(f32)).astype(bf16)
-
-            @pl.when(upper_ref[0] == k)
-            def _():
-                mine_ref[...] = total
-
-            @pl.when(upper_ref[0] != k)
-            def _():
-                far_ref[...] = total
-
-    return call(
-        kernel,
-        (upper, kept, near),
+        (flags, kept, near),
         [SCALARS, WHOLE, WHOLE],
         [shaped(*shape)] * 2,
         [WHOLE] * 2,
@@ -1326,13 +1331,46 @@
     )
 
 
+def half_sums_and_cross(flags, kept, near, other, other_far, deps=()):
+    shape = kept.shape[1:]
+    held = other.shape[0]
+
+    def kernel(flags_ref, kept_ref, near_ref, other_ref, more_ref, far_ref, mine_ref, cross_ref):
+        for k in range(2):
+            total = (kept_ref[k].astype(f32) + near_ref[k].astype(f32)).astype(bf16)
+
+            @pl.when(flags_ref[1] == k)
+            def _():
+                mine_ref[...] = total
+                cross_ref[...] = total
+
+            @pl.when(flags_ref[1] != k)
+            def _():
+                far_ref[...] = total
+
+        @pl.when(flags_ref[0] == 0)
+        def _():
+            total = other_ref[...].astype(f32) + more_ref[...].astype(f32)
+            cross_ref[0:held, :] = total.astype(bf16)
+
+    return call(
+        kernel,
+        (flags, kept, near, other, other_far),
+        [SCALARS] + [WHOLE] * 4,
+        [shaped(*shape)] * 3,
+        [WHOLE] * 3,
+        deps=deps,
+        micros=2,
+    )
+
+
 def finish(section, deep, shard, room, own_global, own_local, crossed, fars, table_parts, patch_parts):
     width = own_local.shape[1]
     chunks = deep // shard
     p = len(patch_parts)
 
     def kernel(section_ref, global_ref, local_ref, crossed_ref, table_ref, *refs):
-        (global_one, global_two, local_one, local_two), refs = refs[:4], refs[4:]
+        (global_one, global_two, local_two), refs = refs[:3], refs[3:]
         patch_refs = refs[:p]
         contract, expand, ins, out, table, small, patch = refs[p:]
 
@@ -1359,7 +1397,7 @@
 
         @pl.when(section_ref[0] != 0)
         def _():
-            one, two = (crossed_ref, local_one), (local_ref, local_two)
+            one, two = (crossed_ref,), (local_ref, local_two)
             contract[...] = total(one, 0, deep)
             out[...] = total(one, deep, shard)
             ins[:, 0:width] = total(one, deep + shard, shard)
@@ -1373,7 +1411,7 @@
     return call(
         kernel,
         (section, own_global, own_local, crossed, table_parts, *fars, *patch_parts),
-        [SCALARS] + [WHOLE] * (8 + p),
+        [SCALARS] + [WHOLE] * (7 + p),
         [
             shaped(deep, width, kind=f32),
             shaped(shard, chunks * width, kind=f32),
@@ -1622,7 +1660,7 @@
         ]
 
     upper = (group >> 1) & 1
-    upper_flag = upper.reshape(1).astype(jnp.int32)
+    half_flags = jnp.stack([section, upper, group & 1]).astype(jnp.int32)
 
     def group_pairs(step):
         return [(i, i ^ (step * span)) for i in range(count)]
@@ -1705,7 +1743,7 @@
     if in_plane:
         in_planes = lax.psum_scatter(half_locals, "member", scatter_dimension=0, tiled=True)
         parity_flag = (group & 1).reshape(1).astype(jnp.int32)
-        local_kept, local_leaving = by_parity(parity_flag, in_planes, [crossed])
+        local_leaving = by_parity(parity_flag, in_planes, [crossed])
         local_near = both_send(local_leaving, group_pairs(1))
     else:
         own_local = place_sum(half_locals)
@@ -1731,30 +1769,26 @@
         )
 
     if in_plane:
-        local_far, local_mine = half_sums(upper_flag, local_kept, local_near)
+        local_far, local_mine = half_sums(half_flags, in_planes, local_near)
         across = group_pairs(2)
-        local_fars = [
-            section_send(local_far, 0, 1, across),
-            section_send(local_far, 1, 1, across),
-        ]
+        local_far = both_send(local_far, across)
         kept, leaving = plane_gradients(
             flag,
             group_flag,
             arrived_parts,
             contract.shape[0],
             width,
-            [patch_share, *local_fars],
+            [patch_share, local_far],
         )
         near = both_send(leaving, group_pairs(1))
-        far, mine = half_sums(upper_flag, kept, near, patch_parts[1:])
-        extra = mine.shape[0] - local_mine.shape[0]
-        crossed = section_swap(
-            jnp.where(is_global, jnp.pad(local_mine, ((0, extra), (0, 0))), mine)
-        )
+        far, mine, crossed = half_sums_and_cross(
+            half_flags, kept, near, local_mine, local_far, patch_parts[1:]
+        )
+        crossed = section_swap(crossed)
         fars = [
             section_send(far, 0, 0, across),
             section_send(far, 1, 0, across),
-            *local_fars,
+            local_far,
         ]
         contract_grad, expand_grad, in_grad, out_grads, table_grad, small, patch_grads = finish(
             flag,

time: 398 us -> 395 us (level)
  starting transfers between devices: 104 us -> 99.2 us
    ppermute x5 -> x6, waiting for transfers between devices: 32.3 us -> 37.9 us  [both_send(): return lax.ppermute(x, ('section',) + SEQ, joint)]
    ppermute x5 -> x6, starting transfers between devices: 13.2 us -> 8.13 us  [both_send(): return lax.ppermute(x, ('section',) + SEQ, joint)]
    pallas_call x14 -> x13, Pallas kernels: 62.7 us -> 59.6 us  [call(): pl.pallas_call(body, in_specs=list(specs) + [ANY] * len(deps), out_specs=...]
    ppermute x27 -> x25, waiting for transfers between devices: 48.7 us -> 46.5 us  [section_send(): return lax.ppermute(x, ('section',) + SEQ, joint)]
    ppermute x27 -> x25, starting transfers between devices: 54.3 us -> 54.2 us  [section_send(): return lax.ppermute(x, ('section',) + SEQ, joint)]
    unnamed x96 -> x92, local copies, waits for them, and re-layouts: 10.9 us -> 11 us
  transfers between devices with their start and end apart: 50 -> 49, of which waited for: 26 -> 27; matrix products, arithmetic and copies ran while one was open for 3% -> 3% of each run, Pallas kernels for 15% -> 15%
where the time goes in v7:
time: 395 us; the launch traced here: 387 us
  waiting for transfers between devices  120 us (30%)
  Pallas kernels  115 us (29%)
  starting transfers between devices  99.2 us (25%)
  blocking collectives  15.3 us (4%)
  between operations  15.2 us (4%)
  local copies, waits for them, and re-layouts  14 us (4%)
  other arithmetic  9.03 us (2%)
    pallas_call x13, Pallas kernels, call(): pl.pallas_call(body, in_specs=list(specs) + [ANY] * len(deps), out_specs=...  59.6 us
    ppermute x25, starting transfers between devices, section_send(): return lax.ppermute(x, ('section',) + SEQ, joint)  54.2 us
    ppermute x25, waiting for transfers between devices, section_send(): return lax.ppermute(x, ('section',) + SEQ, joint)  46.5 us
    ppermute x6, waiting for transfers between devices, both_send(): return lax.ppermute(x, ('section',) + SEQ, joint)  37.9 us
    pallas_call x1, Pallas kernels, local_block(): pl.pallas_call(partial(local_kernel, patch_rows), in_specs=[SCALARS] + [W...  31.6 us
    all_to_all x1, blocking collectives, from_tasks(): lax.all_to_all(results.reshape(count, patch_rows, columns), SEQ, 0, 0)  15.3 us
    all_to_all x2, waiting for transfers between devices, to_tasks(): landed = lax.all_to_all(slots, SEQ, 0, 0)  13.4 us
    pallas_call x1, Pallas kernels, local_gradients(): pl.pallas_call(kernel, in_specs=[SCALARS, WHOLE, ANY, ANY] + [ANY] * len(...  11.5 us
  transfers between devices with their start and end apart: 49, of which 27 were waited for; matrix products, arithmetic and copies ran while one was open for 3% of the time, Pallas kernels for 15%

profile of v7, /device:TPU:0, one launch (start us, length us, event | category | flops | bytes accessed | tf_op | source)
XLA Modules:
  0.0 387.2 jit_solution(11909870339152762122)
XLA Ops:
  20.5 3.9 %collective-permute-start.3 = (s32[3,256]{1,0:T(4,128)}, s32[3,256]{1,0:T(4,128)S(1)}, u32[]{:S(2)}, u32[]{:S(2)}) collective-permute-start(s32[3,256]{1,0:T(4,128)} %ids_ref.3), channel_id=1, source_target_pairs={{0,12},{1,13},{2,14},{3,15},{4,8},{5,9},{6,10},{7,11},{8,4},{9,5},... | collective-permute-start | bytes 9224 | tf_op jit(solution)/shard_map/ppermute | solution.py:1535
  27.9 4.0 %shard_map.178 = (bf16[384,768]{1,0:T(8,128)(2,1)}, bf16[768,768]{1,0:T(8,128)(2,1)}, f32[384,768]{1,0:T(8,128)}, bf16[384,768]{1,0:T(8,128)(2,1)}, bf16[256,384]{1,0:T(8,128)(2,1)}) custom-call(s32[3]{0:T(128)} %pad_add_fusion.1.refs_0_, bf16[256,768]{1,0:T(8,128)(2,1)} %bitcast.72, bf16[256,768]{1,0:T(8,128)(2,1)} %copy-done.26, s32[3,256]{1,0:T(4,128)} %ids_ref.3, ...), custom_call_target="tpu_custom_call" | custom-call | flops 4400000000 | bytes 1 | tf_op jit(solution)/shard_map/pallas_call | solution.py:747
  37.4 5.7 %collective-permute-start.10 = (bf16[96,768]{1,0:T(8,128)(2,1)S(1)}, bf16[96,768]{1,0:T(8,128)(2,1)S(1)}, u32[]{:S(2)}, u32[]{:S(2)}) collective-permute-start(bf16[96,768]{1,0:T(8,128)(2,1)S(1)} %get-tuple-element.117), channel_id=1, source_target_pairs={{0,12},{1,13},{2,14},{3,15},{4,8},{5,9},{6,10},{7,11},{8,4},{9,5},... | collective-permute-start | bytes 442376 | tf_op jit(solution)/shard_map/ppermute | solution.py:1469
  50.2 4.4 %collective-permute-done.9.refs_5_ = bf16[96,768]{1,0:T(8,128)(2,1)S(1)} collective-permute-done((bf16[96,768]{1,0:T(8,128)(2,1)S(1)}, bf16[96,768]{1,0:T(8,128)(2,1)S(1)}, u32[]{:S(2)}, u32[]{:S(2)}) %collective-permute-start.9) | collective-permute-done | bytes 147488 | tf_op jit(solution)/shard_map/ppermute | solution.py:1469
  55.2 4.6 %shard_map.179 = (f32[96,768]{1,0:T(8,128)}, bf16[96,768]{1,0:T(8,128)(2,1)}, bf16[4,96,192]{2,1,0:T(8,128)(2,1)}, bf16[16,32,384]{2,1,0:T(8,128)(2,1)}, bf16[2,32,384]{2,1,0:T(8,128)(2,1)}) custom-call(f32[96,768]{1,0:T(8,128)} %slice.43.refs_0_, f32[2,768]{1,0:T(2,128)} %bitcast.48, f32[2,768]{1,0:T(2,128)} %bitcast.45, bf16[768,2304]{1,0:T(8,128)(2,1)} %bitcast.61, ...), custom_call_target="tpu_custom_call" | custom-call | flops 5500000256 | bytes 1 | tf_op jit(solution)/shard_map/pallas_call | solution.py:747
  64.0 4.7 %all-to-all-start = ((bf16[16,32,384]{2,1,0:T(8,128)(2,1)}), bf16[16,32,384]{2,1,0:T(8,128)(2,1)S(1)}, u32[]{:S(2)}, u32[]{:S(2)}) async-start(bf16[16,32,384]{2,1,0:T(8,128)(2,1)} %pad_select_fusion), calls=%async_computation | async-start | bytes 786432 | tf_op jit(solution)/shard_map/all_to_all | solution.py:1563
  70.8 10.1 %all-to-all-done = bf16[16,32,384]{2,1,0:T(8,128)(2,1)S(1)} async-done(((bf16[16,32,384]{2,1,0:T(8,128)(2,1)}), bf16[16,32,384]{2,1,0:T(8,128)(2,1)S(1)}, u32[]{:S(2)}, u32[]{:S(2)}) %all-to-all-start) | async-done | bytes 393248 | tf_op jit(solution)/shard_map/all_to_all | solution.py:1563
  81.7 4.1 %shard_map.180 = bf16[512,128]{1,0:T(8,128)(2,1)} custom-call(s32[13]{0:T(128)} %pad_add_fusion.2.numbers_ref.refs_0_, bf16[512,384]{1,0:T(8,128)(2,1)} %bitcast.40), custom_call_target="tpu_custom_call" | custom-call | flops 16499999744 | bytes 1 | tf_op jit(solution)/shard_map/pallas_call | solution.py:716
  85.8 3.6 all-to-all-start.1
  90.8 6.4 %all-to-all-done.1.refs_6_ = bf16[16,32,128]{2,1,0:T(8,128)(2,1)S(1)} async-done(((bf16[16,32,128]{2,1,0:T(8,128)(2,1)}), bf16[16,32,128]{2,1,0:T(8,128)(2,1)S(1)}, u32[]{:S(2)}, u32[]{:S(2)}) %all-to-all-start.1) | async-done | bytes 131104 | tf_op jit(solution)/shard_map/all_to_all | solution.py:1568
  100.9 7.3 %shard_map.181 = (bf16[96,768]{1,0:T(8,128)(2,1)}, f32[96,768]{1,0:T(8,128)}, bf16[96,768]{1,0:T(8,128)(2,1)}, bf16[96,3072]{1,0:T(8,128)(2,1)}, bf16[96,3072]{1...) custom-call(f32[96,768]{1,0:T(8,128)} %get-tuple-element.62.refs_0_,, ...), custom_call_target="tpu_custom_call" | custom-call | flops 8800000000 | bytes 1 | tf_op jit(solution)/shard_map/pallas_call | solution.py:747
  115.6 31.6 %shard_map.182 = (bf16[384,768]{1,0:T(8,128)(2,1)}, bf16[48,768]{1,0:T(8,128)(2,1)}, bf16[16,768]{1,0:T(8,128)(2,1)}, bf16[400,7680]{1,0:T(8,128)(2,1)}, bf16[400,7680]{1,0:T(8,128)(2,1)}) custom-call(s32[15]{0:T(128)} %pad_add_fusion.numbers_ref.refs_0_, s32[3,256]{1,0:T(4,128)} %ids_ref.3, bf16[256,768]{1,0:T(8,128)(2,1)} %bitcast.73, ...), custom_call_target="tpu_custom_call" | custom-call | flops 38499999744 | bytes 1 | tf_op jit(solution)/shard_map/pallas_call | solution.py:474
  150.0 4.9 %collective-permute-done.22.rest_1_.refs_2_ = bf16[16,768]{1,0:T(8,128)(2,1)S(1)} collective-permute-done((bf16[16,768]{1,0:T(8,128)(2,1)}, bf16[16,768]{1,0:T(8,128)(2,1)S(1)}, u32[]{:S(2)}, u32[]{:S(2)}) %collective-permute-start.22) | collective-permute-done | bytes 24608 | tf_op jit(solution)/shard_map/ppermute | solution.py:1469
  158.2 11.5 %shard_map.184.refs_9_ = bf16[16,304,768]{2,1,0:T(8,128)(2,1)} custom-call(s32[15]{0:T(128)} %pad_add_fusion.numbers_ref.refs_0_, s32[3,256]{1,0:T(4,128)} %ids_ref.3, bf16[400,7680]{1,0:T(8,128)(2,1)} %get-tuple-element.75.keep_ref, bf16[400,7680]{1,0:T(8,128)(2,1)} %collective-permute-done.23.new_ref, bf16[48,768]{1,0:T(8,128)(2,1)} %copy-done.37, ...), custom_call_target="tpu_custom_call" | custom-call | flops 13200000000 | bytes 1 | tf_op jit(solution)/shard_map/pallas_call | solution.py:598
  169.7 8.7 %shard_map.185 = (bf16[96,3072]{1,0:T(8,128)(2,1)}, f32[96,768]{1,0:T(8,128)}, bf16[96,768]{1,0:T(8,128)(2,1)}, f32[2,768]{1,0:T(2,128)}, bf16[96,768]{1,0:T(8,1...) custom-call(bf16[48,768]{1,0:T(8,128)(2,1)} %get-tuple-element.71.refs_0_, ...), custom_call_target="tpu_custom_call" | custom-call | flops 11000000512 | bytes 1 | tf_op jit(solution)/shard_map/pallas_call | solution.py:747
  183.9 5.7 %all-to-all-start.2 = ((bf16[16,32,128]{2,1,0:T(8,128)(2,1)}), bf16[16,32,128]{2,1,0:T(8,128)(2,1)S(1)}, u32[]{:S(2)}, u32[]{:S(2)}) async-start(bf16[16,32,128]{2,1,0:T(8,128)(2,1)} %pad_select_fusion.1), calls=%async_computation.2 | async-start | bytes 262144 | tf_op jit(solution)/shard_map/all_to_all | solution.py:1563
  198.1 5.8 %shard_map.186 = bf16[512,384]{1,0:T(8,128)(2,1)} custom-call(s32[13]{0:T(128)} %pad_add_fusion.2.numbers_ref.refs_0_, bf16[512,384]{1,0:T(8,128)(2,1)} %bitcast.41, bf16[512,128]{1,0:T(8,128)(2,1)} %bitcast.43), custom_call_target="tpu_custom_call" | custom-call | flops 32999999488 | bytes 1 | tf_op jit(solution)/shard_map/pallas_call | solution.py:729
  204.0 15.3 %all_to_all.25.refs_5_ = bf16[16,32,384]{2,1,0:T(8,128)(2,1)S(1)} all-to-all(bf16[16,32,384]{2,1,0:T(8,128)(2,1)} %bitcast.42), channel_id=1, replica_groups=mesh['section'=2,'group'=4,'member'=4] {'group','member'}, dimensions={0} | all-to-all | bytes 786432 | tf_op jit(solution)/shard_map/all_to_all | solution.py:1568
  223.0 5.2 %shard_map.187 = (bf16[96,2304]{1,0:T(8,128)(2,1)}, bf16[112,768]{1,0:T(8,128)(2,1)}, f32[4,768]{1,0:T(4,128)}) custom-call(f32[96,768]{1,0:T(8,128)} %get-tuple-element.62.refs_0_, f32[96,768]{1,0:T(8,128)} %get-tuple-element.78.refs_1_, f32[2,768]{1,0:T(2,128)} %get-tuple-element.79.refs_2_, f32[2,768]{1,0:T(2,128)} %bitcast.51, ...), custom_call_target="tpu_custom_call" | custom-call | flops 6600000000 | bytes 1 | tf_op jit(solution)/shard_map/pallas_call | solution.py:747
  230.0 3.7 shard_map.189
  239.8 4.0 %collective-permute-start.32 = (bf16[112,768]{1,0:T(8,128)(2,1)}, bf16[112,768]{1,0:T(8,128)(2,1)S(1)}, u32[]{:S(2)}, u32[]{:S(2)}) collective-permute-start(bf16[112,768]{1,0:T(8,128)(2,1)} %get-tuple-element.94.refs_5_), channel_id=1, source_target_pairs={{0,12},{1,13},{2,14},{3,15},{4,8},{5,9},{6,10},{7,11},{8,4},{9,5},... | collective-permute-start | bytes 516104 | tf_op jit(solution)/shard_map/ppermute | solution.py:1469
  264.0 17.1 %collective-permute-done.34.refs_2_ = bf16[2,304,768]{2,1,0:T(8,128)(2,1)S(1)} collective-permute-done((bf16[2,304,768]{2,1,0:T(8,128)(2,1)}, bf16[2,304,768]{2,1,0:T(8,128)(2,1)S(1)}, u32[]{:S(2)}, u32[]{:S(2)}) %collective-permute-start.34) | collective-permute-done | bytes 933920 | tf_op jit(solution)/shard_map/ppermute | solution.py:1670
  287.6 10.3 %collective-permute-done.29.refs_11_.refs_5_ = bf16[96,4224]{1,0:T(8,128)(2,1)} collective-permute-done((bf16[96,4224]{1,0:T(8,128)(2,1)S(1)}, bf16[96,4224]{1,0:T(8,128)(2,1)}, u32[]{:S(2)}, u32[]{:S(2)}) %collective-permute-start.29) | collective-permute-done | bytes 811040 | tf_op jit(solution)/shard_map/ppermute | solution.py:1670
  298.0 4.5 %shard_map.190 = (bf16[4,208,768]{2,1,0:T(8,128)(2,1)}, bf16[256,768]{1,0:T(8,128)(2,1)}) custom-call(s32[1]{0:T(128)} %bitcast.refs_0_, bf16[256,384]{1,0:T(8,128)(2,1)} %get-tuple-element.91.refs_1_, bf16[384,768]{1,0:T(8,128)(2,1)} %get-tuple-element.92.refs_2_, bf16[768,768]{1,0:T(8,128)(2,1)} %get-tuple-element.93.refs_3_, bf16[448,768]{1,0:T(8,128)(2,1)} %copy-done.20, ...), custom_call_target="tpu_custom_call" | custom-call | flops 6600000000 | bytes 1 | tf_op jit(solution)/shard_map/pallas_call | solution.py:747
  302.5 5.5 %collective-permute-done.35.refs_7_.refs_4_ = bf16[304,768]{1,0:T(8,128)(2,1)S(1)} collective-permute-done((bf16[304,768]{1,0:T(8,128)(2,1)}, bf16[304,768]{1,0:T(8,128)(2,1)S(1)}, u32[]{:S(2)}, u32[]{:S(2)}) %collective-permute-start.35) | collective-permute-done | bytes 466976 | tf_op jit(solution)/shard_map/ppermute | solution.py:1670
  308.7 4.6 %shard_map.193 = (bf16[2,336,768]{2,1,0:T(8,128)(2,1)}, bf16[2,336,768]{2,1,0:T(8,128)(2,1)}) custom-call(s32[1]{0:T(128)} %bitcast.refs_0_, s32[1]{0:T(128)} %bitcast.18.refs_1_, bf16[96,4224]{1,0:T(8,128)(2,1)} %get-tuple-element.87.refs_2_, bf16[96,4224]{1,0:T(8,128)(2,1)} %collective-permute-done.27.refs_9_.refs_3_, ...), custom_call_target="tpu_custom_call" | custom-call | flops 6600000000 | bytes 1 | tf_op jit(solution)/shard_map/pallas_call | solution.py:747
  322.8 5.5 %all-to-all-start.4 = ((bf16[16,16,768]{2,1,0:T(8,128)(2,1)}), bf16[16,16,768]{2,1,0:T(8,128)(2,1)S(1)}, u32[]{:S(2)}, u32[]{:S(2)}) async-start(bf16[16,16,768]{2,1,0:T(8,128)(2,1)} %bitcast.25), calls=%async_computation.5 | async-start | bytes 786432 | tf_op jit(solution)/shard_map/all_to_all | solution.py:1755
  328.3 7.7 %collective-permute-done.38.refs_6_.refs_10_ = bf16[208,768]{1,0:T(8,128)(2,1)S(1)} collective-permute-done((bf16[208,768]{1,0:T(8,128)(2,1)S(1)}, bf16[208,768]{1,0:T(8,128)(2,1)S(1)}, u32[]{:S(2)}, u32[]{:S(2)}) %collective-permute-start.38) | collective-permute-done | bytes 319520 | tf_op jit(solution)/shard_map/ppermute | solution.py:1753
  336.1 5.0 %collective-permute-done.36.refs_2_ = bf16[2,336,768]{2,1,0:T(8,128)(2,1)} collective-permute-done((bf16[2,336,768]{2,1,0:T(8,128)(2,1)}, bf16[2,336,768]{2,1,0:T(8,128)(2,1)}, u32[]{:S(2)}, u32[]{:S(2)}) %collective-permute-start.36) | collective-permute-done | bytes 1032224 | tf_op jit(solution)/shard_map/ppermute | solution.py:1670
  344.6 5.2 %collective-permute-start.42 = (bf16[336,768]{1,0:T(8,128)(2,1)}, bf16[336,768]{1,0:T(8,128)(2,1)S(1)}, u32[]{:S(2)}, u32[]{:S(2)}) collective-permute-start(bf16[336,768]{1,0:T(8,128)(2,1)} %get-tuple-element.103), channel_id=1, source_target_pairs={{0,8},{1,9},{2,10},{3,11},{4,12},{5,13},{6,14},{7,15},{8,0},{9,1},... | collective-permute-start | bytes 1548296 | tf_op jit(solution)/shard_map/ppermute | solution.py:1469
  354.9 16.7 %collective-permute-done.42.refs_5_ = bf16[336,768]{1,0:T(8,128)(2,1)S(1)} collective-permute-done((bf16[336,768]{1,0:T(8,128)(2,1)}, bf16[336,768]{1,0:T(8,128)(2,1)S(1)}, u32[]{:S(2)}, u32[]{:S(2)}) %collective-permute-start.42) | collective-permute-done | bytes 516128 | tf_op jit(solution)/shard_map/ppermute | solution.py:1469
  374.5 4.1 %shard_map.195 = (f32[192,768]{1,0:T(8,128)}, f32[48,3072]{1,0:T(8,128)}, f32[48,2304]{1,0:T(8,128)}, f32[48,768]{1,0:T(8,128)}, f32[16,768]{1,0:T(8,128)}, /*index=5*/f32[16,768]{1,0:T(8,128)}, f32[192,768]{1,0:T(8,128)}) custom-call(s32[1]{0:T(128)} %bitcast.refs_0_, bf16[336,768]{1,0:T(8,128)(2,1)} %get-tuple-element.100.refs_1_, ...), custom_call_target="tpu_custom_call" | custom-call | flops 4400000000 | bytes 1 | tf_op jit(solution)/shard_map/pallas_call | solution.py:747
  (197 shorter events, 130.4 us)
Async XLA Ops:
  7.2 19.1 %collective-permute-start = (bf16[256,768]{1,0:T(8,128)(2,1)}, bf16[256,768]{1,0:T(8,128)(2,1)S(1)}, u32[]{:S(2)}, u32[]{:S(2)}) collective-permute-start(bf16[256,768]{1,0:T(8,128)(2,1)} %bitcast.71), channel_id=1, source_target_pairs={{0,16},{16,0},{1,17},{17,1},{2,18},{18,2},{3,19},{19,3},{4,20},{20... | collective-permute-start | bytes 1179656 | tf_op jit(solution)/shard_map/ppermute | solution.py:1473
  7.7 18.5 %collective-permute-start.4 = (bf16[192,768]{1,0:T(8,128)(2,1)}, bf16[192,768]{1,0:T(8,128)(2,1)S(1)}, u32[]{:S(2)}, u32[]{:S(2)}) collective-permute-start(bf16[192,768]{1,0:T(8,128)(2,1)} %refs_7_.1), channel_id=1, source_target_pairs={{0,1},{1,0},{2,3},{3,2},{4,5},{5,4},{6,7},{7,6},{8,9},{9,8},{10,11... | collective-permute-start | bytes 884744 | tf_op jit(solution)/shard_map/ppermute | solution.py:1530
  10.3 15.9 %collective-permute-start.5 = (bf16[192,768]{1,0:T(8,128)(2,1)}, bf16[192,768]{1,0:T(8,128)(2,1)S(1)}, u32[]{:S(2)}, u32[]{:S(2)}) collective-permute-start(bf16[192,768]{1,0:T(8,128)(2,1)} %refs_7_.1), channel_id=1, source_target_pairs={{0,2},{1,3},{2,0},{3,1},{4,6},{5,7},{6,4},{7,5},{8,10},{9,11},{10,... | collective-permute-start | bytes 884744 | tf_op jit(solution)/shard_map/ppermute | solution.py:1530
  11.8 14.4 %collective-permute-start.6 = (bf16[192,768]{1,0:T(8,128)(2,1)}, bf16[192,768]{1,0:T(8,128)(2,1)S(1)}, u32[]{:S(2)}, u32[]{:S(2)}) collective-permute-start(bf16[192,768]{1,0:T(8,128)(2,1)} %refs_7_.1), channel_id=1, source_target_pairs={{0,3},{1,2},{2,1},{3,0},{4,7},{5,6},{6,5},{7,4},{8,11},{9,10},{10,... | collective-permute-start | bytes 884744 | tf_op jit(solution)/shard_map/ppermute | solution.py:1530
  33.1 81.9 %collective-permute-start.18 = (bf16[768,3072]{1,0:T(8,128)(2,1)}, bf16[768,3072]{1,0:T(8,128)(2,1)}, u32[]{:S(2)}, u32[]{:S(2)}) collective-permute-start(bf16[768,3072]{1,0:T(8,128)(2,1)} %bitcast.53), channel_id=1, source_target_pairs={{16,0},{17,1},{18,2},{19,3},{20,4},{21,5},{22,6},{23,7},{24,8},{25... | collective-permute-start | bytes 14155784 | tf_op jit(solution)/shard_map/ppermute | solution.py:1469
  34.4 80.6 %collective-permute-start.19 = (bf16[3072,768]{1,0:T(8,128)(2,1)}, bf16[3072,768]{1,0:T(8,128)(2,1)}, u32[]{:S(2)}, u32[]{:S(2)}) collective-permute-start(bf16[3072,768]{1,0:T(8,128)(2,1)} %bitcast.57), channel_id=1, source_target_pairs={{16,0},{17,1},{18,2},{19,3},{20,4},{21,5},{22,6},{23,7},{24,8},{25... | collective-permute-start | bytes 14155784 | tf_op jit(solution)/shard_map/ppermute | solution.py:1469
  37.4 10.9 %collective-permute-start.10 = (bf16[96,768]{1,0:T(8,128)(2,1)S(1)}, bf16[96,768]{1,0:T(8,128)(2,1)S(1)}, u32[]{:S(2)}, u32[]{:S(2)}) collective-permute-start(bf16[96,768]{1,0:T(8,128)(2,1)S(1)} %get-tuple-element.117), channel_id=1, source_target_pairs={{0,12},{1,13},{2,14},{3,15},{4,8},{5,9},{6,10},{7,11},{8,4},{9,5},... | collective-permute-start | bytes 442376 | tf_op jit(solution)/shard_map/ppermute | solution.py:1469
  64.0 16.8 %all-to-all-start = ((bf16[16,32,384]{2,1,0:T(8,128)(2,1)}), bf16[16,32,384]{2,1,0:T(8,128)(2,1)S(1)}, u32[]{:S(2)}, u32[]{:S(2)}) async-start(bf16[16,32,384]{2,1,0:T(8,128)(2,1)} %pad_select_fusion), calls=%async_computation | async-start | bytes 786432 | tf_op jit(solution)/shard_map/all_to_all | solution.py:1563
  68.8 46.2 %collective-permute-start.16 = (bf16[768,2304]{1,0:T(8,128)(2,1)}, bf16[768,2304]{1,0:T(8,128)(2,1)}, u32[]{:S(2)}, u32[]{:S(2)}) collective-permute-start(bf16[768,2304]{1,0:T(8,128)(2,1)} %bitcast.62), channel_id=1, source_target_pairs={{16,0},{17,1},{18,2},{19,3},{20,4},{21,5},{22,6},{23,7},{24,8},{25... | collective-permute-start | bytes 10616840 | tf_op jit(solution)/shard_map/ppermute | solution.py:1469
  85.8 11.4 %all-to-all-start.1 = ((bf16[16,32,128]{2,1,0:T(8,128)(2,1)}), bf16[16,32,128]{2,1,0:T(8,128)(2,1)S(1)}, u32[]{:S(2)}, u32[]{:S(2)}) async-start(bf16[16,32,128]{2,1,0:T(8,128)(2,1)} %bitcast.44), calls=%async_computation.1 | async-start | bytes 262144 | tf_op jit(solution)/shard_map/all_to_all | solution.py:1568
  89.4 166.9 %reduce-scatter.2.cloned.1.call-start = ((), (), s32[]{:S(2)}) async-start(), calls=%async_computation.6 | async-start | bytes 9338880 | tf_op jit(solution)/shard_map/reduce_scatter | solution.py:1744
  89.5 20.8 %collective-permute-start.17 = (bf16[768,768]{1,0:T(8,128)(2,1)S(1)}, bf16[768,768]{1,0:T(8,128)(2,1)S(1)}, u32[]{:S(2)}, u32[]{:S(2)}) collective-permute-start(bf16[768,768]{1,0:T(8,128)(2,1)S(1)} %bitcast.68), channel_id=1, source_target_pairs={{16,0},{17,1},{18,2},{19,3},{20,4},{21,5},{22,6},{23,7},{24,8},{25... | collective-permute-start | bytes 3538952 | tf_op jit(solution)/shard_map/ppermute | solution.py:1469
  147.3 10.4 %collective-permute-start.23 = (bf16[400,7680]{1,0:T(8,128)(2,1)}, bf16[400,7680]{1,0:T(8,128)(2,1)}, u32[]{:S(2)}, u32[]{:S(2)}) collective-permute-start(bf16[400,7680]{1,0:T(8,128)(2,1)} %get-tuple-element.76), channel_id=1, source_target_pairs={{0,16},{16,0},{1,17},{17,1},{2,18},{18,2},{3,19},{19,3},{4,20},{20... | collective-permute-start | bytes 18432008 | tf_op jit(solution)/shard_map/ppermute | solution.py:1473
  147.4 10.2 %collective-permute-start.21 = (bf16[48,768]{1,0:T(8,128)(2,1)}, bf16[48,768]{1,0:T(8,128)(2,1)S(1)}, u32[]{:S(2)}, u32[]{:S(2)}) collective-permute-start(bf16[48,768]{1,0:T(8,128)(2,1)} %get-tuple-element.71.refs_0_), channel_id=1, source_target_pairs={{16,0},{17,1},{18,2},{19,3},{20,4},{21,5},{22,6},{23,7},{24,8},{25... | collective-permute-start | bytes 221192 | tf_op jit(solution)/shard_map/ppermute | solution.py:1469
  183.9 13.6 %all-to-all-start.2 = ((bf16[16,32,128]{2,1,0:T(8,128)(2,1)}), bf16[16,32,128]{2,1,0:T(8,128)(2,1)S(1)}, u32[]{:S(2)}, u32[]{:S(2)}) async-start(bf16[16,32,128]{2,1,0:T(8,128)(2,1)} %pad_select_fusion.1), calls=%async_computation.2 | async-start | bytes 262144 | tf_op jit(solution)/shard_map/all_to_all | solution.py:1563
  192.7 35.6 %collective-permute-start.26 = (bf16[4,96,4224]{2,1,0:T(8,128)(2,1)}, bf16[4,96,4224]{2,1,0:T(8,128)(2,1)S(1)}, u32[]{:S(2)}, u32[]{:S(2)}) collective-permute-start(bf16[4,96,4224]{2,1,0:T(8,128)(2,1)} %shard_map.188), channel_id=1, source_target_pairs={{0,16},{1,17},{2,18},{3,19},{4,20},{5,21},{6,22},{7,23},{8,24},{9,... | collective-permute-start | bytes 9732104 | tf_op jit(solution)/shard_map/ppermute | solution.py:1469
  233.7 10.1 %collective-permute-start.30 = (bf16[112,768]{1,0:T(8,128)(2,1)}, bf16[112,768]{1,0:T(8,128)(2,1)S(1)}, u32[]{:S(2)}, u32[]{:S(2)}) collective-permute-start(bf16[112,768]{1,0:T(8,128)(2,1)} %get-tuple-element.94.refs_5_), channel_id=1, source_target_pairs={{0,4},{1,5},{2,6},{3,7},{4,0},{5,1},{6,2},{7,3},{8,12},{9,13},{10,... | collective-permute-start | bytes 516104 | tf_op jit(solution)/shard_map/ppermute | solution.py:1469
  237.2 10.2 %collective-permute-start.31 = (bf16[112,768]{1,0:T(8,128)(2,1)}, bf16[112,768]{1,0:T(8,128)(2,1)S(1)}, u32[]{:S(2)}, u32[]{:S(2)}) collective-permute-start(bf16[112,768]{1,0:T(8,128)(2,1)} %get-tuple-element.94.refs_5_), channel_id=1, source_target_pairs={{0,8},{1,9},{2,10},{3,11},{4,12},{5,13},{6,14},{7,15},{8,0},{9,1},... | collective-permute-start | bytes 516104 | tf_op jit(solution)/shard_map/ppermute | solution.py:1469
  258.4 22.7 %collective-permute-start.34 = (bf16[2,304,768]{2,1,0:T(8,128)(2,1)}, bf16[2,304,768]{2,1,0:T(8,128)(2,1)S(1)}, u32[]{:S(2)}, u32[]{:S(2)}) collective-permute-start(bf16[2,304,768]{2,1,0:T(8,128)(2,1)} %shard_map.191), channel_id=1, source_target_pairs={{0,4},{1,5},{2,6},{3,7},{4,0},{5,1},{6,2},{7,3},{8,12},{9,13},{10,... | collective-permute-start | bytes 2801672 | tf_op jit(solution)/shard_map/ppermute | solution.py:1670
  259.9 27.7 %collective-permute-start.27 = (bf16[96,4224]{1,0:T(8,128)(2,1)}, bf16[96,4224]{1,0:T(8,128)(2,1)}, u32[]{:S(2)}, u32[]{:S(2)}) collective-permute-start(bf16[96,4224]{1,0:T(8,128)(2,1)} %get-tuple-element.88), channel_id=1, source_target_pairs={{0,1},{1,0},{2,3},{3,2},{4,5},{5,4},{6,7},{7,6},{8,9},{9,8},{10,11... | collective-permute-start | bytes 2433032 | tf_op jit(solution)/shard_map/ppermute | solution.py:1670
  261.2 26.4 %collective-permute-start.28 = (bf16[96,4224]{1,0:T(8,128)(2,1)S(1)}, bf16[96,4224]{1,0:T(8,128)(2,1)}, u32[]{:S(2)}, u32[]{:S(2)}) collective-permute-start(bf16[96,4224]{1,0:T(8,128)(2,1)S(1)} %copy-done.19), channel_id=1, source_target_pairs={{0,2},{1,3},{2,0},{3,1},{4,6},{5,7},{6,4},{7,5},{8,10},{9,11},{10,... | collective-permute-start | bytes 2433032 | tf_op jit(solution)/shard_map/ppermute | solution.py:1670
  262.0 36.0 %collective-permute-start.29 = (bf16[96,4224]{1,0:T(8,128)(2,1)S(1)}, bf16[96,4224]{1,0:T(8,128)(2,1)}, u32[]{:S(2)}, u32[]{:S(2)}) collective-permute-start(bf16[96,4224]{1,0:T(8,128)(2,1)S(1)} %copy-done.18), channel_id=1, source_target_pairs={{0,3},{1,2},{2,1},{3,0},{4,7},{5,6},{6,5},{7,4},{8,11},{9,10},{10,... | collective-permute-start | bytes 2433032 | tf_op jit(solution)/shard_map/ppermute | solution.py:1670
  285.2 22.8 %collective-permute-start.35 = (bf16[304,768]{1,0:T(8,128)(2,1)}, bf16[304,768]{1,0:T(8,128)(2,1)S(1)}, u32[]{:S(2)}, u32[]{:S(2)}) collective-permute-start(bf16[304,768]{1,0:T(8,128)(2,1)} %get-tuple-element.96), channel_id=1, source_target_pairs={{0,8},{1,9},{2,10},{3,11},{4,12},{5,13},{6,14},{7,15},{8,0},{9,1},... | collective-permute-start | bytes 1400840 | tf_op jit(solution)/shard_map/ppermute | solution.py:1670
  313.4 27.6 %collective-permute-start.36 = (bf16[2,336,768]{2,1,0:T(8,128)(2,1)}, bf16[2,336,768]{2,1,0:T(8,128)(2,1)}, u32[]{:S(2)}, u32[]{:S(2)}) collective-permute-start(bf16[2,336,768]{2,1,0:T(8,128)(2,1)} %get-tuple-element.98), channel_id=1, source_target_pairs={{0,4},{1,5},{2,6},{3,7},{4,0},{5,1},{6,2},{7,3},{8,12},{9,13},{10,... | collective-permute-start | bytes 3096584 | tf_op jit(solution)/shard_map/ppermute | solution.py:1670
  316.2 12.1 %collective-permute-start.37 = (bf16[208,768]{1,0:T(8,128)(2,1)S(1)}, bf16[208,768]{1,0:T(8,128)(2,1)S(1)}, u32[]{:S(2)}, u32[]{:S(2)}) collective-permute-start(bf16[208,768]{1,0:T(8,128)(2,1)S(1)} %get-tuple-element.116), channel_id=1, source_target_pairs={{0,1},{1,0},{2,3},{3,2},{4,5},{5,4},{6,7},{7,6},{8,9},{9,8},{10,11... | collective-permute-start | bytes 958472 | tf_op jit(solution)/shard_map/ppermute | solution.py:1753
  317.5 18.6 %collective-permute-start.38 = (bf16[208,768]{1,0:T(8,128)(2,1)S(1)}, bf16[208,768]{1,0:T(8,128)(2,1)S(1)}, u32[]{:S(2)}, u32[]{:S(2)}) collective-permute-start(bf16[208,768]{1,0:T(8,128)(2,1)S(1)} %get-tuple-element.115), channel_id=1, source_target_pairs={{0,2},{1,3},{2,0},{3,1},{4,6},{5,7},{6,4},{7,5},{8,10},{9,11},{10,... | collective-permute-start | bytes 958472 | tf_op jit(solution)/shard_map/ppermute | solution.py:1753
  318.2 17.8 %collective-permute-start.39 = (bf16[208,768]{1,0:T(8,128)(2,1)S(1)}, bf16[208,768]{1,0:T(8,128)(2,1)S(1)}, u32[]{:S(2)}, u32[]{:S(2)}) collective-permute-start(bf16[208,768]{1,0:T(8,128)(2,1)S(1)} %get-tuple-element.114), channel_id=1, source_target_pairs={{0,3},{1,2},{2,1},{3,0},{4,7},{5,6},{6,5},{7,4},{8,11},{9,10},{10,... | collective-permute-start | bytes 958472 | tf_op jit(solution)/shard_map/ppermute | solution.py:1753
  319.7 31.4 %collective-permute-start.20 = (bf16[3,128,768]{2,1,0:T(8,128)(2,1)}, bf16[3,128,768]{2,1,0:T(8,128)(2,1)S(1)}, u32[]{:S(2)}, u32[]{:S(2)}) collective-permute-start(bf16[3,128,768]{2,1,0:T(8,128)(2,1)} %bitcast.69), channel_id=1, source_target_pairs={{0,16},{1,17},{2,18},{3,19},{4,20},{5,21},{6,22},{7,23},{8,24},{9,... | collective-permute-start | bytes 1769480 | tf_op jit(solution)/shard_map/ppermute | solution.py:1469
  322.8 32.1 %all-to-all-start.4 = ((bf16[16,16,768]{2,1,0:T(8,128)(2,1)}), bf16[16,16,768]{2,1,0:T(8,128)(2,1)S(1)}, u32[]{:S(2)}, u32[]{:S(2)}) async-start(bf16[16,16,768]{2,1,0:T(8,128)(2,1)} %bitcast.25), calls=%async_computation.5 | async-start | bytes 786432 | tf_op jit(solution)/shard_map/all_to_all | solution.py:1755
  344.6 10.3 %collective-permute-start.40 = (bf16[336,768]{1,0:T(8,128)(2,1)}, bf16[336,768]{1,0:T(8,128)(2,1)S(1)}, u32[]{:S(2)}, u32[]{:S(2)}) collective-permute-start(bf16[336,768]{1,0:T(8,128)(2,1)} %get-tuple-element.101), channel_id=1, source_target_pairs={{0,16},{16,0},{1,17},{17,1},{2,18},{18,2},{3,19},{19,3},{4,20},{20... | collective-permute-start | bytes 1548296 | tf_op jit(solution)/shard_map/ppermute | solution.py:1473
  344.6 27.0 %collective-permute-start.42 = (bf16[336,768]{1,0:T(8,128)(2,1)}, bf16[336,768]{1,0:T(8,128)(2,1)S(1)}, u32[]{:S(2)}, u32[]{:S(2)}) collective-permute-start(bf16[336,768]{1,0:T(8,128)(2,1)} %get-tuple-element.103), channel_id=1, source_target_pairs={{0,8},{1,9},{2,10},{3,11},{4,12},{5,13},{6,14},{7,15},{8,0},{9,1},... | collective-permute-start | bytes 1548296 | tf_op jit(solution)/shard_map/ppermute | solution.py:1469
  349.8 23.9 %collective-permute-start.43 = (bf16[336,768]{1,0:T(8,128)(2,1)}, bf16[336,768]{1,0:T(8,128)(2,1)S(1)}, u32[]{:S(2)}, u32[]{:S(2)}) collective-permute-start(bf16[336,768]{1,0:T(8,128)(2,1)} %get-tuple-element.103), channel_id=1, source_target_pairs={{16,8},{17,9},{18,10},{19,11},{20,12},{21,13},{22,14},{23,15},{24,... | collective-permute-start | bytes 1548296 | tf_op jit(solution)/shard_map/ppermute | solution.py:1469
  (63 other events, 337.0 us)
Sparse Core Ops, SparseCore 0:
  169.8 86.3 reduce-scatter.1

commit v8 on v7

--- a/solution.py
+++ b/solution.py
@@ -1331,11 +1331,13 @@
     )
 
 
-def half_sums_and_cross(flags, kept, near, other, other_far, deps=()):
+def half_sums_and_cross(flags, kept, near, other, other_far, short, deps=()):
     shape = kept.shape[1:]
     held = other.shape[0]
 
-    def kernel(flags_ref, kept_ref, near_ref, other_ref, more_ref, far_ref, mine_ref, cross_ref):
+    def kernel(
+        flags_ref, kept_ref, near_ref, other_ref, more_ref, far_ref, short_ref, mine_ref, cross_ref
+    ):
         for k in range(2):
             total = (kept_ref[k].astype(f32) + near_ref[k].astype(f32)).astype(bf16)
 
@@ -1347,6 +1349,7 @@
             @pl.when(flags_ref[1] != k)
             def _():
                 far_ref[...] = total
+                short_ref[...] = total[0:short]
 
         @pl.when(flags_ref[0] == 0)
         def _():
@@ -1357,8 +1360,8 @@
         kernel,
         (flags, kept, near, other, other_far),
         [SCALARS] + [WHOLE] * 4,
-        [shaped(*shape)] * 3,
-        [WHOLE] * 3,
+        [shaped(*shape), shaped(short, shape[1]), shaped(*shape), shaped(*shape)],
+        [WHOLE] * 4,
         deps=deps,
         micros=2,
     )
@@ -1730,6 +1733,13 @@
         pairs = [(i, i ^ (k * span)) for i in range(count)]
         gathered.append(section_send(own_rows, 0, 0, pairs))
     crossed = section_send(jnp.concatenate(gathered), 0, 1, straight)
+    if in_plane:
+        in_planes = lax.psum_scatter(half_locals, "member", scatter_dimension=0, tiled=True)
+        parity_flag = (group & 1).reshape(1).astype(jnp.int32)
+        local_leaving = by_parity(parity_flag, in_planes, [crossed])
+        local_near = both_send(local_leaving, group_pairs(1))
+    else:
+        own_local = place_sum(half_locals)
     patch_share, table_share = patch_backward(
         flag,
         byte_onehot,
@@ -1738,15 +1748,8 @@
         gathered,
         crossed,
         span,
-        arrived_parts[1:] if in_plane else (),
-    )
-    if in_plane:
-        in_planes = lax.psum_scatter(half_locals, "member", scatter_dimension=0, tiled=True)
-        parity_flag = (group & 1).reshape(1).astype(jnp.int32)
-        local_leaving = by_parity(parity_flag, in_planes, [crossed])
-        local_near = both_send(local_leaving, group_pairs(1))
-    else:
-        own_local = place_sum(half_locals)
+        [local_leaving] if in_plane else (),
+    )
     patch_parts = [lax.dynamic_index_in_dim(patch_share, member, 0, keepdims=False)]
     for k in range(1, span):
         leaving = lax.dynamic_index_in_dim(patch_share, member ^ k, 0, keepdims=False)
@@ -1778,16 +1781,17 @@
             arrived_parts,
             contract.shape[0],
             width,
-            [patch_share, local_far],
+            [table_parts, local_far],
         )
         near = both_send(leaving, group_pairs(1))
-        far, mine, crossed = half_sums_and_cross(
-            half_flags, kept, near, local_mine, local_far, patch_parts[1:]
+        short = expand.shape[1] // GROUPS + shard
+        far, far_short, mine, crossed = half_sums_and_cross(
+            half_flags, kept, near, local_mine, local_far, short, patch_parts[1:]
         )
         crossed = section_swap(crossed)
         fars = [
             section_send(far, 0, 0, across),
-            section_send(far, 1, 0, across),
+            section_send(far_short, 1, 0, across),
             local_far,
         ]
         contract_grad, expand_grad, in_grad, out_grads, table_grad, small, patch_grads = finish(

time: 395 us -> 391 us (0.990)
  starting transfers between devices: 99.2 us -> 95 us
    unnamed x92 -> x94, local copies, waits for them, and re-layouts: 11 us -> 12.1 us
  transfers between devices with their start and end apart: 49 -> 49, of which waited for: 27 -> 28; matrix products, arithmetic and copies ran while one was open for 3% -> 3% of each run, Pallas kernels for 15% -> 15%
where the time goes in v8:
time: 391 us; the launch traced here: 383 us
  waiting for transfers between devices  118 us (30%)
  Pallas kernels  115 us (29%)
  starting transfers between devices  95 us (24%)
  blocking collectives  15.3 us (4%)
  between operations  15.2 us (4%)
  local copies, waits for them, and re-layouts  15.1 us (4%)
  other arithmetic  10.1 us (3%)
    pallas_call x13, Pallas kernels, call(): pl.pallas_call(body, in_specs=list(specs) + [ANY] * len(deps), out_specs=...  59.8 us
    ppermute x25, starting transfers between devices, section_send(): return lax.ppermute(x, ('section',) + SEQ, joint)  52.4 us
    ppermute x25, waiting for transfers between devices, section_send(): return lax.ppermute(x, ('section',) + SEQ, joint)  43.8 us
    ppermute x6, waiting for transfers between devices, both_send(): return lax.ppermute(x, ('section',) + SEQ, joint)  34.9 us
    pallas_call x1, Pallas kernels, local_block(): pl.pallas_call(partial(local_kernel, patch_rows), in_specs=[SCALARS] + [W...  31.6 us
    all_to_all x1, blocking collectives, from_tasks(): lax.all_to_all(results.reshape(count, patch_rows, columns), SEQ, 0, 0)  15.3 us
    all_to_all x2, waiting for transfers between devices, to_tasks(): landed = lax.all_to_all(slots, SEQ, 0, 0)  13.3 us
    unnamed x94, local copies, waits for them, and re-layouts  12.1 us
  transfers between devices with their start and end apart: 49, of which 28 were waited for; matrix products, arithmetic and copies ran while one was open for 3% of the time, Pallas kernels for 15%

profile of v8, /device:TPU:0, one launch (start us, length us, event | category | flops | bytes accessed | tf_op | source)
XLA Modules:
  0.0 383.5 jit_solution(3491051067777043368)
XLA Ops:
  20.5 3.9 %collective-permute-start.3 = (s32[3,256]{1,0:T(4,128)}, s32[3,256]{1,0:T(4,128)S(1)}, u32[]{:S(2)}, u32[]{:S(2)}) collective-permute-start(s32[3,256]{1,0:T(4,128)} %ids_ref.3), channel_id=1, source_target_pairs={{0,12},{1,13},{2,14},{3,15},{4,8},{5,9},{6,10},{7,11},{8,4},{9,5},... | collective-permute-start | bytes 9224 | tf_op jit(solution)/shard_map/ppermute | solution.py:1538
  27.9 4.0 %shard_map.178 = (bf16[384,768]{1,0:T(8,128)(2,1)}, bf16[768,768]{1,0:T(8,128)(2,1)}, f32[384,768]{1,0:T(8,128)}, bf16[384,768]{1,0:T(8,128)(2,1)}, bf16[256,384]{1,0:T(8,128)(2,1)}) custom-call(s32[3]{0:T(128)} %pad_add_fusion.1.refs_0_, bf16[256,768]{1,0:T(8,128)(2,1)} %bitcast.72, bf16[256,768]{1,0:T(8,128)(2,1)} %copy-done.26, s32[3,256]{1,0:T(4,128)} %ids_ref.3, ...), custom_call_target="tpu_custom_call" | custom-call | flops 4400000000 | bytes 1 | tf_op jit(solution)/shard_map/pallas_call | solution.py:747
  37.4 5.7 %collective-permute-start.10 = (bf16[96,768]{1,0:T(8,128)(2,1)S(1)}, bf16[96,768]{1,0:T(8,128)(2,1)S(1)}, u32[]{:S(2)}, u32[]{:S(2)}) collective-permute-start(bf16[96,768]{1,0:T(8,128)(2,1)S(1)} %get-tuple-element.119), channel_id=1, source_target_pairs={{0,12},{1,13},{2,14},{3,15},{4,8},{5,9},{6,10},{7,11},{8,4},{9,5},... | collective-permute-start | bytes 442376 | tf_op jit(solution)/shard_map/ppermute | solution.py:1472
  50.2 4.4 %collective-permute-done.9.refs_5_ = bf16[96,768]{1,0:T(8,128)(2,1)S(1)} collective-permute-done((bf16[96,768]{1,0:T(8,128)(2,1)S(1)}, bf16[96,768]{1,0:T(8,128)(2,1)S(1)}, u32[]{:S(2)}, u32[]{:S(2)}) %collective-permute-start.9) | collective-permute-done | bytes 147488 | tf_op jit(solution)/shard_map/ppermute | solution.py:1472
  55.2 4.6 %shard_map.179 = (f32[96,768]{1,0:T(8,128)}, bf16[96,768]{1,0:T(8,128)(2,1)}, bf16[4,96,192]{2,1,0:T(8,128)(2,1)}, bf16[16,32,384]{2,1,0:T(8,128)(2,1)}, bf16[2,32,384]{2,1,0:T(8,128)(2,1)}) custom-call(f32[96,768]{1,0:T(8,128)} %slice.43.refs_0_, f32[2,768]{1,0:T(2,128)} %bitcast.48, f32[2,768]{1,0:T(2,128)} %bitcast.45, bf16[768,2304]{1,0:T(8,128)(2,1)} %bitcast.61, ...), custom_call_target="tpu_custom_call" | custom-call | flops 5500000256 | bytes 1 | tf_op jit(solution)/shard_map/pallas_call | solution.py:747
  64.1 4.7 %all-to-all-start = ((bf16[16,32,384]{2,1,0:T(8,128)(2,1)}), bf16[16,32,384]{2,1,0:T(8,128)(2,1)S(1)}, u32[]{:S(2)}, u32[]{:S(2)}) async-start(bf16[16,32,384]{2,1,0:T(8,128)(2,1)} %pad_select_fusion), calls=%async_computation | async-start | bytes 786432 | tf_op jit(solution)/shard_map/all_to_all | solution.py:1566
  70.9 10.0 %all-to-all-done = bf16[16,32,384]{2,1,0:T(8,128)(2,1)S(1)} async-done(((bf16[16,32,384]{2,1,0:T(8,128)(2,1)}), bf16[16,32,384]{2,1,0:T(8,128)(2,1)S(1)}, u32[]{:S(2)}, u32[]{:S(2)}) %all-to-all-start) | async-done | bytes 393248 | tf_op jit(solution)/shard_map/all_to_all | solution.py:1566
  81.7 4.1 %shard_map.180 = bf16[512,128]{1,0:T(8,128)(2,1)} custom-call(s32[13]{0:T(128)} %pad_add_fusion.2.numbers_ref.refs_0_, bf16[512,384]{1,0:T(8,128)(2,1)} %bitcast.40), custom_call_target="tpu_custom_call" | custom-call | flops 16499999744 | bytes 1 | tf_op jit(solution)/shard_map/pallas_call | solution.py:716
  90.8 6.4 %all-to-all-done.1.refs_6_ = bf16[16,32,128]{2,1,0:T(8,128)(2,1)S(1)} async-done(((bf16[16,32,128]{2,1,0:T(8,128)(2,1)}), bf16[16,32,128]{2,1,0:T(8,128)(2,1)S(1)}, u32[]{:S(2)}, u32[]{:S(2)}) %all-to-all-start.1) | async-done | bytes 131104 | tf_op jit(solution)/shard_map/all_to_all | solution.py:1571
  100.9 7.3 %shard_map.181 = (bf16[96,768]{1,0:T(8,128)(2,1)}, f32[96,768]{1,0:T(8,128)}, bf16[96,768]{1,0:T(8,128)(2,1)}, bf16[96,3072]{1,0:T(8,128)(2,1)}, bf16[96,3072]{1...) custom-call(f32[96,768]{1,0:T(8,128)} %get-tuple-element.63.refs_0_,, ...), custom_call_target="tpu_custom_call" | custom-call | flops 8800000000 | bytes 1 | tf_op jit(solution)/shard_map/pallas_call | solution.py:747
  115.7 31.6 %shard_map.182 = (bf16[384,768]{1,0:T(8,128)(2,1)}, bf16[48,768]{1,0:T(8,128)(2,1)}, bf16[16,768]{1,0:T(8,128)(2,1)}, bf16[400,7680]{1,0:T(8,128)(2,1)}, bf16[400,7680]{1,0:T(8,128)(2,1)}) custom-call(s32[15]{0:T(128)} %pad_add_fusion.numbers_ref.refs_0_, s32[3,256]{1,0:T(4,128)} %ids_ref.3, bf16[256,768]{1,0:T(8,128)(2,1)} %bitcast.73, ...), custom_call_target="tpu_custom_call" | custom-call | flops 38499999744 | bytes 1 | tf_op jit(solution)/shard_map/pallas_call | solution.py:474
  150.0 4.9 %collective-permute-done.22.rest_1_.refs_2_ = bf16[16,768]{1,0:T(8,128)(2,1)S(1)} collective-permute-done((bf16[16,768]{1,0:T(8,128)(2,1)}, bf16[16,768]{1,0:T(8,128)(2,1)S(1)}, u32[]{:S(2)}, u32[]{:S(2)}) %collective-permute-start.22) | collective-permute-done | bytes 24608 | tf_op jit(solution)/shard_map/ppermute | solution.py:1472
  158.2 11.5 %shard_map.184.refs_9_ = bf16[16,304,768]{2,1,0:T(8,128)(2,1)} custom-call(s32[15]{0:T(128)} %pad_add_fusion.numbers_ref.refs_0_, s32[3,256]{1,0:T(4,128)} %ids_ref.3, bf16[400,7680]{1,0:T(8,128)(2,1)} %get-tuple-element.76.keep_ref, bf16[400,7680]{1,0:T(8,128)(2,1)} %collective-permute-done.23.new_ref, bf16[48,768]{1,0:T(8,128)(2,1)} %copy-done.38, ...), custom_call_target="tpu_custom_call" | custom-call | flops 13200000000 | bytes 1 | tf_op jit(solution)/shard_map/pallas_call | solution.py:598
  169.8 8.7 %shard_map.185 = (bf16[96,3072]{1,0:T(8,128)(2,1)}, f32[96,768]{1,0:T(8,128)}, bf16[96,768]{1,0:T(8,128)(2,1)}, f32[2,768]{1,0:T(2,128)}, bf16[96,768]{1,0:T(8,1...) custom-call(bf16[48,768]{1,0:T(8,128)(2,1)} %get-tuple-element.72.refs_0_, ...), custom_call_target="tpu_custom_call" | custom-call | flops 11000000512 | bytes 1 | tf_op jit(solution)/shard_map/pallas_call | solution.py:747
  184.0 5.7 %all-to-all-start.2 = ((bf16[16,32,128]{2,1,0:T(8,128)(2,1)}), bf16[16,32,128]{2,1,0:T(8,128)(2,1)S(1)}, u32[]{:S(2)}, u32[]{:S(2)}) async-start(bf16[16,32,128]{2,1,0:T(8,128)(2,1)} %pad_select_fusion.1), calls=%async_computation.2 | async-start | bytes 262144 | tf_op jit(solution)/shard_map/all_to_all | solution.py:1566
  198.2 5.8 %shard_map.186 = bf16[512,384]{1,0:T(8,128)(2,1)} custom-call(s32[13]{0:T(128)} %pad_add_fusion.2.numbers_ref.refs_0_, bf16[512,384]{1,0:T(8,128)(2,1)} %bitcast.41, bf16[512,128]{1,0:T(8,128)(2,1)} %bitcast.43), custom_call_target="tpu_custom_call" | custom-call | flops 32999999488 | bytes 1 | tf_op jit(solution)/shard_map/pallas_call | solution.py:729
  204.0 15.3 %all_to_all.25.refs_5_ = bf16[16,32,384]{2,1,0:T(8,128)(2,1)S(1)} all-to-all(bf16[16,32,384]{2,1,0:T(8,128)(2,1)} %bitcast.42), channel_id=1, replica_groups=mesh['section'=2,'group'=4,'member'=4] {'group','member'}, dimensions={0} | all-to-all | bytes 786432 | tf_op jit(solution)/shard_map/all_to_all | solution.py:1571
  223.1 5.2 %shard_map.187 = (bf16[96,2304]{1,0:T(8,128)(2,1)}, bf16[112,768]{1,0:T(8,128)(2,1)}, f32[4,768]{1,0:T(4,128)}) custom-call(f32[96,768]{1,0:T(8,128)} %get-tuple-element.63.refs_0_, f32[96,768]{1,0:T(8,128)} %get-tuple-element.79.refs_1_, f32[2,768]{1,0:T(2,128)} %get-tuple-element.80.refs_2_, f32[2,768]{1,0:T(2,128)} %bitcast.51, ...), custom_call_target="tpu_custom_call" | custom-call | flops 6600000000 | bytes 1 | tf_op jit(solution)/shard_map/pallas_call | solution.py:747
  230.0 3.8 shard_map.189
  239.9 4.0 %collective-permute-start.32 = (bf16[112,768]{1,0:T(8,128)(2,1)}, bf16[112,768]{1,0:T(8,128)(2,1)S(1)}, u32[]{:S(2)}, u32[]{:S(2)}) collective-permute-start(bf16[112,768]{1,0:T(8,128)(2,1)} %get-tuple-element.95.refs_5_), channel_id=1, source_target_pairs={{0,12},{1,13},{2,14},{3,15},{4,8},{5,9},{6,10},{7,11},{8,4},{9,5},... | collective-permute-start | bytes 516104 | tf_op jit(solution)/shard_map/ppermute | solution.py:1472
  259.9 4.6 %shard_map.191 = (bf16[4,208,768]{2,1,0:T(8,128)(2,1)}, bf16[256,768]{1,0:T(8,128)(2,1)}) custom-call(s32[1]{0:T(128)} %bitcast.refs_0_, bf16[256,384]{1,0:T(8,128)(2,1)} %get-tuple-element.92.refs_1_, bf16[384,768]{1,0:T(8,128)(2,1)} %get-tuple-element.93.refs_2_, bf16[768,768]{1,0:T(8,128)(2,1)} %get-tuple-element.94.refs_3_, bf16[448,768]{1,0:T(8,128)(2,1)} %copy-done.20, ...), custom_call_target="tpu_custom_call" | custom-call | flops 6600000000 | bytes 1 | tf_op jit(solution)/shard_map/pallas_call | solution.py:747
  271.2 4.7 %all-to-all-start.4 = ((bf16[16,16,768]{2,1,0:T(8,128)(2,1)}), bf16[16,16,768]{2,1,0:T(8,128)(2,1)S(1)}, u32[]{:S(2)}, u32[]{:S(2)}) async-start(bf16[16,16,768]{2,1,0:T(8,128)(2,1)} %bitcast.22), calls=%async_computation.5 | async-start | bytes 786432 | tf_op jit(solution)/shard_map/all_to_all | solution.py:1758
  276.5 9.0 %collective-permute-done.35.refs_2_ = bf16[2,304,768]{2,1,0:T(8,128)(2,1)S(1)} collective-permute-done((bf16[2,304,768]{2,1,0:T(8,128)(2,1)}, bf16[2,304,768]{2,1,0:T(8,128)(2,1)S(1)}, u32[]{:S(2)}, u32[]{:S(2)}) %collective-permute-start.35) | collective-permute-done | bytes 933920 | tf_op jit(solution)/shard_map/ppermute | solution.py:1673
  290.5 18.8 %collective-permute-done.28.refs_4_ = bf16[96,4224]{1,0:T(8,128)(2,1)} collective-permute-done((bf16[96,4224]{1,0:T(8,128)(2,1)S(1)}, bf16[96,4224]{1,0:T(8,128)(2,1)}, u32[]{:S(2)}, u32[]{:S(2)}) %collective-permute-start.28) | collective-permute-done | bytes 811040 | tf_op jit(solution)/shard_map/ppermute | solution.py:1673
  310.5 4.6 %shard_map.193 = (bf16[2,336,768]{2,1,0:T(8,128)(2,1)}, bf16[2,336,768]{2,1,0:T(8,128)(2,1)}) custom-call(s32[1]{0:T(128)} %bitcast.refs_0_, s32[1]{0:T(128)} %bitcast.18.refs_1_, bf16[96,4224]{1,0:T(8,128)(2,1)} %get-tuple-element.88.refs_2_, bf16[96,4224]{1,0:T(8,128)(2,1)} %collective-permute-done.27.refs_3_, ...), custom_call_target="tpu_custom_call" | custom-call | flops 6600000000 | bytes 1 | tf_op jit(solution)/shard_map/pallas_call | solution.py:747
  321.3 5.7 %collective-permute-done.38.refs_5_.refs_9_ = bf16[208,768]{1,0:T(8,128)(2,1)S(1)} collective-permute-done((bf16[208,768]{1,0:T(8,128)(2,1)S(1)}, bf16[208,768]{1,0:T(8,128)(2,1)S(1)}, u32[]{:S(2)}, u32[]{:S(2)}) %collective-permute-start.38) | collective-permute-done | bytes 319520 | tf_op jit(solution)/shard_map/ppermute | solution.py:1756
  327.0 5.7 %collective-permute-done.39.refs_6_.refs_10_ = bf16[208,768]{1,0:T(8,128)(2,1)S(1)} collective-permute-done((bf16[208,768]{1,0:T(8,128)(2,1)S(1)}, bf16[208,768]{1,0:T(8,128)(2,1)S(1)}, u32[]{:S(2)}, u32[]{:S(2)}) %collective-permute-start.39) | collective-permute-done | bytes 319520 | tf_op jit(solution)/shard_map/ppermute | solution.py:1756
  332.7 7.1 %collective-permute-done.37.refs_2_ = bf16[2,336,768]{2,1,0:T(8,128)(2,1)S(1)} collective-permute-done((bf16[2,336,768]{2,1,0:T(8,128)(2,1)}, bf16[2,336,768]{2,1,0:T(8,128)(2,1)S(1)}, u32[]{:S(2)}, u32[]{:S(2)}) %collective-permute-start.37) | collective-permute-done | bytes 1032224 | tf_op jit(solution)/shard_map/ppermute | solution.py:1673
  340.8 3.7 shard_map.194
  344.5 4.3 %collective-permute-start.42 = (bf16[336,768]{1,0:T(8,128)(2,1)}, bf16[336,768]{1,0:T(8,128)(2,1)S(1)}, u32[]{:S(2)}, u32[]{:S(2)}) collective-permute-start(bf16[336,768]{1,0:T(8,128)(2,1)} %get-tuple-element.104), channel_id=1, source_target_pairs={{0,8},{1,9},{2,10},{3,11},{4,12},{5,13},{6,14},{7,15},{8,0},{9,1},... | collective-permute-start | bytes 1548296 | tf_op jit(solution)/shard_map/ppermute | solution.py:1472
  353.9 14.6 %collective-permute-done.43.refs_6_ = bf16[240,768]{1,0:T(8,128)(2,1)S(1)} collective-permute-done((bf16[240,768]{1,0:T(8,128)(2,1)}, bf16[240,768]{1,0:T(8,128)(2,1)S(1)}, u32[]{:S(2)}, u32[]{:S(2)}) %collective-permute-start.43) | collective-permute-done | bytes 368672 | tf_op jit(solution)/shard_map/ppermute | solution.py:1472
  370.8 4.0 %shard_map.195 = (f32[192,768]{1,0:T(8,128)}, f32[48,3072]{1,0:T(8,128)}, f32[48,2304]{1,0:T(8,128)}, f32[48,768]{1,0:T(8,128)}, f32[16,768]{1,0:T(8,128)}, /*index=5*/f32[16,768]{1,0:T(8,128)}, f32[192,768]{1,0:T(8,128)}) custom-call(s32[1]{0:T(128)} %bitcast.refs_0_, bf16[336,768]{1,0:T(8,128)(2,1)} %get-tuple-element.102.refs_1_, ...), custom_call_target="tpu_custom_call" | custom-call | flops 4400000000 | bytes 1 | tf_op jit(solution)/shard_map/pallas_call | solution.py:747
  (199 shorter events, 129.8 us)
Async XLA Ops:
  7.2 19.1 %collective-permute-start = (bf16[256,768]{1,0:T(8,128)(2,1)}, bf16[256,768]{1,0:T(8,128)(2,1)S(1)}, u32[]{:S(2)}, u32[]{:S(2)}) collective-permute-start(bf16[256,768]{1,0:T(8,128)(2,1)} %bitcast.71), channel_id=1, source_target_pairs={{0,16},{16,0},{1,17},{17,1},{2,18},{18,2},{3,19},{19,3},{4,20},{20... | collective-permute-start | bytes 1179656 | tf_op jit(solution)/shard_map/ppermute | solution.py:1476
  7.7 18.5 %collective-permute-start.4 = (bf16[192,768]{1,0:T(8,128)(2,1)}, bf16[192,768]{1,0:T(8,128)(2,1)S(1)}, u32[]{:S(2)}, u32[]{:S(2)}) collective-permute-start(bf16[192,768]{1,0:T(8,128)(2,1)} %refs_7_.1), channel_id=1, source_target_pairs={{0,1},{1,0},{2,3},{3,2},{4,5},{5,4},{6,7},{7,6},{8,9},{9,8},{10,11... | collective-permute-start | bytes 884744 | tf_op jit(solution)/shard_map/ppermute | solution.py:1533
  10.3 15.9 %collective-permute-start.5 = (bf16[192,768]{1,0:T(8,128)(2,1)}, bf16[192,768]{1,0:T(8,128)(2,1)S(1)}, u32[]{:S(2)}, u32[]{:S(2)}) collective-permute-start(bf16[192,768]{1,0:T(8,128)(2,1)} %refs_7_.1), channel_id=1, source_target_pairs={{0,2},{1,3},{2,0},{3,1},{4,6},{5,7},{6,4},{7,5},{8,10},{9,11},{10,... | collective-permute-start | bytes 884744 | tf_op jit(solution)/shard_map/ppermute | solution.py:1533
  11.8 14.4 %collective-permute-start.6 = (bf16[192,768]{1,0:T(8,128)(2,1)}, bf16[192,768]{1,0:T(8,128)(2,1)S(1)}, u32[]{:S(2)}, u32[]{:S(2)}) collective-permute-start(bf16[192,768]{1,0:T(8,128)(2,1)} %refs_7_.1), channel_id=1, source_target_pairs={{0,3},{1,2},{2,1},{3,0},{4,7},{5,6},{6,5},{7,4},{8,11},{9,10},{10,... | collective-permute-start | bytes 884744 | tf_op jit(solution)/shard_map/ppermute | solution.py:1533
  33.1 81.9 %collective-permute-start.18 = (bf16[768,3072]{1,0:T(8,128)(2,1)}, bf16[768,3072]{1,0:T(8,128)(2,1)}, u32[]{:S(2)}, u32[]{:S(2)}) collective-permute-start(bf16[768,3072]{1,0:T(8,128)(2,1)} %bitcast.53), channel_id=1, source_target_pairs={{16,0},{17,1},{18,2},{19,3},{20,4},{21,5},{22,6},{23,7},{24,8},{25... | collective-permute-start | bytes 14155784 | tf_op jit(solution)/shard_map/ppermute | solution.py:1472
  34.4 80.6 %collective-permute-start.19 = (bf16[3072,768]{1,0:T(8,128)(2,1)}, bf16[3072,768]{1,0:T(8,128)(2,1)}, u32[]{:S(2)}, u32[]{:S(2)}) collective-permute-start(bf16[3072,768]{1,0:T(8,128)(2,1)} %bitcast.57), channel_id=1, source_target_pairs={{16,0},{17,1},{18,2},{19,3},{20,4},{21,5},{22,6},{23,7},{24,8},{25... | collective-permute-start | bytes 14155784 | tf_op jit(solution)/shard_map/ppermute | solution.py:1472
  37.4 10.9 %collective-permute-start.10 = (bf16[96,768]{1,0:T(8,128)(2,1)S(1)}, bf16[96,768]{1,0:T(8,128)(2,1)S(1)}, u32[]{:S(2)}, u32[]{:S(2)}) collective-permute-start(bf16[96,768]{1,0:T(8,128)(2,1)S(1)} %get-tuple-element.119), channel_id=1, source_target_pairs={{0,12},{1,13},{2,14},{3,15},{4,8},{5,9},{6,10},{7,11},{8,4},{9,5},... | collective-permute-start | bytes 442376 | tf_op jit(solution)/shard_map/ppermute | solution.py:1472
  64.1 16.8 %all-to-all-start = ((bf16[16,32,384]{2,1,0:T(8,128)(2,1)}), bf16[16,32,384]{2,1,0:T(8,128)(2,1)S(1)}, u32[]{:S(2)}, u32[]{:S(2)}) async-start(bf16[16,32,384]{2,1,0:T(8,128)(2,1)} %pad_select_fusion), calls=%async_computation | async-start | bytes 786432 | tf_op jit(solution)/shard_map/all_to_all | solution.py:1566
  68.8 46.3 %collective-permute-start.16 = (bf16[768,2304]{1,0:T(8,128)(2,1)}, bf16[768,2304]{1,0:T(8,128)(2,1)}, u32[]{:S(2)}, u32[]{:S(2)}) collective-permute-start(bf16[768,2304]{1,0:T(8,128)(2,1)} %bitcast.62), channel_id=1, source_target_pairs={{16,0},{17,1},{18,2},{19,3},{20,4},{21,5},{22,6},{23,7},{24,8},{25... | collective-permute-start | bytes 10616840 | tf_op jit(solution)/shard_map/ppermute | solution.py:1472
  85.8 11.4 %all-to-all-start.1 = ((bf16[16,32,128]{2,1,0:T(8,128)(2,1)}), bf16[16,32,128]{2,1,0:T(8,128)(2,1)S(1)}, u32[]{:S(2)}, u32[]{:S(2)}) async-start(bf16[16,32,128]{2,1,0:T(8,128)(2,1)} %bitcast.44), calls=%async_computation.1 | async-start | bytes 262144 | tf_op jit(solution)/shard_map/all_to_all | solution.py:1571
  89.4 166.9 %reduce-scatter.2.cloned.1.call-start = ((), (), s32[]{:S(2)}) async-start(), calls=%async_computation.6 | async-start | bytes 9338880 | tf_op jit(solution)/shard_map/reduce_scatter | solution.py:1737
  89.5 20.8 %collective-permute-start.17 = (bf16[768,768]{1,0:T(8,128)(2,1)S(1)}, bf16[768,768]{1,0:T(8,128)(2,1)S(1)}, u32[]{:S(2)}, u32[]{:S(2)}) collective-permute-start(bf16[768,768]{1,0:T(8,128)(2,1)S(1)} %bitcast.68), channel_id=1, source_target_pairs={{16,0},{17,1},{18,2},{19,3},{20,4},{21,5},{22,6},{23,7},{24,8},{25... | collective-permute-start | bytes 3538952 | tf_op jit(solution)/shard_map/ppermute | solution.py:1472
  147.3 10.4 %collective-permute-start.23 = (bf16[400,7680]{1,0:T(8,128)(2,1)}, bf16[400,7680]{1,0:T(8,128)(2,1)}, u32[]{:S(2)}, u32[]{:S(2)}) collective-permute-start(bf16[400,7680]{1,0:T(8,128)(2,1)} %get-tuple-element.77), channel_id=1, source_target_pairs={{0,16},{16,0},{1,17},{17,1},{2,18},{18,2},{3,19},{19,3},{4,20},{20... | collective-permute-start | bytes 18432008 | tf_op jit(solution)/shard_map/ppermute | solution.py:1476
  147.4 10.2 %collective-permute-start.21 = (bf16[48,768]{1,0:T(8,128)(2,1)}, bf16[48,768]{1,0:T(8,128)(2,1)S(1)}, u32[]{:S(2)}, u32[]{:S(2)}) collective-permute-start(bf16[48,768]{1,0:T(8,128)(2,1)} %get-tuple-element.72.refs_0_), channel_id=1, source_target_pairs={{16,0},{17,1},{18,2},{19,3},{20,4},{21,5},{22,6},{23,7},{24,8},{25... | collective-permute-start | bytes 221192 | tf_op jit(solution)/shard_map/ppermute | solution.py:1472
  184.0 13.6 %all-to-all-start.2 = ((bf16[16,32,128]{2,1,0:T(8,128)(2,1)}), bf16[16,32,128]{2,1,0:T(8,128)(2,1)S(1)}, u32[]{:S(2)}, u32[]{:S(2)}) async-start(bf16[16,32,128]{2,1,0:T(8,128)(2,1)} %pad_select_fusion.1), calls=%async_computation.2 | async-start | bytes 262144 | tf_op jit(solution)/shard_map/all_to_all | solution.py:1566
  192.7 35.6 %collective-permute-start.26 = (bf16[4,96,4224]{2,1,0:T(8,128)(2,1)}, bf16[4,96,4224]{2,1,0:T(8,128)(2,1)S(1)}, u32[]{:S(2)}, u32[]{:S(2)}) collective-permute-start(bf16[4,96,4224]{2,1,0:T(8,128)(2,1)} %shard_map.188), channel_id=1, source_target_pairs={{0,16},{1,17},{2,18},{3,19},{4,20},{5,21},{6,22},{7,23},{8,24},{9,... | collective-permute-start | bytes 9732104 | tf_op jit(solution)/shard_map/ppermute | solution.py:1472
  233.8 10.1 %collective-permute-start.30 = (bf16[112,768]{1,0:T(8,128)(2,1)}, bf16[112,768]{1,0:T(8,128)(2,1)S(1)}, u32[]{:S(2)}, u32[]{:S(2)}) collective-permute-start(bf16[112,768]{1,0:T(8,128)(2,1)} %get-tuple-element.95.refs_5_), channel_id=1, source_target_pairs={{0,4},{1,5},{2,6},{3,7},{4,0},{5,1},{6,2},{7,3},{8,12},{9,13},{10,... | collective-permute-start | bytes 516104 | tf_op jit(solution)/shard_map/ppermute | solution.py:1472
  237.2 10.2 %collective-permute-start.31 = (bf16[112,768]{1,0:T(8,128)(2,1)}, bf16[112,768]{1,0:T(8,128)(2,1)S(1)}, u32[]{:S(2)}, u32[]{:S(2)}) collective-permute-start(bf16[112,768]{1,0:T(8,128)(2,1)} %get-tuple-element.95.refs_5_), channel_id=1, source_target_pairs={{0,8},{1,9},{2,10},{3,11},{4,12},{5,13},{6,14},{7,15},{8,0},{9,1},... | collective-permute-start | bytes 516104 | tf_op jit(solution)/shard_map/ppermute | solution.py:1472
  258.3 27.2 %collective-permute-start.35 = (bf16[2,304,768]{2,1,0:T(8,128)(2,1)}, bf16[2,304,768]{2,1,0:T(8,128)(2,1)S(1)}, u32[]{:S(2)}, u32[]{:S(2)}) collective-permute-start(bf16[2,304,768]{2,1,0:T(8,128)(2,1)} %shard_map.190.refs_9_), channel_id=1, source_target_pairs={{0,4},{1,5},{2,6},{3,7},{4,0},{5,1},{6,2},{7,3},{8,12},{9,13},{10,... | collective-permute-start | bytes 2801672 | tf_op jit(solution)/shard_map/ppermute | solution.py:1673
  265.8 24.7 %collective-permute-start.27 = (bf16[96,4224]{1,0:T(8,128)(2,1)}, bf16[96,4224]{1,0:T(8,128)(2,1)}, u32[]{:S(2)}, u32[]{:S(2)}) collective-permute-start(bf16[96,4224]{1,0:T(8,128)(2,1)} %get-tuple-element.89), channel_id=1, source_target_pairs={{0,1},{1,0},{2,3},{3,2},{4,5},{5,4},{6,7},{7,6},{8,9},{9,8},{10,11... | collective-permute-start | bytes 2433032 | tf_op jit(solution)/shard_map/ppermute | solution.py:1673
  267.2 42.1 %collective-permute-start.28 = (bf16[96,4224]{1,0:T(8,128)(2,1)S(1)}, bf16[96,4224]{1,0:T(8,128)(2,1)}, u32[]{:S(2)}, u32[]{:S(2)}) collective-permute-start(bf16[96,4224]{1,0:T(8,128)(2,1)S(1)} %copy-done.19), channel_id=1, source_target_pairs={{0,2},{1,3},{2,0},{3,1},{4,6},{5,7},{6,4},{7,5},{8,10},{9,11},{10,... | collective-permute-start | bytes 2433032 | tf_op jit(solution)/shard_map/ppermute | solution.py:1673
  267.9 41.4 %collective-permute-start.29 = (bf16[96,4224]{1,0:T(8,128)(2,1)S(1)}, bf16[96,4224]{1,0:T(8,128)(2,1)}, u32[]{:S(2)}, u32[]{:S(2)}) collective-permute-start(bf16[96,4224]{1,0:T(8,128)(2,1)S(1)} %copy-done.18), channel_id=1, source_target_pairs={{0,3},{1,2},{2,1},{3,0},{4,7},{5,6},{6,5},{7,4},{8,11},{9,10},{10,... | collective-permute-start | bytes 2433032 | tf_op jit(solution)/shard_map/ppermute | solution.py:1673
  271.2 38.4 %all-to-all-start.4 = ((bf16[16,16,768]{2,1,0:T(8,128)(2,1)}), bf16[16,16,768]{2,1,0:T(8,128)(2,1)S(1)}, u32[]{:S(2)}, u32[]{:S(2)}) async-start(bf16[16,16,768]{2,1,0:T(8,128)(2,1)} %bitcast.22), calls=%async_computation.5 | async-start | bytes 786432 | tf_op jit(solution)/shard_map/all_to_all | solution.py:1758
  289.6 20.0 %collective-permute-start.36 = (bf16[304,768]{1,0:T(8,128)(2,1)}, bf16[304,768]{1,0:T(8,128)(2,1)S(1)}, u32[]{:S(2)}, u32[]{:S(2)}) collective-permute-start(bf16[304,768]{1,0:T(8,128)(2,1)} %get-tuple-element.97), channel_id=1, source_target_pairs={{0,8},{1,9},{2,10},{3,11},{4,12},{5,13},{6,14},{7,15},{8,0},{9,1},... | collective-permute-start | bytes 1400840 | tf_op jit(solution)/shard_map/ppermute | solution.py:1673
  315.1 24.7 %collective-permute-start.37 = (bf16[2,336,768]{2,1,0:T(8,128)(2,1)}, bf16[2,336,768]{2,1,0:T(8,128)(2,1)S(1)}, u32[]{:S(2)}, u32[]{:S(2)}) collective-permute-start(bf16[2,336,768]{2,1,0:T(8,128)(2,1)} %get-tuple-element.99), channel_id=1, source_target_pairs={{0,4},{1,5},{2,6},{3,7},{4,0},{5,1},{6,2},{7,3},{8,12},{9,13},{10,... | collective-permute-start | bytes 3096584 | tf_op jit(solution)/shard_map/ppermute | solution.py:1673
  316.5 10.5 %collective-permute-start.38 = (bf16[208,768]{1,0:T(8,128)(2,1)S(1)}, bf16[208,768]{1,0:T(8,128)(2,1)S(1)}, u32[]{:S(2)}, u32[]{:S(2)}) collective-permute-start(bf16[208,768]{1,0:T(8,128)(2,1)S(1)} %get-tuple-element.118), channel_id=1, source_target_pairs={{0,1},{1,0},{2,3},{3,2},{4,5},{5,4},{6,7},{7,6},{8,9},{9,8},{10,11... | collective-permute-start | bytes 958472 | tf_op jit(solution)/shard_map/ppermute | solution.py:1756
  317.3 15.4 %collective-permute-start.39 = (bf16[208,768]{1,0:T(8,128)(2,1)S(1)}, bf16[208,768]{1,0:T(8,128)(2,1)S(1)}, u32[]{:S(2)}, u32[]{:S(2)}) collective-permute-start(bf16[208,768]{1,0:T(8,128)(2,1)S(1)} %get-tuple-element.117), channel_id=1, source_target_pairs={{0,2},{1,3},{2,0},{3,1},{4,6},{5,7},{6,4},{7,5},{8,10},{9,11},{10,... | collective-permute-start | bytes 958472 | tf_op jit(solution)/shard_map/ppermute | solution.py:1756
  318.5 14.2 %collective-permute-start.40 = (bf16[208,768]{1,0:T(8,128)(2,1)S(1)}, bf16[208,768]{1,0:T(8,128)(2,1)S(1)}, u32[]{:S(2)}, u32[]{:S(2)}) collective-permute-start(bf16[208,768]{1,0:T(8,128)(2,1)S(1)} %get-tuple-element.116), channel_id=1, source_target_pairs={{0,3},{1,2},{2,1},{3,0},{4,7},{5,6},{6,5},{7,4},{8,11},{9,10},{10,... | collective-permute-start | bytes 958472 | tf_op jit(solution)/shard_map/ppermute | solution.py:1756
  320.0 30.1 %collective-permute-start.20 = (bf16[3,128,768]{2,1,0:T(8,128)(2,1)S(1)}, bf16[3,128,768]{2,1,0:T(8,128)(2,1)S(1)}, u32[]{:S(2)}, u32[]{:S(2)}) collective-permute-start(bf16[3,128,768]{2,1,0:T(8,128)(2,1)S(1)} %bitcast.70), channel_id=1, source_target_pairs={{0,16},{1,17},{2,18},{3,19},{4,20},{5,21},{6,22},{7,23},{8,24},{9,... | collective-permute-start | bytes 1769480 | tf_op jit(solution)/shard_map/ppermute | solution.py:1472
  344.5 24.0 %collective-permute-start.41 = (bf16[336,768]{1,0:T(8,128)(2,1)}, bf16[336,768]{1,0:T(8,128)(2,1)S(1)}, u32[]{:S(2)}, u32[]{:S(2)}) collective-permute-start(bf16[336,768]{1,0:T(8,128)(2,1)} %get-tuple-element.103), channel_id=1, source_target_pairs={{0,16},{16,0},{1,17},{17,1},{2,18},{18,2},{3,19},{19,3},{4,20},{20... | collective-permute-start | bytes 1548296 | tf_op jit(solution)/shard_map/ppermute | solution.py:1476
  344.5 25.5 %collective-permute-start.42 = (bf16[336,768]{1,0:T(8,128)(2,1)}, bf16[336,768]{1,0:T(8,128)(2,1)S(1)}, u32[]{:S(2)}, u32[]{:S(2)}) collective-permute-start(bf16[336,768]{1,0:T(8,128)(2,1)} %get-tuple-element.104), channel_id=1, source_target_pairs={{0,8},{1,9},{2,10},{3,11},{4,12},{5,13},{6,14},{7,15},{8,0},{9,1},... | collective-permute-start | bytes 1548296 | tf_op jit(solution)/shard_map/ppermute | solution.py:1472
  348.8 19.7 %collective-permute-start.43 = (bf16[240,768]{1,0:T(8,128)(2,1)}, bf16[240,768]{1,0:T(8,128)(2,1)S(1)}, u32[]{:S(2)}, u32[]{:S(2)}) collective-permute-start(bf16[240,768]{1,0:T(8,128)(2,1)} %get-tuple-element.105), channel_id=1, source_target_pairs={{16,8},{17,9},{18,10},{19,11},{20,12},{21,13},{22,14},{23,15},{24,... | collective-permute-start | bytes 1105928 | tf_op jit(solution)/shard_map/ppermute | solution.py:1472
  (64 other events, 308.3 us)
Sparse Core Ops, SparseCore 0:
  169.9 86.3 reduce-scatter.1

commit v9 on v8

--- a/solution.py
+++ b/solution.py
@@ -1224,10 +1224,10 @@
         )
         for pairs in halves
     ]
-    block = max(rows_of)
+    block, short = max(rows_of), rows_of[1]
 
     def kernel(section_ref, group_ref, *refs):
-        sent_refs, (keep_ref, leave_ref, buffer, sems) = refs[: len(sent)], refs[len(sent) :]
+        sent_refs, (keep_ref, leave_ref, short_ref, buffer, sems) = refs[: len(sent)], refs[len(sent) :]
 
         def columns(at):
             return jnp.concatenate([ref[:, at] for ref in sent_refs], axis=0)
@@ -1255,26 +1255,35 @@
         def _():
             fill(halves[1])
 
+        def moves(j):
+            mine = ((group_ref[0] ^ j) & 1) == 0
+            other = jnp.logical_not(mine)
+            sem = sems.at[j]
+            return (
+                (mine, pltpu.make_async_copy(buffer.at[j], keep_ref.at[j >> 1], sem)),
+                (
+                    other & (section_ref[0] == 0),
+                    pltpu.make_async_copy(buffer.at[j], leave_ref.at[j >> 1], sem),
+                ),
+                (
+                    other & (section_ref[0] != 0),
+                    pltpu.make_async_copy(buffer.at[j, 0:short], short_ref.at[j >> 1], sem),
+                ),
+            )
+
         for j in range(4):
-            mine = ((group_ref[0] ^ j) & 1) == 0
-
-            @pl.when(mine)
-            def _(j=j):
-                pltpu.make_async_copy(buffer.at[j], keep_ref.at[j >> 1], sems.at[j]).start()
-
-            @pl.when(jnp.logical_not(mine))
-            def _(j=j):
-                pltpu.make_async_copy(buffer.at[j], leave_ref.at[j >> 1], sems.at[j]).start()
-
+            for when, copy in moves(j):
+                pl.when(when)(copy.start)
         for j in range(4):
-            pltpu.make_async_copy(buffer.at[j], keep_ref.at[j >> 1], sems.at[j]).wait()
+            for when, copy in moves(j):
+                pl.when(when)(copy.wait)
 
     return call(
         kernel,
         (section, group, *sent),
         [SCALARS] * 2 + [WHOLE] * len(sent),
-        [shaped(2, block, width)] * 2,
-        [ANY] * 2,
+        [shaped(2, block, width), shaped(2, block, width), shaped(2, short, width)],
+        [ANY] * 3,
         [pltpu.VMEM((4, block, width), bf16), pltpu.SemaphoreType.DMA((4,))],
         deps=deps,
         micros=6,
@@ -1331,15 +1340,18 @@
     )
 
 
-def half_sums_and_cross(flags, kept, near, other, other_far, short, deps=()):
+def half_sums_and_cross(flags, kept, near, near_short, other, other_far, deps=()):
     shape = kept.shape[1:]
-    held = other.shape[0]
+    held, short = other.shape[0], near_short.shape[1]
 
     def kernel(
-        flags_ref, kept_ref, near_ref, other_ref, more_ref, far_ref, short_ref, mine_ref, cross_ref
+        flags_ref, kept_ref, near_ref, low_ref, other_ref, more_ref,
+        far_ref, short_ref, mine_ref, cross_ref,
     ):
         for k in range(2):
-            total = (kept_ref[k].astype(f32) + near_ref[k].astype(f32)).astype(bf16)
+            total = kept_ref[k].astype(f32) + near_ref[k].astype(f32)
+            low = total[0:short] + low_ref[k].astype(f32)
+            total = jnp.concatenate([low, total[short:]], axis=0).astype(bf16)
 
             @pl.when(flags_ref[1] == k)
             def _():
@@ -1358,8 +1370,8 @@
 
     return call(
         kernel,
-        (flags, kept, near, other, other_far),
-        [SCALARS] + [WHOLE] * 4,
+        (flags, kept, near, near_short, other, other_far),
+        [SCALARS] + [WHOLE] * 5,
         [shaped(*shape), shaped(short, shape[1]), shaped(*shape), shaped(*shape)],
         [WHOLE] * 4,
         deps=deps,
@@ -1775,7 +1787,7 @@
         local_far, local_mine = half_sums(half_flags, in_planes, local_near)
         across = group_pairs(2)
         local_far = both_send(local_far, across)
-        kept, leaving = plane_gradients(
+        kept, leaving, leaving_short = plane_gradients(
             flag,
             group_flag,
             arrived_parts,
@@ -1783,10 +1795,10 @@
             width,
             [table_parts, local_far],
         )
-        near = both_send(leaving, group_pairs(1))
-        short = expand.shape[1] // GROUPS + shard
+        near = section_send(leaving, 0, 0, group_pairs(1))
+        near_short = section_send(leaving_short, 1, 1, group_pairs(1))
         far, far_short, mine, crossed = half_sums_and_cross(
-            half_flags, kept, near, local_mine, local_far, short, patch_parts[1:]
+            half_flags, kept, near, near_short, local_mine, local_far, patch_parts[1:]
         )
         crossed = section_swap(crossed)
         fars = [

time: 391 us -> 391 us (level)
    ppermute x6 -> x5, waiting for transfers between devices: 34.9 us -> 27.8 us  [both_send(): return lax.ppermute(x, ('section',) + SEQ, joint)]
    ppermute x25 -> x27, waiting for transfers between devices: 43.8 us -> 47.6 us  [section_send(): return lax.ppermute(x, ('section',) + SEQ, joint)]
    ppermute x25 -> x27, starting transfers between devices: 52.4 us -> 55.5 us  [section_send(): return lax.ppermute(x, ('section',) + SEQ, joint)]
  transfers between devices with their start and end apart: 49 -> 50, of which waited for: 28 -> 28; matrix products, arithmetic and copies ran while one was open for 3% -> 3% of each run, Pallas kernels for 15% -> 15%
where the time goes in v9:
time: 391 us; the launch traced here: 383 us
  waiting for transfers between devices  115 us (29%)
  Pallas kernels  115 us (29%)
  starting transfers between devices  97.6 us (25%)
  blocking collectives  15.3 us (4%)
  local copies, waits for them, and re-layouts  15.2 us (4%)
  between operations  15.2 us (4%)
  other arithmetic  10.1 us (3%)
    pallas_call x13, Pallas kernels, call(): pl.pallas_call(body, in_specs=list(specs) + [ANY] * len(deps), out_specs=...  60.1 us
    ppermute x27, starting transfers between devices, section_send(): return lax.ppermute(x, ('section',) + SEQ, joint)  55.5 us
    ppermute x27, waiting for transfers between devices, section_send(): return lax.ppermute(x, ('section',) + SEQ, joint)  47.6 us
    pallas_call x1, Pallas kernels, local_block(): pl.pallas_call(partial(local_kernel, patch_rows), in_specs=[SCALARS] + [W...  31.7 us
    ppermute x5, waiting for transfers between devices, both_send(): return lax.ppermute(x, ('section',) + SEQ, joint)  27.8 us
    all_to_all x1, blocking collectives, from_tasks(): lax.all_to_all(results.reshape(count, patch_rows, columns), SEQ, 0, 0)  15.3 us
    all_to_all x2, waiting for transfers between devices, to_tasks(): landed = lax.all_to_all(slots, SEQ, 0, 0)  13.4 us
    unnamed x94, local copies, waits for them, and re-layouts  12.1 us
  transfers between devices with their start and end apart: 50, of which 28 were waited for; matrix products, arithmetic and copies ran while one was open for 3% of the time, Pallas kernels for 15%

profile of v9, /device:TPU:0, one launch (start us, length us, event | category | flops | bytes accessed | tf_op | source)
XLA Modules:
  0.0 383.3 jit_solution(6061041028853978409)
XLA Ops:
  20.5 3.9 %collective-permute-start.3 = (s32[3,256]{1,0:T(4,128)}, s32[3,256]{1,0:T(4,128)S(1)}, u32[]{:S(2)}, u32[]{:S(2)}) collective-permute-start(s32[3,256]{1,0:T(4,128)} %ids_ref.3), channel_id=1, source_target_pairs={{0,12},{1,13},{2,14},{3,15},{4,8},{5,9},{6,10},{7,11},{8,4},{9,5},... | collective-permute-start | bytes 9224 | tf_op jit(solution)/shard_map/ppermute | solution.py:1550
  27.9 4.0 %shard_map.178 = (bf16[384,768]{1,0:T(8,128)(2,1)}, bf16[768,768]{1,0:T(8,128)(2,1)}, f32[384,768]{1,0:T(8,128)}, bf16[384,768]{1,0:T(8,128)(2,1)}, bf16[256,384]{1,0:T(8,128)(2,1)}) custom-call(s32[3]{0:T(128)} %pad_add_fusion.1.refs_0_, bf16[256,768]{1,0:T(8,128)(2,1)} %bitcast.70, bf16[256,768]{1,0:T(8,128)(2,1)} %copy-done.26, s32[3,256]{1,0:T(4,128)} %ids_ref.3, ...), custom_call_target="tpu_custom_call" | custom-call | flops 4400000000 | bytes 1 | tf_op jit(solution)/shard_map/pallas_call | solution.py:747
  37.4 5.7 %collective-permute-start.10 = (bf16[96,768]{1,0:T(8,128)(2,1)S(1)}, bf16[96,768]{1,0:T(8,128)(2,1)S(1)}, u32[]{:S(2)}, u32[]{:S(2)}) collective-permute-start(bf16[96,768]{1,0:T(8,128)(2,1)S(1)} %get-tuple-element.121), channel_id=1, source_target_pairs={{0,12},{1,13},{2,14},{3,15},{4,8},{5,9},{6,10},{7,11},{8,4},{9,5},... | collective-permute-start | bytes 442376 | tf_op jit(solution)/shard_map/ppermute | solution.py:1484
  50.2 4.4 %collective-permute-done.9.refs_5_ = bf16[96,768]{1,0:T(8,128)(2,1)S(1)} collective-permute-done((bf16[96,768]{1,0:T(8,128)(2,1)S(1)}, bf16[96,768]{1,0:T(8,128)(2,1)S(1)}, u32[]{:S(2)}, u32[]{:S(2)}) %collective-permute-start.9) | collective-permute-done | bytes 147488 | tf_op jit(solution)/shard_map/ppermute | solution.py:1484
  55.2 4.6 %shard_map.179 = (f32[96,768]{1,0:T(8,128)}, bf16[96,768]{1,0:T(8,128)(2,1)}, bf16[4,96,192]{2,1,0:T(8,128)(2,1)}, bf16[16,32,384]{2,1,0:T(8,128)(2,1)}, bf16[2,32,384]{2,1,0:T(8,128)(2,1)}) custom-call(f32[96,768]{1,0:T(8,128)} %slice.43.refs_0_, f32[2,768]{1,0:T(2,128)} %bitcast.48, f32[2,768]{1,0:T(2,128)} %bitcast.45, bf16[768,2304]{1,0:T(8,128)(2,1)} %bitcast.61, ...), custom_call_target="tpu_custom_call" | custom-call | flops 5500000256 | bytes 1 | tf_op jit(solution)/shard_map/pallas_call | solution.py:747
  64.0 4.7 %all-to-all-start = ((bf16[16,32,384]{2,1,0:T(8,128)(2,1)}), bf16[16,32,384]{2,1,0:T(8,128)(2,1)S(1)}, u32[]{:S(2)}, u32[]{:S(2)}) async-start(bf16[16,32,384]{2,1,0:T(8,128)(2,1)} %pad_select_fusion), calls=%async_computation | async-start | bytes 786432 | tf_op jit(solution)/shard_map/all_to_all | solution.py:1578
  70.8 10.1 %all-to-all-done = bf16[16,32,384]{2,1,0:T(8,128)(2,1)S(1)} async-done(((bf16[16,32,384]{2,1,0:T(8,128)(2,1)}), bf16[16,32,384]{2,1,0:T(8,128)(2,1)S(1)}, u32[]{:S(2)}, u32[]{:S(2)}) %all-to-all-start) | async-done | bytes 393248 | tf_op jit(solution)/shard_map/all_to_all | solution.py:1578
  81.7 4.1 %shard_map.180 = bf16[512,128]{1,0:T(8,128)(2,1)} custom-call(s32[13]{0:T(128)} %pad_add_fusion.2.numbers_ref.refs_0_, bf16[512,384]{1,0:T(8,128)(2,1)} %bitcast.40), custom_call_target="tpu_custom_call" | custom-call | flops 16499999744 | bytes 1 | tf_op jit(solution)/shard_map/pallas_call | solution.py:716
  90.8 6.4 %all-to-all-done.1.refs_6_ = bf16[16,32,128]{2,1,0:T(8,128)(2,1)S(1)} async-done(((bf16[16,32,128]{2,1,0:T(8,128)(2,1)}), bf16[16,32,128]{2,1,0:T(8,128)(2,1)S(1)}, u32[]{:S(2)}, u32[]{:S(2)}) %all-to-all-start.1) | async-done | bytes 131104 | tf_op jit(solution)/shard_map/all_to_all | solution.py:1583
  100.9 7.3 %shard_map.181 = (bf16[96,768]{1,0:T(8,128)(2,1)}, f32[96,768]{1,0:T(8,128)}, bf16[96,768]{1,0:T(8,128)(2,1)}, bf16[96,3072]{1,0:T(8,128)(2,1)}, bf16[96,3072]{1...) custom-call(f32[96,768]{1,0:T(8,128)} %get-tuple-element.64.refs_0_,, ...), custom_call_target="tpu_custom_call" | custom-call | flops 8800000000 | bytes 1 | tf_op jit(solution)/shard_map/pallas_call | solution.py:747
  115.6 31.7 %shard_map.182 = (bf16[384,768]{1,0:T(8,128)(2,1)}, bf16[48,768]{1,0:T(8,128)(2,1)}, bf16[16,768]{1,0:T(8,128)(2,1)}, bf16[400,7680]{1,0:T(8,128)(2,1)}, bf16[400,7680]{1,0:T(8,128)(2,1)}) custom-call(s32[15]{0:T(128)} %pad_add_fusion.numbers_ref.refs_0_, s32[3,256]{1,0:T(4,128)} %ids_ref.3, bf16[256,768]{1,0:T(8,128)(2,1)} %bitcast.71, ...), custom_call_target="tpu_custom_call" | custom-call | flops 38499999744 | bytes 1 | tf_op jit(solution)/shard_map/pallas_call | solution.py:474
  150.0 4.9 %collective-permute-done.22.rest_1_.refs_2_ = bf16[16,768]{1,0:T(8,128)(2,1)S(1)} collective-permute-done((bf16[16,768]{1,0:T(8,128)(2,1)}, bf16[16,768]{1,0:T(8,128)(2,1)S(1)}, u32[]{:S(2)}, u32[]{:S(2)}) %collective-permute-start.22) | collective-permute-done | bytes 24608 | tf_op jit(solution)/shard_map/ppermute | solution.py:1484
  158.3 11.6 %shard_map.184.refs_9_ = bf16[16,304,768]{2,1,0:T(8,128)(2,1)} custom-call(s32[15]{0:T(128)} %pad_add_fusion.numbers_ref.refs_0_, s32[3,256]{1,0:T(4,128)} %ids_ref.3, bf16[400,7680]{1,0:T(8,128)(2,1)} %get-tuple-element.77.keep_ref, bf16[400,7680]{1,0:T(8,128)(2,1)} %collective-permute-done.23.new_ref, bf16[48,768]{1,0:T(8,128)(2,1)} %copy-done.38, ...), custom_call_target="tpu_custom_call" | custom-call | flops 13200000000 | bytes 1 | tf_op jit(solution)/shard_map/pallas_call | solution.py:598
  169.9 8.7 %shard_map.185 = (bf16[96,3072]{1,0:T(8,128)(2,1)}, f32[96,768]{1,0:T(8,128)}, bf16[96,768]{1,0:T(8,128)(2,1)}, f32[2,768]{1,0:T(2,128)}, bf16[96,768]{1,0:T(8,1...) custom-call(bf16[48,768]{1,0:T(8,128)(2,1)} %get-tuple-element.73.refs_0_, ...), custom_call_target="tpu_custom_call" | custom-call | flops 11000000512 | bytes 1 | tf_op jit(solution)/shard_map/pallas_call | solution.py:747
  184.1 5.7 %all-to-all-start.2 = ((bf16[16,32,128]{2,1,0:T(8,128)(2,1)}), bf16[16,32,128]{2,1,0:T(8,128)(2,1)S(1)}, u32[]{:S(2)}, u32[]{:S(2)}) async-start(bf16[16,32,128]{2,1,0:T(8,128)(2,1)} %pad_select_fusion.1), calls=%async_computation.2 | async-start | bytes 262144 | tf_op jit(solution)/shard_map/all_to_all | solution.py:1578
  198.3 5.8 %shard_map.186 = bf16[512,384]{1,0:T(8,128)(2,1)} custom-call(s32[13]{0:T(128)} %pad_add_fusion.2.numbers_ref.refs_0_, bf16[512,384]{1,0:T(8,128)(2,1)} %bitcast.41, bf16[512,128]{1,0:T(8,128)(2,1)} %bitcast.43), custom_call_target="tpu_custom_call" | custom-call | flops 32999999488 | bytes 1 | tf_op jit(solution)/shard_map/pallas_call | solution.py:729
  204.1 15.3 %all_to_all.25.refs_5_ = bf16[16,32,384]{2,1,0:T(8,128)(2,1)S(1)} all-to-all(bf16[16,32,384]{2,1,0:T(8,128)(2,1)} %bitcast.42), channel_id=1, replica_groups=mesh['section'=2,'group'=4,'member'=4] {'group','member'}, dimensions={0} | all-to-all | bytes 786432 | tf_op jit(solution)/shard_map/all_to_all | solution.py:1583
  223.2 5.2 %shard_map.187 = (bf16[96,2304]{1,0:T(8,128)(2,1)}, bf16[112,768]{1,0:T(8,128)(2,1)}, f32[4,768]{1,0:T(4,128)}) custom-call(f32[96,768]{1,0:T(8,128)} %get-tuple-element.64.refs_0_, f32[96,768]{1,0:T(8,128)} %get-tuple-element.80.refs_1_, f32[2,768]{1,0:T(2,128)} %get-tuple-element.81.refs_2_, f32[2,768]{1,0:T(2,128)} %bitcast.51, ...), custom_call_target="tpu_custom_call" | custom-call | flops 6600000000 | bytes 1 | tf_op jit(solution)/shard_map/pallas_call | solution.py:747
  230.1 3.8 shard_map.189
  240.0 4.0 %collective-permute-start.32 = (bf16[112,768]{1,0:T(8,128)(2,1)}, bf16[112,768]{1,0:T(8,128)(2,1)S(1)}, u32[]{:S(2)}, u32[]{:S(2)}) collective-permute-start(bf16[112,768]{1,0:T(8,128)(2,1)} %get-tuple-element.96.refs_5_), channel_id=1, source_target_pairs={{0,12},{1,13},{2,14},{3,15},{4,8},{5,9},{6,10},{7,11},{8,4},{9,5},... | collective-permute-start | bytes 516104 | tf_op jit(solution)/shard_map/ppermute | solution.py:1484
  260.0 4.6 %shard_map.191 = (bf16[4,208,768]{2,1,0:T(8,128)(2,1)}, bf16[256,768]{1,0:T(8,128)(2,1)}) custom-call(s32[1]{0:T(128)} %bitcast.refs_0_, bf16[256,384]{1,0:T(8,128)(2,1)} %get-tuple-element.93.refs_1_, bf16[384,768]{1,0:T(8,128)(2,1)} %get-tuple-element.94.refs_2_, bf16[768,768]{1,0:T(8,128)(2,1)} %get-tuple-element.95.refs_3_, bf16[448,768]{1,0:T(8,128)(2,1)} %copy-done.21, ...), custom_call_target="tpu_custom_call" | custom-call | flops 6600000000 | bytes 1 | tf_op jit(solution)/shard_map/pallas_call | solution.py:747
  271.3 4.7 %all-to-all-start.4 = ((bf16[16,16,768]{2,1,0:T(8,128)(2,1)}), bf16[16,16,768]{2,1,0:T(8,128)(2,1)S(1)}, u32[]{:S(2)}, u32[]{:S(2)}) async-start(bf16[16,16,768]{2,1,0:T(8,128)(2,1)} %bitcast.22), calls=%async_computation.5 | async-start | bytes 786432 | tf_op jit(solution)/shard_map/all_to_all | solution.py:1770
  276.5 9.0 %collective-permute-done.35.refs_2_ = bf16[2,304,768]{2,1,0:T(8,128)(2,1)S(1)} collective-permute-done((bf16[2,304,768]{2,1,0:T(8,128)(2,1)}, bf16[2,304,768]{2,1,0:T(8,128)(2,1)S(1)}, u32[]{:S(2)}, u32[]{:S(2)}) %collective-permute-start.35) | collective-permute-done | bytes 933920 | tf_op jit(solution)/shard_map/ppermute | solution.py:1685
  290.6 18.8 %collective-permute-done.28.refs_4_ = bf16[96,4224]{1,0:T(8,128)(2,1)} collective-permute-done((bf16[96,4224]{1,0:T(8,128)(2,1)S(1)}, bf16[96,4224]{1,0:T(8,128)(2,1)}, u32[]{:S(2)}, u32[]{:S(2)}) %collective-permute-start.28) | collective-permute-done | bytes 811040 | tf_op jit(solution)/shard_map/ppermute | solution.py:1685
  310.6 4.6 %shard_map.193 = (bf16[2,336,768]{2,1,0:T(8,128)(2,1)}, bf16[2,336,768]{2,1,0:T(8,128)(2,1)}, bf16[2,240,768]{2,1,0:T(8,128)(2,1)}) custom-call(s32[1]{0:T(128)} %bitcast.refs_0_, s32[1]{0:T(128)} %bitcast.18.refs_1_, bf16[96,4224]{1,0:T(8,128)(2,1)} %get-tuple-element.89.refs_2_, bf16[96,4224]{1,0:T(8,128)(2,1)} %collective-permute-done.27.refs_3_, ...), custom_call_target="tpu_custom_call" | custom-call | flops 6600000000 | bytes 1 | tf_op jit(solution)/shard_map/pallas_call | solution.py:747
  322.7 7.0 %collective-permute-done.39.refs_6_.refs_9_ = bf16[208,768]{1,0:T(8,128)(2,1)S(1)} collective-permute-done((bf16[208,768]{1,0:T(8,128)(2,1)S(1)}, bf16[208,768]{1,0:T(8,128)(2,1)S(1)}, u32[]{:S(2)}, u32[]{:S(2)}) %collective-permute-start.39) | collective-permute-done | bytes 319520 | tf_op jit(solution)/shard_map/ppermute | solution.py:1768
  331.0 4.3 %collective-permute-done.40.refs_7_.refs_10_ = bf16[208,768]{1,0:T(8,128)(2,1)S(1)} collective-permute-done((bf16[208,768]{1,0:T(8,128)(2,1)S(1)}, bf16[208,768]{1,0:T(8,128)(2,1)S(1)}, u32[]{:S(2)}, u32[]{:S(2)}) %collective-permute-start.40) | collective-permute-done | bytes 319520 | tf_op jit(solution)/shard_map/ppermute | solution.py:1768
  335.4 3.9 %collective-permute-done.37.refs_2_ = bf16[2,336,768]{2,1,0:T(8,128)(2,1)S(1)} collective-permute-done((bf16[2,336,768]{2,1,0:T(8,128)(2,1)}, bf16[2,336,768]{2,1,0:T(8,128)(2,1)S(1)}, u32[]{:S(2)}, u32[]{:S(2)}) %collective-permute-start.37) | collective-permute-done | bytes 1032224 | tf_op jit(solution)/shard_map/ppermute | solution.py:1484
  340.2 4.1 %shard_map.194 = (bf16[336,768]{1,0:T(8,128)(2,1)}, bf16[240,768]{1,0:T(8,128)(2,1)}, bf16[336,768]{1,0:T(8,128)(2,1)}, bf16[336,768]{1,0:T(8,128)(2,1)}) custom-call(s32[3]{0:T(128)} %pad_add_fusion.3.refs_0_, bf16[2,336,768]{2,1,0:T(8,128)(2,1)} %get-tuple-element.99.refs_1_, bf16[2,336,768]{2,1,0:T(8,128)(2,1)} %copy-done.16, ...), custom_call_target="tpu_custom_call" | custom-call | flops 2200000000 | bytes 1 | tf_op jit(solution)/shard_map/pallas_call | solution.py:747
  344.3 4.3 %collective-permute-start.43 = (bf16[336,768]{1,0:T(8,128)(2,1)}, bf16[336,768]{1,0:T(8,128)(2,1)S(1)}, u32[]{:S(2)}, u32[]{:S(2)}) collective-permute-start(bf16[336,768]{1,0:T(8,128)(2,1)} %get-tuple-element.106), channel_id=1, source_target_pairs={{0,8},{1,9},{2,10},{3,11},{4,12},{5,13},{6,14},{7,15},{8,0},{9,1},... | collective-permute-start | bytes 1548296 | tf_op jit(solution)/shard_map/ppermute | solution.py:1484
  353.7 14.6 %collective-permute-done.44.refs_6_ = bf16[240,768]{1,0:T(8,128)(2,1)S(1)} collective-permute-done((bf16[240,768]{1,0:T(8,128)(2,1)}, bf16[240,768]{1,0:T(8,128)(2,1)S(1)}, u32[]{:S(2)}, u32[]{:S(2)}) %collective-permute-start.44) | collective-permute-done | bytes 368672 | tf_op jit(solution)/shard_map/ppermute | solution.py:1484
  370.6 4.1 %shard_map.195 = (f32[192,768]{1,0:T(8,128)}, f32[48,3072]{1,0:T(8,128)}, f32[48,2304]{1,0:T(8,128)}, f32[48,768]{1,0:T(8,128)}, f32[16,768]{1,0:T(8,128)}, /*index=5*/f32[16,768]{1,0:T(8,128)}, f32[192,768]{1,0:T(8,128)}) custom-call(s32[1]{0:T(128)} %bitcast.refs_0_, bf16[336,768]{1,0:T(8,128)(2,1)} %get-tuple-element.104.refs_1_, ...), custom_call_target="tpu_custom_call" | custom-call | flops 4400000000 | bytes 1 | tf_op jit(solution)/shard_map/pallas_call | solution.py:747
  (201 shorter events, 132.3 us)
Async XLA Ops:
  7.2 19.1 %collective-permute-start = (bf16[256,768]{1,0:T(8,128)(2,1)}, bf16[256,768]{1,0:T(8,128)(2,1)S(1)}, u32[]{:S(2)}, u32[]{:S(2)}) collective-permute-start(bf16[256,768]{1,0:T(8,128)(2,1)} %bitcast.69), channel_id=1, source_target_pairs={{0,16},{16,0},{1,17},{17,1},{2,18},{18,2},{3,19},{19,3},{4,20},{20... | collective-permute-start | bytes 1179656 | tf_op jit(solution)/shard_map/ppermute | solution.py:1488
  7.7 18.5 %collective-permute-start.4 = (bf16[192,768]{1,0:T(8,128)(2,1)}, bf16[192,768]{1,0:T(8,128)(2,1)S(1)}, u32[]{:S(2)}, u32[]{:S(2)}) collective-permute-start(bf16[192,768]{1,0:T(8,128)(2,1)} %refs_7_.1), channel_id=1, source_target_pairs={{0,1},{1,0},{2,3},{3,2},{4,5},{5,4},{6,7},{7,6},{8,9},{9,8},{10,11... | collective-permute-start | bytes 884744 | tf_op jit(solution)/shard_map/ppermute | solution.py:1545
  10.3 15.9 %collective-permute-start.5 = (bf16[192,768]{1,0:T(8,128)(2,1)}, bf16[192,768]{1,0:T(8,128)(2,1)S(1)}, u32[]{:S(2)}, u32[]{:S(2)}) collective-permute-start(bf16[192,768]{1,0:T(8,128)(2,1)} %refs_7_.1), channel_id=1, source_target_pairs={{0,2},{1,3},{2,0},{3,1},{4,6},{5,7},{6,4},{7,5},{8,10},{9,11},{10,... | collective-permute-start | bytes 884744 | tf_op jit(solution)/shard_map/ppermute | solution.py:1545
  11.8 14.4 %collective-permute-start.6 = (bf16[192,768]{1,0:T(8,128)(2,1)}, bf16[192,768]{1,0:T(8,128)(2,1)S(1)}, u32[]{:S(2)}, u32[]{:S(2)}) collective-permute-start(bf16[192,768]{1,0:T(8,128)(2,1)} %refs_7_.1), channel_id=1, source_target_pairs={{0,3},{1,2},{2,1},{3,0},{4,7},{5,6},{6,5},{7,4},{8,11},{9,10},{10,... | collective-permute-start | bytes 884744 | tf_op jit(solution)/shard_map/ppermute | solution.py:1545
  33.1 81.9 %collective-permute-start.18 = (bf16[768,3072]{1,0:T(8,128)(2,1)}, bf16[768,3072]{1,0:T(8,128)(2,1)}, u32[]{:S(2)}, u32[]{:S(2)}) collective-permute-start(bf16[768,3072]{1,0:T(8,128)(2,1)} %bitcast.53), channel_id=1, source_target_pairs={{16,0},{17,1},{18,2},{19,3},{20,4},{21,5},{22,6},{23,7},{24,8},{25... | collective-permute-start | bytes 14155784 | tf_op jit(solution)/shard_map/ppermute | solution.py:1484
  34.4 80.6 %collective-permute-start.19 = (bf16[3072,768]{1,0:T(8,128)(2,1)}, bf16[3072,768]{1,0:T(8,128)(2,1)}, u32[]{:S(2)}, u32[]{:S(2)}) collective-permute-start(bf16[3072,768]{1,0:T(8,128)(2,1)} %bitcast.57), channel_id=1, source_target_pairs={{16,0},{17,1},{18,2},{19,3},{20,4},{21,5},{22,6},{23,7},{24,8},{25... | collective-permute-start | bytes 14155784 | tf_op jit(solution)/shard_map/ppermute | solution.py:1484
  37.4 10.9 %collective-permute-start.10 = (bf16[96,768]{1,0:T(8,128)(2,1)S(1)}, bf16[96,768]{1,0:T(8,128)(2,1)S(1)}, u32[]{:S(2)}, u32[]{:S(2)}) collective-permute-start(bf16[96,768]{1,0:T(8,128)(2,1)S(1)} %get-tuple-element.121), channel_id=1, source_target_pairs={{0,12},{1,13},{2,14},{3,15},{4,8},{5,9},{6,10},{7,11},{8,4},{9,5},... | collective-permute-start | bytes 442376 | tf_op jit(solution)/shard_map/ppermute | solution.py:1484
  64.0 16.8 %all-to-all-start = ((bf16[16,32,384]{2,1,0:T(8,128)(2,1)}), bf16[16,32,384]{2,1,0:T(8,128)(2,1)S(1)}, u32[]{:S(2)}, u32[]{:S(2)}) async-start(bf16[16,32,384]{2,1,0:T(8,128)(2,1)} %pad_select_fusion), calls=%async_computation | async-start | bytes 786432 | tf_op jit(solution)/shard_map/all_to_all | solution.py:1578
  68.8 46.2 %collective-permute-start.16 = (bf16[768,2304]{1,0:T(8,128)(2,1)}, bf16[768,2304]{1,0:T(8,128)(2,1)}, u32[]{:S(2)}, u32[]{:S(2)}) collective-permute-start(bf16[768,2304]{1,0:T(8,128)(2,1)} %bitcast.62), channel_id=1, source_target_pairs={{16,0},{17,1},{18,2},{19,3},{20,4},{21,5},{22,6},{23,7},{24,8},{25... | collective-permute-start | bytes 10616840 | tf_op jit(solution)/shard_map/ppermute | solution.py:1484
  85.8 11.4 %all-to-all-start.1 = ((bf16[16,32,128]{2,1,0:T(8,128)(2,1)}), bf16[16,32,128]{2,1,0:T(8,128)(2,1)S(1)}, u32[]{:S(2)}, u32[]{:S(2)}) async-start(bf16[16,32,128]{2,1,0:T(8,128)(2,1)} %bitcast.44), calls=%async_computation.1 | async-start | bytes 262144 | tf_op jit(solution)/shard_map/all_to_all | solution.py:1583
  89.4 167.0 %reduce-scatter.2.cloned.1.call-start = ((), (), s32[]{:S(2)}) async-start(), calls=%async_computation.6 | async-start | bytes 9338880 | tf_op jit(solution)/shard_map/reduce_scatter | solution.py:1749
  89.5 20.8 %collective-permute-start.17 = (bf16[768,768]{1,0:T(8,128)(2,1)S(1)}, bf16[768,768]{1,0:T(8,128)(2,1)S(1)}, u32[]{:S(2)}, u32[]{:S(2)}) collective-permute-start(bf16[768,768]{1,0:T(8,128)(2,1)S(1)} %bitcast.68), channel_id=1, source_target_pairs={{16,0},{17,1},{18,2},{19,3},{20,4},{21,5},{22,6},{23,7},{24,8},{25... | collective-permute-start | bytes 3538952 | tf_op jit(solution)/shard_map/ppermute | solution.py:1484
  147.3 10.4 %collective-permute-start.23 = (bf16[400,7680]{1,0:T(8,128)(2,1)}, bf16[400,7680]{1,0:T(8,128)(2,1)}, u32[]{:S(2)}, u32[]{:S(2)}) collective-permute-start(bf16[400,7680]{1,0:T(8,128)(2,1)} %get-tuple-element.78), channel_id=1, source_target_pairs={{0,16},{16,0},{1,17},{17,1},{2,18},{18,2},{3,19},{19,3},{4,20},{20... | collective-permute-start | bytes 18432008 | tf_op jit(solution)/shard_map/ppermute | solution.py:1488
  147.4 10.2 %collective-permute-start.21 = (bf16[48,768]{1,0:T(8,128)(2,1)}, bf16[48,768]{1,0:T(8,128)(2,1)S(1)}, u32[]{:S(2)}, u32[]{:S(2)}) collective-permute-start(bf16[48,768]{1,0:T(8,128)(2,1)} %get-tuple-element.73.refs_0_), channel_id=1, source_target_pairs={{16,0},{17,1},{18,2},{19,3},{20,4},{21,5},{22,6},{23,7},{24,8},{25... | collective-permute-start | bytes 221192 | tf_op jit(solution)/shard_map/ppermute | solution.py:1484
  184.1 13.6 %all-to-all-start.2 = ((bf16[16,32,128]{2,1,0:T(8,128)(2,1)}), bf16[16,32,128]{2,1,0:T(8,128)(2,1)S(1)}, u32[]{:S(2)}, u32[]{:S(2)}) async-start(bf16[16,32,128]{2,1,0:T(8,128)(2,1)} %pad_select_fusion.1), calls=%async_computation.2 | async-start | bytes 262144 | tf_op jit(solution)/shard_map/all_to_all | solution.py:1578
  192.8 35.6 %collective-permute-start.26 = (bf16[4,96,4224]{2,1,0:T(8,128)(2,1)}, bf16[4,96,4224]{2,1,0:T(8,128)(2,1)S(1)}, u32[]{:S(2)}, u32[]{:S(2)}) collective-permute-start(bf16[4,96,4224]{2,1,0:T(8,128)(2,1)} %shard_map.188), channel_id=1, source_target_pairs={{0,16},{1,17},{2,18},{3,19},{4,20},{5,21},{6,22},{7,23},{8,24},{9,... | collective-permute-start | bytes 9732104 | tf_op jit(solution)/shard_map/ppermute | solution.py:1484
  237.3 10.2 %collective-permute-start.31 = (bf16[112,768]{1,0:T(8,128)(2,1)}, bf16[112,768]{1,0:T(8,128)(2,1)S(1)}, u32[]{:S(2)}, u32[]{:S(2)}) collective-permute-start(bf16[112,768]{1,0:T(8,128)(2,1)} %get-tuple-element.96.refs_5_), channel_id=1, source_target_pairs={{0,8},{1,9},{2,10},{3,11},{4,12},{5,13},{6,14},{7,15},{8,0},{9,1},... | collective-permute-start | bytes 516104 | tf_op jit(solution)/shard_map/ppermute | solution.py:1484
  258.4 27.2 %collective-permute-start.35 = (bf16[2,304,768]{2,1,0:T(8,128)(2,1)}, bf16[2,304,768]{2,1,0:T(8,128)(2,1)S(1)}, u32[]{:S(2)}, u32[]{:S(2)}) collective-permute-start(bf16[2,304,768]{2,1,0:T(8,128)(2,1)} %shard_map.190.refs_9_), channel_id=1, source_target_pairs={{0,4},{1,5},{2,6},{3,7},{4,0},{5,1},{6,2},{7,3},{8,12},{9,13},{10,... | collective-permute-start | bytes 2801672 | tf_op jit(solution)/shard_map/ppermute | solution.py:1685
  265.9 24.7 %collective-permute-start.27 = (bf16[96,4224]{1,0:T(8,128)(2,1)}, bf16[96,4224]{1,0:T(8,128)(2,1)}, u32[]{:S(2)}, u32[]{:S(2)}) collective-permute-start(bf16[96,4224]{1,0:T(8,128)(2,1)} %get-tuple-element.90), channel_id=1, source_target_pairs={{0,1},{1,0},{2,3},{3,2},{4,5},{5,4},{6,7},{7,6},{8,9},{9,8},{10,11... | collective-permute-start | bytes 2433032 | tf_op jit(solution)/shard_map/ppermute | solution.py:1685
  267.2 42.1 %collective-permute-start.28 = (bf16[96,4224]{1,0:T(8,128)(2,1)S(1)}, bf16[96,4224]{1,0:T(8,128)(2,1)}, u32[]{:S(2)}, u32[]{:S(2)}) collective-permute-start(bf16[96,4224]{1,0:T(8,128)(2,1)S(1)} %copy-done.19), channel_id=1, source_target_pairs={{0,2},{1,3},{2,0},{3,1},{4,6},{5,7},{6,4},{7,5},{8,10},{9,11},{10,... | collective-permute-start | bytes 2433032 | tf_op jit(solution)/shard_map/ppermute | solution.py:1685
  267.9 41.4 %collective-permute-start.29 = (bf16[96,4224]{1,0:T(8,128)(2,1)S(1)}, bf16[96,4224]{1,0:T(8,128)(2,1)}, u32[]{:S(2)}, u32[]{:S(2)}) collective-permute-start(bf16[96,4224]{1,0:T(8,128)(2,1)S(1)} %copy-done.18), channel_id=1, source_target_pairs={{0,3},{1,2},{2,1},{3,0},{4,7},{5,6},{6,5},{7,4},{8,11},{9,10},{10,... | collective-permute-start | bytes 2433032 | tf_op jit(solution)/shard_map/ppermute | solution.py:1685
  271.3 38.4 %all-to-all-start.4 = ((bf16[16,16,768]{2,1,0:T(8,128)(2,1)}), bf16[16,16,768]{2,1,0:T(8,128)(2,1)S(1)}, u32[]{:S(2)}, u32[]{:S(2)}) async-start(bf16[16,16,768]{2,1,0:T(8,128)(2,1)} %bitcast.22), calls=%async_computation.5 | async-start | bytes 786432 | tf_op jit(solution)/shard_map/all_to_all | solution.py:1770
  289.6 20.0 %collective-permute-start.36 = (bf16[304,768]{1,0:T(8,128)(2,1)}, bf16[304,768]{1,0:T(8,128)(2,1)S(1)}, u32[]{:S(2)}, u32[]{:S(2)}) collective-permute-start(bf16[304,768]{1,0:T(8,128)(2,1)} %get-tuple-element.98), channel_id=1, source_target_pairs={{0,8},{1,9},{2,10},{3,11},{4,12},{5,13},{6,14},{7,15},{8,0},{9,1},... | collective-permute-start | bytes 1400840 | tf_op jit(solution)/shard_map/ppermute | solution.py:1685
  315.2 24.0 %collective-permute-start.37 = (bf16[2,336,768]{2,1,0:T(8,128)(2,1)}, bf16[2,336,768]{2,1,0:T(8,128)(2,1)S(1)}, u32[]{:S(2)}, u32[]{:S(2)}) collective-permute-start(bf16[2,336,768]{2,1,0:T(8,128)(2,1)} %get-tuple-element.100), channel_id=1, source_target_pairs={{0,4},{1,5},{2,6},{3,7},{4,0},{5,1},{6,2},{7,3},{8,12},{9,13},{10,... | collective-permute-start | bytes 3096584 | tf_op jit(solution)/shard_map/ppermute | solution.py:1484
  317.7 17.7 %collective-permute-start.38 = (bf16[2,240,768]{2,1,0:T(8,128)(2,1)}, bf16[2,240,768]{2,1,0:T(8,128)(2,1)S(1)}, u32[]{:S(2)}, u32[]{:S(2)}) collective-permute-start(bf16[2,240,768]{2,1,0:T(8,128)(2,1)} %get-tuple-element.101), channel_id=1, source_target_pairs={{16,20},{17,21},{18,22},{19,23},{20,16},{21,17},{22,18},{23,19},{2... | collective-permute-start | bytes 2211848 | tf_op jit(solution)/shard_map/ppermute | solution.py:1484
  319.2 10.5 %collective-permute-start.39 = (bf16[208,768]{1,0:T(8,128)(2,1)S(1)}, bf16[208,768]{1,0:T(8,128)(2,1)S(1)}, u32[]{:S(2)}, u32[]{:S(2)}) collective-permute-start(bf16[208,768]{1,0:T(8,128)(2,1)S(1)} %get-tuple-element.120), channel_id=1, source_target_pairs={{0,1},{1,0},{2,3},{3,2},{4,5},{5,4},{6,7},{7,6},{8,9},{9,8},{10,11... | collective-permute-start | bytes 958472 | tf_op jit(solution)/shard_map/ppermute | solution.py:1768
  320.0 15.3 %collective-permute-start.40 = (bf16[208,768]{1,0:T(8,128)(2,1)S(1)}, bf16[208,768]{1,0:T(8,128)(2,1)S(1)}, u32[]{:S(2)}, u32[]{:S(2)}) collective-permute-start(bf16[208,768]{1,0:T(8,128)(2,1)S(1)} %get-tuple-element.119), channel_id=1, source_target_pairs={{0,2},{1,3},{2,0},{3,1},{4,6},{5,7},{6,4},{7,5},{8,10},{9,11},{10,... | collective-permute-start | bytes 958472 | tf_op jit(solution)/shard_map/ppermute | solution.py:1768
  321.3 14.1 %collective-permute-start.41 = (bf16[208,768]{1,0:T(8,128)(2,1)S(1)}, bf16[208,768]{1,0:T(8,128)(2,1)S(1)}, u32[]{:S(2)}, u32[]{:S(2)}) collective-permute-start(bf16[208,768]{1,0:T(8,128)(2,1)S(1)} %get-tuple-element.118), channel_id=1, source_target_pairs={{0,3},{1,2},{2,1},{3,0},{4,7},{5,6},{6,5},{7,4},{8,11},{9,10},{10,... | collective-permute-start | bytes 958472 | tf_op jit(solution)/shard_map/ppermute | solution.py:1768
  329.7 20.2 %collective-permute-start.20 = (bf16[3,128,768]{2,1,0:T(8,128)(2,1)}, bf16[3,128,768]{2,1,0:T(8,128)(2,1)S(1)}, u32[]{:S(2)}, u32[]{:S(2)}) collective-permute-start(bf16[3,128,768]{2,1,0:T(8,128)(2,1)} %bitcast.14.refs_3_), channel_id=1, source_target_pairs={{0,16},{1,17},{2,18},{3,19},{4,20},{5,21},{6,22},{7,23},{8,24},{9,... | collective-permute-start | bytes 1769480 | tf_op jit(solution)/shard_map/ppermute | solution.py:1484
  344.3 24.0 %collective-permute-start.42 = (bf16[336,768]{1,0:T(8,128)(2,1)}, bf16[336,768]{1,0:T(8,128)(2,1)S(1)}, u32[]{:S(2)}, u32[]{:S(2)}) collective-permute-start(bf16[336,768]{1,0:T(8,128)(2,1)} %get-tuple-element.105), channel_id=1, source_target_pairs={{0,16},{16,0},{1,17},{17,1},{2,18},{18,2},{3,19},{19,3},{4,20},{20... | collective-permute-start | bytes 1548296 | tf_op jit(solution)/shard_map/ppermute | solution.py:1488
  344.3 25.5 %collective-permute-start.43 = (bf16[336,768]{1,0:T(8,128)(2,1)}, bf16[336,768]{1,0:T(8,128)(2,1)S(1)}, u32[]{:S(2)}, u32[]{:S(2)}) collective-permute-start(bf16[336,768]{1,0:T(8,128)(2,1)} %get-tuple-element.106), channel_id=1, source_target_pairs={{0,8},{1,9},{2,10},{3,11},{4,12},{5,13},{6,14},{7,15},{8,0},{9,1},... | collective-permute-start | bytes 1548296 | tf_op jit(solution)/shard_map/ppermute | solution.py:1484
  348.6 19.7 %collective-permute-start.44 = (bf16[240,768]{1,0:T(8,128)(2,1)}, bf16[240,768]{1,0:T(8,128)(2,1)S(1)}, u32[]{:S(2)}, u32[]{:S(2)}) collective-permute-start(bf16[240,768]{1,0:T(8,128)(2,1)} %get-tuple-element.107), channel_id=1, source_target_pairs={{16,8},{17,9},{18,10},{19,11},{20,12},{21,13},{22,14},{23,15},{24,... | collective-permute-start | bytes 1105928 | tf_op jit(solution)/shard_map/ppermute | solution.py:1484
  (65 other events, 310.3 us)
Sparse Core Ops, SparseCore 0:
  170.0 86.3 reduce-scatter.1
